TPU v7x, 128 devices: a whole 4x4x4 slice. The times are simulated.
128 devices in a mesh: tm: 16 (over y, z_hi, core), space: 8 (over z_lo, x).
Axes of the slice: x: 4, y: 4, z: 4 (z_hi: 2, z_lo: 2; z = z_hi * 2 + z_lo), core: 2. Of those that a mesh axis runs over, the one named last changes fastest.
Arguments:
- slab_starts: float32 [16, 2, 16, 128, 256], P('tm', None, 'space'), may hold values from 0 to 0.5
- slab_nodes: float32 [16, 2, 2, 16, 128, 256], P('tm', None, None, 'space'), may hold values from 0 to 0.5
- first_slab: int32 [1], replicated, may hold values from 0 to 15
- converged: int32 [2], replicated, may hold values 0 or 1
Outputs:
- new_starts: float32 [16, 2, 16, 128, 256], P('tm', None, 'space')
- new_nodes: float32 [16, 2, 2, 16, 128, 256], P('tm', None, None, 'space')
All inputs are finite; a program needn't handle non-finite values.
Results may differ from a plain program's by a relative error of at most 0.00002.
Values sent between devices are 32-bit elements; how exact they have to be, the bound alone decides.
No kernel may reach another device: no remote copies, remote signals or barrier semaphores. Data moves between devices by JAX's collectives and lax.ppermute only.
A program may use at most 64 MiB of HBM per device.

v0:
```python
import jax
import jax.numpy as jnp
from jax import lax
from jax.sharding import PartitionSpec as P

ITERS = 2


slab_step = 0.5
spread_p = 0.2
spread_v = 0.1
feed_rate = 0.04
kill_rate = 0.06
weight_end = 5.0 / 24.0
weight_mid = 1.0 / 3.0
weight_far = 1.0 / 24.0


def with_halo(block, sides, width):
    for axis, dim in sides:
        count = lax.axis_size(axis)
        forward = [(i, i + 1) for i in range(count - 1)]
        backward = [(target, source) for source, target in forward]
        low = lax.ppermute(
            lax.slice_in_dim(block, block.shape[dim] - width, None, axis=dim), axis, forward
        )
        high = lax.ppermute(lax.slice_in_dim(block, 0, width, axis=dim), axis, backward)
        block = jnp.concatenate([low, block, high], axis=dim)
    return block


def shifted(x, axis, by):
    size = lax.axis_size(axis)
    return lax.ppermute(x, axis, [(i, (i + by) % size) for i in range(size)])


def tendency(field):
    padded = with_halo(field, (("space", 1),), 1)
    interior = padded[:, 1:-1]
    beside = padded[:, 2:] + padded[:, :-2]
    sideways = jnp.pad(interior, ((0, 0), (0, 0), (1, 1), (1, 1)))
    beside = beside + sideways[:, :, 2:, 1:-1] + sideways[:, :, :-2, 1:-1]
    beside = beside + sideways[:, :, 1:-1, 2:] + sideways[:, :, 1:-1, :-2]
    laplace_term = beside - 6.0 * interior
    depleted = interior[0]
    catalyst = interior[1]
    reaction = (1.0 - depleted) * catalyst * catalyst
    rate_p = spread_p * laplace_term[0] + reaction - feed_rate * depleted
    rate_v = spread_v * laplace_term[1] + reaction - (feed_rate + kill_rate) * catalyst
    return jnp.stack([rate_p, rate_v])


def body(slab_starts, slab_nodes, first_slab, converged):
    slab_count = lax.axis_size("tm")
    device_index = lax.axis_index("tm")
    slab_state = slab_starts[0]
    old_one = slab_nodes[0, 0]
    old_two = slab_nodes[0, 1]
    leader = first_slab[0]
    for iteration in range(ITERS):
        conv_flag = converged[iteration]
        position = jnp.mod(device_index - leader, slab_count)
        rate_start = tendency(slab_state)
        rate_one = tendency(old_one)
        rate_two = tendency(old_two)
        node_one = slab_state + slab_step * (
            weight_end * rate_start + weight_mid * rate_one - weight_far * rate_two
        )
        rate_new = tendency(node_one)
        node_two = (
            node_one
            + 0.5 * slab_step * (rate_new - rate_one)
            + slab_step * (-weight_far * rate_start + weight_mid * rate_one + weight_end * rate_two)
        )
        correction = node_two - (slab_state + slab_step * rate_start)

        def chain_step(link_step, current):
            proposal = current + slab_step * tendency(current) + correction
            received = shifted(proposal, "tm", 1)
            target = jnp.mod(link_step + 1, slab_count)
            accept_now = (position == target) & ((link_step + 1 < slab_count) | (conv_flag > 0))
            return jnp.where(accept_now, received, current)

        begin = jnp.where(position == 0, slab_state, 0.0)
        current = lax.fori_loop(0, slab_count, chain_step, begin)
        newest = (position == 0) & (conv_flag > 0)
        slab_state = current
        old_one = jnp.where(newest, current, node_one)
        old_two = jnp.where(newest, current, node_two)
        leader = jnp.mod(leader + conv_flag, slab_count)
    return (slab_state[None], jnp.stack([old_one, old_two])[None])


def solution(mesh):
    placed = (
        P("tm", None, "space", None, None),
        P("tm", None, None, "space", None, None),
        P(),
        P(),
    )
    return jax.shard_map(
        body,
        mesh=mesh,
        in_specs=placed,
        out_specs=(P("tm", None, "space", None, None), P("tm", None, None, "space", None, None)),
        check_vma=False,
    )
```

profile of v0, /device:TPU:1, one launch (start us, length us, event | category | flops | bytes accessed | tf_op | source)
XLA Modules:
  0.0 937.5 jit_solution(17921849523269863443)
XLA Ops:
  36.0 424.9 %while.30 = (s32[]{:T(128)}, f32[2,2,128,256]{3,2,1,0:T(8,128)S(1)}, s32[]{:T(128)}, pred[]{:T(512)}, f32[2,2,128,256]{3,2,1,0:T(8,128)S(1)}, /*index=5*/s32[]{:T(128)}, s32[]{:T(128)}, s32[]{:T(128)}, s32[]{:T(128)}) while((s32[]{:T(128)}, f32[2,2,128,256]{3,2,1,0:T(8,128)S(1)}, s32[]{:T(128)}, pred[]{:T(512)}, ...), condition=%wide.region_1.2_spmd, body=%wide.region_0.1_spmd.sunk | while | flops 2555921 | bytes 12058971 | solution.py:85
  50.6 8.8 collective-permute-start.2
  75.2 6.8 collective-permute-done.1
  94.1 8.5 collective-permute-start
  122.1 6.6 collective-permute-start
  148.2 6.6 collective-permute-start
  174.2 6.6 collective-permute-start
  200.3 6.6 collective-permute-start
  226.4 6.6 collective-permute-start
  252.5 6.6 collective-permute-start
  304.6 6.6 collective-permute-start
  330.7 6.6 collective-permute-start
  356.7 6.6 collective-permute-start
  382.8 6.6 collective-permute-start
  408.9 6.6 collective-permute-start
  435.0 6.6 collective-permute-start
  462.5 7.9 collective-permute-start.15
  481.8 7.4 collective-permute-start.19
  506.2 428.6 %while.31 = (s32[]{:T(128)}, f32[2,2,128,256]{3,2,1,0:T(8,128)S(1)}, s32[]{:T(128)}, pred[]{:T(512)}, f32[2,2,128,256]{3,2,1,0:T(8,128)S(1)}, /*index=5*/s32[]{:T(128)}, s32[]{:T(128)}, s32[]{:T(128)}, s32[]{:T(128)}) while((s32[]{:T(128)}, f32[2,2,128,256]{3,2,1,0:T(8,128)S(1)}, s32[]{:T(128)}, pred[]{:T(512)}, ...), condition=%wide.region_3.4_spmd, body=%wide.region_2.3_spmd.sunk | while | flops 2555921 | bytes 12058971 | solution.py:85
  522.4 13.1 %collective-permute-start.5 = (f32[2,2,128,256]{3,2,1,0:T(8,128)S(1)}, f32[2,2,128,256]{3,2,1,0:T(8,128)S(1)}, u32[]{:S(2)}, u32[]{:S(2)}) collective-permute-start(f32[2,2,128,256]{3,2,1,0:T(8,128)S(1)} %fusion.138), channel_id=1, source_target_pairs={{0,8},{8,16},{16,24},{24,32},{32,40},{40,48},{48,56},{56,64},{64,7... | collective-permute-start | bytes 1572872 | tf_op jit(solution)/shard_map/while/body/eval_jaxpr/ppermute | solution.py:34
  553.9 7.1 collective-permute-done.4
  570.1 8.5 collective-permute-start.3
  674.1 6.6 collective-permute-start.3
  908.8 6.6 collective-permute-start.3
  (419 shorter events, 772.0 us)
Async XLA Ops:
  1.8 12.9 %collective-permute-start.6 = (f32[2,1,128,256]{3,2,1,0:T(8,128)S(1)}, f32[2,1,128,256]{3,2,1,0:T(8,128)S(1)}, u32[]{:S(2)}, u32[]{:S(2)}) collective-permute-start(f32[2,1,128,256]{3,2,1,0:T(8,128)S(1)} %get-tuple-element.349), channel_id=1, source_target_pairs={{1,0},{2,1},{3,2},{4,3},{5,4},{6,5},{7,6},{9,8},{10,9},{11,10},{12... | collective-permute-start | bytes 786440 | tf_op jit(solution)/shard_map/ppermute | solution.py:27
  3.1 15.6 %collective-permute-start.7 = (f32[2,1,128,256]{3,2,1,0:T(8,128)S(1)}, f32[2,1,128,256]{3,2,1,0:T(8,128)S(1)}, u32[]{:S(2)}, u32[]{:S(2)}) collective-permute-start(f32[2,1,128,256]{3,2,1,0:T(8,128)S(1)} %get-tuple-element.350), channel_id=1, source_target_pairs={{0,1},{1,2},{2,3},{3,4},{4,5},{5,6},{6,7},{8,9},{9,10},{10,11},{11... | collective-permute-start | bytes 786440 | tf_op jit(solution)/shard_map/ppermute | solution.py:24
  50.6 14.9 %collective-permute-start.2 = (f32[2,2,128,256]{3,2,1,0:T(8,128)S(1)}, f32[2,2,128,256]{3,2,1,0:T(8,128)S(1)}, u32[]{:S(2)}, u32[]{:S(2)}) collective-permute-start(f32[2,2,128,256]{3,2,1,0:T(8,128)S(1)} %fusion.134), channel_id=1, source_target_pairs={{0,8},{8,16},{16,24},{24,32},{32,40},{40,48},{48,56},{56,64},{64,7... | collective-permute-start | bytes 1572872 | tf_op jit(solution)/shard_map/while/body/eval_jaxpr/ppermute | solution.py:34
  94.1 11.8 %collective-permute-start = (f32[2,1,128,256]{3,2,1,0:T(8,128)S(1)}, f32[2,1,128,256]{3,2,1,0:T(8,128)S(1)}, u32[]{:S(2)}, u32[]{:S(2)}) collective-permute-start(f32[2,1,128,256]{3,2,1,0:T(8,128)S(1)} %get-tuple-element.418), channel_id=1, source_target_pairs={{0,1},{1,2},{2,3},{3,4},{4,5},{5,6},{6,7},{8,9},{9,10},{10,11},{11... | collective-permute-start | bytes 786440 | tf_op jit(solution)/shard_map/while/body/eval_jaxpr/ppermute | solution.py:24
  162.7 11.3 %collective-permute-start.2 = (f32[2,2,128,256]{3,2,1,0:T(8,128)S(1)}, f32[2,2,128,256]{3,2,1,0:T(8,128)S(1)}, u32[]{:S(2)}, u32[]{:S(2)}) collective-permute-start(f32[2,2,128,256]{3,2,1,0:T(8,128)S(1)} %fusion.134), channel_id=1, source_target_pairs={{0,8},{8,16},{16,24},{24,32},{32,40},{40,48},{48,56},{56,64},{64,7... | collective-permute-start | bytes 1572872 | tf_op jit(solution)/shard_map/while/body/eval_jaxpr/ppermute | solution.py:34
  188.8 11.3 %collective-permute-start.2 = (f32[2,2,128,256]{3,2,1,0:T(8,128)S(1)}, f32[2,2,128,256]{3,2,1,0:T(8,128)S(1)}, u32[]{:S(2)}, u32[]{:S(2)}) collective-permute-start(f32[2,2,128,256]{3,2,1,0:T(8,128)S(1)} %fusion.134), channel_id=1, source_target_pairs={{0,8},{8,16},{16,24},{24,32},{32,40},{40,48},{48,56},{56,64},{64,7... | collective-permute-start | bytes 1572872 | tf_op jit(solution)/shard_map/while/body/eval_jaxpr/ppermute | solution.py:34
  267.0 11.3 %collective-permute-start.2 = (f32[2,2,128,256]{3,2,1,0:T(8,128)S(1)}, f32[2,2,128,256]{3,2,1,0:T(8,128)S(1)}, u32[]{:S(2)}, u32[]{:S(2)}) collective-permute-start(f32[2,2,128,256]{3,2,1,0:T(8,128)S(1)} %fusion.134), channel_id=1, source_target_pairs={{0,8},{8,16},{16,24},{24,32},{32,40},{40,48},{48,56},{56,64},{64,7... | collective-permute-start | bytes 1572872 | tf_op jit(solution)/shard_map/while/body/eval_jaxpr/ppermute | solution.py:34
  293.1 11.3 %collective-permute-start.2 = (f32[2,2,128,256]{3,2,1,0:T(8,128)S(1)}, f32[2,2,128,256]{3,2,1,0:T(8,128)S(1)}, u32[]{:S(2)}, u32[]{:S(2)}) collective-permute-start(f32[2,2,128,256]{3,2,1,0:T(8,128)S(1)} %fusion.134), channel_id=1, source_target_pairs={{0,8},{8,16},{16,24},{24,32},{32,40},{40,48},{48,56},{56,64},{64,7... | collective-permute-start | bytes 1572872 | tf_op jit(solution)/shard_map/while/body/eval_jaxpr/ppermute | solution.py:34
  319.1 11.3 %collective-permute-start.2 = (f32[2,2,128,256]{3,2,1,0:T(8,128)S(1)}, f32[2,2,128,256]{3,2,1,0:T(8,128)S(1)}, u32[]{:S(2)}, u32[]{:S(2)}) collective-permute-start(f32[2,2,128,256]{3,2,1,0:T(8,128)S(1)} %fusion.134), channel_id=1, source_target_pairs={{0,8},{8,16},{16,24},{24,32},{32,40},{40,48},{48,56},{56,64},{64,7... | collective-permute-start | bytes 1572872 | tf_op jit(solution)/shard_map/while/body/eval_jaxpr/ppermute | solution.py:34
  345.2 11.3 %collective-permute-start.2 = (f32[2,2,128,256]{3,2,1,0:T(8,128)S(1)}, f32[2,2,128,256]{3,2,1,0:T(8,128)S(1)}, u32[]{:S(2)}, u32[]{:S(2)}) collective-permute-start(f32[2,2,128,256]{3,2,1,0:T(8,128)S(1)} %fusion.134), channel_id=1, source_target_pairs={{0,8},{8,16},{16,24},{24,32},{32,40},{40,48},{48,56},{56,64},{64,7... | collective-permute-start | bytes 1572872 | tf_op jit(solution)/shard_map/while/body/eval_jaxpr/ppermute | solution.py:34
  371.3 11.3 %collective-permute-start.2 = (f32[2,2,128,256]{3,2,1,0:T(8,128)S(1)}, f32[2,2,128,256]{3,2,1,0:T(8,128)S(1)}, u32[]{:S(2)}, u32[]{:S(2)}) collective-permute-start(f32[2,2,128,256]{3,2,1,0:T(8,128)S(1)} %fusion.134), channel_id=1, source_target_pairs={{0,8},{8,16},{16,24},{24,32},{32,40},{40,48},{48,56},{56,64},{64,7... | collective-permute-start | bytes 1572872 | tf_op jit(solution)/shard_map/while/body/eval_jaxpr/ppermute | solution.py:34
  397.4 11.3 %collective-permute-start.2 = (f32[2,2,128,256]{3,2,1,0:T(8,128)S(1)}, f32[2,2,128,256]{3,2,1,0:T(8,128)S(1)}, u32[]{:S(2)}, u32[]{:S(2)}) collective-permute-start(f32[2,2,128,256]{3,2,1,0:T(8,128)S(1)} %fusion.134), channel_id=1, source_target_pairs={{0,8},{8,16},{16,24},{24,32},{32,40},{40,48},{48,56},{56,64},{64,7... | collective-permute-start | bytes 1572872 | tf_op jit(solution)/shard_map/while/body/eval_jaxpr/ppermute | solution.py:34
  423.4 11.3 %collective-permute-start.2 = (f32[2,2,128,256]{3,2,1,0:T(8,128)S(1)}, f32[2,2,128,256]{3,2,1,0:T(8,128)S(1)}, u32[]{:S(2)}, u32[]{:S(2)}) collective-permute-start(f32[2,2,128,256]{3,2,1,0:T(8,128)S(1)} %fusion.134), channel_id=1, source_target_pairs={{0,8},{8,16},{16,24},{24,32},{32,40},{40,48},{48,56},{56,64},{64,7... | collective-permute-start | bytes 1572872 | tf_op jit(solution)/shard_map/while/body/eval_jaxpr/ppermute | solution.py:34
  449.5 11.3 %collective-permute-start.2 = (f32[2,2,128,256]{3,2,1,0:T(8,128)S(1)}, f32[2,2,128,256]{3,2,1,0:T(8,128)S(1)}, u32[]{:S(2)}, u32[]{:S(2)}) collective-permute-start(f32[2,2,128,256]{3,2,1,0:T(8,128)S(1)} %fusion.134), channel_id=1, source_target_pairs={{0,8},{8,16},{16,24},{24,32},{32,40},{40,48},{48,56},{56,64},{64,7... | collective-permute-start | bytes 1572872 | tf_op jit(solution)/shard_map/while/body/eval_jaxpr/ppermute | solution.py:34
  474.6 14.8 %collective-permute-start.16 = (f32[2,1,128,256]{3,2,1,0:T(8,128)S(1)}, f32[2,1,128,256]{3,2,1,0:T(8,128)S(1)}, u32[]{:S(2)}, u32[]{:S(2)}) collective-permute-start(f32[2,1,128,256]{3,2,1,0:T(8,128)S(1)} %get-tuple-element.333), channel_id=1, source_target_pairs={{1,0},{2,1},{3,2},{4,3},{5,4},{6,5},{7,6},{9,8},{10,9},{11,10},{12... | collective-permute-start | bytes 786440 | tf_op jit(solution)/shard_map/ppermute | solution.py:27
  475.9 13.5 %collective-permute-start.17 = (f32[2,1,128,256]{3,2,1,0:T(8,128)S(1)}, f32[2,1,128,256]{3,2,1,0:T(8,128)S(1)}, u32[]{:S(2)}, u32[]{:S(2)}) collective-permute-start(f32[2,1,128,256]{3,2,1,0:T(8,128)S(1)} %get-tuple-element.334), channel_id=1, source_target_pairs={{0,1},{1,2},{2,3},{3,4},{4,5},{5,6},{6,7},{8,9},{9,10},{10,11},{11... | collective-permute-start | bytes 786440 | tf_op jit(solution)/shard_map/ppermute | solution.py:24
  522.4 19.2 %collective-permute-start.5 = (f32[2,2,128,256]{3,2,1,0:T(8,128)S(1)}, f32[2,2,128,256]{3,2,1,0:T(8,128)S(1)}, u32[]{:S(2)}, u32[]{:S(2)}) collective-permute-start(f32[2,2,128,256]{3,2,1,0:T(8,128)S(1)} %fusion.138), channel_id=1, source_target_pairs={{0,8},{8,16},{16,24},{24,32},{32,40},{40,48},{48,56},{56,64},{64,7... | collective-permute-start | bytes 1572872 | tf_op jit(solution)/shard_map/while/body/eval_jaxpr/ppermute | solution.py:34
  541.8 12.1 %collective-permute-start.3 = (f32[2,1,128,256]{3,2,1,0:T(8,128)S(1)}, f32[2,1,128,256]{3,2,1,0:T(8,128)S(1)}, u32[]{:S(2)}, u32[]{:S(2)}) collective-permute-start(f32[2,1,128,256]{3,2,1,0:T(8,128)S(1)} %get-tuple-element.427), channel_id=1, source_target_pairs={{0,1},{1,2},{2,3},{3,4},{4,5},{5,6},{6,7},{8,9},{9,10},{10,11},{11... | collective-permute-start | bytes 786440 | tf_op jit(solution)/shard_map/while/body/eval_jaxpr/ppermute | solution.py:24
  547.9 13.1 %collective-permute-start.4 = (f32[2,1,128,256]{3,2,1,0:T(8,128)S(1)}, f32[2,1,128,256]{3,2,1,0:T(8,128)S(1)}, u32[]{:S(2)}, u32[]{:S(2)}) collective-permute-start(f32[2,1,128,256]{3,2,1,0:T(8,128)S(1)} %get-tuple-element.428), channel_id=1, source_target_pairs={{1,0},{2,1},{3,2},{4,3},{5,4},{6,5},{7,6},{9,8},{10,9},{11,10},{12... | collective-permute-start | bytes 786440 | tf_op jit(solution)/shard_map/while/body/eval_jaxpr/ppermute | solution.py:27
  570.1 14.4 %collective-permute-start.3 = (f32[2,1,128,256]{3,2,1,0:T(8,128)S(1)}, f32[2,1,128,256]{3,2,1,0:T(8,128)S(1)}, u32[]{:S(2)}, u32[]{:S(2)}) collective-permute-start(f32[2,1,128,256]{3,2,1,0:T(8,128)S(1)} %get-tuple-element.427), channel_id=1, source_target_pairs={{0,1},{1,2},{2,3},{3,4},{4,5},{5,6},{6,7},{8,9},{9,10},{10,11},{11... | collective-permute-start | bytes 786440 | tf_op jit(solution)/shard_map/while/body/eval_jaxpr/ppermute | solution.py:24
  598.0 11.8 %collective-permute-start.3 = (f32[2,1,128,256]{3,2,1,0:T(8,128)S(1)}, f32[2,1,128,256]{3,2,1,0:T(8,128)S(1)}, u32[]{:S(2)}, u32[]{:S(2)}) collective-permute-start(f32[2,1,128,256]{3,2,1,0:T(8,128)S(1)} %get-tuple-element.427), channel_id=1, source_target_pairs={{0,1},{1,2},{2,3},{3,4},{4,5},{5,6},{6,7},{8,9},{9,10},{10,11},{11... | collective-permute-start | bytes 786440 | tf_op jit(solution)/shard_map/while/body/eval_jaxpr/ppermute | solution.py:24
  688.7 11.3 %collective-permute-start.5 = (f32[2,2,128,256]{3,2,1,0:T(8,128)S(1)}, f32[2,2,128,256]{3,2,1,0:T(8,128)S(1)}, u32[]{:S(2)}, u32[]{:S(2)}) collective-permute-start(f32[2,2,128,256]{3,2,1,0:T(8,128)S(1)} %fusion.138), channel_id=1, source_target_pairs={{0,8},{8,16},{16,24},{24,32},{32,40},{40,48},{48,56},{56,64},{64,7... | collective-permute-start | bytes 1572872 | tf_op jit(solution)/shard_map/while/body/eval_jaxpr/ppermute | solution.py:34
  714.7 11.3 %collective-permute-start.5 = (f32[2,2,128,256]{3,2,1,0:T(8,128)S(1)}, f32[2,2,128,256]{3,2,1,0:T(8,128)S(1)}, u32[]{:S(2)}, u32[]{:S(2)}) collective-permute-start(f32[2,2,128,256]{3,2,1,0:T(8,128)S(1)} %fusion.138), channel_id=1, source_target_pairs={{0,8},{8,16},{16,24},{24,32},{32,40},{40,48},{48,56},{56,64},{64,7... | collective-permute-start | bytes 1572872 | tf_op jit(solution)/shard_map/while/body/eval_jaxpr/ppermute | solution.py:34
  740.8 11.3 %collective-permute-start.5 = (f32[2,2,128,256]{3,2,1,0:T(8,128)S(1)}, f32[2,2,128,256]{3,2,1,0:T(8,128)S(1)}, u32[]{:S(2)}, u32[]{:S(2)}) collective-permute-start(f32[2,2,128,256]{3,2,1,0:T(8,128)S(1)} %fusion.138), channel_id=1, source_target_pairs={{0,8},{8,16},{16,24},{24,32},{32,40},{40,48},{48,56},{56,64},{64,7... | collective-permute-start | bytes 1572872 | tf_op jit(solution)/shard_map/while/body/eval_jaxpr/ppermute | solution.py:34
  (101 other events, 947.5 us)
where the time goes:
time: 948 us; the launch traced here: 938 us
  starting transfers between devices  475 us (50%)
  waiting for transfers between devices  418 us (44%)
  other arithmetic  34.5 us (4%)
    ppermute x40, starting transfers between devices, with_halo(): lax.ppermute(lax.slice_in_dim(block, block.shape[dim] - width, None, axis...  254 us
    ppermute x32, waiting for transfers between devices, shifted(): return lax.ppermute(x, axis, [(i, (i + by) % size) for i in range(size)])  196 us
    ppermute x32, starting transfers between devices, shifted(): return lax.ppermute(x, axis, [(i, (i + by) % size) for i in range(size)])  169 us
    ppermute x40, waiting for transfers between devices, with_halo(): lax.ppermute(lax.slice_in_dim(block, 0, width, axis=dim), axis, backward)  145 us
    ppermute x40, waiting for transfers between devices, with_halo(): lax.ppermute(lax.slice_in_dim(block, block.shape[dim] - width, None, axis...  77 us
    ppermute x40, starting transfers between devices, with_halo(): lax.ppermute(lax.slice_in_dim(block, 0, width, axis=dim), axis, backward)  51.9 us
  transfers between devices with their start and end apart: 112, of which 103 were waited for; matrix products, arithmetic and copies ran while one was open for 0% of the time, Pallas kernels for 0%

commit v1 on v0

v1 whole, which is shorter than its diff:
```python
import functools

import jax
import jax.numpy as jnp
from jax import lax
from jax.experimental import pallas as pl
from jax.experimental.pallas import tpu as pltpu
from jax.sharding import PartitionSpec as P

SLABS = 16
NX = 16
TILES_Y = 8
TILES_Z = 16
EDGE = 16
RIM = 8
BLOCK = 6
H = 0.5
AXES = ("tm", "space")
F32 = jnp.float32
VMEM_LIMIT = 48 * 1024 * 1024
PLANE = (8, 128)


def device_of(i, j):
    i, j = i % TILES_Y, j % TILES_Z
    zb, x = (0, i) if i < 4 else (1, 7 - i)
    cj = j // 2
    core = (j % 2) ^ (cj % 2)
    za, y = (0, cj) if cj < 4 else (1, 7 - cj)
    zl = za ^ zb
    return (y * 4 + za * 2 + core) * 8 + zl * 4 + x


def own_tile():
    tm, space = lax.axis_index("tm"), lax.axis_index("space")
    y, za, core = tm // 4, (tm // 2) % 2, tm % 2
    zl, x = space // 4, space % 4
    zb = za ^ zl
    ti = jnp.where(zb == 0, x, 7 - x)
    cj = jnp.where(za == 0, y, 7 - y)
    return ti, 2 * cj + (core ^ (cj % 2))


def roll(v, by, axis):
    by %= v.shape[axis]
    return v if by == 0 else pltpu.roll(v, by, axis)


def lanes():
    return lax.broadcasted_iota(jnp.int32, PLANE, 1)


def rows():
    return lax.broadcasted_iota(jnp.int32, PLANE, 0)


def spread_kernel(start_ref, one_ref, two_ref, out_ref, padded):
    lane = lanes()
    column, part = lane % 32, lane // 32
    zero = jnp.zeros(PLANE, F32)
    for half in range(2):
        padded[half, 0:RIM] = zero
        padded[half, RIM + 128 : RIM + 136] = zero
    for array, ref in enumerate((start_ref, one_ref, two_ref)):
        for half in range(2):
            at = (0,) * (len(ref.shape) - 2) + (slice(None), slice(128 * half, 128 * half + 128))
            padded[half, RIM : RIM + 128] = ref[at]

        def tile_row(ti):
            rolled = {}

            def piece(q, half, tj):
                by = (32 * q - EDGE * tj + RIM) % 128
                if (q, half, by) not in rolled:
                    block = padded[half, pl.ds(EDGE * ti + q, 8, stride=4)]
                    rolled[q, half, by] = roll(block, by, 1)
                return rolled[q, half, by]

            for tj in range(TILES_Z):
                value = None
                for q in range(4):
                    if tj == 7:
                        v = jnp.where(column < 24, piece(q, 0, tj), piece(q, 1, tj))
                    elif tj == 8:
                        v = jnp.where(column < 8, piece(q, 0, tj), piece(q, 1, tj))
                    else:
                        v = piece(q, tj // 8, tj)
                    value = v if q == 0 else jnp.where(part == q, v, value)
                if tj == 0:
                    value = jnp.where(column < 8, 0.0, value)
                if tj == 15:
                    value = jnp.where(column < 24, value, 0.0)
                out_ref[device_of(ti, tj), array, 0, 0] = value

        for ti in range(TILES_Y):
            tile_row(ti)


def spread(starts, nodes):
    plane = (1, 1, 128, 256)
    return pl.pallas_call(
        spread_kernel,
        grid=(2, 2),
        in_specs=[
            pl.BlockSpec(plane, lambda f, x: (f, x, 0, 0)),
            pl.BlockSpec((1,) + plane, lambda f, x: (0, f, x, 0, 0)),
            pl.BlockSpec((1,) + plane, lambda f, x: (1, f, x, 0, 0)),
        ],
        out_specs=pl.BlockSpec((128, 3, 1, 1, 8, 128), lambda f, x: (0, 0, f, x, 0, 0)),
        out_shape=jax.ShapeDtypeStruct((128, 3, 2, 2, 8, 128), F32),
        scratch_shapes=[pltpu.VMEM((2, 144, 128), F32)],
        compiler_params=pltpu.CompilerParams(vmem_limit_bytes=VMEM_LIMIT),
        name="spread",
    )(starts, nodes, nodes)


def collect_kernel(in_ref, starts_ref, nodes_ref, planes):
    lane, row = lanes(), rows()
    block = lane // 16
    for array in range(3):
        for ti in range(0, TILES_Y, 2):
            for half in range(2):
                halves = []
                for i in (ti, ti + 1):
                    whole = [None] * 8
                    for t in range(8):
                        v = in_ref[device_of(i, 8 * half + t), array]
                        for k in range(8):
                            moved = roll(v, 16 * (t - k), 1)
                            whole[k] = moved if t == 0 else jnp.where(block == t, moved, whole[k])
                    halves.append(whole)
                for q in range(4):
                    for xp in range(2):
                        low, high = halves[0][2 * q + xp], halves[1][2 * q + xp]
                        fields = (
                            jnp.where(row < 4, low, roll(high, 4, 0)),
                            jnp.where(row < 4, roll(low, 4, 0), high),
                        )
                        for f in range(2):
                            planes[f, xp, half, pl.ds(EDGE * ti + q, 8, stride=4)] = fields[f]
        for f in range(2):
            for xp in range(2):
                for half in range(2):
                    where = (slice(None), slice(128 * half, 128 * half + 128))
                    if array == 0:
                        starts_ref[(f, xp) + where] = planes[f, xp, half]
                    else:
                        nodes_ref[(array - 1, f, xp) + where] = planes[f, xp, half]


def collect(tiles):
    return pl.pallas_call(
        collect_kernel,
        out_shape=(
            jax.ShapeDtypeStruct((2, 2, 128, 256), F32),
            jax.ShapeDtypeStruct((2, 2, 2, 128, 256), F32),
        ),
        in_specs=[pl.BlockSpec(memory_space=pltpu.VMEM)],
        out_specs=(pl.BlockSpec(memory_space=pltpu.VMEM),) * 2,
        scratch_shapes=[pltpu.VMEM((2, 2, 2, 128, 128), F32)],
        compiler_params=pltpu.CompilerParams(vmem_limit_bytes=VMEM_LIMIT),
        name="collect",
    )(tiles)


class Tile:
    def __init__(self, scalars):
        lane, row = lanes(), rows()
        self.lane, self.row = lane, row
        self.not_last, self.not_first = lane < 96, lane >= 32
        y = EDGE * scalars[3] - RIM + 4 * row + lane // 32
        z = EDGE * scalars[4] - RIM + lane % 32
        self.inside = (y >= 0) & (y < 128) & (z >= 0) & (z < 256)

    def around(self, v):
        up, down = roll(v, -32, 1), roll(v, 32, 1)
        up = jnp.where(self.not_last, up, roll(up, -1, 0))
        down = jnp.where(self.not_first, down, roll(down, 1, 0))
        return (roll(v, -1, 1) + roll(v, 1, 1)) + (up + down)

    def tendency(self, load, x):
        mid = [load(f, x) for f in range(2)]
        total = []
        for f in range(2):
            s = self.around(mid[f])
            if x > 0:
                s = s + load(f, x - 1)
            if x < NX - 1:
                s = s + load(f, x + 1)
            total.append(s)
        p, v = mid
        reaction = (1.0 - p) * (v * v)
        rate_p = 0.2 * total[0] + (reaction - 1.24 * p)
        rate_v = 0.1 * total[1] + (reaction - 0.7 * v)
        return (jnp.where(self.inside, rate_p, 0.0), jnp.where(self.inside, rate_v, 0.0)), mid


def sweep_kernel(first, scalars, in_ref, out_ref, one, two, ahead, rate):
    tile = Tile(scalars)

    def old(array):
        return lambda f, x: in_ref[0, x // 2, array, f, x % 2]

    for x in range(NX):
        f0, y0 = tile.tendency(old(0), x)
        f1, _ = tile.tendency(old(1), x)
        f2, _ = tile.tendency(old(2), x)
        for f in range(2):
            one[f, x] = y0[f] + (5 * H / 24) * f0[f] + ((H / 3) * f1[f] - (H / 24) * f2[f])
            out_ref[0, 0, f, x] = (H / 6) * (f1[f] + f2[f]) - (5 * H / 6) * f0[f]
            ahead[f, x] = y0[f] + H * f0[f]
    for x in range(NX):
        r1, _ = tile.tendency(lambda f, x: one[f, x], x)
        for f in range(2):
            correction = out_ref[0, 0, f, x] + (H / 2) * r1[f]
            out_ref[0, 0, f, x] = correction
            two[f, x] = ahead[f, x] + correction
            rate[f, x] = r1[f]
    for x in range(NX):
        r2, _ = tile.tendency(lambda f, x: two[f, x], x)
        for f in range(2):
            r1 = rate[f, x]
            out_ref[0, 1, f, x] = (H / 3) * r1 - (H / 24) * r2[f]
            out_ref[0, 2, f, x] = (H / 6) * (r1 + r2[f])


def sweep(scalars, tiles, first, count):
    def slab(i, s):
        return (lax.rem(s[0] + (first + i), SLABS), 0, 0, 0, 0, 0, 0)

    planes = pltpu.VMEM((2, NX, 8, 128), F32)
    return pl.pallas_call(
        functools.partial(sweep_kernel, first),
        grid_spec=pltpu.PrefetchScalarGridSpec(
            num_scalar_prefetch=1,
            grid=(count,),
            in_specs=[pl.BlockSpec((1, 8, 3, 2, 2, 8, 128), slab)],
            out_specs=pl.BlockSpec((1, 3, 2, NX, 8, 128), lambda i, s: (i, 0, 0, 0, 0, 0)),
            scratch_shapes=[planes] * 4,
        ),
        out_shape=jax.ShapeDtypeStruct((count, 3, 2, NX, 8, 128), F32),
        compiler_params=pltpu.CompilerParams(vmem_limit_bytes=VMEM_LIMIT),
        cost_estimate=pl.CostEstimate(flops=count * 5 * 32 * 1024 * 40, bytes_accessed=count * 1200000, transcendentals=0),
        name=f"sweep_{first}",
    )(scalars, tiles)


def core_pack(tile, load, pair):
    left = tile.lane % 32 < 16
    packed = [jnp.where(left, roll(load(f, 2 * pair), -8, 1), roll(load(f, 2 * pair + 1), 8, 1)) for f in range(2)]
    return jnp.where(tile.row < 4, roll(packed[0], -2, 0), roll(packed[1], 2, 0))


def chain_steps(tile, scalars, first, count, sweeps, z, late, corr, one, two, ahead, packs):
    take_first = scalars[1] > 0

    def step(p, at, final=False):
        now, other = p % 2, (p + 1) % 2
        reset = (p == 0) | ((p == 1) & take_first)
        for x in range(NX):
            fl, l = tile.tendency(lambda f, x: late[other, f, x], x)
            f0, y0 = tile.tendency(lambda f, x: z[now, f, x], x)
            for f in range(2):
                late[now, f, x] = jnp.where(reset, y0[f], l[f] + H * fl[f] + corr[f, x])
                g = y0[f] + H * f0[f]
                ahead[f, x] = g
                if final:
                    one[f, x] = y0[f] + (H / 2) * f0[f]
                    two[f, x] = (-H / 2) * f0[f]
                else:
                    z[other, f, x] = g + sweeps[at, 0, f, x]
                    one[f, x] = y0[f] + (5 * H / 24) * f0[f] + sweeps[at, 1, f, x]
                    two[f, x] = sweeps[at, 2, f, x] - (5 * H / 6) * f0[f]
        for x in range(NX):
            f1, _ = tile.tendency(lambda f, x: one[f, x], x)
            for f in range(2):
                c = two[f, x] + (H / 2) * f1[f]
                corr[f, x] = c
                two[f, x] = ahead[f, x] + c
        for pair in range(8):
            packs[at, pair, 0] = core_pack(tile, lambda f, x: late[now, f, x], pair)
            packs[at, pair, 1] = core_pack(tile, lambda f, x: one[f, x], pair)
            packs[at, pair, 2] = core_pack(tile, lambda f, x: two[f, x], pair)

    def looped(at, carry):
        step(first + at, at)
        return carry

    lax.fori_loop(0, count, looped, 0)
    return step


def send_out(tile, end, z, late, corr, state_ref, low_ref, high_ref):
    now, before = end % 2, (end + 1) % 2
    loads = (lambda f, x: z[now, f, x], lambda f, x: late[before, f, x], lambda f, x: corr[f, x])
    row = tile.row
    for k, load in enumerate(loads):
        for f in range(2):
            for x in range(NX):
                state_ref[k, f, x] = load(f, x)
        for m in range(4):
            a, b = core_pack(tile, load, 2 * m), core_pack(tile, load, 2 * m + 1)
            low = jnp.where(row < 2, a, jnp.where(row < 4, roll(a, -2, 0), jnp.where(row < 6, roll(b, 4, 0), roll(b, 2, 0))))
            high = jnp.where(row < 2, roll(a, -2, 0), jnp.where(row < 4, roll(a, -4, 0), jnp.where(row < 6, roll(b, 2, 0), b)))
            low_ref[4 * k + m] = low
            high_ref[4 * k + m] = high


def take_in(tile, start, z, late, corr, state_ref, got):
    row, column = tile.row, tile.lane % 32
    now, before = start % 2, (start + 1) % 2
    own = (row >= 2) & (row < 6)

    def place(v, at, to):
        return roll(v, to - at, 0)

    def tall(dj, k, f, pair):
        at, where = 4 * (pair % 2) + 2 * f, 4 * k + pair // 2
        top = place(got[-1, dj][where], at, 0)
        bottom = place(got[1, dj][where], at, 6)
        if dj == 0:
            return jnp.where(row < 2, top, bottom)
        low = place(got[0, dj][where], at, 2)
        high = place(got[0, dj][12 + where], at, 4)
        return jnp.where(row < 2, top, jnp.where(row < 4, low, jnp.where(row < 6, high, bottom)))

    for k in range(3):
        for f in range(2):
            for pair in range(8):
                left, mid, right = (tall(dj, k, f, pair) for dj in (-1, 0, 1))
                for xp in range(2):
                    x = 2 * pair + xp
                    centre = jnp.where(own, state_ref[k, f, x], roll(mid, 8 - 16 * xp, 1))
                    v = jnp.where(
                        column < 8,
                        roll(left, -8 - 16 * xp, 1),
                        jnp.where(column < 24, centre, roll(right, 24 - 16 * xp, 1)),
                    )
                    v = jnp.where(tile.inside, v, 0.0)
                    if k == 0:
                        z[now, f, x] = v
                    elif k == 1:
                        late[before, f, x] = v
                    else:
                        corr[f, x] = v


AROUND = [(di, dj) for di in (-1, 0, 1) for dj in (-1, 0, 1) if (di, dj) != (0, 0)]


def chain_kernel(first, count, scalars, sweeps, *refs):
    tile = Tile(scalars)
    last = first + count >= SLABS
    z, late, corr, one, two, ahead = refs[-6:]
    refs = refs[:-6]
    if first == 0:
        start_ref, refs = refs[0], refs[1:]
        for f in range(2):
            for x in range(NX):
                z[0, f, x] = start_ref[0, x // 2, 0, f, x % 2]
    else:
        got = dict(zip(AROUND, refs[1:9], strict=True))
        take_in(tile, first, z, late, corr, refs[0], got)
        refs = refs[9:]
    work = (z, late, corr, one, two, ahead)
    if not last:
        packs, state_ref, low_ref, high_ref = refs
        chain_steps(tile, scalars, first, count, sweeps, *work, packs)
        send_out(tile, first + count, z, late, corr, state_ref, low_ref, high_ref)
        return
    earlier, (out_ref, packs) = refs[:-2], refs[-2:]
    step = chain_steps(tile, scalars, first, count, sweeps, *work, packs)
    step(SLABS, count, final=True)
    end = SLABS % 2
    for x in range(NX):
        fl, l = tile.tendency(lambda f, x: late[end, f, x], x)
        for f in range(2):
            one[f, x] = l[f] + H * fl[f] + corr[f, x]
    leader, conv_one, conv_two = scalars[0], scalars[1] > 0, scalars[2] > 0

    def put(p, source):
        slab = lax.rem(leader + p, SLABS)
        for pair in range(8):
            for array in range(3):
                out_ref[slab * 8 + pair, array] = source(pair, array)

    for b, ref in enumerate(earlier):
        def move(i, carry, b=b, ref=ref):
            put(b * BLOCK + i, lambda pair, array: ref[i, pair, array])
            return carry

        lax.fori_loop(0, BLOCK, move, 0)

    def move_last(i, carry):
        put(first + i, lambda pair, array: packs[i, pair, array])
        return carry

    lax.fori_loop(0, count, move_last, 0)

    @pl.when(conv_one)
    def _():
        put(0, lambda pair, array: packs[count, pair, array])

    @pl.when(conv_two & conv_one)
    def _():
        put(1, lambda pair, array: core_pack(tile, lambda f, x: one[f, x], pair))

    @pl.when(conv_two & jnp.logical_not(conv_one))
    def _():
        put(0, lambda pair, array: packs[count, pair, 0])


def chain(scalars, first, count, sweeps, inputs, in_specs):
    last = first + count >= SLABS
    vmem = pl.BlockSpec(memory_space=pltpu.VMEM)
    if last:
        out_shape = jax.ShapeDtypeStruct((128, 3, 8, 128), F32)
        out_specs = vmem
        scratch = [pltpu.VMEM((count + 1, 8, 3, 8, 128), F32)]
    else:
        out_shape = (
            jax.ShapeDtypeStruct((count, 8, 3, 8, 128), F32),
            jax.ShapeDtypeStruct((3, 2, NX, 8, 128), F32),
            jax.ShapeDtypeStruct((12, 8, 128), F32),
            jax.ShapeDtypeStruct((12, 8, 128), F32),
        )
        out_specs = (vmem,) * 4
        scratch = []
    planes, double = pltpu.VMEM((2, NX, 8, 128), F32), pltpu.VMEM((2, 2, NX, 8, 128), F32)
    return pl.pallas_call(
        functools.partial(chain_kernel, first, count),
        grid_spec=pltpu.PrefetchScalarGridSpec(
            num_scalar_prefetch=1,
            grid=(1,),
            in_specs=[vmem] + in_specs,
            out_specs=out_specs,
            scratch_shapes=scratch + [double, double, planes, planes, planes, planes],
        ),
        out_shape=out_shape,
        compiler_params=pltpu.CompilerParams(vmem_limit_bytes=VMEM_LIMIT),
        name=f"chain_{first}",
    )(scalars, sweeps, *inputs)


def exchange(low, high):
    both = jnp.concatenate([low, high])
    got = []
    for di, dj in AROUND:
        payload = both if di == 0 else (high if di < 0 else low)
        pairs = [(device_of(i + di, j + dj), device_of(i, j)) for i in range(TILES_Y) for j in range(TILES_Z)]
        got.append(lax.ppermute(payload, AXES, pairs))
    return got


def body(slab_starts, slab_nodes, first_slab, converged):
    ti, tj = own_tile()
    scalars = jnp.stack([first_slab[0], converged[0], converged[1], ti.astype(jnp.int32), tj.astype(jnp.int32)])
    vmem = pl.BlockSpec(memory_space=pltpu.VMEM)
    chunks = spread(slab_starts[0], slab_nodes[0])
    tiles = lax.all_to_all(chunks.reshape(128, 96, 128), AXES, 0, 0, tiled=True)
    tiles = tiles.reshape(SLABS, 8, 3, 2, 2, 8, 128)

    sweeps = sweep(scalars, tiles, 0, BLOCK)
    start_spec = pl.BlockSpec((1, 8, 1, 2, 2, 8, 128), lambda i, s: (lax.rem(s[0], SLABS), 0, 0, 0, 0, 0, 0))
    packs_a, state, low, high = chain(scalars, 0, BLOCK, sweeps, [tiles], [start_spec])
    got = exchange(low, high)
    sweeps = sweep(scalars, tiles, BLOCK, BLOCK)
    last_sweeps = sweep(scalars, tiles, 2 * BLOCK, SLABS - 2 * BLOCK)
    packs_b, state, low, high = chain(scalars, BLOCK, BLOCK, sweeps, [state, *got], [vmem] * 9)
    got = exchange(low, high)
    out = chain(
        scalars, 2 * BLOCK, SLABS - 2 * BLOCK, last_sweeps, [state, *got, packs_a, packs_b], [vmem] * 11
    )
    out = lax.all_to_all(out.reshape(128, 24, 128), AXES, 0, 0, tiled=True)
    starts, nodes = collect(out.reshape(128, 3, 8, 128))
    return starts[None], nodes[None]


def solution(mesh):
    slab_spec = P("tm", None, "space", None, None)
    node_spec = P("tm", None, None, "space", None, None)
    return jax.shard_map(
        body,
        mesh=mesh,
        in_specs=(slab_spec, node_spec, P(), P()),
        out_specs=(slab_spec, node_spec),
        check_vma=False,
    )
```

time: 948 us -> 199 us (0.21); the launches traced: 938 us -> 198 us
  starting transfers between devices: 475 us -> 31.9 us
  waiting for transfers between devices: 418 us -> 83.6 us
  Pallas kernels: 0 us -> 44 us
  blocking collectives: 0 us -> 34.7 us
  other arithmetic: 34.5 us -> 0.08 us
    ppermute x112 -> x16, starting transfers between devices: 475 us -> 20 us  [exchange(): got.append(lax.ppermute(payload, AXES, pairs))]
    ppermute x112 -> x16, waiting for transfers between devices: 418 us -> 5.07 us  [exchange(): got.append(lax.ppermute(payload, AXES, pairs))]
    all_to_all x0 -> x1, waiting for transfers between devices: none -> 78.6 us  [body(): tiles = lax.all_to_all(chunks.reshape(128, 96, 128), AXES, 0, 0, tiled=True)]
    pallas_call x0 -> x8, Pallas kernels: none -> 44 us  [the longest x3 18.2 us: sweep(): pl.pallas_call(functools.partial(sweep_kernel, first), grid_spec=pltpu.Pr...]
    all_to_all x0 -> x1, blocking collectives: none -> 34.7 us  [body(): out = lax.all_to_all(out.reshape(128, 24, 128), AXES, 0, 0, tiled=True)]
    sub x80 -> x0, other arithmetic: 22.9 us -> none  [the longest x39 15.6 us: tendency(): laplace_term = beside - 6.0 * interior]
    all_to_all x0 -> x1, starting transfers between devices: none -> 11.9 us  [body(): tiles = lax.all_to_all(chunks.reshape(128, 96, 128), AXES, 0, 0, tiled=True)]
  transfers between devices with their start and end apart: 112 -> 17, of which waited for: 103 -> 3; matrix products, arithmetic and copies ran while one was open for 0% -> 0% of each run, Pallas kernels for 0% -> 6%
where the time goes in v1:
time: 199 us; the launch traced here: 198 us
  waiting for transfers between devices  83.6 us (42%)
  Pallas kernels  44 us (22%)
  blocking collectives  34.7 us (17%)
  starting transfers between devices  31.9 us (16%)
  local copies, waits for them, and re-layouts  2.28 us (1%)
    all_to_all x1, waiting for transfers between devices, body(): tiles = lax.all_to_all(chunks.reshape(128, 96, 128), AXES, 0, 0, tiled=True)  78.6 us
    all_to_all x1, blocking collectives, body(): out = lax.all_to_all(out.reshape(128, 24, 128), AXES, 0, 0, tiled=True)  34.7 us
    ppermute x16, starting transfers between devices, exchange(): got.append(lax.ppermute(payload, AXES, pairs))  20 us
    pallas_call x3, Pallas kernels, sweep(): pl.pallas_call(functools.partial(sweep_kernel, first), grid_spec=pltpu.Pr...  18.2 us
    pallas_call x3, Pallas kernels, chain(): pl.pallas_call(functools.partial(chain_kernel, first, count), grid_spec=p...  13.8 us
    all_to_all x1, starting transfers between devices, body(): tiles = lax.all_to_all(chunks.reshape(128, 96, 128), AXES, 0, 0, tiled=True)  11.9 us
    pallas_call x1, Pallas kernels, spread(): pl.pallas_call(spread_kernel, grid=(2, 2), in_specs=[pl.BlockSpec(plane,...  8.08 us
    ppermute x16, waiting for transfers between devices, exchange(): got.append(lax.ppermute(payload, AXES, pairs))  5.07 us
  transfers between devices with their start and end apart: 17, of which 3 were waited for; matrix products, arithmetic and copies ran while one was open for 0% of the time, Pallas kernels for 6%

profile of v1, /device:TPU:1, one launch (start us, length us, event | category | flops | bytes accessed | tf_op | source)
XLA Modules:
  0.0 198.2 jit_solution(16959789860765540523)
XLA Ops:
  0.6 1.2 copy-done
  1.9 1.0 copy-done.1
  2.9 8.1 %spread.1 = f32[128,3,2,2,8,128]{5,4,3,2,1,0:T(8,128)} custom-call(f32[2,2,128,256]{3,2,1,0:T(8,128)S(1)} %bitcast.14, f32[2,2,2,128,256]{4,3,2,1,0:T(8,128)S(1)} %bitcast.12, f32[2,2,2,128,256]{4,3,2,1,0:T(8,128)S(1)} %bitcast.13), custom_call_target="tpu_custom_call" | custom-call | tf_op jit(solution)/shard_map/spread/pallas_call | solution.py:101
  11.0 11.9 %all-to-all-start = ((f32[128,96,128]{2,1,0:T(8,128)}), f32[128,96,128]{2,1,0:T(8,128)}, u32[]{:S(2)}, u32[]{:S(2)}) async-start(f32[128,96,128]{2,1,0:T(8,128)} %bitcast.15), calls=%async_computation | async-start | bytes 12582912 | tf_op jit(solution)/shard_map/all_to_all | solution.py:460
  23.7 78.6 %all-to-all-done = f32[128,96,128]{2,1,0:T(8,128)} async-done(((f32[128,96,128]{2,1,0:T(8,128)}), f32[128,96,128]{2,1,0:T(8,128)}, u32[]{:S(2)}, u32[]{:S(2)}) %all-to-all-start) | async-done | bytes 6291488 | tf_op jit(solution)/shard_map/all_to_all | solution.py:460
  102.3 6.6 %sweep_0.1.sweeps = f32[6,3,2,16,8,128]{5,4,3,2,1,0:T(8,128)S(1)} custom-call(s32[5]{0:T(128)S(1)} %pad_add_fusion.scalars, f32[16,8,3,2,2,8,128]{6,5,4,3,2,1,0:T(8,128)} %bitcast.5.in_ref.refs_0_), custom_call_target="tpu_custom_call" | custom-call | flops 39321600 | bytes 7200000 | tf_op jit(solution)/shard_map/sweep_0/pallas_call | solution.py:232
  108.9 5.1 %chain_0.1 = (f32[6,8,3,8,128]{4,3,2,1,0:T(8,128)S(1)}, f32[3,2,16,8,128]{4,3,2,1,0:T(8,128)S(1)}, f32[12,8,128]{2,1,0:T(8,128)S(1)}, f32[12,8,128]{2,1,0:T(8,128)S(1)}) custom-call(s32[5]{0:T(128)S(1)} %pad_add_fusion.scalars, f32[6,3,2,16,8,128]{5,4,3,2,1,0:T(8,128)S(1)} %sweep_0.1.sweeps, f32[16,8,3,2,2,8,128]{6,5,4,3,2,1,0:T(8,128)} %bitcast.5.in_ref.refs_0_), custom_call_target="tpu_custom_call" | custom-call | tf_op jit(solution)/shard_map/chain_0/pallas_call | solution.py:430
  114.0 0.3 collective-permute-start.2
  114.3 6.5 %collective-permute-start = (f32[12,8,128]{2,1,0:T(8,128)S(1)}, f32[12,8,128]{2,1,0:T(8,128)S(1)}, u32[]{:S(2)}, u32[]{:S(2)}) collective-permute-start(f32[12,8,128]{2,1,0:T(8,128)S(1)} %get-tuple-element.13), channel_id=1, source_target_pairs={{16,0},{4,8},{12,40},{44,32},{36,64},{68,72},{76,104},{108,96},{10... | collective-permute-start | bytes 147464 | tf_op jit(solution)/shard_map/ppermute | solution.py:451
  120.8 0.2 collective-permute-start.4
  121.0 1.3 collective-permute-start.3
  122.4 0.1 collective-permute-start.5
  122.5 6.6 %sweep_6.1.sweeps = f32[6,3,2,16,8,128]{5,4,3,2,1,0:T(8,128)S(1)} custom-call(s32[5]{0:T(128)S(1)} %pad_add_fusion.scalars, f32[16,8,3,2,2,8,128]{6,5,4,3,2,1,0:T(8,128)} %bitcast.5.in_ref.refs_0_), custom_call_target="tpu_custom_call" | custom-call | flops 39321600 | bytes 7200000 | tf_op jit(solution)/shard_map/sweep_6/pallas_call | solution.py:232
  129.2 1.3 collective-permute-done.5.refs_6_
  130.5 4.5 %chain_6.1 = (f32[6,8,3,8,128]{4,3,2,1,0:T(8,128)S(1)}, f32[3,2,16,8,128]{4,3,2,1,0:T(8,128)S(1)}, f32[12,8,128]{2,1,0:T(8,128)S(1)}, f32[12,8,128]{2,1,0:T(8,128)S(1)}) custom-call(s32[5]{0:T(128)S(1)} %pad_add_fusion.scalars, f32[6,3,2,16,8,128]{5,4,3,2,1,0:T(8,128)S(1)} %sweep_6.1.sweeps, f32[3,2,16,8,128]{4,3,2,1,0:T(8,128)S(1)} %get-tuple-element.12.refs_0_, ...), custom_call_target="tpu_custom_call" | custom-call | tf_op jit(solution)/shard_map/chain_6/pallas_call | solution.py:430
  135.0 3.8 %collective-permute-start.10 = (f32[12,8,128]{2,1,0:T(8,128)S(1)}, f32[12,8,128]{2,1,0:T(8,128)S(1)}, u32[]{:S(2)}, u32[]{:S(2)}) collective-permute-start(f32[12,8,128]{2,1,0:T(8,128)S(1)} %get-tuple-element.16), channel_id=1, source_target_pairs={{12,0},{44,8},{36,40},{68,32},{76,64},{108,72},{100,104},{112,96},... | collective-permute-start | bytes 147464 | tf_op jit(solution)/shard_map/ppermute | solution.py:451
  138.8 1.7 collective-permute-start.9
  140.5 2.9 %collective-permute-start.12 = (f32[24,8,128]{2,1,0:T(8,128)S(1)}, f32[24,8,128]{2,1,0:T(8,128)S(1)}, u32[]{:S(2)}, u32[]{:S(2)}) collective-permute-start(f32[24,8,128]{2,1,0:T(8,128)S(1)} %constant_dynamic-update-slice_fusion.2), channel_id=1, source_target_pairs={{8,0},{40,8},{32,40},{64,32},{72,64},{104,72},{96,104},{116,96},{1... | collective-permute-start | bytes 294920 | tf_op jit(solution)/shard_map/ppermute | solution.py:451
  143.4 3.1 %collective-permute-start.15 = (f32[12,8,128]{2,1,0:T(8,128)S(1)}, f32[12,8,128]{2,1,0:T(8,128)S(1)}, u32[]{:S(2)}, u32[]{:S(2)}) collective-permute-start(f32[12,8,128]{2,1,0:T(8,128)S(1)} %get-tuple-element.17), channel_id=1, source_target_pairs={{9,0},{41,8},{33,40},{65,32},{73,64},{105,72},{97,104},{117,96},{1... | collective-permute-start | bytes 147464 | tf_op jit(solution)/shard_map/ppermute | solution.py:451
  146.6 4.9 %sweep_12.1.sweeps = f32[4,3,2,16,8,128]{5,4,3,2,1,0:T(8,128)S(1)} custom-call(s32[5]{0:T(128)S(1)} %pad_add_fusion.scalars, f32[16,8,3,2,2,8,128]{6,5,4,3,2,1,0:T(8,128)} %bitcast.5.in_ref.refs_0_), custom_call_target="tpu_custom_call" | custom-call | flops 26214400 | bytes 4800000 | tf_op jit(solution)/shard_map/sweep_12/pallas_call | solution.py:232
  151.5 3.7 %collective-permute-done.13.refs_6_ = f32[12,8,128]{2,1,0:T(8,128)S(1)} collective-permute-done((f32[12,8,128]{2,1,0:T(8,128)S(1)}, f32[12,8,128]{2,1,0:T(8,128)S(1)}, u32[]{:S(2)}, u32[]{:S(2)}) %collective-permute-start.13) | collective-permute-done | bytes 49184 | tf_op jit(solution)/shard_map/ppermute | solution.py:451
  155.3 4.1 %chain_12.1 = f32[128,3,8,128]{3,2,1,0:T(8,128)S(1)} custom-call(s32[5]{0:T(128)S(1)} %pad_add_fusion.scalars, f32[4,3,2,16,8,128]{5,4,3,2,1,0:T(8,128)S(1)} %sweep_12.1.sweeps, f32[3,2,16,8,128]{4,3,2,1,0:T(8,128)S(1)} %get-tuple-element.15.refs_0_, f32[12,8,128]{2,1,0:T(8,128)S(1)} %collective-permute-done.8.refs_1_, ...), custom_call_target="tpu_custom_call" | custom-call | tf_op jit(solution)/shard_map/chain_12/pallas_call | solution.py:430
  159.4 34.7 %all_to_all.10 = f32[128,24,128]{2,1,0:T(8,128)S(1)} all-to-all(f32[128,24,128]{2,1,0:T(8,128)S(1)} %bitcast.11), channel_id=1, replica_groups=mesh['tm'=16,'space'=8] {'tm','space'}, dimensions={0} | all-to-all | bytes 3145728 | tf_op jit(solution)/shard_map/all_to_all | solution.py:474
  194.1 4.0 %collect.1 = (f32[2,2,128,256]{3,2,1,0:T(8,128)}, f32[2,2,2,128,256]{4,3,2,1,0:T(8,128)}) custom-call(f32[128,3,8,128]{3,2,1,0:T(8,128)S(1)} %bitcast.10), custom_call_target="tpu_custom_call" | custom-call | tf_op jit(solution)/shard_map/collect/pallas_call | solution.py:152
  (30 shorter events, 0.3 us)
Async XLA Ops:
  0.6 1.2 copy-start
  1.9 1.0 copy-start.1
  11.0 12.6 %copy-start.2 = (s32[2]{0:T(128)S(1)}, s32[2]{0:T(128)}, u32[]{:S(2)}) copy-start(s32[2]{0:T(128)} %param.7) | copy-start | bytes 28
  11.0 91.3 %all-to-all-start = ((f32[128,96,128]{2,1,0:T(8,128)}), f32[128,96,128]{2,1,0:T(8,128)}, u32[]{:S(2)}, u32[]{:S(2)}) async-start(f32[128,96,128]{2,1,0:T(8,128)} %bitcast.15), calls=%async_computation | async-start | bytes 12582912 | tf_op jit(solution)/shard_map/all_to_all | solution.py:460
  114.0 8.3 %collective-permute-start.2 = (f32[12,8,128]{2,1,0:T(8,128)S(1)}, f32[12,8,128]{2,1,0:T(8,128)S(1)}, u32[]{:S(2)}, u32[]{:S(2)}) collective-permute-start(f32[12,8,128]{2,1,0:T(8,128)S(1)} %get-tuple-element.13), channel_id=1, source_target_pairs={{12,0},{44,8},{36,40},{68,32},{76,64},{108,72},{100,104},{112,96},... | collective-permute-start | bytes 147464 | tf_op jit(solution)/shard_map/ppermute | solution.py:451
  114.3 8.0 %collective-permute-start.1 = (f32[12,8,128]{2,1,0:T(8,128)S(1)}, f32[12,8,128]{2,1,0:T(8,128)S(1)}, u32[]{:S(2)}, u32[]{:S(2)}) collective-permute-start(f32[12,8,128]{2,1,0:T(8,128)S(1)} %get-tuple-element.13), channel_id=1, source_target_pairs={{4,0},{12,8},{44,40},{36,32},{68,64},{76,72},{108,104},{100,96},{1... | collective-permute-start | bytes 147464 | tf_op jit(solution)/shard_map/ppermute | solution.py:451
  114.3 8.1 %collective-permute-start = (f32[12,8,128]{2,1,0:T(8,128)S(1)}, f32[12,8,128]{2,1,0:T(8,128)S(1)}, u32[]{:S(2)}, u32[]{:S(2)}) collective-permute-start(f32[12,8,128]{2,1,0:T(8,128)S(1)} %get-tuple-element.13), channel_id=1, source_target_pairs={{16,0},{4,8},{12,40},{44,32},{36,64},{68,72},{76,104},{108,96},{10... | collective-permute-start | bytes 147464 | tf_op jit(solution)/shard_map/ppermute | solution.py:451
  120.8 9.7 %collective-permute-start.4 = (f32[24,8,128]{2,1,0:T(8,128)S(1)}, f32[24,8,128]{2,1,0:T(8,128)S(1)}, u32[]{:S(2)}, u32[]{:S(2)}) collective-permute-start(f32[24,8,128]{2,1,0:T(8,128)S(1)} %constant_dynamic-update-slice_fusion), channel_id=1, source_target_pairs={{8,0},{40,8},{32,40},{64,32},{72,64},{104,72},{96,104},{116,96},{1... | collective-permute-start | bytes 294920 | tf_op jit(solution)/shard_map/ppermute | solution.py:451
  121.0 9.5 %collective-permute-start.3 = (f32[24,8,128]{2,1,0:T(8,128)S(1)}, f32[24,8,128]{2,1,0:T(8,128)S(1)}, u32[]{:S(2)}, u32[]{:S(2)}) collective-permute-start(f32[24,8,128]{2,1,0:T(8,128)S(1)} %constant_dynamic-update-slice_fusion), channel_id=1, source_target_pairs={{20,0},{0,8},{8,40},{40,32},{32,64},{64,72},{72,104},{104,96},{96,... | collective-permute-start | bytes 294920 | tf_op jit(solution)/shard_map/ppermute | solution.py:451
  122.3 6.8 %collective-permute-start.7 = (f32[12,8,128]{2,1,0:T(8,128)S(1)}, f32[12,8,128]{2,1,0:T(8,128)S(1)}, u32[]{:S(2)}, u32[]{:S(2)}) collective-permute-start(f32[12,8,128]{2,1,0:T(8,128)S(1)} %get-tuple-element.14), channel_id=1, source_target_pairs={{9,0},{41,8},{33,40},{65,32},{73,64},{105,72},{97,104},{117,96},{1... | collective-permute-start | bytes 147464 | tf_op jit(solution)/shard_map/ppermute | solution.py:451
  122.3 6.9 %collective-permute-start.6 = (f32[12,8,128]{2,1,0:T(8,128)S(1)}, f32[12,8,128]{2,1,0:T(8,128)S(1)}, u32[]{:S(2)}, u32[]{:S(2)}) collective-permute-start(f32[12,8,128]{2,1,0:T(8,128)S(1)} %get-tuple-element.14), channel_id=1, source_target_pairs={{1,0},{9,8},{41,40},{33,32},{65,64},{73,72},{105,104},{97,96},{117... | collective-permute-start | bytes 147464 | tf_op jit(solution)/shard_map/ppermute | solution.py:451
  122.4 8.1 %collective-permute-start.5 = (f32[12,8,128]{2,1,0:T(8,128)S(1)}, f32[12,8,128]{2,1,0:T(8,128)S(1)}, u32[]{:S(2)}, u32[]{:S(2)}) collective-permute-start(f32[12,8,128]{2,1,0:T(8,128)S(1)} %get-tuple-element.14), channel_id=1, source_target_pairs={{21,0},{1,8},{9,40},{41,32},{33,64},{65,72},{73,104},{105,96},{97,... | collective-permute-start | bytes 147464 | tf_op jit(solution)/shard_map/ppermute | solution.py:451
  135.0 8.4 %collective-permute-start.10 = (f32[12,8,128]{2,1,0:T(8,128)S(1)}, f32[12,8,128]{2,1,0:T(8,128)S(1)}, u32[]{:S(2)}, u32[]{:S(2)}) collective-permute-start(f32[12,8,128]{2,1,0:T(8,128)S(1)} %get-tuple-element.16), channel_id=1, source_target_pairs={{12,0},{44,8},{36,40},{68,32},{76,64},{108,72},{100,104},{112,96},... | collective-permute-start | bytes 147464 | tf_op jit(solution)/shard_map/ppermute | solution.py:451
  138.8 7.7 %collective-permute-start.9 = (f32[12,8,128]{2,1,0:T(8,128)S(1)}, f32[12,8,128]{2,1,0:T(8,128)S(1)}, u32[]{:S(2)}, u32[]{:S(2)}) collective-permute-start(f32[12,8,128]{2,1,0:T(8,128)S(1)} %get-tuple-element.16), channel_id=1, source_target_pairs={{4,0},{12,8},{44,40},{36,32},{68,64},{76,72},{108,104},{100,96},{1... | collective-permute-start | bytes 147464 | tf_op jit(solution)/shard_map/ppermute | solution.py:451
  140.5 6.1 %collective-permute-start.8 = (f32[12,8,128]{2,1,0:T(8,128)S(1)}, f32[12,8,128]{2,1,0:T(8,128)S(1)}, u32[]{:S(2)}, u32[]{:S(2)}) collective-permute-start(f32[12,8,128]{2,1,0:T(8,128)S(1)} %get-tuple-element.16), channel_id=1, source_target_pairs={{16,0},{4,8},{12,40},{44,32},{36,64},{68,72},{76,104},{108,96},{10... | collective-permute-start | bytes 147464 | tf_op jit(solution)/shard_map/ppermute | solution.py:451
  140.5 14.8 %collective-permute-start.12 = (f32[24,8,128]{2,1,0:T(8,128)S(1)}, f32[24,8,128]{2,1,0:T(8,128)S(1)}, u32[]{:S(2)}, u32[]{:S(2)}) collective-permute-start(f32[24,8,128]{2,1,0:T(8,128)S(1)} %constant_dynamic-update-slice_fusion.2), channel_id=1, source_target_pairs={{8,0},{40,8},{32,40},{64,32},{72,64},{104,72},{96,104},{116,96},{1... | collective-permute-start | bytes 294920 | tf_op jit(solution)/shard_map/ppermute | solution.py:451
  143.4 11.8 %collective-permute-start.11 = (f32[24,8,128]{2,1,0:T(8,128)S(1)}, f32[24,8,128]{2,1,0:T(8,128)S(1)}, u32[]{:S(2)}, u32[]{:S(2)}) collective-permute-start(f32[24,8,128]{2,1,0:T(8,128)S(1)} %constant_dynamic-update-slice_fusion.2), channel_id=1, source_target_pairs={{20,0},{0,8},{8,40},{40,32},{32,64},{64,72},{72,104},{104,96},{96,... | collective-permute-start | bytes 294920 | tf_op jit(solution)/shard_map/ppermute | solution.py:451
  143.4 8.1 %collective-permute-start.15 = (f32[12,8,128]{2,1,0:T(8,128)S(1)}, f32[12,8,128]{2,1,0:T(8,128)S(1)}, u32[]{:S(2)}, u32[]{:S(2)}) collective-permute-start(f32[12,8,128]{2,1,0:T(8,128)S(1)} %get-tuple-element.17), channel_id=1, source_target_pairs={{9,0},{41,8},{33,40},{65,32},{73,64},{105,72},{97,104},{117,96},{1... | collective-permute-start | bytes 147464 | tf_op jit(solution)/shard_map/ppermute | solution.py:451
  146.5 5.0 %collective-permute-start.14 = (f32[12,8,128]{2,1,0:T(8,128)S(1)}, f32[12,8,128]{2,1,0:T(8,128)S(1)}, u32[]{:S(2)}, u32[]{:S(2)}) collective-permute-start(f32[12,8,128]{2,1,0:T(8,128)S(1)} %get-tuple-element.17), channel_id=1, source_target_pairs={{1,0},{9,8},{41,40},{33,32},{65,64},{73,72},{105,104},{97,96},{117... | collective-permute-start | bytes 147464 | tf_op jit(solution)/shard_map/ppermute | solution.py:451
  146.5 8.7 %collective-permute-start.13 = (f32[12,8,128]{2,1,0:T(8,128)S(1)}, f32[12,8,128]{2,1,0:T(8,128)S(1)}, u32[]{:S(2)}, u32[]{:S(2)}) collective-permute-start(f32[12,8,128]{2,1,0:T(8,128)S(1)} %get-tuple-element.17), channel_id=1, source_target_pairs={{21,0},{1,8},{9,40},{41,32},{33,64},{65,72},{73,104},{105,96},{97,... | collective-permute-start | bytes 147464 | tf_op jit(solution)/shard_map/ppermute | solution.py:451

commit v2 on v0

v2 whole, which is shorter than its diff:
```python
import functools

import jax
import jax.numpy as jnp
from jax import lax
from jax.experimental import pallas as pl
from jax.experimental.pallas import tpu as pltpu
from jax.sharding import PartitionSpec as P

SLABS = 16
TILES_Y = 8
TILES_Z = 16
EDGE = 16
RIM = 8
BLOCK = 6
H = 0.5
AXES = ("tm", "space")
F32 = jnp.float32
VMEM_LIMIT = 40 * 1024 * 1024
SHAPE = (8, 128)
SLAB_ROWS = 192
AROUND = [(di, dj) for di in (-1, 0, 1) for dj in (-1, 0, 1) if (di, dj) != (0, 0)]


def device_of(i, j):
    i, j = i % TILES_Y, j % TILES_Z
    zb, x = (0, i) if i < 4 else (1, 7 - i)
    cj = j // 2
    core = (j % 2) ^ (cj % 2)
    za, y = (0, cj) if cj < 4 else (1, 7 - cj)
    zl = za ^ zb
    return (y * 4 + za * 2 + core) * 8 + zl * 4 + x


def own_tile():
    tm, space = lax.axis_index("tm"), lax.axis_index("space")
    y, za, core = tm // 4, (tm // 2) % 2, tm % 2
    zl, x = space // 4, space % 4
    zb = za ^ zl
    ti = jnp.where(zb == 0, x, 7 - x)
    cj = jnp.where(za == 0, y, 7 - y)
    return ti, 2 * cj + (core ^ (cj % 2))


def roll(v, by, axis=1):
    by %= v.shape[axis]
    return v if by == 0 else pltpu.roll(v, by, axis)


def lanes():
    return lax.broadcasted_iota(jnp.int32, SHAPE, 1)


def rows():
    return lax.broadcasted_iota(jnp.int32, SHAPE, 0)


def swap_bits(arrays, pairs):
    arrays, lane = list(arrays), lanes()
    for index_bit, lane_bit in pairs:
        step, low = 1 << lane_bit, (lane >> lane_bit) % 2 == 0
        for a in range(len(arrays)):
            b = a | (1 << index_bit)
            if a != b:
                u, v = arrays[a], arrays[b]
                arrays[a] = jnp.where(low, u, roll(v, step))
                arrays[b] = jnp.where(low, roll(u, -step), v)
    return arrays


def turn_pairs(v):
    v = roll(v, 4, 0)
    return jnp.where(rows() // 2 % 2 == 0, roll(v, -2, 0), roll(v, 2, 0))


def spread_kernel(starts_ref, nodes_ref, out_ref, planes):
    for array in range(3):
        for f in range(2):
            for xp in range(2):
                for half in range(2):
                    z = slice(128 * half, 128 * half + 128)
                    planes[f, xp, half] = starts_ref[f, xp, :, z] if array == 0 else nodes_ref[array - 1, f, xp, :, z]
        for f in range(2):
            for half in range(2):
                for upper in range(2):
                    loads = [
                        planes[f, xp, half, pl.ds(64 * upper + ys, 8, stride=8)] for ys in range(8) for xp in range(2)
                    ]
                    for k, v in enumerate(swap_bits(loads, [(3, 6), (2, 5), (1, 4), (0, 3)])):
                        tj, rz = 8 * half + k // 2, k % 2
                        device = device_of(7 if upper else 0, tj)
                        at = device * 24 + array * 4 + f * 2 + rz
                        out_ref[pl.ds(at, 8, stride=12)] = turn_pairs(v) if upper else v


def spread(starts, nodes):
    vmem = pl.BlockSpec(memory_space=pltpu.VMEM)
    return pl.pallas_call(
        spread_kernel,
        in_specs=[vmem, vmem],
        out_specs=vmem,
        out_shape=jax.ShapeDtypeStruct((128 * 24, 128), F32),
        scratch_shapes=[pltpu.VMEM((2, 2, 2, 128, 128), F32)],
        compiler_params=pltpu.CompilerParams(vmem_limit_bytes=VMEM_LIMIT),
        name="spread",
    )(starts, nodes)


def collect_kernel(in_ref, starts_ref, nodes_ref, planes):
    for array in range(3):
        for f in range(2):
            for xp in range(2):
                for half in range(2):
                    for upper in range(2):
                        loads = []
                        for t in range(8):
                            device = device_of(7 if upper else 0, 8 * half + t)
                            v = in_ref[pl.ds(device * 24 + array * 4 + f * 2 + xp, 8, stride=12)]
                            loads.append(turn_pairs(v) if upper else v)
                        for ys, v in enumerate(swap_bits(loads, [(2, 6), (1, 5), (0, 4)])):
                            planes[f, xp, half, pl.ds(64 * upper + ys, 8, stride=8)] = v
                    z = slice(128 * half, 128 * half + 128)
                    if array == 0:
                        starts_ref[f, xp, :, z] = planes[f, xp, half]
                    else:
                        nodes_ref[array - 1, f, xp, :, z] = planes[f, xp, half]


def collect(tiles):
    vmem = pl.BlockSpec(memory_space=pltpu.VMEM)
    return pl.pallas_call(
        collect_kernel,
        out_shape=(
            jax.ShapeDtypeStruct((2, 2, 128, 256), F32),
            jax.ShapeDtypeStruct((2, 2, 2, 128, 256), F32),
        ),
        in_specs=[vmem],
        out_specs=(vmem, vmem),
        scratch_shapes=[pltpu.VMEM((2, 2, 2, 128, 128), F32)],
        compiler_params=pltpu.CompilerParams(vmem_limit_bytes=VMEM_LIMIT),
        name="collect",
    )(tiles)


def deal_kernel(scalars, in_ref, low_ref, high_ref, left_ref, right_ref):
    for u in range(6):
        for ry, y_ref in enumerate((low_ref, high_ref)):
            for rz, z_ref in enumerate((left_ref, right_ref)):
                v = in_ref[pl.ds(ry * 12 + 2 * u + rz, 8, stride=24)]
                y_ref[rz, 0, u] = v
                z_ref[ry, 0, u] = v


def slab_at(first):
    return lambda i, s: (lax.rem(s[0] + (first + i), SLABS), 0)


def halves_spec():
    return pl.BlockSpec((2, 1, 6, 8, 128), lambda i, s: (0, i, 0, 0, 0))


def deal(scalars, tiles, first, count):
    return pl.pallas_call(
        deal_kernel,
        grid_spec=pltpu.PrefetchScalarGridSpec(
            num_scalar_prefetch=1,
            grid=(count,),
            in_specs=[pl.BlockSpec((SLAB_ROWS, 128), slab_at(first))],
            out_specs=(halves_spec(),) * 4,
        ),
        out_shape=(jax.ShapeDtypeStruct((2, count, 6, 8, 128), F32),) * 4,
        compiler_params=pltpu.CompilerParams(vmem_limit_bytes=VMEM_LIMIT),
        cost_estimate=pl.CostEstimate(flops=0, bytes_accessed=count * 300000, transcendentals=0),
        name=f"deal_{first}",
    )(scalars, tiles)


def exchange(low, high, left, right):
    got = []
    for di, dj in AROUND:
        if dj == 0:
            payload = high if di < 0 else low
        elif di == 0:
            payload = right if dj < 0 else left
        else:
            payload = (high if di < 0 else low)[1 if dj < 0 else 0]
        pairs = [(device_of(i + di, j + dj), device_of(i, j)) for i in range(TILES_Y) for j in range(TILES_Z)]
        got.append(lax.ppermute(payload, AXES, pairs))
    return got


def assemble(tile, u, low, high, got):
    pieces = []
    for rp in range(4):
        for cp in range(4):
            di, ry = ((-1, 1), (0, 0), (0, 1), (1, 0))[rp]
            dj, rz = ((-1, 1), (0, 0), (0, 1), (1, 0))[cp]
            if (di, dj) == (0, 0):
                pieces.append((high if ry else low)[rz, 0, u])
            elif dj == 0:
                pieces.append(got[di, dj][rz, 0, u])
            elif di == 0:
                pieces.append(got[di, dj][ry, 0, u])
            else:
                pieces.append(got[di, dj][0, u])
    whole = swap_bits(pieces, [(3, 6), (2, 5), (1, 4), (0, 3)])
    return [jnp.where(tile.inside, v, 0.0) for v in whole]


def quarters(arrays):
    lane = lanes()
    merged = []
    for k in range(8):
        merged.append(jnp.where(lane < 64, roll(arrays[k], -40), roll(arrays[k + 8], 24)))
    merged = [
        jnp.where((lane >> 4) % 2 == 0, merged[k], roll(merged[k + 2], 16)) for k in (0, 1, 4, 5)
    ]
    merged = swap_bits(merged, [(1, 5), (0, 3)])
    return [[merged[2 * ry + rz] for rz in range(2)] for ry in range(2)]


def core_rows(arrays):
    lane = lanes()
    merged = [jnp.where(lane < 64, roll(arrays[k], -40), roll(arrays[k + 4], 24)) for k in range(4)]
    merged = [jnp.where((lane >> 4) % 2 == 0, merged[k], roll(merged[k + 1], 16)) for k in (0, 2)]
    return swap_bits(merged, [(0, 5)])


class Tile:
    def __init__(self, scalars):
        lane, row = lanes(), rows()
        y = EDGE * scalars[3] - RIM + 8 * (lane // 32)
        z = EDGE * scalars[4] - RIM + lane % 32
        self.inside = (y >= 0) & (y < 128) & (z >= 0) & (z < 256)
        self.below_top, self.above_bottom = row < 7, row > 0

    def around(self, load, f, xp, ys):
        mid = load(f, xp, ys)
        total = roll(mid, -1) + roll(mid, 1)
        total = total + (load(f, xp, ys + 1) if ys < 7 else roll(load(f, xp, 0), -32))
        total = total + (load(f, xp, ys - 1) if ys > 0 else roll(load(f, xp, 7), 32))
        other = load(f, 1 - xp, ys)
        if xp == 0:
            far = jnp.where(self.above_bottom, roll(other, 1, 0), 0.0)
        else:
            far = jnp.where(self.below_top, roll(other, -1, 0), 0.0)
        return total + (other + far), mid

    def tendency(self, load, xp, ys):
        around_p, p = self.around(load, 0, xp, ys)
        around_v, v = self.around(load, 1, xp, ys)
        reaction = (1.0 - p) * (v * v)
        rate_p = 0.2 * around_p + (reaction - 1.24 * p)
        rate_v = 0.1 * around_v + (reaction - 0.7 * v)
        return (jnp.where(self.inside, rate_p, 0.0), jnp.where(self.inside, rate_v, 0.0)), (p, v)


CELLS = [(xp, ys) for ys in range(8) for xp in range(2)]
FIELD = (2, 2, 8, 8, 128)


def reader(ref, *at):
    return lambda f, xp, ys: ref[at + (f, xp, ys)]


def sweep_kernel(scalars, low, high, *refs):
    got, (out_ref, start_ref, old, one, two, ahead, rate) = dict(zip(AROUND, refs[:8], strict=True)), refs[8:]
    tile = Tile(scalars)
    for array in range(3):
        for f in range(2):
            for (xp, ys), v in zip(CELLS, assemble(tile, 2 * array + f, low, high, got), strict=True):
                old[array, f, xp, ys] = v

    @pl.when(pl.program_id(0) == 0)
    def _():
        start_ref[...] = old[0]

    for xp, ys in CELLS:
        f0, y0 = tile.tendency(reader(old, 0), xp, ys)
        f1, _ = tile.tendency(reader(old, 1), xp, ys)
        f2, _ = tile.tendency(reader(old, 2), xp, ys)
        for f in range(2):
            one[f, xp, ys] = y0[f] + (5 * H / 24) * f0[f] + ((H / 3) * f1[f] - (H / 24) * f2[f])
            out_ref[0, 0, f, xp, ys] = (H / 6) * (f1[f] + f2[f]) - (5 * H / 6) * f0[f]
            ahead[f, xp, ys] = y0[f] + H * f0[f]
    for xp, ys in CELLS:
        r1, _ = tile.tendency(reader(one), xp, ys)
        for f in range(2):
            correction = out_ref[0, 0, f, xp, ys] + (H / 2) * r1[f]
            out_ref[0, 0, f, xp, ys] = correction
            two[f, xp, ys] = ahead[f, xp, ys] + correction
            rate[f, xp, ys] = r1[f]
    for xp, ys in CELLS:
        r2, _ = tile.tendency(reader(two), xp, ys)
        for f in range(2):
            r1 = rate[f, xp, ys]
            out_ref[0, 1, f, xp, ys] = (H / 3) * r1 - (H / 24) * r2[f]
            out_ref[0, 2, f, xp, ys] = (H / 6) * (r1 + r2[f])


def sweep(scalars, low, high, got, first, count):
    corner = pl.BlockSpec((1, 6, 8, 128), lambda i, s: (i, 0, 0, 0))
    specs = [halves_spec(), halves_spec()]
    specs += [corner if di and dj else halves_spec() for di, dj in AROUND]
    field = pltpu.VMEM(FIELD, F32)
    return pl.pallas_call(
        sweep_kernel,
        grid_spec=pltpu.PrefetchScalarGridSpec(
            num_scalar_prefetch=1,
            grid=(count,),
            in_specs=specs,
            out_specs=(
                pl.BlockSpec((1, 3) + FIELD, lambda i, s: (i,) + (0,) * 6),
                pl.BlockSpec(FIELD, lambda i, s: (0,) * 5),
            ),
            scratch_shapes=[pltpu.VMEM((3,) + FIELD, F32)] + [field] * 4,
        ),
        out_shape=(jax.ShapeDtypeStruct((count, 3) + FIELD, F32), jax.ShapeDtypeStruct(FIELD, F32)),
        compiler_params=pltpu.CompilerParams(vmem_limit_bytes=VMEM_LIMIT),
        cost_estimate=pl.CostEstimate(flops=count * 5 * 32 * 1024 * 40, bytes_accessed=count * 1200000, transcendentals=0),
        name=f"sweep_{first}",
    )(scalars, low, high, *got)


def write_pack(ref, at, array, load):
    for f in range(2):
        for xp in range(2):
            for ry, v in enumerate(core_rows([load(f, xp, ys) for ys in range(8)])):
                ref[at, ry * 12 + array * 4 + f * 2 + xp] = v


def chain_kernel(first, count, scalars, sweeps, *refs):
    tile = Tile(scalars)
    last = first + count >= SLABS
    z, late, corr, one, two, ahead = refs[-6:]
    refs = refs[:-6]
    take_first = scalars[1] > 0
    if first == 0:
        start_ref, refs = refs[0], refs[1:]
        z[0] = start_ref[...]
    else:
        got = dict(zip(AROUND, refs[2:10], strict=True))
        for k in range(3):
            for f in range(2):
                for (xp, ys), v in zip(CELLS, assemble(tile, 2 * k + f, refs[0], refs[1], got), strict=True):
                    if k == 0:
                        z[first % 2, f, xp, ys] = v
                    elif k == 1:
                        late[(first + 1) % 2, f, xp, ys] = v
                    else:
                        corr[f, xp, ys] = v
        refs = refs[10:]
    packs = refs[-1] if last else refs[0]

    def step(p, at, final=False):
        now, other = p % 2, (p + 1) % 2
        reset = (p == 0) | ((p == 1) & take_first)
        for xp, ys in CELLS:
            fl, l = tile.tendency(reader(late, other), xp, ys)
            f0, y0 = tile.tendency(reader(z, now), xp, ys)
            for f in range(2):
                late[now, f, xp, ys] = jnp.where(reset, y0[f], l[f] + H * fl[f] + corr[f, xp, ys])
                g = y0[f] + H * f0[f]
                ahead[f, xp, ys] = g
                if final:
                    one[f, xp, ys] = y0[f] + (H / 2) * f0[f]
                    two[f, xp, ys] = (-H / 2) * f0[f]
                else:
                    z[other, f, xp, ys] = g + sweeps[at, 0, f, xp, ys]
                    one[f, xp, ys] = y0[f] + (5 * H / 24) * f0[f] + sweeps[at, 1, f, xp, ys]
                    two[f, xp, ys] = sweeps[at, 2, f, xp, ys] - (5 * H / 6) * f0[f]
        for xp, ys in CELLS:
            f1, _ = tile.tendency(reader(one), xp, ys)
            for f in range(2):
                c = two[f, xp, ys] + (H / 2) * f1[f]
                corr[f, xp, ys] = c
                two[f, xp, ys] = ahead[f, xp, ys] + c
        write_pack(packs, at, 0, reader(late, now))
        write_pack(packs, at, 1, reader(one))
        write_pack(packs, at, 2, reader(two))

    def looped(at, carry):
        step(first + at, at)
        return carry

    lax.fori_loop(0, count, looped, 0)

    if not last:
        end = first + count
        _, low_ref, high_ref, left_ref, right_ref = refs
        for k, load in enumerate((reader(z, end % 2), reader(late, (end + 1) % 2), reader(corr))):
            for f in range(2):
                parts = quarters([load(f, xp, ys) for xp, ys in CELLS])
                for ry, y_ref in enumerate((low_ref, high_ref)):
                    for rz, z_ref in enumerate((left_ref, right_ref)):
                        y_ref[rz, 0, 2 * k + f] = parts[ry][rz]
                        z_ref[ry, 0, 2 * k + f] = parts[ry][rz]
        return

    step(SLABS, count, final=True)
    end = SLABS % 2
    for xp, ys in CELLS:
        fl, l = tile.tendency(reader(late, end), xp, ys)
        for f in range(2):
            one[f, xp, ys] = l[f] + H * fl[f] + corr[f, xp, ys]
    write_pack(packs, count + 1, 0, reader(one))
    leader, conv_one, conv_two = scalars[0], scalars[1] > 0, scalars[2] > 0
    out_ref = refs[-2]

    def put(p, ref, i, newest=False):
        base = lax.rem(leader + p, SLABS) * SLAB_ROWS
        for ry in range(2):
            for array in range(3):
                for k in range(4):
                    r = ry * 12 + array * 4 + k
                    out_ref[pl.ds(base + r, 8, stride=24)] = ref[i, ry * 12 + k] if newest else ref[i, r]

    for b, ref in enumerate((*refs[:-2], packs)):

        def move(i, carry, b=b, ref=ref):
            put(b * BLOCK + i, ref, i)
            return carry

        lax.fori_loop(0, count if ref is packs else BLOCK, move, 0)

    @pl.when(conv_one)
    def _():
        put(0, packs, count)

    @pl.when(conv_two & conv_one)
    def _():
        put(1, packs, count + 1, newest=True)

    @pl.when(conv_two & jnp.logical_not(conv_one))
    def _():
        put(0, packs, count, newest=True)


def chain(scalars, first, count, sweeps, inputs):
    last = first + count >= SLABS
    vmem = pl.BlockSpec(memory_space=pltpu.VMEM)
    if last:
        out_shape = jax.ShapeDtypeStruct((SLABS * SLAB_ROWS, 128), F32)
        scratch = [pltpu.VMEM((count + 2, 24, 8, 128), F32)]
    else:
        out_shape = (jax.ShapeDtypeStruct((count, 24, 8, 128), F32),)
        out_shape += (jax.ShapeDtypeStruct((2, 1, 6, 8, 128), F32),) * 4
        scratch = []
    field, double = pltpu.VMEM(FIELD, F32), pltpu.VMEM((2,) + FIELD, F32)
    return pl.pallas_call(
        functools.partial(chain_kernel, first, count),
        grid_spec=pltpu.PrefetchScalarGridSpec(
            num_scalar_prefetch=1,
            grid=(1,),
            in_specs=[vmem] * (1 + len(inputs)),
            out_specs=vmem if last else (vmem,) * 5,
            scratch_shapes=scratch + [double, double, field, field, field, field],
        ),
        out_shape=out_shape,
        compiler_params=pltpu.CompilerParams(vmem_limit_bytes=VMEM_LIMIT),
        cost_estimate=pl.CostEstimate(flops=count * 3 * 32 * 1024 * 40, bytes_accessed=count * 500000, transcendentals=0),
        name=f"chain_{first}",
    )(scalars, sweeps, *inputs)


def body(slab_starts, slab_nodes, first_slab, converged):
    ti, tj = own_tile()
    scalars = jnp.stack([first_slab[0], converged[0], converged[1], ti.astype(jnp.int32), tj.astype(jnp.int32)])
    chunks = spread(slab_starts[0], slab_nodes[0])
    tiles = lax.all_to_all(chunks.reshape(128, 24, 128), AXES, 0, 0, tiled=True).reshape(SLABS * SLAB_ROWS, 128)

    blocks = [(0, BLOCK), (BLOCK, BLOCK), (2 * BLOCK, SLABS - 2 * BLOCK)]
    dealt = [deal(scalars, tiles, *block) for block in blocks]
    got = exchange(*dealt[0])
    sweeps, start = sweep(scalars, dealt[0][0], dealt[0][1], got, *blocks[0])
    inputs = [start]
    packs = []
    for b, block in enumerate(blocks[:-1]):
        follow = blocks[b + 1]
        quarter_tiles, _ = lax.optimization_barrier((dealt[b + 1], got))
        beside = exchange(*quarter_tiles)
        pack, *state = chain(scalars, *block, sweeps, inputs)
        packs.append(pack)
        got = exchange(*state)
        sweeps, _ = sweep(scalars, quarter_tiles[0], quarter_tiles[1], beside, *follow)
        inputs = [state[0], state[1], *got]
    out = chain(scalars, *blocks[-1], sweeps, inputs + packs)
    out = lax.all_to_all(out.reshape(128, 24, 128), AXES, 0, 0, tiled=True)
    starts, nodes = collect(out.reshape(128 * 24, 128))
    return starts[None], nodes[None]


def solution(mesh):
    slab_spec = P("tm", None, "space", None, None)
    node_spec = P("tm", None, None, "space", None, None)
    return jax.shard_map(
        body,
        mesh=mesh,
        in_specs=(slab_spec, node_spec, P(), P()),
        out_specs=(slab_spec, node_spec),
        check_vma=False,
    )
```

time: 948 us -> 220 us (0.23); the launches traced: 938 us -> 219 us
  starting transfers between devices: 475 us -> 61.4 us
  waiting for transfers between devices: 418 us -> 62 us
  Pallas kernels: 0 us -> 63 us
  other arithmetic: 34.5 us -> 0.08 us
  blocking collectives: 0 us -> 28.9 us
    ppermute x112 -> x40, starting transfers between devices: 475 us -> 49.9 us  [exchange(): got.append(lax.ppermute(payload, AXES, pairs))]
    ppermute x112 -> x40, waiting for transfers between devices: 418 us -> 37.9 us  [exchange(): got.append(lax.ppermute(payload, AXES, pairs))]
    pallas_call x0 -> x11, Pallas kernels: none -> 63 us  [the longest x3 26.7 us: sweep(): pl.pallas_call(sweep_kernel, grid_spec=pltpu.PrefetchScalarGridSpec(num_s...]
    all_to_all x0 -> x1, blocking collectives: none -> 28.9 us  [body(): out = lax.all_to_all(out.reshape(128, 24, 128), AXES, 0, 0, tiled=True)]
    all_to_all x0 -> x1, waiting for transfers between devices: none -> 24.1 us  [body(): lax.all_to_all(chunks.reshape(128, 24, 128), AXES, 0, 0, tiled=True)]
    sub x80 -> x0, other arithmetic: 22.9 us -> none  [the longest x39 15.6 us: tendency(): laplace_term = beside - 6.0 * interior]
    all_to_all x0 -> x1, starting transfers between devices: none -> 11.5 us  [body(): lax.all_to_all(chunks.reshape(128, 24, 128), AXES, 0, 0, tiled=True)]
  transfers between devices with their start and end apart: 112 -> 41, of which waited for: 103 -> 9; matrix products, arithmetic and copies ran while one was open for 0% -> 0% of each run, Pallas kernels for 0% -> 12%
where the time goes in v2:
time: 220 us; the launch traced here: 219 us
  Pallas kernels  63 us (29%)
  waiting for transfers between devices  62 us (28%)
  starting transfers between devices  61.4 us (28%)
  blocking collectives  28.9 us (13%)
  local copies, waits for them, and re-layouts  2.39 us (1%)
    ppermute x40, starting transfers between devices, exchange(): got.append(lax.ppermute(payload, AXES, pairs))  49.9 us
    ppermute x40, waiting for transfers between devices, exchange(): got.append(lax.ppermute(payload, AXES, pairs))  37.9 us
    all_to_all x1, blocking collectives, body(): out = lax.all_to_all(out.reshape(128, 24, 128), AXES, 0, 0, tiled=True)  28.9 us
    pallas_call x3, Pallas kernels, sweep(): pl.pallas_call(sweep_kernel, grid_spec=pltpu.PrefetchScalarGridSpec(num_s...  26.7 us
    all_to_all x1, waiting for transfers between devices, body(): lax.all_to_all(chunks.reshape(128, 24, 128), AXES, 0, 0, tiled=True)  24.1 us
    pallas_call x3, Pallas kernels, chain(): pl.pallas_call(functools.partial(chain_kernel, first, count), grid_spec=p...  20.1 us
    all_to_all x1, starting transfers between devices, body(): lax.all_to_all(chunks.reshape(128, 24, 128), AXES, 0, 0, tiled=True)  11.5 us
    pallas_call x1, Pallas kernels, collect(): pl.pallas_call(collect_kernel, out_shape=(jax.ShapeDtypeStruct((2, 2, 128...  7.3 us
  transfers between devices with their start and end apart: 41, of which 9 were waited for; matrix products, arithmetic and copies ran while one was open for 0% of the time, Pallas kernels for 12%

profile of v2, /device:TPU:1, one launch (start us, length us, event | category | flops | bytes accessed | tf_op | source)
XLA Modules:
  0.0 219.5 jit_solution(5256749357699186122)
XLA Ops:
  2.9 6.4 %spread.1 = f32[3072,128]{1,0:T(8,128)} custom-call(f32[2,2,128,256]{3,2,1,0:T(8,128)S(1)} %bitcast.56, f32[2,2,2,128,256]{4,3,2,1,0:T(8,128)S(1)} %bitcast.55), custom_call_target="tpu_custom_call" | custom-call | tf_op jit(solution)/shard_map/spread/pallas_call | solution.py:98
  9.3 11.5 %all-to-all-start = ((f32[128,24,128]{2,1,0:T(8,128)}), f32[128,24,128]{2,1,0:T(8,128)S(1)}, u32[]{:S(2)}, u32[]{:S(2)}) async-start(f32[128,24,128]{2,1,0:T(8,128)} %bitcast.4), calls=%async_computation | async-start | bytes 3145728 | tf_op jit(solution)/shard_map/all_to_all | solution.py:470
  21.6 24.1 %all-to-all-done = f32[128,24,128]{2,1,0:T(8,128)S(1)} async-done(((f32[128,24,128]{2,1,0:T(8,128)}), f32[128,24,128]{2,1,0:T(8,128)S(1)}, u32[]{:S(2)}, u32[]{:S(2)}) %all-to-all-start) | async-done | bytes 1572896 | tf_op jit(solution)/shard_map/all_to_all | solution.py:470
  50.3 10.1 %collective-permute-done.refs_0_ = f32[6,6,8,128]{3,2,1,0:T(8,128)S(1)} collective-permute-done((f32[6,6,8,128]{3,2,1,0:T(8,128)S(1)}, f32[6,6,8,128]{3,2,1,0:T(8,128)S(1)}, u32[]{:S(2)}, u32[]{:S(2)}) %collective-permute-start) | collective-permute-done | bytes 147488 | tf_op jit(solution)/shard_map/ppermute | solution.py:188
  65.0 8.3 %collective-permute-done.7.refs_7_ = f32[6,6,8,128]{3,2,1,0:T(8,128)S(1)} collective-permute-done((f32[6,6,8,128]{3,2,1,0:T(8,128)S(1)}, f32[6,6,8,128]{3,2,1,0:T(8,128)S(1)}, u32[]{:S(2)}, u32[]{:S(2)}) %collective-permute-start.7) | collective-permute-done | bytes 147488 | tf_op jit(solution)/shard_map/ppermute | solution.py:188
  73.4 9.9 %sweep_0.1 = (f32[6,3,2,2,8,8,128]{6,5,4,3,2,1,0:T(8,128)S(1)}, f32[2,2,8,8,128]{4,3,2,1,0:T(8,128)S(1)}) custom-call(s32[5]{0:T(128)S(1)} %pad_add_fusion.scalars, f32[2,6,6,8,128]{4,3,2,1,0:T(8,128)S(1)} %get-tuple-element.42.low, f32[2,6,6,8,128]{4,3,2,1,0:T(8,128)S(1)} %get-tuple-element.43.high, f32[6,6,8,128]{3,2,1,0:T(8,128)S(1)} %collective-permute-done.refs_0_, ...), custom_call_target="tpu_custom_call" | custom-call | flops 39321600 | bytes 7200000 | tf_op jit(solution)/shard_map/sweep_0/pallas_call | solution.py:306
  83.3 6.0 %chain_0.1 = (f32[6,24,8,128]{3,2,1,0:T(8,128)S(1)}, f32[2,1,6,8,128]{4,3,2,1,0:T(8,128)S(1)}, f32[2,1,6,8,128]{4,3,2,1,0:T(8,128)S(1)}, f32[2,1,6,8,128]{4,3,2,1,0:T(8,128)S(1)}, f32[2,1,6,8,128]{4,3,2,1,0:T(8,128)S(1)}) custom-call(s32[5]{0:T(128)S(1)} %pad_add_fusion.scalars, f32[6,3,2,2,8,8,128]{6,5,4,3,2,1,0:T(8,128)S(1)} %get-tuple-element.46.sweeps, ...), custom_call_target="tpu_custom_call" | custom-call | flops 23592960 | bytes 3000000 | tf_op jit(solution)/shard_map/chain_0/pallas_call | solution.py:450
  97.5 4.1 %collective-permute-start.12 = (f32[2,1,6,8,128]{4,3,2,1,0:T(8,128)S(1)}, f32[2,1,6,8,128]{4,3,2,1,0:T(8,128)S(1)}, u32[]{:S(2)}, u32[]{:S(2)}) collective-permute-start(f32[2,1,6,8,128]{4,3,2,1,0:T(8,128)S(1)} %get-tuple-element.50), channel_id=1, source_target_pairs={{8,0},{40,8},{32,40},{64,32},{72,64},{104,72},{96,104},{116,96},{1... | collective-permute-start | bytes 147464 | tf_op jit(solution)/shard_map/ppermute | solution.py:188
  104.9 4.5 %collective-permute-done.24.refs_0_ = f32[6,6,8,128]{3,2,1,0:T(8,128)S(1)} collective-permute-done((f32[6,6,8,128]{3,2,1,0:T(8,128)S(1)}, f32[6,6,8,128]{3,2,1,0:T(8,128)S(1)}, u32[]{:S(2)}, u32[]{:S(2)}) %collective-permute-start.24) | collective-permute-done | bytes 147488 | tf_op jit(solution)/shard_map/ppermute | solution.py:188
  110.9 8.0 %collective-permute-done.29.refs_5_ = f32[6,6,8,128]{3,2,1,0:T(8,128)S(1)} collective-permute-done((f32[6,6,8,128]{3,2,1,0:T(8,128)S(1)}, f32[6,6,8,128]{3,2,1,0:T(8,128)S(1)}, u32[]{:S(2)}, u32[]{:S(2)}) %collective-permute-start.29) | collective-permute-done | bytes 147488 | tf_op jit(solution)/shard_map/ppermute | solution.py:188
  120.4 3.4 %collective-permute-done.31.refs_7_ = f32[6,6,8,128]{3,2,1,0:T(8,128)S(1)} collective-permute-done((f32[6,6,8,128]{3,2,1,0:T(8,128)S(1)}, f32[6,6,8,128]{3,2,1,0:T(8,128)S(1)}, u32[]{:S(2)}, u32[]{:S(2)}) %collective-permute-start.31) | collective-permute-done | bytes 147488 | tf_op jit(solution)/shard_map/ppermute | solution.py:188
  126.1 2.7 %collective-permute-start.18 = (f32[4,6,8,128]{3,2,1,0:T(8,128)S(1)}, f32[4,6,8,128]{3,2,1,0:T(8,128)S(1)}, u32[]{:S(2)}, u32[]{:S(2)}) collective-permute-start(f32[4,6,8,128]{3,2,1,0:T(8,128)S(1)} %get-tuple-element.84), channel_id=1, source_target_pairs={{12,0},{44,8},{36,40},{68,32},{76,64},{108,72},{100,104},{112,96},... | collective-permute-start | bytes 294920 | tf_op jit(solution)/shard_map/ppermute | solution.py:188
  128.9 3.5 %collective-permute-start.23 = (f32[4,6,8,128]{3,2,1,0:T(8,128)S(1)}, f32[4,6,8,128]{3,2,1,0:T(8,128)S(1)}, u32[]{:S(2)}, u32[]{:S(2)}) collective-permute-start(f32[4,6,8,128]{3,2,1,0:T(8,128)S(1)} %get-tuple-element.82), channel_id=1, source_target_pairs={{9,0},{41,8},{33,40},{65,32},{73,64},{105,72},{97,104},{117,96},{1... | collective-permute-start | bytes 294920 | tf_op jit(solution)/shard_map/ppermute | solution.py:188
  132.4 9.9 %sweep_6.1 = (f32[6,3,2,2,8,8,128]{6,5,4,3,2,1,0:T(8,128)S(1)}, f32[2,2,8,8,128]{4,3,2,1,0:T(8,128)}) custom-call(s32[5]{0:T(128)S(1)} %pad_add_fusion.scalars, f32[2,6,6,8,128]{4,3,2,1,0:T(8,128)S(1)} %get-tuple-element.61.low, f32[2,6,6,8,128]{4,3,2,1,0:T(8,128)S(1)} %get-tuple-element.62.high, f32[6,6,8,128]{3,2,1,0:T(8,128)S(1)} %collective-permute-done.24.refs_0_, ...), custom_call_target="tpu_custom_call" | custom-call | flops 39321600 | bytes 7200000 | tf_op jit(solution)/shard_map/sweep_6/pallas_call | solution.py:306
  142.3 6.8 %chain_6.1 = (f32[6,24,8,128]{3,2,1,0:T(8,128)S(1)}, f32[2,1,6,8,128]{4,3,2,1,0:T(8,128)S(1)}, f32[2,1,6,8,128]{4,3,2,1,0:T(8,128)S(1)}, f32[2,1,6,8,128]{4,3,2,1,0:T(8,128)S(1)}, f32[2,1,6,8,128]{4,3,2,1,0:T(8,128)S(1)}) custom-call(s32[5]{0:T(128)S(1)} %pad_add_fusion.scalars, f32[6,3,2,2,8,8,128]{6,5,4,3,2,1,0:T(8,128)S(1)} %get-tuple-element.65.sweeps, ...), custom_call_target="tpu_custom_call" | custom-call | flops 23592960 | bytes 3000000 | tf_op jit(solution)/shard_map/chain_6/pallas_call | solution.py:450
  149.5 2.5 %collective-permute-start.20 = (f32[2,4,6,8,128]{4,3,2,1,0:T(8,128)S(1)}, f32[2,4,6,8,128]{4,3,2,1,0:T(8,128)S(1)}, u32[]{:S(2)}, u32[]{:S(2)}) collective-permute-start(f32[2,4,6,8,128]{4,3,2,1,0:T(8,128)S(1)} %get-tuple-element.55), channel_id=1, source_target_pairs={{8,0},{40,8},{32,40},{64,32},{72,64},{104,72},{96,104},{116,96},{1... | collective-permute-start | bytes 589832 | tf_op jit(solution)/shard_map/ppermute | solution.py:188
  153.1 3.7 %collective-permute-start.34 = (f32[1,6,8,128]{3,2,1,0:T(8,128)S(1)}, f32[1,6,8,128]{3,2,1,0:T(8,128)S(1)}, u32[]{:S(2)}, u32[]{:S(2)}) collective-permute-start(f32[1,6,8,128]{3,2,1,0:T(8,128)S(1)} %get-tuple-element.88), channel_id=1, source_target_pairs={{12,0},{44,8},{36,40},{68,32},{76,64},{108,72},{100,104},{112,96},... | collective-permute-start | bytes 73736 | tf_op jit(solution)/shard_map/ppermute | solution.py:188
  156.8 2.5 %collective-permute-start.33 = (f32[2,1,6,8,128]{4,3,2,1,0:T(8,128)S(1)}, f32[2,1,6,8,128]{4,3,2,1,0:T(8,128)S(1)}, u32[]{:S(2)}, u32[]{:S(2)}) collective-permute-start(f32[2,1,6,8,128]{4,3,2,1,0:T(8,128)S(1)} %get-tuple-element.67.refs_1_), channel_id=1, source_target_pairs={{4,0},{12,8},{44,40},{36,32},{68,64},{76,72},{108,104},{100,96},{1... | collective-permute-start | bytes 147464 | tf_op jit(solution)/shard_map/ppermute | solution.py:188
  159.4 4.7 %collective-permute-start.36 = (f32[2,1,6,8,128]{4,3,2,1,0:T(8,128)S(1)}, f32[2,1,6,8,128]{4,3,2,1,0:T(8,128)S(1)}, u32[]{:S(2)}, u32[]{:S(2)}) collective-permute-start(f32[2,1,6,8,128]{4,3,2,1,0:T(8,128)S(1)} %get-tuple-element.69), channel_id=1, source_target_pairs={{8,0},{40,8},{32,40},{64,32},{72,64},{104,72},{96,104},{116,96},{1... | collective-permute-start | bytes 147464 | tf_op jit(solution)/shard_map/ppermute | solution.py:188
  165.4 3.7 %collective-permute-start.39 = (f32[1,6,8,128]{3,2,1,0:T(8,128)S(1)}, f32[1,6,8,128]{3,2,1,0:T(8,128)S(1)}, u32[]{:S(2)}, u32[]{:S(2)}) collective-permute-start(f32[1,6,8,128]{3,2,1,0:T(8,128)S(1)} %get-tuple-element.86), channel_id=1, source_target_pairs={{9,0},{41,8},{33,40},{65,32},{73,64},{105,72},{97,104},{117,96},{1... | collective-permute-start | bytes 73736 | tf_op jit(solution)/shard_map/ppermute | solution.py:188
  169.1 6.8 %sweep_12.1 = (f32[4,3,2,2,8,8,128]{6,5,4,3,2,1,0:T(8,128)S(1)}, f32[2,2,8,8,128]{4,3,2,1,0:T(8,128)}) custom-call(s32[5]{0:T(128)S(1)} %pad_add_fusion.scalars, f32[2,4,6,8,128]{4,3,2,1,0:T(8,128)S(1)} %get-tuple-element.52.low, f32[2,4,6,8,128]{4,3,2,1,0:T(8,128)S(1)} %get-tuple-element.53.high, f32[4,6,8,128]{3,2,1,0:T(8,128)S(1)} %collective-permute-done.16.refs_0_, ...), custom_call_target="tpu_custom_call" | custom-call | flops 26214400 | bytes 4800000 | tf_op jit(solution)/shard_map/sweep_12/pallas_call | solution.py:306
  175.9 7.3 %chain_12.1 = f32[3072,128]{1,0:T(8,128)S(1)} custom-call(s32[5]{0:T(128)S(1)} %pad_add_fusion.scalars, f32[4,3,2,2,8,8,128]{6,5,4,3,2,1,0:T(8,128)S(1)} %get-tuple-element.56.sweeps, f32[2,1,6,8,128]{4,3,2,1,0:T(8,128)S(1)} %get-tuple-element.66.refs_0_, f32[2,1,6,8,128]{4,3,2,1,0:T(8,128)S(1)} %get-tuple-element.67.refs_1_, ...), custom_call_target="tpu_custom_call" | custom-call | flops 15728640 | bytes 2000000 | tf_op jit(solution)/shard_map/chain_12/pallas_call | solution.py:450
  183.2 28.9 %all_to_all.10 = f32[128,24,128]{2,1,0:T(8,128)S(1)} all-to-all(f32[128,24,128]{2,1,0:T(8,128)S(1)} %bitcast.53), channel_id=1, replica_groups=mesh['tm'=16,'space'=8] {'tm','space'}, dimensions={0} | all-to-all | bytes 3145728 | tf_op jit(solution)/shard_map/all_to_all | solution.py:488
  212.2 7.3 %collect.1 = (f32[2,2,128,256]{3,2,1,0:T(8,128)}, f32[2,2,2,128,256]{4,3,2,1,0:T(8,128)}) custom-call(f32[3072,128]{1,0:T(8,128)S(1)} %bitcast.54), custom_call_target="tpu_custom_call" | custom-call | tf_op jit(solution)/shard_map/collect/pallas_call | solution.py:131
  (87 shorter events, 31.2 us)
Async XLA Ops:
  9.3 36.4 %all-to-all-start = ((f32[128,24,128]{2,1,0:T(8,128)}), f32[128,24,128]{2,1,0:T(8,128)S(1)}, u32[]{:S(2)}, u32[]{:S(2)}) async-start(f32[128,24,128]{2,1,0:T(8,128)} %bitcast.4), calls=%async_computation | async-start | bytes 3145728 | tf_op jit(solution)/shard_map/all_to_all | solution.py:470
  46.6 26.8 %collective-permute-start.1 = (f32[2,6,6,8,128]{4,3,2,1,0:T(8,128)S(1)}, f32[2,6,6,8,128]{4,3,2,1,0:T(8,128)S(1)}, u32[]{:S(2)}, u32[]{:S(2)}) collective-permute-start(f32[2,6,6,8,128]{4,3,2,1,0:T(8,128)S(1)} %get-tuple-element.43.high), channel_id=1, source_target_pairs={{4,0},{12,8},{44,40},{36,32},{68,64},{76,72},{108,104},{100,96},{1... | collective-permute-start | bytes 884744 | tf_op jit(solution)/shard_map/ppermute | solution.py:188
  47.1 13.4 %collective-permute-start = (f32[6,6,8,128]{3,2,1,0:T(8,128)S(1)}, f32[6,6,8,128]{3,2,1,0:T(8,128)S(1)}, u32[]{:S(2)}, u32[]{:S(2)}) collective-permute-start(f32[6,6,8,128]{3,2,1,0:T(8,128)S(1)} %get-tuple-element.81), channel_id=1, source_target_pairs={{16,0},{4,8},{12,40},{44,32},{36,64},{68,72},{76,104},{108,96},{10... | collective-permute-start | bytes 442376 | tf_op jit(solution)/shard_map/ppermute | solution.py:188
  47.2 13.9 %collective-permute-start.2 = (f32[6,6,8,128]{3,2,1,0:T(8,128)S(1)}, f32[6,6,8,128]{3,2,1,0:T(8,128)S(1)}, u32[]{:S(2)}, u32[]{:S(2)}) collective-permute-start(f32[6,6,8,128]{3,2,1,0:T(8,128)S(1)} %get-tuple-element.80), channel_id=1, source_target_pairs={{12,0},{44,8},{36,40},{68,32},{76,64},{108,72},{100,104},{112,96},... | collective-permute-start | bytes 442376 | tf_op jit(solution)/shard_map/ppermute | solution.py:188
  49.0 12.9 %collective-permute-start.5 = (f32[6,6,8,128]{3,2,1,0:T(8,128)S(1)}, f32[6,6,8,128]{3,2,1,0:T(8,128)S(1)}, u32[]{:S(2)}, u32[]{:S(2)}) collective-permute-start(f32[6,6,8,128]{3,2,1,0:T(8,128)S(1)} %get-tuple-element.79), channel_id=1, source_target_pairs={{21,0},{1,8},{9,40},{41,32},{33,64},{65,72},{73,104},{105,96},{97,... | collective-permute-start | bytes 442376 | tf_op jit(solution)/shard_map/ppermute | solution.py:188
  49.9 23.4 %collective-permute-start.3 = (f32[2,6,6,8,128]{4,3,2,1,0:T(8,128)S(1)}, f32[2,6,6,8,128]{4,3,2,1,0:T(8,128)S(1)}, u32[]{:S(2)}, u32[]{:S(2)}) collective-permute-start(f32[2,6,6,8,128]{4,3,2,1,0:T(8,128)S(1)} %get-tuple-element.44), channel_id=1, source_target_pairs={{20,0},{0,8},{8,40},{40,32},{32,64},{64,72},{72,104},{104,96},{96,... | collective-permute-start | bytes 884744 | tf_op jit(solution)/shard_map/ppermute | solution.py:188
  60.4 12.9 %collective-permute-start.4 = (f32[2,6,6,8,128]{4,3,2,1,0:T(8,128)S(1)}, f32[2,6,6,8,128]{4,3,2,1,0:T(8,128)S(1)}, u32[]{:S(2)}, u32[]{:S(2)}) collective-permute-start(f32[2,6,6,8,128]{4,3,2,1,0:T(8,128)S(1)} %get-tuple-element.45), channel_id=1, source_target_pairs={{8,0},{40,8},{32,40},{64,32},{72,64},{104,72},{96,104},{116,96},{1... | collective-permute-start | bytes 884744 | tf_op jit(solution)/shard_map/ppermute | solution.py:188
  61.1 12.2 %collective-permute-start.6 = (f32[2,6,6,8,128]{4,3,2,1,0:T(8,128)S(1)}, f32[2,6,6,8,128]{4,3,2,1,0:T(8,128)S(1)}, u32[]{:S(2)}, u32[]{:S(2)}) collective-permute-start(f32[2,6,6,8,128]{4,3,2,1,0:T(8,128)S(1)} %get-tuple-element.42.low), channel_id=1, source_target_pairs={{1,0},{9,8},{41,40},{33,32},{65,64},{73,72},{105,104},{97,96},{117... | collective-permute-start | bytes 884744 | tf_op jit(solution)/shard_map/ppermute | solution.py:188
  62.0 11.4 %collective-permute-start.7 = (f32[6,6,8,128]{3,2,1,0:T(8,128)S(1)}, f32[6,6,8,128]{3,2,1,0:T(8,128)S(1)}, u32[]{:S(2)}, u32[]{:S(2)}) collective-permute-start(f32[6,6,8,128]{3,2,1,0:T(8,128)S(1)} %get-tuple-element.78), channel_id=1, source_target_pairs={{9,0},{41,8},{33,40},{65,32},{73,64},{105,72},{97,104},{117,96},{1... | collective-permute-start | bytes 442376 | tf_op jit(solution)/shard_map/ppermute | solution.py:188
  89.3 12.3 %collective-permute-start.9 = (f32[2,1,6,8,128]{4,3,2,1,0:T(8,128)S(1)}, f32[2,1,6,8,128]{4,3,2,1,0:T(8,128)S(1)}, u32[]{:S(2)}, u32[]{:S(2)}) collective-permute-start(f32[2,1,6,8,128]{4,3,2,1,0:T(8,128)S(1)} %get-tuple-element.48.refs_1_), channel_id=1, source_target_pairs={{4,0},{12,8},{44,40},{36,32},{68,64},{76,72},{108,104},{100,96},{1... | collective-permute-start | bytes 147464 | tf_op jit(solution)/shard_map/ppermute | solution.py:188
  102.5 23.5 %collective-permute-start.25 = (f32[2,6,6,8,128]{4,3,2,1,0:T(8,128)S(1)}, f32[2,6,6,8,128]{4,3,2,1,0:T(8,128)S(1)}, u32[]{:S(2)}, u32[]{:S(2)}) collective-permute-start(f32[2,6,6,8,128]{4,3,2,1,0:T(8,128)S(1)} %get-tuple-element.62.high), channel_id=1, source_target_pairs={{4,0},{12,8},{44,40},{36,32},{68,64},{76,72},{108,104},{100,96},{1... | collective-permute-start | bytes 884744 | tf_op jit(solution)/shard_map/ppermute | solution.py:188
  104.8 24.1 %collective-permute-start.30 = (f32[2,6,6,8,128]{4,3,2,1,0:T(8,128)S(1)}, f32[2,6,6,8,128]{4,3,2,1,0:T(8,128)S(1)}, u32[]{:S(2)}, u32[]{:S(2)}) collective-permute-start(f32[2,6,6,8,128]{4,3,2,1,0:T(8,128)S(1)} %get-tuple-element.61.low), channel_id=1, source_target_pairs={{1,0},{9,8},{41,40},{33,32},{65,64},{73,72},{105,104},{97,96},{117... | collective-permute-start | bytes 884744 | tf_op jit(solution)/shard_map/ppermute | solution.py:188
  104.8 21.3 %collective-permute-start.27 = (f32[2,6,6,8,128]{4,3,2,1,0:T(8,128)S(1)}, f32[2,6,6,8,128]{4,3,2,1,0:T(8,128)S(1)}, u32[]{:S(2)}, u32[]{:S(2)}) collective-permute-start(f32[2,6,6,8,128]{4,3,2,1,0:T(8,128)S(1)} %get-tuple-element.63), channel_id=1, source_target_pairs={{20,0},{0,8},{8,40},{40,32},{32,64},{64,72},{72,104},{104,96},{96,... | collective-permute-start | bytes 884744 | tf_op jit(solution)/shard_map/ppermute | solution.py:188
  109.4 19.4 %collective-permute-start.28 = (f32[2,6,6,8,128]{4,3,2,1,0:T(8,128)S(1)}, f32[2,6,6,8,128]{4,3,2,1,0:T(8,128)S(1)}, u32[]{:S(2)}, u32[]{:S(2)}) collective-permute-start(f32[2,6,6,8,128]{4,3,2,1,0:T(8,128)S(1)} %get-tuple-element.64), channel_id=1, source_target_pairs={{8,0},{40,8},{32,40},{64,32},{72,64},{104,72},{96,104},{116,96},{1... | collective-permute-start | bytes 884744 | tf_op jit(solution)/shard_map/ppermute | solution.py:188
  123.8 29.3 %collective-permute-start.17 = (f32[2,4,6,8,128]{4,3,2,1,0:T(8,128)S(1)}, f32[2,4,6,8,128]{4,3,2,1,0:T(8,128)S(1)}, u32[]{:S(2)}, u32[]{:S(2)}) collective-permute-start(f32[2,4,6,8,128]{4,3,2,1,0:T(8,128)S(1)} %get-tuple-element.53.high), channel_id=1, source_target_pairs={{4,0},{12,8},{44,40},{36,32},{68,64},{76,72},{108,104},{100,96},{1... | collective-permute-start | bytes 589832 | tf_op jit(solution)/shard_map/ppermute | solution.py:188
  126.0 23.2 %collective-permute-start.16 = (f32[4,6,8,128]{3,2,1,0:T(8,128)S(1)}, f32[4,6,8,128]{3,2,1,0:T(8,128)S(1)}, u32[]{:S(2)}, u32[]{:S(2)}) collective-permute-start(f32[4,6,8,128]{3,2,1,0:T(8,128)S(1)} %get-tuple-element.85), channel_id=1, source_target_pairs={{16,0},{4,8},{12,40},{44,32},{36,64},{68,72},{76,104},{108,96},{10... | collective-permute-start | bytes 294920 | tf_op jit(solution)/shard_map/ppermute | solution.py:188
  126.1 23.3 %collective-permute-start.18 = (f32[4,6,8,128]{3,2,1,0:T(8,128)S(1)}, f32[4,6,8,128]{3,2,1,0:T(8,128)S(1)}, u32[]{:S(2)}, u32[]{:S(2)}) collective-permute-start(f32[4,6,8,128]{3,2,1,0:T(8,128)S(1)} %get-tuple-element.84), channel_id=1, source_target_pairs={{12,0},{44,8},{36,40},{68,32},{76,64},{108,72},{100,104},{112,96},... | collective-permute-start | bytes 294920 | tf_op jit(solution)/shard_map/ppermute | solution.py:188
  128.9 20.6 %collective-permute-start.21 = (f32[4,6,8,128]{3,2,1,0:T(8,128)S(1)}, f32[4,6,8,128]{3,2,1,0:T(8,128)S(1)}, u32[]{:S(2)}, u32[]{:S(2)}) collective-permute-start(f32[4,6,8,128]{3,2,1,0:T(8,128)S(1)} %get-tuple-element.83), channel_id=1, source_target_pairs={{21,0},{1,8},{9,40},{41,32},{33,64},{65,72},{73,104},{105,96},{97,... | collective-permute-start | bytes 294920 | tf_op jit(solution)/shard_map/ppermute | solution.py:188
  128.9 23.1 %collective-permute-start.23 = (f32[4,6,8,128]{3,2,1,0:T(8,128)S(1)}, f32[4,6,8,128]{3,2,1,0:T(8,128)S(1)}, u32[]{:S(2)}, u32[]{:S(2)}) collective-permute-start(f32[4,6,8,128]{3,2,1,0:T(8,128)S(1)} %get-tuple-element.82), channel_id=1, source_target_pairs={{9,0},{41,8},{33,40},{65,32},{73,64},{105,72},{97,104},{117,96},{1... | collective-permute-start | bytes 294920 | tf_op jit(solution)/shard_map/ppermute | solution.py:188
  153.1 11.0 %collective-permute-start.34 = (f32[1,6,8,128]{3,2,1,0:T(8,128)S(1)}, f32[1,6,8,128]{3,2,1,0:T(8,128)S(1)}, u32[]{:S(2)}, u32[]{:S(2)}) collective-permute-start(f32[1,6,8,128]{3,2,1,0:T(8,128)S(1)} %get-tuple-element.88), channel_id=1, source_target_pairs={{12,0},{44,8},{36,40},{68,32},{76,64},{108,72},{100,104},{112,96},... | collective-permute-start | bytes 73736 | tf_op jit(solution)/shard_map/ppermute | solution.py:188
  156.8 19.1 %collective-permute-start.33 = (f32[2,1,6,8,128]{4,3,2,1,0:T(8,128)S(1)}, f32[2,1,6,8,128]{4,3,2,1,0:T(8,128)S(1)}, u32[]{:S(2)}, u32[]{:S(2)}) collective-permute-start(f32[2,1,6,8,128]{4,3,2,1,0:T(8,128)S(1)} %get-tuple-element.67.refs_1_), channel_id=1, source_target_pairs={{4,0},{12,8},{44,40},{36,32},{68,64},{76,72},{108,104},{100,96},{1... | collective-permute-start | bytes 147464 | tf_op jit(solution)/shard_map/ppermute | solution.py:188
  159.3 16.6 %collective-permute-start.35 = (f32[2,1,6,8,128]{4,3,2,1,0:T(8,128)S(1)}, f32[2,1,6,8,128]{4,3,2,1,0:T(8,128)S(1)}, u32[]{:S(2)}, u32[]{:S(2)}) collective-permute-start(f32[2,1,6,8,128]{4,3,2,1,0:T(8,128)S(1)} %get-tuple-element.68), channel_id=1, source_target_pairs={{20,0},{0,8},{8,40},{40,32},{32,64},{64,72},{72,104},{104,96},{96,... | collective-permute-start | bytes 147464 | tf_op jit(solution)/shard_map/ppermute | solution.py:188
  159.4 16.5 %collective-permute-start.36 = (f32[2,1,6,8,128]{4,3,2,1,0:T(8,128)S(1)}, f32[2,1,6,8,128]{4,3,2,1,0:T(8,128)S(1)}, u32[]{:S(2)}, u32[]{:S(2)}) collective-permute-start(f32[2,1,6,8,128]{4,3,2,1,0:T(8,128)S(1)} %get-tuple-element.69), channel_id=1, source_target_pairs={{8,0},{40,8},{32,40},{64,32},{72,64},{104,72},{96,104},{116,96},{1... | collective-permute-start | bytes 147464 | tf_op jit(solution)/shard_map/ppermute | solution.py:188
  164.1 11.8 %collective-permute-start.38 = (f32[2,1,6,8,128]{4,3,2,1,0:T(8,128)S(1)}, f32[2,1,6,8,128]{4,3,2,1,0:T(8,128)S(1)}, u32[]{:S(2)}, u32[]{:S(2)}) collective-permute-start(f32[2,1,6,8,128]{4,3,2,1,0:T(8,128)S(1)} %get-tuple-element.66.refs_0_), channel_id=1, source_target_pairs={{1,0},{9,8},{41,40},{33,32},{65,64},{73,72},{105,104},{97,96},{117... | collective-permute-start | bytes 147464 | tf_op jit(solution)/shard_map/ppermute | solution.py:188
  (20 other events, 146.1 us)

commit v3 on v2

v3 whole, which is shorter than its diff:
```python
import functools

import jax
import jax.numpy as jnp
from jax import lax
from jax.experimental import pallas as pl
from jax.experimental.pallas import tpu as pltpu
from jax.sharding import PartitionSpec as P

SLABS = 16
TILES_Y = 8
TILES_Z = 16
EDGE = 16
RIM = 8
BLOCK = 6
H = 0.5
AXES = ("tm", "space")
F32 = jnp.float32
VMEM_LIMIT = 40 * 1024 * 1024
SHAPE = (8, 128)
SLAB_ROWS = 192


def device_of(i, j):
    i, j = i % TILES_Y, j % TILES_Z
    zb, x = (0, i) if i < 4 else (1, 7 - i)
    cj = j // 2
    core = (j % 2) ^ (cj % 2)
    za, y = (0, cj) if cj < 4 else (1, 7 - cj)
    zl = za ^ zb
    return (y * 4 + za * 2 + core) * 8 + zl * 4 + x


def own_tile():
    tm, space = lax.axis_index("tm"), lax.axis_index("space")
    y, za, core = tm // 4, (tm // 2) % 2, tm % 2
    zl, x = space // 4, space % 4
    zb = za ^ zl
    ti = jnp.where(zb == 0, x, 7 - x)
    cj = jnp.where(za == 0, y, 7 - y)
    return ti, 2 * cj + (core ^ (cj % 2))


def roll(v, by, axis=1):
    by %= v.shape[axis]
    return v if by == 0 else pltpu.roll(v, by, axis)


def lanes():
    return lax.broadcasted_iota(jnp.int32, SHAPE, 1)


def rows():
    return lax.broadcasted_iota(jnp.int32, SHAPE, 0)


def swap_bits(arrays, pairs):
    arrays, lane = list(arrays), lanes()
    for index_bit, lane_bit in pairs:
        step, low = 1 << lane_bit, (lane >> lane_bit) % 2 == 0
        for a in range(len(arrays)):
            b = a | (1 << index_bit)
            if a != b:
                u, v = arrays[a], arrays[b]
                arrays[a] = jnp.where(low, u, roll(v, step))
                arrays[b] = jnp.where(low, roll(u, -step), v)
    return arrays


def turn_pairs(v):
    v = roll(v, 4, 0)
    return jnp.where(rows() // 2 % 2 == 0, roll(v, -2, 0), roll(v, 2, 0))


def spread_kernel(starts_ref, nodes_ref, out_ref, planes):
    for array in range(3):
        source = starts_ref if array == 0 else nodes_ref.at[array - 1]
        for f in range(2):
            for xp in range(2):
                for half in range(2):
                    planes[2 * array + f, xp, half] = source[f, xp, :, 128 * half : 128 * half + 128]

    def unit(u, carry):
        row = u // 2 * 4 + u % 2 * 2
        for half in range(2):
            for upper in range(2):
                loads = [
                    planes[u, xp, half, pl.ds(64 * upper + ys, 8, stride=8)] for ys in range(8) for xp in range(2)
                ]
                for k, v in enumerate(swap_bits(loads, [(3, 6), (2, 5), (1, 4), (0, 3)])):
                    tj, rz = 8 * half + k // 2, k % 2
                    device = device_of(7 if upper else 0, tj)
                    out_ref[pl.ds(device * 24 + rz + row, 8, stride=12)] = turn_pairs(v) if upper else v
        return carry

    lax.fori_loop(0, 6, unit, 0)


def spread(starts, nodes):
    vmem = pl.BlockSpec(memory_space=pltpu.VMEM)
    return pl.pallas_call(
        spread_kernel,
        in_specs=[vmem, vmem],
        out_specs=vmem,
        out_shape=jax.ShapeDtypeStruct((128 * 24, 128), F32),
        scratch_shapes=[pltpu.VMEM((6, 2, 2, 128, 128), F32)],
        compiler_params=pltpu.CompilerParams(vmem_limit_bytes=VMEM_LIMIT),
        name="spread",
    )(starts, nodes)


def collect_kernel(in_ref, starts_ref, nodes_ref, planes):
    def unit(u, carry):
        for half in range(2):
            for upper in range(2):
                loads = []
                for t in range(8):
                    device = device_of(7 if upper else 0, 8 * half + t)
                    v = in_ref[pl.ds(device * 24 + u, 8, stride=12)]
                    loads.append(turn_pairs(v) if upper else v)
                for ys, v in enumerate(swap_bits(loads, [(2, 6), (1, 5), (0, 4)])):
                    planes[u, half, pl.ds(64 * upper + ys, 8, stride=8)] = v
        return carry

    lax.fori_loop(0, 12, unit, 0)
    for array in range(3):
        target = starts_ref if array == 0 else nodes_ref.at[array - 1]
        for f in range(2):
            for xp in range(2):
                for half in range(2):
                    target[f, xp, :, 128 * half : 128 * half + 128] = planes[array * 4 + f * 2 + xp, half]


def collect(tiles):
    vmem = pl.BlockSpec(memory_space=pltpu.VMEM)
    return pl.pallas_call(
        collect_kernel,
        out_shape=(
            jax.ShapeDtypeStruct((2, 2, 128, 256), F32),
            jax.ShapeDtypeStruct((2, 2, 2, 128, 256), F32),
        ),
        in_specs=[vmem],
        out_specs=(vmem, vmem),
        scratch_shapes=[pltpu.VMEM((12, 2, 128, 128), F32)],
        compiler_params=pltpu.CompilerParams(vmem_limit_bytes=VMEM_LIMIT),
        name="collect",
    )(tiles)


def deal_kernel(scalars, in_ref, low_ref, high_ref):
    def position(p, carry):
        base = lax.rem(scalars[0] + p, SLABS) * SLAB_ROWS
        for u in range(6):
            for ry, ref in enumerate((low_ref, high_ref)):
                for rz in range(2):
                    ref[rz, p, u] = in_ref[pl.ds(base + ry * 12 + 2 * u + rz, 8, stride=24)]
        return carry

    lax.fori_loop(0, SLABS, position, 0)


VMEM = pl.BlockSpec(memory_space=pltpu.VMEM)
SMEM = pl.BlockSpec(memory_space=pltpu.SMEM)


def deal(scalars, tiles):
    return pl.pallas_call(
        deal_kernel,
        in_specs=[SMEM, VMEM],
        out_specs=(VMEM,) * 2,
        out_shape=(jax.ShapeDtypeStruct((2, SLABS, 6, 8, 128), F32),) * 2,
        compiler_params=pltpu.CompilerParams(vmem_limit_bytes=VMEM_LIMIT),
        cost_estimate=pl.CostEstimate(flops=0, bytes_accessed=3000000, transcendentals=0),
        name="deal",
    )(scalars, tiles)


def from_neighbour(payload, di, dj):
    pairs = [(device_of(i + di, j + dj), device_of(i, j)) for i in range(TILES_Y) for j in range(TILES_Z)]
    return lax.ppermute(payload, AXES, pairs)


def exchange(low, high):
    up, down = from_neighbour(high, -1, 0), from_neighbour(low, 1, 0)
    column = [jnp.stack([up[rz], low[rz], high[rz], down[rz]]) for rz in range(2)]
    left, right = from_neighbour(column[1], 0, -1), from_neighbour(column[0], 0, 1)
    return low, high, up, down, left, right


def assemble(tile, p, u, low, high, up, down, left, right):
    pieces = []
    for row, ref in enumerate((up, low, high, down)):
        pieces += [left[row, p, u], ref[0, p, u], ref[1, p, u], right[row, p, u]]
    whole = swap_bits(pieces, [(3, 6), (2, 5), (1, 4), (0, 3)])
    return [jnp.where(tile.inside, v, 0.0) for v in whole]


def quarters(arrays):
    lane = lanes()
    merged = []
    for k in range(8):
        merged.append(jnp.where(lane < 64, roll(arrays[k], -40), roll(arrays[k + 8], 24)))
    merged = [
        jnp.where((lane >> 4) % 2 == 0, merged[k], roll(merged[k + 2], 16)) for k in (0, 1, 4, 5)
    ]
    merged = swap_bits(merged, [(1, 5), (0, 3)])
    return [[merged[2 * ry + rz] for rz in range(2)] for ry in range(2)]


def core_rows(arrays):
    lane = lanes()
    merged = [jnp.where(lane < 64, roll(arrays[k], -40), roll(arrays[k + 4], 24)) for k in range(4)]
    merged = [jnp.where((lane >> 4) % 2 == 0, merged[k], roll(merged[k + 1], 16)) for k in (0, 2)]
    return swap_bits(merged, [(0, 5)])


class Tile:
    def __init__(self, scalars):
        lane, row = lanes(), rows()
        y = EDGE * scalars[3] - RIM + 8 * (lane // 32)
        z = EDGE * scalars[4] - RIM + lane % 32
        self.inside = (y >= 0) & (y < 128) & (z >= 0) & (z < 256)
        self.below_top, self.above_bottom = row < 7, row > 0

    def around(self, load, f, xp, ys):
        mid = load(f, xp, ys)
        total = roll(mid, -1) + roll(mid, 1)
        total = total + (load(f, xp, ys + 1) if ys < 7 else roll(load(f, xp, 0), -32))
        total = total + (load(f, xp, ys - 1) if ys > 0 else roll(load(f, xp, 7), 32))
        other = load(f, 1 - xp, ys)
        if xp == 0:
            far = jnp.where(self.above_bottom, roll(other, 1, 0), 0.0)
        else:
            far = jnp.where(self.below_top, roll(other, -1, 0), 0.0)
        return total + (other + far), mid

    def tendency(self, load, xp, ys):
        around_p, p = self.around(load, 0, xp, ys)
        around_v, v = self.around(load, 1, xp, ys)
        reaction = (1.0 - p) * (v * v)
        rate_p = 0.2 * around_p + (reaction - 1.24 * p)
        rate_v = 0.1 * around_v + (reaction - 0.7 * v)
        return (jnp.where(self.inside, rate_p, 0.0), jnp.where(self.inside, rate_v, 0.0)), (p, v)


CELLS = [(xp, ys) for ys in range(8) for xp in range(2)]
FIELD = (2, 2, 8, 8, 128)


def reader(ref, *at):
    return lambda f, xp, ys: ref[at + (f, xp, ys)]


def sweep_kernel(first, count, scalars, *refs):
    halo, (out_ref, start_ref, old, one, two, ahead, rate, base) = refs[:6], refs[6:]
    tile = Tile(scalars)

    def position(at, carry):
        for array in range(3):
            both = [assemble(tile, first + at, 2 * array + f, *halo) for f in range(2)]
            for f in range(2):
                for (xp, ys), v in zip(CELLS, both[f], strict=True):
                    old[array, f, xp, ys] = v

        if first == 0:

            @pl.when(at == 0)
            def _():
                start_ref[...] = old[0]

        for xp, ys in CELLS:
            f0, y0 = tile.tendency(reader(old, 0), xp, ys)
            f1, _ = tile.tendency(reader(old, 1), xp, ys)
            f2, _ = tile.tendency(reader(old, 2), xp, ys)
            for f in range(2):
                one[f, xp, ys] = y0[f] + (5 * H / 24) * f0[f] + ((H / 3) * f1[f] - (H / 24) * f2[f])
                base[f, xp, ys] = (H / 6) * (f1[f] + f2[f]) - (5 * H / 6) * f0[f]
                ahead[f, xp, ys] = y0[f] + H * f0[f]
        for xp, ys in CELLS:
            r1, _ = tile.tendency(reader(one), xp, ys)
            for f in range(2):
                correction = base[f, xp, ys] + (H / 2) * r1[f]
                base[f, xp, ys] = correction
                two[f, xp, ys] = ahead[f, xp, ys] + correction
                rate[f, xp, ys] = r1[f]
        for xp, ys in CELLS:
            r2, _ = tile.tendency(reader(two), xp, ys)
            for f in range(2):
                r1 = rate[f, xp, ys]
                one[f, xp, ys] = (H / 3) * r1 - (H / 24) * r2[f]
                ahead[f, xp, ys] = (H / 6) * (r1 + r2[f])
        out_ref[at, 0] = base[...]
        out_ref[at, 1] = one[...]
        out_ref[at, 2] = ahead[...]
        return carry

    lax.fori_loop(0, count, position, 0)


def sweep(scalars, halo, first, count):
    field = pltpu.VMEM(FIELD, F32)
    return pl.pallas_call(
        functools.partial(sweep_kernel, first, count),
        in_specs=[SMEM] + [VMEM] * 6,
        out_specs=(VMEM,) * 2,
        scratch_shapes=[pltpu.VMEM((3,) + FIELD, F32)] + [field] * 5,
        out_shape=(jax.ShapeDtypeStruct((count, 3) + FIELD, F32), jax.ShapeDtypeStruct(FIELD, F32)),
        compiler_params=pltpu.CompilerParams(vmem_limit_bytes=VMEM_LIMIT),
        cost_estimate=pl.CostEstimate(flops=count * 5 * 32 * 1024 * 40, bytes_accessed=count * 1200000, transcendentals=0),
        name=f"sweep_{first}",
    )(scalars, *halo)


def write_packs(ref, at, loads):
    values = {}
    for array, load in enumerate(loads):
        for f in range(2):
            for xp in range(2):
                for ry, v in enumerate(core_rows([load(f, xp, ys) for ys in range(8)])):
                    values[ry * 12 + array * 4 + f * 2 + xp] = v
    for r, v in values.items():
        ref[at, r] = v


def pack_kernel(in_ref, out_ref):
    def position(i, carry):
        write_packs(out_ref, i, [reader(in_ref, i, array) for array in range(3)])
        return carry

    lax.fori_loop(0, out_ref.shape[0], position, 0)


def pack(raw):
    count = raw.shape[0]
    return pl.pallas_call(
        pack_kernel,
        in_specs=[VMEM],
        out_specs=VMEM,
        out_shape=jax.ShapeDtypeStruct((count, 24, 8, 128), F32),
        compiler_params=pltpu.CompilerParams(vmem_limit_bytes=VMEM_LIMIT),
        cost_estimate=pl.CostEstimate(flops=count * 1000000, bytes_accessed=count * 500000, transcendentals=0),
        name="pack",
    )(raw)


def chain_kernel(first, count, scalars, sweeps, *refs):
    tile = Tile(scalars)
    last = first + count >= SLABS
    z, late, corr, one, two, ahead, next_z, next_late = refs[-8:]
    refs = refs[:-8]
    take_first = scalars[1] > 0
    if first == 0:
        start_ref, refs = refs[0], refs[1:]
        z[...] = start_ref[...]
    else:
        for k, ref in enumerate((z, late, corr)):
            both = [assemble(tile, 0, 2 * k + f, *refs[:6]) for f in range(2)]
            for f in range(2):
                for (xp, ys), v in zip(CELLS, both[f], strict=True):
                    ref[f, xp, ys] = v
        refs = refs[6:]
    raw = refs[-1] if last else refs[0]

    def step(at, final=False):
        p = first + at
        reset = (p == 0) | ((p == 1) & take_first)
        for xp, ys in CELLS:
            fl, l = tile.tendency(reader(late), xp, ys)
            f0, y0 = tile.tendency(reader(z), xp, ys)
            for f in range(2):
                next_late[f, xp, ys] = jnp.where(reset, y0[f], l[f] + H * fl[f] + corr[f, xp, ys])
                g = y0[f] + H * f0[f]
                ahead[f, xp, ys] = g
                if final:
                    one[f, xp, ys] = y0[f] + (H / 2) * f0[f]
                    two[f, xp, ys] = (-H / 2) * f0[f]
                else:
                    next_z[f, xp, ys] = g + sweeps[at, 0, f, xp, ys]
                    one[f, xp, ys] = y0[f] + (5 * H / 24) * f0[f] + sweeps[at, 1, f, xp, ys]
                    two[f, xp, ys] = sweeps[at, 2, f, xp, ys] - (5 * H / 6) * f0[f]
        for xp, ys in CELLS:
            f1, _ = tile.tendency(reader(one), xp, ys)
            for f in range(2):
                c = two[f, xp, ys] + (H / 2) * f1[f]
                corr[f, xp, ys] = c
                two[f, xp, ys] = ahead[f, xp, ys] + c
        late[...] = next_late[...]
        if not final:
            z[...] = next_z[...]
        raw[at, 0] = next_late[...]
        raw[at, 1] = one[...]
        raw[at, 2] = two[...]

    def looped(at, carry):
        step(at)
        return carry

    lax.fori_loop(0, count, looped, 0)

    if not last:
        _, low_ref, high_ref = refs
        for k, ref in enumerate((z, late, corr)):
            both = [quarters([ref[f, xp, ys] for xp, ys in CELLS]) for f in range(2)]
            for f in range(2):
                for ry, half_ref in enumerate((low_ref, high_ref)):
                    for rz in range(2):
                        half_ref[rz, 0, 2 * k + f] = both[f][ry][rz]
        return

    step(count, final=True)
    for xp, ys in CELLS:
        fl, l = tile.tendency(reader(late), xp, ys)
        for f in range(2):
            raw[count + 1, 0, f, xp, ys] = l[f] + H * fl[f] + corr[f, xp, ys]
    leader, conv_one, conv_two = scalars[0], scalars[1] > 0, scalars[2] > 0
    *earlier, out_ref, packs, _ = refs

    def pack_at(i, carry):
        write_packs(packs, i, [reader(raw, i, array) for array in range(3)])
        return carry

    lax.fori_loop(0, count + 2, pack_at, 0)

    def put(p, ref, i, newest=False):
        base = lax.rem(leader + p, SLABS) * SLAB_ROWS
        for ry in range(2):
            for array in range(3):
                for k in range(4):
                    r = ry * 12 + array * 4 + k
                    out_ref[pl.ds(base + r, 8, stride=24)] = ref[i, ry * 12 + k] if newest else ref[i, r]

    for b, ref in enumerate((*earlier, packs)):

        def move(i, carry, b=b, ref=ref):
            put(b * BLOCK + i, ref, i)
            return carry

        lax.fori_loop(0, count if ref is packs else BLOCK, move, 0)

    @pl.when(conv_one)
    def _():
        put(0, packs, count)

    @pl.when(conv_two & conv_one)
    def _():
        put(1, packs, count + 1, newest=True)

    @pl.when(conv_two & jnp.logical_not(conv_one))
    def _():
        put(0, packs, count, newest=True)


def chain(scalars, first, count, sweeps, inputs):
    last = first + count >= SLABS
    if last:
        out_shape = jax.ShapeDtypeStruct((SLABS * SLAB_ROWS, 128), F32)
        scratch = [pltpu.VMEM((count + 2, 24, 8, 128), F32), pltpu.VMEM((count + 2, 3) + FIELD, F32)]
    else:
        out_shape = (jax.ShapeDtypeStruct((count, 3) + FIELD, F32),)
        out_shape += (jax.ShapeDtypeStruct((2, 1, 6, 8, 128), F32),) * 2
        scratch = []
    return pl.pallas_call(
        functools.partial(chain_kernel, first, count),
        in_specs=[SMEM] + [VMEM] * (1 + len(inputs)),
        out_specs=VMEM if last else (VMEM,) * 3,
        scratch_shapes=scratch + [pltpu.VMEM(FIELD, F32)] * 8,
        out_shape=out_shape,
        compiler_params=pltpu.CompilerParams(vmem_limit_bytes=VMEM_LIMIT),
        cost_estimate=pl.CostEstimate(flops=count * 3 * 32 * 1024 * 40, bytes_accessed=count * 500000, transcendentals=0),
        name=f"chain_{first}",
    )(scalars, sweeps, *inputs)


def body(slab_starts, slab_nodes, first_slab, converged):
    ti, tj = own_tile()
    scalars = jnp.stack([first_slab[0], converged[0], converged[1], ti.astype(jnp.int32), tj.astype(jnp.int32)])
    chunks = spread(slab_starts[0], slab_nodes[0])
    tiles = lax.all_to_all(chunks.reshape(128, 24, 128), AXES, 0, 0, tiled=True).reshape(SLABS * SLAB_ROWS, 128)

    blocks = [(0, BLOCK), (BLOCK, BLOCK), (2 * BLOCK, SLABS - 2 * BLOCK)]
    halo = exchange(*deal(scalars, tiles))
    sweeps = [sweep(scalars, halo, *block) for block in blocks]
    inputs = [sweeps[0][1]]
    packs = []
    for block, (swept, _) in zip(blocks[:-1], sweeps, strict=False):
        raw, *state = chain(scalars, *block, swept, inputs)
        packs.append(pack(raw))
        inputs = exchange(*state)
    out = chain(scalars, *blocks[-1], sweeps[-1][0], [*inputs, *packs])
    out = lax.all_to_all(out.reshape(128, 24, 128), AXES, 0, 0, tiled=True)
    starts, nodes = collect(out.reshape(128 * 24, 128))
    return starts[None], nodes[None]


def solution(mesh):
    slab_spec = P("tm", None, "space", None, None)
    node_spec = P("tm", None, None, "space", None, None)
    return jax.shard_map(
        body,
        mesh=mesh,
        in_specs=(slab_spec, node_spec, P(), P()),
        out_specs=(slab_spec, node_spec),
        check_vma=False,
    )
```

time: 220 us -> 181 us (0.82)
  starting transfers between devices: 61.4 us -> 27.7 us
  Pallas kernels: 63 us -> 53.2 us
    ppermute x40 -> x12, starting transfers between devices: 49.9 us -> 16.2 us  [from_neighbour(): return lax.ppermute(payload, AXES, pairs)]
    pallas_call x9, Pallas kernels: 49.4 us -> 44.8 us  [the longest x3 27.3 us: sweep(): pl.pallas_call(functools.partial(sweep_kernel, first, count), in_specs=[S...]
    pallas_call x1, Pallas kernels: 7.3 us -> 4.24 us  [collect(): pl.pallas_call(collect_kernel, out_shape=(jax.ShapeDtypeStruct((2, 2, 128...]
    ppermute x40 -> x12, waiting for transfers between devices: 37.9 us -> 39.9 us  [from_neighbour(): return lax.ppermute(payload, AXES, pairs)]
  transfers between devices with their start and end apart: 41 -> 13, of which waited for: 9 -> 7; matrix products, arithmetic and copies ran while one was open for 0% -> 0% of each run, Pallas kernels for 12% -> 12%
where the time goes in v3:
time: 181 us; the launch traced here: 180 us
  waiting for transfers between devices  64 us (35%)
  Pallas kernels  53.2 us (29%)
  blocking collectives  31 us (17%)
  starting transfers between devices  27.7 us (15%)
  local copies, waits for them, and re-layouts  2.54 us (1%)
    ppermute x12, waiting for transfers between devices, from_neighbour(): return lax.ppermute(payload, AXES, pairs)  39.9 us
    all_to_all x1, blocking collectives, body(): out = lax.all_to_all(out.reshape(128, 24, 128), AXES, 0, 0, tiled=True)  31 us
    pallas_call x3, Pallas kernels, sweep(): pl.pallas_call(functools.partial(sweep_kernel, first, count), in_specs=[S...  27.3 us
    all_to_all x1, waiting for transfers between devices, body(): lax.all_to_all(chunks.reshape(128, 24, 128), AXES, 0, 0, tiled=True)  24.1 us
    ppermute x12, starting transfers between devices, from_neighbour(): return lax.ppermute(payload, AXES, pairs)  16.2 us
    pallas_call x3, Pallas kernels, chain(): pl.pallas_call(functools.partial(chain_kernel, first, count), in_specs=[S...  12.8 us
    all_to_all x1, starting transfers between devices, body(): lax.all_to_all(chunks.reshape(128, 24, 128), AXES, 0, 0, tiled=True)  11.5 us
    pallas_call x1, Pallas kernels, collect(): pl.pallas_call(collect_kernel, out_shape=(jax.ShapeDtypeStruct((2, 2, 128...  4.24 us
  transfers between devices with their start and end apart: 13, of which 7 were waited for; matrix products, arithmetic and copies ran while one was open for 0% of the time, Pallas kernels for 12%

profile of v3, /device:TPU:1, one launch (start us, length us, event | category | flops | bytes accessed | tf_op | source)
XLA Modules:
  0.0 180.4 jit_solution(696101391137506709)
XLA Ops:
  0.6 1.2 copy-done
  2.9 4.2 %spread.1 = f32[3072,128]{1,0:T(8,128)} custom-call(f32[2,2,128,256]{3,2,1,0:T(8,128)S(1)} %bitcast.14, f32[2,2,2,128,256]{4,3,2,1,0:T(8,128)S(1)} %bitcast.13), custom_call_target="tpu_custom_call" | custom-call | tf_op jit(solution)/shard_map/spread/pallas_call | solution.py:101
  7.1 11.5 %all-to-all-start = ((f32[128,24,128]{2,1,0:T(8,128)}), f32[128,24,128]{2,1,0:T(8,128)S(1)}, u32[]{:S(2)}, u32[]{:S(2)}) async-start(f32[128,24,128]{2,1,0:T(8,128)} %bitcast.4), calls=%async_computation | async-start | bytes 3145728 | tf_op jit(solution)/shard_map/all_to_all | solution.py:478
  19.4 24.1 %all-to-all-done = f32[128,24,128]{2,1,0:T(8,128)S(1)} async-done(((f32[128,24,128]{2,1,0:T(8,128)}), f32[128,24,128]{2,1,0:T(8,128)S(1)}, u32[]{:S(2)}, u32[]{:S(2)}) %all-to-all-start) | async-done | bytes 1572896 | tf_op jit(solution)/shard_map/all_to_all | solution.py:478
  46.2 16.3 %collective-permute-done.1.refs_3_ = f32[2,16,6,8,128]{4,3,2,1,0:T(8,128)S(1)} collective-permute-done((f32[2,16,6,8,128]{4,3,2,1,0:T(8,128)S(1)}, f32[2,16,6,8,128]{4,3,2,1,0:T(8,128)S(1)}, u32[]{:S(2)}, u32[]{:S(2)}) %collective-permute-start.1) | collective-permute-done | bytes 786464 | tf_op jit(solution)/shard_map/ppermute | solution.py:180
  64.1 1.4 collective-permute-start.3
  65.5 15.8 %collective-permute-done.2.refs_4_ = f32[4,16,6,8,128]{4,3,2,1,0:T(8,128)S(1)} collective-permute-done((f32[4,16,6,8,128]{4,3,2,1,0:T(8,128)S(1)}, f32[4,16,6,8,128]{4,3,2,1,0:T(8,128)S(1)}, u32[]{:S(2)}, u32[]{:S(2)}) %collective-permute-start.2) | collective-permute-done | bytes 1572896 | tf_op jit(solution)/shard_map/ppermute | solution.py:180
  81.3 2.6 %collective-permute-done.3.refs_5_ = f32[4,16,6,8,128]{4,3,2,1,0:T(8,128)S(1)} collective-permute-done((f32[4,16,6,8,128]{4,3,2,1,0:T(8,128)S(1)}, f32[4,16,6,8,128]{4,3,2,1,0:T(8,128)S(1)}, u32[]{:S(2)}, u32[]{:S(2)}) %collective-permute-start.3) | collective-permute-done | bytes 1572896 | tf_op jit(solution)/shard_map/ppermute | solution.py:180
  84.0 9.4 %sweep_0.1 = (f32[6,3,2,2,8,8,128]{6,5,4,3,2,1,0:T(8,128)S(1)}, f32[2,2,8,8,128]{4,3,2,1,0:T(8,128)S(1)}) custom-call(s32[5]{0:T(128)S(1)} %pad_add_fusion.scalars, f32[2,16,6,8,128]{4,3,2,1,0:T(8,128)S(1)} %get-tuple-element.16.refs_0_, f32[2,16,6,8,128]{4,3,2,1,0:T(8,128)S(1)} %get-tuple-element.17.refs_1_, ...), custom_call_target="tpu_custom_call" | custom-call | flops 39321600 | bytes 7200000 | tf_op jit(solution)/shard_map/sweep_0/pallas_call | solution.py:302
  93.4 3.1 %chain_0.1 = (f32[6,3,2,2,8,8,128]{6,5,4,3,2,1,0:T(8,128)S(1)}, f32[2,1,6,8,128]{4,3,2,1,0:T(8,128)S(1)}, f32[2,1,6,8,128]{4,3,2,1,0:T(8,128)S(1)}) custom-call(s32[5]{0:T(128)S(1)} %pad_add_fusion.scalars, f32[6,3,2,2,8,8,128]{6,5,4,3,2,1,0:T(8,128)S(1)} %get-tuple-element.20.sweeps, f32[2,2,8,8,128]{4,3,2,1,0:T(8,128)S(1)} %get-tuple-element.21.refs_0_), custom_call_target="tpu_custom_call" | custom-call | flops 23592960 | bytes 3000000 | tf_op jit(solution)/shard_map/chain_0/pallas_call | solution.py:462
  96.5 1.1 collective-permute-start.4
  98.0 2.5 %collective-permute-done.5.refs_3_ = f32[2,1,6,8,128]{4,3,2,1,0:T(8,128)S(1)} collective-permute-done((f32[2,1,6,8,128]{4,3,2,1,0:T(8,128)S(1)}, f32[2,1,6,8,128]{4,3,2,1,0:T(8,128)S(1)}, u32[]{:S(2)}, u32[]{:S(2)}) %collective-permute-start.5) | collective-permute-done | bytes 49184 | tf_op jit(solution)/shard_map/ppermute | solution.py:180
  100.7 4.5 %collective-permute-start.7 = (f32[4,1,6,8,128]{4,3,2,1,0:T(8,128)S(1)}, f32[4,1,6,8,128]{4,3,2,1,0:T(8,128)S(1)}, u32[]{:S(2)}, u32[]{:S(2)}) collective-permute-start(f32[4,1,6,8,128]{4,3,2,1,0:T(8,128)S(1)} %pad_maximum_fusion.3), channel_id=1, source_target_pairs={{8,0},{40,8},{32,40},{64,32},{72,64},{104,72},{96,104},{116,96},{1... | collective-permute-start | bytes 294920 | tf_op jit(solution)/shard_map/ppermute | solution.py:180
  105.1 10.6 %sweep_6.1 = (f32[6,3,2,2,8,8,128]{6,5,4,3,2,1,0:T(8,128)S(1)}, f32[2,2,8,8,128]{4,3,2,1,0:T(8,128)}) custom-call(s32[5]{0:T(128)S(1)} %pad_add_fusion.scalars, f32[2,16,6,8,128]{4,3,2,1,0:T(8,128)S(1)} %get-tuple-element.16.refs_0_, f32[2,16,6,8,128]{4,3,2,1,0:T(8,128)S(1)} %get-tuple-element.17.refs_1_, ...), custom_call_target="tpu_custom_call" | custom-call | flops 39321600 | bytes 7200000 | tf_op jit(solution)/shard_map/sweep_6/pallas_call | solution.py:302
  115.8 4.0 %chain_6.1 = (f32[6,3,2,2,8,8,128]{6,5,4,3,2,1,0:T(8,128)S(1)}, f32[2,1,6,8,128]{4,3,2,1,0:T(8,128)S(1)}, f32[2,1,6,8,128]{4,3,2,1,0:T(8,128)S(1)}) custom-call(s32[5]{0:T(128)S(1)} %pad_add_fusion.scalars, f32[6,3,2,2,8,8,128]{6,5,4,3,2,1,0:T(8,128)S(1)} %get-tuple-element.19.sweeps, f32[2,1,6,8,128]{4,3,2,1,0:T(8,128)S(1)} %get-tuple-element.22.refs_0_, ...), custom_call_target="tpu_custom_call" | custom-call | flops 23592960 | bytes 3000000 | tf_op jit(solution)/shard_map/chain_6/pallas_call | solution.py:462
  120.3 1.1 collective-permute-start.9
  121.3 1.9 %collective-permute-done.9.refs_3_ = f32[2,1,6,8,128]{4,3,2,1,0:T(8,128)S(1)} collective-permute-done((f32[2,1,6,8,128]{4,3,2,1,0:T(8,128)S(1)}, f32[2,1,6,8,128]{4,3,2,1,0:T(8,128)S(1)}, u32[]{:S(2)}, u32[]{:S(2)}) %collective-permute-start.9) | collective-permute-done | bytes 49184 | tf_op jit(solution)/shard_map/ppermute | solution.py:180
  123.4 5.1 %collective-permute-start.11 = (f32[4,1,6,8,128]{4,3,2,1,0:T(8,128)S(1)}, f32[4,1,6,8,128]{4,3,2,1,0:T(8,128)S(1)}, u32[]{:S(2)}, u32[]{:S(2)}) collective-permute-start(f32[4,1,6,8,128]{4,3,2,1,0:T(8,128)S(1)} %pad_maximum_fusion.5), channel_id=1, source_target_pairs={{8,0},{40,8},{32,40},{64,32},{72,64},{104,72},{96,104},{116,96},{1... | collective-permute-start | bytes 294920 | tf_op jit(solution)/shard_map/ppermute | solution.py:180
  128.5 1.8 %pack.2.refs_6_ = f32[6,24,8,128]{3,2,1,0:T(8,128)S(1)} custom-call(f32[6,3,2,2,8,8,128]{6,5,4,3,2,1,0:T(8,128)S(1)} %get-tuple-element.26.in_ref), custom_call_target="tpu_custom_call" | custom-call | flops 6000000 | bytes 3000000 | tf_op jit(solution)/shard_map/pack/pallas_call | solution.py:335
  130.3 7.3 %sweep_12.1 = (f32[4,3,2,2,8,8,128]{6,5,4,3,2,1,0:T(8,128)S(1)}, f32[2,2,8,8,128]{4,3,2,1,0:T(8,128)}) custom-call(s32[5]{0:T(128)S(1)} %pad_add_fusion.scalars, f32[2,16,6,8,128]{4,3,2,1,0:T(8,128)S(1)} %get-tuple-element.16.refs_0_, f32[2,16,6,8,128]{4,3,2,1,0:T(8,128)S(1)} %get-tuple-element.17.refs_1_, ...), custom_call_target="tpu_custom_call" | custom-call | flops 26214400 | bytes 4800000 | tf_op jit(solution)/shard_map/sweep_12/pallas_call | solution.py:302
  137.6 1.8 %pack.3.refs_7_ = f32[6,24,8,128]{3,2,1,0:T(8,128)S(1)} custom-call(f32[6,3,2,2,8,8,128]{6,5,4,3,2,1,0:T(8,128)S(1)} %get-tuple-element.27.in_ref), custom_call_target="tpu_custom_call" | custom-call | flops 6000000 | bytes 3000000 | tf_op jit(solution)/shard_map/pack/pallas_call | solution.py:335
  139.4 5.7 %chain_12.1 = f32[3072,128]{1,0:T(8,128)S(1)} custom-call(s32[5]{0:T(128)S(1)} %pad_add_fusion.scalars, f32[4,3,2,2,8,8,128]{6,5,4,3,2,1,0:T(8,128)S(1)} %get-tuple-element.18.sweeps, f32[2,1,6,8,128]{4,3,2,1,0:T(8,128)S(1)} %get-tuple-element.24.refs_0_, f32[2,1,6,8,128]{4,3,2,1,0:T(8,128)S(1)} %get-tuple-element.25.refs_1_, ...), custom_call_target="tpu_custom_call" | custom-call | flops 15728640 | bytes 2000000 | tf_op jit(solution)/shard_map/chain_12/pallas_call | solution.py:462
  145.2 31.0 %all_to_all.10 = f32[128,24,128]{2,1,0:T(8,128)S(1)} all-to-all(f32[128,24,128]{2,1,0:T(8,128)S(1)} %bitcast.11), channel_id=1, replica_groups=mesh['tm'=16,'space'=8] {'tm','space'}, dimensions={0} | all-to-all | bytes 3145728 | tf_op jit(solution)/shard_map/all_to_all | solution.py:490
  176.2 4.2 %collect.1 = (f32[2,2,128,256]{3,2,1,0:T(8,128)}, f32[2,2,2,128,256]{4,3,2,1,0:T(8,128)}) custom-call(f32[3072,128]{1,0:T(8,128)S(1)} %bitcast.12), custom_call_target="tpu_custom_call" | custom-call | tf_op jit(solution)/shard_map/collect/pallas_call | solution.py:136
  (38 shorter events, 6.6 us)
Async XLA Ops:
  0.6 1.2 copy-start
  1.9 1.0 copy-start.1
  7.1 12.2 %copy-start.2 = (s32[2]{0:T(128)S(1)}, s32[2]{0:T(128)}, u32[]{:S(2)}) copy-start(s32[2]{0:T(128)} %param.7) | copy-start | bytes 28
  7.1 36.4 %all-to-all-start = ((f32[128,24,128]{2,1,0:T(8,128)}), f32[128,24,128]{2,1,0:T(8,128)S(1)}, u32[]{:S(2)}, u32[]{:S(2)}) async-start(f32[128,24,128]{2,1,0:T(8,128)} %bitcast.4), calls=%async_computation | async-start | bytes 3145728 | tf_op jit(solution)/shard_map/all_to_all | solution.py:478
  44.5 17.9 %collective-permute-start.1 = (f32[2,16,6,8,128]{4,3,2,1,0:T(8,128)S(1)}, f32[2,16,6,8,128]{4,3,2,1,0:T(8,128)S(1)}, u32[]{:S(2)}, u32[]{:S(2)}) collective-permute-start(f32[2,16,6,8,128]{4,3,2,1,0:T(8,128)S(1)} %get-tuple-element.16.refs_0_), channel_id=1, source_target_pairs={{1,0},{9,8},{41,40},{33,32},{65,64},{73,72},{105,104},{97,96},{117... | collective-permute-start | bytes 2359304 | tf_op jit(solution)/shard_map/ppermute | solution.py:180
  45.1 18.3 %collective-permute-start = (f32[2,16,6,8,128]{4,3,2,1,0:T(8,128)S(1)}, f32[2,16,6,8,128]{4,3,2,1,0:T(8,128)S(1)}, u32[]{:S(2)}, u32[]{:S(2)}) collective-permute-start(f32[2,16,6,8,128]{4,3,2,1,0:T(8,128)S(1)} %get-tuple-element.17.refs_1_), channel_id=1, source_target_pairs={{4,0},{12,8},{44,40},{36,32},{68,64},{76,72},{108,104},{100,96},{1... | collective-permute-start | bytes 2359304 | tf_op jit(solution)/shard_map/ppermute | solution.py:180
  63.5 17.8 %collective-permute-start.2 = (f32[4,16,6,8,128]{4,3,2,1,0:T(8,128)S(1)}, f32[4,16,6,8,128]{4,3,2,1,0:T(8,128)S(1)}, u32[]{:S(2)}, u32[]{:S(2)}) collective-permute-start(f32[4,16,6,8,128]{4,3,2,1,0:T(8,128)S(1)} %pad_maximum_fusion), channel_id=1, source_target_pairs={{20,0},{0,8},{8,40},{40,32},{32,64},{64,72},{72,104},{104,96},{96,... | collective-permute-start | bytes 4718600 | tf_op jit(solution)/shard_map/ppermute | solution.py:180
  64.1 19.8 %collective-permute-start.3 = (f32[4,16,6,8,128]{4,3,2,1,0:T(8,128)S(1)}, f32[4,16,6,8,128]{4,3,2,1,0:T(8,128)S(1)}, u32[]{:S(2)}, u32[]{:S(2)}) collective-permute-start(f32[4,16,6,8,128]{4,3,2,1,0:T(8,128)S(1)} %pad_maximum_fusion.1), channel_id=1, source_target_pairs={{8,0},{40,8},{32,40},{64,32},{72,64},{104,72},{96,104},{116,96},{1... | collective-permute-start | bytes 4718600 | tf_op jit(solution)/shard_map/ppermute | solution.py:180
  96.5 4.0 %collective-permute-start.4 = (f32[2,1,6,8,128]{4,3,2,1,0:T(8,128)S(1)}, f32[2,1,6,8,128]{4,3,2,1,0:T(8,128)S(1)}, u32[]{:S(2)}, u32[]{:S(2)}) collective-permute-start(f32[2,1,6,8,128]{4,3,2,1,0:T(8,128)S(1)} %get-tuple-element.23.refs_1_), channel_id=1, source_target_pairs={{4,0},{12,8},{44,40},{36,32},{68,64},{76,72},{108,104},{100,96},{1... | collective-permute-start | bytes 147464 | tf_op jit(solution)/shard_map/ppermute | solution.py:180
  97.6 2.9 %collective-permute-start.5 = (f32[2,1,6,8,128]{4,3,2,1,0:T(8,128)S(1)}, f32[2,1,6,8,128]{4,3,2,1,0:T(8,128)S(1)}, u32[]{:S(2)}, u32[]{:S(2)}) collective-permute-start(f32[2,1,6,8,128]{4,3,2,1,0:T(8,128)S(1)} %get-tuple-element.22.refs_0_), channel_id=1, source_target_pairs={{1,0},{9,8},{41,40},{33,32},{65,64},{73,72},{105,104},{97,96},{117... | collective-permute-start | bytes 147464 | tf_op jit(solution)/shard_map/ppermute | solution.py:180
  100.5 15.2 %collective-permute-start.6 = (f32[4,1,6,8,128]{4,3,2,1,0:T(8,128)S(1)}, f32[4,1,6,8,128]{4,3,2,1,0:T(8,128)S(1)}, u32[]{:S(2)}, u32[]{:S(2)}) collective-permute-start(f32[4,1,6,8,128]{4,3,2,1,0:T(8,128)S(1)} %pad_maximum_fusion.2), channel_id=1, source_target_pairs={{20,0},{0,8},{8,40},{40,32},{32,64},{64,72},{72,104},{104,96},{96,... | collective-permute-start | bytes 294920 | tf_op jit(solution)/shard_map/ppermute | solution.py:180
  100.7 15.1 %collective-permute-start.7 = (f32[4,1,6,8,128]{4,3,2,1,0:T(8,128)S(1)}, f32[4,1,6,8,128]{4,3,2,1,0:T(8,128)S(1)}, u32[]{:S(2)}, u32[]{:S(2)}) collective-permute-start(f32[4,1,6,8,128]{4,3,2,1,0:T(8,128)S(1)} %pad_maximum_fusion.3), channel_id=1, source_target_pairs={{8,0},{40,8},{32,40},{64,32},{72,64},{104,72},{96,104},{116,96},{1... | collective-permute-start | bytes 294920 | tf_op jit(solution)/shard_map/ppermute | solution.py:180
  119.8 3.4 %collective-permute-start.8 = (f32[2,1,6,8,128]{4,3,2,1,0:T(8,128)S(1)}, f32[2,1,6,8,128]{4,3,2,1,0:T(8,128)S(1)}, u32[]{:S(2)}, u32[]{:S(2)}) collective-permute-start(f32[2,1,6,8,128]{4,3,2,1,0:T(8,128)S(1)} %get-tuple-element.25.refs_1_), channel_id=1, source_target_pairs={{4,0},{12,8},{44,40},{36,32},{68,64},{76,72},{108,104},{100,96},{1... | collective-permute-start | bytes 147464 | tf_op jit(solution)/shard_map/ppermute | solution.py:180
  120.3 2.9 %collective-permute-start.9 = (f32[2,1,6,8,128]{4,3,2,1,0:T(8,128)S(1)}, f32[2,1,6,8,128]{4,3,2,1,0:T(8,128)S(1)}, u32[]{:S(2)}, u32[]{:S(2)}) collective-permute-start(f32[2,1,6,8,128]{4,3,2,1,0:T(8,128)S(1)} %get-tuple-element.24.refs_0_), channel_id=1, source_target_pairs={{1,0},{9,8},{41,40},{33,32},{65,64},{73,72},{105,104},{97,96},{117... | collective-permute-start | bytes 147464 | tf_op jit(solution)/shard_map/ppermute | solution.py:180
  123.2 16.2 %collective-permute-start.10 = (f32[4,1,6,8,128]{4,3,2,1,0:T(8,128)S(1)}, f32[4,1,6,8,128]{4,3,2,1,0:T(8,128)S(1)}, u32[]{:S(2)}, u32[]{:S(2)}) collective-permute-start(f32[4,1,6,8,128]{4,3,2,1,0:T(8,128)S(1)} %pad_maximum_fusion.4), channel_id=1, source_target_pairs={{20,0},{0,8},{8,40},{40,32},{32,64},{64,72},{72,104},{104,96},{96,... | collective-permute-start | bytes 294920 | tf_op jit(solution)/shard_map/ppermute | solution.py:180
  123.4 16.1 %collective-permute-start.11 = (f32[4,1,6,8,128]{4,3,2,1,0:T(8,128)S(1)}, f32[4,1,6,8,128]{4,3,2,1,0:T(8,128)S(1)}, u32[]{:S(2)}, u32[]{:S(2)}) collective-permute-start(f32[4,1,6,8,128]{4,3,2,1,0:T(8,128)S(1)} %pad_maximum_fusion.5), channel_id=1, source_target_pairs={{8,0},{40,8},{32,40},{64,32},{72,64},{104,72},{96,104},{116,96},{1... | collective-permute-start | bytes 294920 | tf_op jit(solution)/shard_map/ppermute | solution.py:180

commit v4 on v3

--- a/solution.py
+++ b/solution.py
@@ -12,12 +12,15 @@
 TILES_Z = 16
 EDGE = 16
 RIM = 8
-BLOCK = 6
+BLOCKS = ((0, 6), (6, 6), (12, 4))
 H = 0.5
 AXES = ("tm", "space")
 F32 = jnp.float32
 VMEM_LIMIT = 40 * 1024 * 1024
 SHAPE = (8, 128)
+VMEM = pl.BlockSpec(memory_space=pltpu.VMEM)
+SMEM = pl.BlockSpec(memory_space=pltpu.SMEM)
+ANY = pl.BlockSpec(memory_space=pl.ANY)
 SLAB_ROWS = 192
 
 
@@ -72,15 +75,22 @@
     return jnp.where(rows() // 2 % 2 == 0, roll(v, -2, 0), roll(v, 2, 0))
 
 
-def spread_kernel(starts_ref, nodes_ref, out_ref, planes):
-    for array in range(3):
-        source = starts_ref if array == 0 else nodes_ref.at[array - 1]
-        for f in range(2):
-            for xp in range(2):
-                for half in range(2):
-                    planes[2 * array + f, xp, half] = source[f, xp, :, 128 * half : 128 * half + 128]
-
-    def unit(u, carry):
+def spread_kernel(starts_ref, nodes_ref, out_ref, planes, arrived):
+    def copies(u):
+        source = starts_ref if u < 2 else nodes_ref.at[u // 2 - 1]
+        return [
+            pltpu.make_async_copy(
+                source.at[u % 2, xp, :, pl.ds(128 * half, 128)], planes.at[u, xp, half], arrived.at[4 * u + 2 * xp + half]
+            )
+            for xp in range(2)
+            for half in range(2)
+        ]
+
+    for u in range(6):
+        for copy in copies(u):
+            copy.start()
+
+    def unit(u):
         row = u // 2 * 4 + u % 2 * 2
         for half in range(2):
             for upper in range(2):
@@ -91,25 +101,37 @@
                     tj, rz = 8 * half + k // 2, k % 2
                     device = device_of(7 if upper else 0, tj)
                     out_ref[pl.ds(device * 24 + rz + row, 8, stride=12)] = turn_pairs(v) if upper else v
+
+    for copy in copies(0) + copies(1):
+        copy.wait()
+
+    def pair(k, carry):
+        for n in (1, 2):
+
+            @pl.when(k == n)
+            def _(n=n):
+                for copy in copies(2 * n) + copies(2 * n + 1):
+                    copy.wait()
+
+        lax.fori_loop(2 * k, 2 * k + 2, lambda u, c: (unit(u), c)[1], 0)
         return carry
 
-    lax.fori_loop(0, 6, unit, 0)
+    lax.fori_loop(0, 3, pair, 0)
 
 
 def spread(starts, nodes):
-    vmem = pl.BlockSpec(memory_space=pltpu.VMEM)
     return pl.pallas_call(
         spread_kernel,
-        in_specs=[vmem, vmem],
-        out_specs=vmem,
+        in_specs=[ANY, ANY],
+        out_specs=VMEM,
         out_shape=jax.ShapeDtypeStruct((128 * 24, 128), F32),
-        scratch_shapes=[pltpu.VMEM((6, 2, 2, 128, 128), F32)],
+        scratch_shapes=[pltpu.VMEM((6, 2, 2, 128, 128), F32), pltpu.SemaphoreType.DMA((24,))],
         compiler_params=pltpu.CompilerParams(vmem_limit_bytes=VMEM_LIMIT),
         name="spread",
     )(starts, nodes)
 
 
-def collect_kernel(in_ref, starts_ref, nodes_ref, planes):
+def collect_kernel(in_ref, starts_ref, nodes_ref, planes, left):
     def unit(u, carry):
         for half in range(2):
             for upper in range(2):
@@ -122,57 +144,77 @@
                     planes[u, half, pl.ds(64 * upper + ys, 8, stride=8)] = v
         return carry
 
-    lax.fori_loop(0, 12, unit, 0)
-    for array in range(3):
+    def copies(array):
         target = starts_ref if array == 0 else nodes_ref.at[array - 1]
-        for f in range(2):
-            for xp in range(2):
-                for half in range(2):
-                    target[f, xp, :, 128 * half : 128 * half + 128] = planes[array * 4 + f * 2 + xp, half]
+        return [
+            pltpu.make_async_copy(
+                planes.at[4 * array + 2 * f + xp, half],
+                target.at[f, xp, :, pl.ds(128 * half, 128)],
+                left.at[8 * array + 4 * f + 2 * xp + half],
+            )
+            for f in range(2)
+            for xp in range(2)
+            for half in range(2)
+        ]
+
+    def array_at(k, carry):
+        lax.fori_loop(4 * k, 4 * k + 4, unit, 0)
+        for n in range(3):
+
+            @pl.when(k == n)
+            def _(n=n):
+                for copy in copies(n):
+                    copy.start()
+
+        return carry
+
+    lax.fori_loop(0, 3, array_at, 0)
+    for n in range(3):
+        for copy in copies(n):
+            copy.wait()
 
 
 def collect(tiles):
-    vmem = pl.BlockSpec(memory_space=pltpu.VMEM)
     return pl.pallas_call(
         collect_kernel,
         out_shape=(
             jax.ShapeDtypeStruct((2, 2, 128, 256), F32),
             jax.ShapeDtypeStruct((2, 2, 2, 128, 256), F32),
         ),
-        in_specs=[vmem],
-        out_specs=(vmem, vmem),
-        scratch_shapes=[pltpu.VMEM((12, 2, 128, 128), F32)],
+        in_specs=[VMEM],
+        out_specs=(ANY, ANY),
+        scratch_shapes=[pltpu.VMEM((12, 2, 128, 128), F32), pltpu.SemaphoreType.DMA((24,))],
         compiler_params=pltpu.CompilerParams(vmem_limit_bytes=VMEM_LIMIT),
         name="collect",
     )(tiles)
 
 
-def deal_kernel(scalars, in_ref, low_ref, high_ref):
-    def position(p, carry):
-        base = lax.rem(scalars[0] + p, SLABS) * SLAB_ROWS
-        for u in range(6):
-            for ry, ref in enumerate((low_ref, high_ref)):
-                for rz in range(2):
-                    ref[rz, p, u] = in_ref[pl.ds(base + ry * 12 + 2 * u + rz, 8, stride=24)]
-        return carry
-
-    lax.fori_loop(0, SLABS, position, 0)
-
-
-VMEM = pl.BlockSpec(memory_space=pltpu.VMEM)
-SMEM = pl.BlockSpec(memory_space=pltpu.SMEM)
+def deal_kernel(scalars, in_ref, *out_refs):
+    for b, (first, count) in enumerate(BLOCKS):
+
+        def position(i, carry, b=b, first=first):
+            base = lax.rem(scalars[0] + (first + i), SLABS) * SLAB_ROWS
+            for u in range(6):
+                for ry in range(2):
+                    for rz in range(2):
+                        v = in_ref[pl.ds(base + ry * 12 + 2 * u + rz, 8, stride=24)]
+                        out_refs[2 * b + ry][rz, i, u] = v
+            return carry
+
+        lax.fori_loop(0, count, position, 0)
 
 
 def deal(scalars, tiles):
-    return pl.pallas_call(
+    outs = pl.pallas_call(
         deal_kernel,
         in_specs=[SMEM, VMEM],
-        out_specs=(VMEM,) * 2,
-        out_shape=(jax.ShapeDtypeStruct((2, SLABS, 6, 8, 128), F32),) * 2,
+        out_specs=(VMEM,) * (2 * len(BLOCKS)),
+        out_shape=tuple(jax.ShapeDtypeStruct((2, n, 6, 8, 128), F32) for _, n in BLOCKS for _ in range(2)),
         compiler_params=pltpu.CompilerParams(vmem_limit_bytes=VMEM_LIMIT),
         cost_estimate=pl.CostEstimate(flops=0, bytes_accessed=3000000, transcendentals=0),
         name="deal",
     )(scalars, tiles)
+    return [outs[2 * b : 2 * b + 2] for b in range(len(BLOCKS))]
 
 
 def from_neighbour(payload, di, dj):
@@ -180,18 +222,46 @@
     return lax.ppermute(payload, AXES, pairs)
 
 
-def exchange(low, high):
-    up, down = from_neighbour(high, -1, 0), from_neighbour(low, 1, 0)
-    column = [jnp.stack([up[rz], low[rz], high[rz], down[rz]]) for rz in range(2)]
-    left, right = from_neighbour(column[1], 0, -1), from_neighbour(column[0], 0, 1)
-    return low, high, up, down, left, right
-
-
-def assemble(tile, p, u, low, high, up, down, left, right):
-    pieces = []
-    for row, ref in enumerate((up, low, high, down)):
-        pieces += [left[row, p, u], ref[0, p, u], ref[1, p, u], right[row, p, u]]
-    whole = swap_bits(pieces, [(3, 6), (2, 5), (1, 4), (0, 3)])
+def rows_beside(low, high):
+    return from_neighbour(high, -1, 0), from_neighbour(low, 1, 0)
+
+
+def columns_beside(columns):
+    return from_neighbour(columns[1], 0, -1), from_neighbour(columns[0], 0, 1)
+
+
+def columns_kernel(low, high, up, down, *refs):
+    for rz, ref in enumerate(refs[-2:]):
+
+        def position(i, carry, rz=rz, ref=ref):
+            for u in range(6):
+                arrays = [r[rz, i, u] for r in (up, low, high, down)]
+                for k, v in enumerate(swap_bits(arrays, [(1, 6), (0, 5)])):
+                    ref[k, i, u] = v
+            return carry
+
+        lax.fori_loop(0, ref.shape[1], position, 0)
+
+
+def columns(low, high, up, down, after=(), held=()):
+    n = low.shape[1]
+    outs = pl.pallas_call(
+        lambda *refs: columns_kernel(*refs[:4], *refs[-2:]),
+        in_specs=[VMEM] * 4 + [ANY] * (len(after) + len(held)),
+        out_specs=(ANY,) * len(held) + (VMEM,) * 2,
+        out_shape=tuple(jax.ShapeDtypeStruct(h.shape, F32) for h in held)
+        + (jax.ShapeDtypeStruct((4, n, 6, 8, 128), F32),) * 2,
+        input_output_aliases={4 + len(after) + k: k for k in range(len(held))},
+        compiler_params=pltpu.CompilerParams(vmem_limit_bytes=VMEM_LIMIT),
+        cost_estimate=pl.CostEstimate(flops=0, bytes_accessed=n * 800000, transcendentals=0),
+        name="columns",
+    )(low, high, up, down, *after, *held)
+    return outs[-2:], outs[:-2]
+
+
+def assemble(tile, p, u, first_half, second_half, left, right):
+    pieces = [ref[k, p, u] for k in range(4) for ref in (left, first_half, second_half, right)]
+    whole = swap_bits(pieces, [(1, 4), (0, 3)])
     return [jnp.where(tile.inside, v, 0.0) for v in whole]
 
 
@@ -251,18 +321,18 @@
     return lambda f, xp, ys: ref[at + (f, xp, ys)]
 
 
-def sweep_kernel(first, count, scalars, *refs):
-    halo, (out_ref, start_ref, old, one, two, ahead, rate, base) = refs[:6], refs[6:]
+def sweep_kernel(first, begin, count, scalars, *refs):
+    halo, (out_ref, start_ref, old, one, two, ahead, rate, base) = refs[:4], refs[-8:]
     tile = Tile(scalars)
 
     def position(at, carry):
         for array in range(3):
-            both = [assemble(tile, first + at, 2 * array + f, *halo) for f in range(2)]
+            both = [assemble(tile, begin + at, 2 * array + f, *halo) for f in range(2)]
             for f in range(2):
                 for (xp, ys), v in zip(CELLS, both[f], strict=True):
                     old[array, f, xp, ys] = v
 
-        if first == 0:
+        if first == begin == 0:
 
             @pl.when(at == 0)
             def _():
@@ -297,18 +367,18 @@
     lax.fori_loop(0, count, position, 0)
 
 
-def sweep(scalars, halo, first, count):
+def sweep(scalars, halo, first, begin, count, after=()):
     field = pltpu.VMEM(FIELD, F32)
     return pl.pallas_call(
-        functools.partial(sweep_kernel, first, count),
-        in_specs=[SMEM] + [VMEM] * 6,
+        functools.partial(sweep_kernel, first, begin, count),
+        in_specs=[SMEM] + [VMEM] * 4 + [ANY] * len(after),
         out_specs=(VMEM,) * 2,
         scratch_shapes=[pltpu.VMEM((3,) + FIELD, F32)] + [field] * 5,
         out_shape=(jax.ShapeDtypeStruct((count, 3) + FIELD, F32), jax.ShapeDtypeStruct(FIELD, F32)),
         compiler_params=pltpu.CompilerParams(vmem_limit_bytes=VMEM_LIMIT),
         cost_estimate=pl.CostEstimate(flops=count * 5 * 32 * 1024 * 40, bytes_accessed=count * 1200000, transcendentals=0),
-        name=f"sweep_{first}",
-    )(scalars, *halo)
+        name=f"sweep_{first + begin}",
+    )(scalars, *halo, *after)
 
 
 def write_packs(ref, at, loads):
@@ -322,7 +392,9 @@
         ref[at, r] = v
 
 
-def pack_kernel(in_ref, out_ref):
+def pack_kernel(in_ref, *refs):
+    out_ref = refs[-1]
+
     def position(i, carry):
         write_packs(out_ref, i, [reader(in_ref, i, array) for array in range(3)])
         return carry
@@ -330,38 +402,40 @@
     lax.fori_loop(0, out_ref.shape[0], position, 0)
 
 
-def pack(raw):
+def pack(raw, after=()):
     count = raw.shape[0]
     return pl.pallas_call(
         pack_kernel,
-        in_specs=[VMEM],
+        in_specs=[VMEM] + [ANY] * len(after),
         out_specs=VMEM,
         out_shape=jax.ShapeDtypeStruct((count, 24, 8, 128), F32),
         compiler_params=pltpu.CompilerParams(vmem_limit_bytes=VMEM_LIMIT),
         cost_estimate=pl.CostEstimate(flops=count * 1000000, bytes_accessed=count * 500000, transcendentals=0),
         name="pack",
-    )(raw)
-
-
-def chain_kernel(first, count, scalars, sweeps, *refs):
+    )(raw, *after)
+
+
+def chain_kernel(first, count, scalars, *refs):
     tile = Tile(scalars)
     last = first + count >= SLABS
     z, late, corr, one, two, ahead, next_z, next_late = refs[-8:]
-    refs = refs[:-8]
+    parts = 1 if first == 0 else 2
+    swept, refs = refs[:parts], refs[parts:-8]
     take_first = scalars[1] > 0
     if first == 0:
         start_ref, refs = refs[0], refs[1:]
         z[...] = start_ref[...]
     else:
         for k, ref in enumerate((z, late, corr)):
-            both = [assemble(tile, 0, 2 * k + f, *refs[:6]) for f in range(2)]
+            both = [assemble(tile, 0, 2 * k + f, *refs[:4]) for f in range(2)]
             for f in range(2):
                 for (xp, ys), v in zip(CELLS, both[f], strict=True):
                     ref[f, xp, ys] = v
-        refs = refs[6:]
+        refs = refs[4:]
     raw = refs[-1] if last else refs[0]
 
-    def step(at, final=False):
+    def step(at, sweeps=None, j=None):
+        final = sweeps is None
         p = first + at
         reset = (p == 0) | ((p == 1) & take_first)
         for xp, ys in CELLS:
@@ -375,9 +449,9 @@
                     one[f, xp, ys] = y0[f] + (H / 2) * f0[f]
                     two[f, xp, ys] = (-H / 2) * f0[f]
                 else:
-                    next_z[f, xp, ys] = g + sweeps[at, 0, f, xp, ys]
-                    one[f, xp, ys] = y0[f] + (5 * H / 24) * f0[f] + sweeps[at, 1, f, xp, ys]
-                    two[f, xp, ys] = sweeps[at, 2, f, xp, ys] - (5 * H / 6) * f0[f]
+                    next_z[f, xp, ys] = g + sweeps[j, 0, f, xp, ys]
+                    one[f, xp, ys] = y0[f] + (5 * H / 24) * f0[f] + sweeps[j, 1, f, xp, ys]
+                    two[f, xp, ys] = sweeps[j, 2, f, xp, ys] - (5 * H / 6) * f0[f]
         for xp, ys in CELLS:
             f1, _ = tile.tendency(reader(one), xp, ys)
             for f in range(2):
@@ -391,11 +465,15 @@
         raw[at, 1] = one[...]
         raw[at, 2] = two[...]
 
-    def looped(at, carry):
-        step(at)
-        return carry
-
-    lax.fori_loop(0, count, looped, 0)
+    at = 0
+    for ref in swept:
+
+        def looped(j, carry, at=at, ref=ref):
+            step(at + j, ref, j)
+            return carry
+
+        lax.fori_loop(0, ref.shape[0], looped, 0)
+        at += ref.shape[0]
 
     if not last:
         _, low_ref, high_ref = refs
@@ -407,7 +485,7 @@
                         half_ref[rz, 0, 2 * k + f] = both[f][ry][rz]
         return
 
-    step(count, final=True)
+    step(count)
     for xp, ys in CELLS:
         fl, l = tile.tendency(reader(late), xp, ys)
         for f in range(2):
@@ -432,10 +510,10 @@
     for b, ref in enumerate((*earlier, packs)):
 
         def move(i, carry, b=b, ref=ref):
-            put(b * BLOCK + i, ref, i)
+            put(BLOCKS[b][0] + i, ref, i)
             return carry
 
-        lax.fori_loop(0, count if ref is packs else BLOCK, move, 0)
+        lax.fori_loop(0, BLOCKS[b][1], move, 0)
 
     @pl.when(conv_one)
     def _():
@@ -450,7 +528,7 @@
         put(0, packs, count, newest=True)
 
 
-def chain(scalars, first, count, sweeps, inputs):
+def chain(scalars, first, count, inputs):
     last = first + count >= SLABS
     if last:
         out_shape = jax.ShapeDtypeStruct((SLABS * SLAB_ROWS, 128), F32)
@@ -461,14 +539,14 @@
         scratch = []
     return pl.pallas_call(
         functools.partial(chain_kernel, first, count),
-        in_specs=[SMEM] + [VMEM] * (1 + len(inputs)),
+        in_specs=[SMEM] + [VMEM] * len(inputs),
         out_specs=VMEM if last else (VMEM,) * 3,
         scratch_shapes=scratch + [pltpu.VMEM(FIELD, F32)] * 8,
         out_shape=out_shape,
         compiler_params=pltpu.CompilerParams(vmem_limit_bytes=VMEM_LIMIT),
         cost_estimate=pl.CostEstimate(flops=count * 3 * 32 * 1024 * 40, bytes_accessed=count * 500000, transcendentals=0),
         name=f"chain_{first}",
-    )(scalars, sweeps, *inputs)
+    )(scalars, *inputs)
 
 
 def body(slab_starts, slab_nodes, first_slab, converged):
@@ -477,16 +555,37 @@
     chunks = spread(slab_starts[0], slab_nodes[0])
     tiles = lax.all_to_all(chunks.reshape(128, 24, 128), AXES, 0, 0, tiled=True).reshape(SLABS * SLAB_ROWS, 128)
 
-    blocks = [(0, BLOCK), (BLOCK, BLOCK), (2 * BLOCK, SLABS - 2 * BLOCK)]
-    halo = exchange(*deal(scalars, tiles))
-    sweeps = [sweep(scalars, halo, *block) for block in blocks]
-    inputs = [sweeps[0][1]]
-    packs = []
-    for block, (swept, _) in zip(blocks[:-1], sweeps, strict=False):
-        raw, *state = chain(scalars, *block, swept, inputs)
-        packs.append(pack(raw))
-        inputs = exchange(*state)
-    out = chain(scalars, *blocks[-1], sweeps[-1][0], [*inputs, *packs])
+    half_a, half_b, half_c = deal(scalars, tiles)
+
+    rows = rows_beside(*half_a)
+    columns_a, half_b = columns(*half_a, *rows, held=half_b)
+    beside = columns_beside(columns_a)
+    rows = rows_beside(*half_b)
+    columns_b, half_c = columns(*half_b, *rows, after=beside, held=half_c)
+    beside_b = columns_beside(columns_b)
+    rows_c = rows_beside(*half_c)
+    swept, start = sweep(scalars, [*columns_a, *beside], 0, 0, 6, after=columns_b)
+    raw, *state = chain(scalars, *BLOCKS[0], [swept, start])
+
+    rows = rows_beside(*state)
+    columns_c, _ = columns(*half_c, *rows_c, after=state)
+    beside_c = columns_beside(columns_c)
+    halo_b = [*columns_b, *beside_b]
+    swept, _ = sweep(scalars, halo_b, 6, 0, 3, after=columns_c)
+    inside, _ = columns(*state, *rows, after=[swept])
+    beside = columns_beside(inside)
+    more, _ = sweep(scalars, halo_b, 6, 3, 3, after=inside)
+    raw_b, *state = chain(scalars, *BLOCKS[1], [swept, more, *inside, *beside])
+
+    rows = rows_beside(*state)
+    halo_c = [*columns_c, *beside_c]
+    packs_a = pack(raw, after=state)
+    swept, _ = sweep(scalars, halo_c, 12, 0, 2, after=state)
+    inside, _ = columns(*state, *rows, after=[swept, packs_a])
+    beside = columns_beside(inside)
+    more, _ = sweep(scalars, halo_c, 12, 2, 2, after=inside)
+    packs_b = pack(raw_b, after=inside)
+    out = chain(scalars, *BLOCKS[2], [swept, more, *inside, *beside, packs_a, packs_b])
     out = lax.all_to_all(out.reshape(128, 24, 128), AXES, 0, 0, tiled=True)
     starts, nodes = collect(out.reshape(128 * 24, 128))
     return starts[None], nodes[None]

time: 181 us -> 160 us (0.88)
  waiting for transfers between devices: 64 us -> 36.6 us
  starting transfers between devices: 27.7 us -> 36.4 us
  Pallas kernels: 53.2 us -> 50.9 us
    ppermute x12 -> x20, waiting for transfers between devices: 39.9 us -> 12.5 us  [from_neighbour(): return lax.ppermute(payload, AXES, pairs)]
    ppermute x12 -> x20, starting transfers between devices: 16.2 us -> 24.9 us  [from_neighbour(): return lax.ppermute(payload, AXES, pairs)]
    pallas_call x7 -> x14, Pallas kernels: 36.1 us -> 34.6 us  [the longest x5 19.8 us: sweep(): pl.pallas_call(functools.partial(sweep_kernel, first, begin, count), in_s...]
  transfers between devices with their start and end apart: 13 -> 21, of which waited for: 7 -> 6; matrix products, arithmetic and copies ran while one was open for 0% -> 0% of each run, Pallas kernels for 12% -> 20%
where the time goes in v4:
time: 160 us
  Pallas kernels  50.9 us (32%)
  waiting for transfers between devices  36.6 us (23%)
  starting transfers between devices  36.4 us (23%)
  blocking collectives  31.6 us (20%)
  local copies, waits for them, and re-layouts  2.27 us (1%)
  between operations  1.79 us (1%)
    all_to_all x1, blocking collectives, body(): out = lax.all_to_all(out.reshape(128, 24, 128), AXES, 0, 0, tiled=True)  31.6 us
    ppermute x20, starting transfers between devices, from_neighbour(): return lax.ppermute(payload, AXES, pairs)  24.9 us
    all_to_all x1, waiting for transfers between devices, body(): lax.all_to_all(chunks.reshape(128, 24, 128), AXES, 0, 0, tiled=True)  24.1 us
    pallas_call x5, Pallas kernels, sweep(): pl.pallas_call(functools.partial(sweep_kernel, first, begin, count), in_s...  19.8 us
    ppermute x20, waiting for transfers between devices, from_neighbour(): return lax.ppermute(payload, AXES, pairs)  12.5 us
    pallas_call x3, Pallas kernels, chain(): pl.pallas_call(functools.partial(chain_kernel, first, count), in_specs=[S...  12.1 us
    all_to_all x1, starting transfers between devices, body(): lax.all_to_all(chunks.reshape(128, 24, 128), AXES, 0, 0, tiled=True)  11.5 us
    pallas_call x5, Pallas kernels, columns(): pl.pallas_call(lambda *refs: columns_kernel(*refs[:4], *refs[-2:]), in_sp...  5.6 us
  transfers between devices with their start and end apart: 21, of which 6 were waited for; matrix products, arithmetic and copies ran while one was open for 0% of the time, Pallas kernels for 20%

profile of v4, /device:TPU:1, one launch (start us, length us, event | category | flops | bytes accessed | tf_op | source)
XLA Modules:
  0.0 159.7 jit_solution(10385017880189018104)
XLA Ops:
  2.9 4.6 %spread.1 = f32[3072,128]{1,0:T(8,128)} custom-call(f32[2,2,128,256]{3,2,1,0:T(8,128)S(1)} %bitcast.14, f32[2,2,2,128,256]{4,3,2,1,0:T(8,128)S(1)} %bitcast.13), custom_call_target="tpu_custom_call" | custom-call | tf_op jit(solution)/shard_map/spread/pallas_call | solution.py:123
  7.5 11.5 %all-to-all-start = ((f32[128,24,128]{2,1,0:T(8,128)}), f32[128,24,128]{2,1,0:T(8,128)S(1)}, u32[]{:S(2)}, u32[]{:S(2)}) async-start(f32[128,24,128]{2,1,0:T(8,128)} %bitcast.4), calls=%async_computation | async-start | bytes 3145728 | tf_op jit(solution)/shard_map/all_to_all | solution.py:556
  19.8 24.1 %all-to-all-done = f32[128,24,128]{2,1,0:T(8,128)S(1)} async-done(((f32[128,24,128]{2,1,0:T(8,128)}), f32[128,24,128]{2,1,0:T(8,128)S(1)}, u32[]{:S(2)}, u32[]{:S(2)}) %all-to-all-start) | async-done | bytes 1572896 | tf_op jit(solution)/shard_map/all_to_all | solution.py:556
  46.4 5.9 %collective-permute-done.refs_2_ = f32[2,6,6,8,128]{4,3,2,1,0:T(8,128)S(1)} collective-permute-done((f32[2,6,6,8,128]{4,3,2,1,0:T(8,128)S(1)}, f32[2,6,6,8,128]{4,3,2,1,0:T(8,128)S(1)}, u32[]{:S(2)}, u32[]{:S(2)}) %collective-permute-start) | collective-permute-done | bytes 294944 | tf_op jit(solution)/shard_map/ppermute | solution.py:222
  52.5 2.0 %columns.5 = (f32[2,6,6,8,128]{4,3,2,1,0:T(8,128)S(1)}, f32[2,6,6,8,128]{4,3,2,1,0:T(8,128)S(1)}, f32[4,6,6,8,128]{4,3,2,1,0:T(8,128)S(1)}, f32[4,6,6,8,128]{4,3,2,1,0:T(8,128)S(1)}) custom-call(f32[2,6,6,8,128]{4,3,2,1,0:T(8,128)S(1)} %get-tuple-element.36.refs_0_, ...), custom_call_target="tpu_custom_call", output_to_operand_aliasing={{0}: (4, {}), {1}: (5, {})} | custom-call | bytes 4800000 | tf_op jit(solution)/shard_map/columns/pallas_call | solution.py:248
  54.9 2.0 %collective-permute-start.5 = (f32[4,6,6,8,128]{4,3,2,1,0:T(8,128)S(1)}, f32[4,6,6,8,128]{4,3,2,1,0:T(8,128)S(1)}, u32[]{:S(2)}, u32[]{:S(2)}) collective-permute-start(f32[4,6,6,8,128]{4,3,2,1,0:T(8,128)S(1)} %get-tuple-element.43.refs_0_), channel_id=1, source_target_pairs={{8,0},{40,8},{32,40},{64,32},{72,64},{104,72},{96,104},{116,96},{1... | collective-permute-start | bytes 1769480 | tf_op jit(solution)/shard_map/ppermute | solution.py:222
  58.4 4.4 %collective-permute-done.2.refs_2_ = f32[2,6,6,8,128]{4,3,2,1,0:T(8,128)S(1)} collective-permute-done((f32[2,6,6,8,128]{4,3,2,1,0:T(8,128)S(1)}, f32[2,6,6,8,128]{4,3,2,1,0:T(8,128)S(1)}, u32[]{:S(2)}, u32[]{:S(2)}) %collective-permute-start.2) | collective-permute-done | bytes 294944 | tf_op jit(solution)/shard_map/ppermute | solution.py:222
  64.7 2.0 %columns.6 = (f32[2,4,6,8,128]{4,3,2,1,0:T(8,128)S(1)}, f32[2,4,6,8,128]{4,3,2,1,0:T(8,128)S(1)}, f32[4,6,6,8,128]{4,3,2,1,0:T(8,128)S(1)}, f32[4,6,6,8,128]{4,3,2,1,0:T(8,128)S(1)}) custom-call(f32[2,6,6,8,128]{4,3,2,1,0:T(8,128)S(1)} %get-tuple-element.40.refs_0_, ...), custom_call_target="tpu_custom_call", output_to_operand_aliasing={{0}: (6, {}), {1}: (7, {})} | custom-call | bytes 4800000 | tf_op jit(solution)/shard_map/columns/pallas_call | solution.py:248
  67.3 2.8 %collective-permute-start.11 = (f32[4,6,6,8,128]{4,3,2,1,0:T(8,128)S(1)}, f32[4,6,6,8,128]{4,3,2,1,0:T(8,128)S(1)}, u32[]{:S(2)}, u32[]{:S(2)}) collective-permute-start(f32[4,6,6,8,128]{4,3,2,1,0:T(8,128)S(1)} %get-tuple-element.48.refs_4_.refs_0_), channel_id=1, source_target_pairs={{8,0},{40,8},{32,40},{64,32},{72,64},{104,72},{96,104},{116,96},{1... | collective-permute-start | bytes 1769480 | tf_op jit(solution)/shard_map/ppermute | solution.py:222
  71.5 6.8 %sweep_0.1 = (f32[6,3,2,2,8,8,128]{6,5,4,3,2,1,0:T(8,128)S(1)}, f32[2,2,8,8,128]{4,3,2,1,0:T(8,128)S(1)}) custom-call(s32[5]{0:T(128)S(1)} %pad_add_fusion.scalars, f32[4,6,6,8,128]{4,3,2,1,0:T(8,128)S(1)} %get-tuple-element.43.refs_0_, f32[4,6,6,8,128]{4,3,2,1,0:T(8,128)S(1)} %get-tuple-element.42.refs_1_, ...), custom_call_target="tpu_custom_call" | custom-call | flops 39321600 | bytes 7200000 | tf_op jit(solution)/shard_map/sweep_0/pallas_call | solution.py:372
  78.3 3.1 %chain_0.1 = (f32[6,3,2,2,8,8,128]{6,5,4,3,2,1,0:T(8,128)S(1)}, f32[2,1,6,8,128]{4,3,2,1,0:T(8,128)S(1)}, f32[2,1,6,8,128]{4,3,2,1,0:T(8,128)S(1)}) custom-call(s32[5]{0:T(128)S(1)} %pad_add_fusion.scalars, f32[6,3,2,2,8,8,128]{6,5,4,3,2,1,0:T(8,128)S(1)} %get-tuple-element.50.refs_0_, f32[2,2,8,8,128]{4,3,2,1,0:T(8,128)S(1)} %get-tuple-element.51.refs_1_), custom_call_target="tpu_custom_call" | custom-call | flops 23592960 | bytes 3000000 | tf_op jit(solution)/shard_map/chain_0/pallas_call | solution.py:540
  82.8 3.9 %collective-permute-start.9 = (f32[4,4,6,8,128]{4,3,2,1,0:T(8,128)S(1)}, f32[4,4,6,8,128]{4,3,2,1,0:T(8,128)S(1)}, u32[]{:S(2)}, u32[]{:S(2)}) collective-permute-start(f32[4,4,6,8,128]{4,3,2,1,0:T(8,128)S(1)} %get-tuple-element.54.refs_4_.refs_0_), channel_id=1, source_target_pairs={{8,0},{40,8},{32,40},{64,32},{72,64},{104,72},{96,104},{116,96},{1... | collective-permute-start | bytes 1179656 | tf_op jit(solution)/shard_map/ppermute | solution.py:222
  88.2 3.8 %sweep_6.1 = (f32[3,3,2,2,8,8,128]{6,5,4,3,2,1,0:T(8,128)S(1)}, f32[2,2,8,8,128]{4,3,2,1,0:T(8,128)}) custom-call(s32[5]{0:T(128)S(1)} %pad_add_fusion.scalars, f32[4,6,6,8,128]{4,3,2,1,0:T(8,128)S(1)} %get-tuple-element.48.refs_4_.refs_0_, f32[4,6,6,8,128]{4,3,2,1,0:T(8,128)S(1)} %get-tuple-element.49.refs_5_.refs_1_, ...), custom_call_target="tpu_custom_call" | custom-call | flops 19660800 | bytes 3600000 | tf_op jit(solution)/shard_map/sweep_6/pallas_call | solution.py:372
  92.3 4.0 %collective-permute-start.15 = (f32[4,1,6,8,128]{4,3,2,1,0:T(8,128)S(1)}, f32[4,1,6,8,128]{4,3,2,1,0:T(8,128)S(1)}, u32[]{:S(2)}, u32[]{:S(2)}) collective-permute-start(f32[4,1,6,8,128]{4,3,2,1,0:T(8,128)S(1)} %get-tuple-element.57.refs_4_.refs_2_), channel_id=1, source_target_pairs={{8,0},{40,8},{32,40},{64,32},{72,64},{104,72},{96,104},{116,96},{1... | collective-permute-start | bytes 294920 | tf_op jit(solution)/shard_map/ppermute | solution.py:222
  96.3 3.8 %sweep_9.1 = (f32[3,3,2,2,8,8,128]{6,5,4,3,2,1,0:T(8,128)S(1)}, f32[2,2,8,8,128]{4,3,2,1,0:T(8,128)}) custom-call(s32[5]{0:T(128)S(1)} %pad_add_fusion.scalars, f32[4,6,6,8,128]{4,3,2,1,0:T(8,128)S(1)} %get-tuple-element.48.refs_4_.refs_0_, f32[4,6,6,8,128]{4,3,2,1,0:T(8,128)S(1)} %get-tuple-element.49.refs_5_.refs_1_, ...), custom_call_target="tpu_custom_call" | custom-call | flops 19660800 | bytes 3600000 | tf_op jit(solution)/shard_map/sweep_9/pallas_call | solution.py:372
  100.1 3.7 %chain_6.1 = (f32[6,3,2,2,8,8,128]{6,5,4,3,2,1,0:T(8,128)S(1)}, f32[2,1,6,8,128]{4,3,2,1,0:T(8,128)S(1)}, f32[2,1,6,8,128]{4,3,2,1,0:T(8,128)S(1)}) custom-call(s32[5]{0:T(128)S(1)} %pad_add_fusion.scalars, f32[3,3,2,2,8,8,128]{6,5,4,3,2,1,0:T(8,128)S(1)} %get-tuple-element.56.refs_4_.refs_0_, f32[3,3,2,2,8,8,128]{6,5,4,3,2,1,0:T(8,128)S(1)} %get-tuple-element.59.refs_1_, ...), custom_call_target="tpu_custom_call" | custom-call | flops 23592960 | bytes 3000000 | tf_op jit(solution)/shard_map/chain_6/pallas_call | solution.py:540
  105.4 1.8 %pack.2.refs_5_.refs_6_ = f32[6,24,8,128]{3,2,1,0:T(8,128)S(1)} custom-call(f32[6,3,2,2,8,8,128]{6,5,4,3,2,1,0:T(8,128)S(1)} %get-tuple-element.63.in_ref, f32[2,1,6,8,128]{4,3,2,1,0:T(8,128)S(1)} %get-tuple-element.60.refs_4_.refs_0_, f32[2,1,6,8,128]{4,3,2,1,0:T(8,128)S(1)} %get-tuple-element.61.refs_5_.refs_1_), custom_call_target="tpu_custom_call" | custom-call | flops 6000000 | bytes 3000000 | tf_op jit(solution)/shard_map/pack/pallas_call | solution.py:407
  107.2 2.7 %sweep_12.1 = (f32[2,3,2,2,8,8,128]{6,5,4,3,2,1,0:T(8,128)S(1)}, f32[2,2,8,8,128]{4,3,2,1,0:T(8,128)}) custom-call(s32[5]{0:T(128)S(1)} %pad_add_fusion.scalars, f32[4,4,6,8,128]{4,3,2,1,0:T(8,128)S(1)} %get-tuple-element.54.refs_4_.refs_0_, f32[4,4,6,8,128]{4,3,2,1,0:T(8,128)S(1)} %get-tuple-element.55.refs_5_.refs_1_, ...), custom_call_target="tpu_custom_call" | custom-call | flops 13107200 | bytes 2400000 | tf_op jit(solution)/shard_map/sweep_12/pallas_call | solution.py:372
  110.2 3.6 %collective-permute-start.19 = (f32[4,1,6,8,128]{4,3,2,1,0:T(8,128)S(1)}, f32[4,1,6,8,128]{4,3,2,1,0:T(8,128)S(1)}, u32[]{:S(2)}, u32[]{:S(2)}) collective-permute-start(f32[4,1,6,8,128]{4,3,2,1,0:T(8,128)S(1)} %get-tuple-element.64.refs_4_.refs_0_.refs_2_), channel_id=1, source_target_pairs={{8,0},{40,8},{32,40},{64,32},{72,64},{104,72},{96,104},{116,96},{1... | collective-permute-start | bytes 294920 | tf_op jit(solution)/shard_map/ppermute | solution.py:222
  113.8 1.8 %pack.3.refs_7_ = f32[6,24,8,128]{3,2,1,0:T(8,128)S(1)} custom-call(f32[6,3,2,2,8,8,128]{6,5,4,3,2,1,0:T(8,128)S(1)} %get-tuple-element.67.in_ref, f32[4,1,6,8,128]{4,3,2,1,0:T(8,128)S(1)} %get-tuple-element.64.refs_4_.refs_0_.refs_2_, f32[4,1,6,8,128]{4,3,2,1,0:T(8,128)S(1)} %get-tuple-element.65.refs_5_.refs_1_.refs_3_), custom_call_target="tpu_custom_call" | custom-call | flops 6000000 | bytes 3000000 | tf_op jit(solution)/shard_map/pack/pallas_call | solution.py:407
  115.7 2.7 %sweep_14.1 = (f32[2,3,2,2,8,8,128]{6,5,4,3,2,1,0:T(8,128)S(1)}, f32[2,2,8,8,128]{4,3,2,1,0:T(8,128)}) custom-call(s32[5]{0:T(128)S(1)} %pad_add_fusion.scalars, f32[4,4,6,8,128]{4,3,2,1,0:T(8,128)S(1)} %get-tuple-element.54.refs_4_.refs_0_, f32[4,4,6,8,128]{4,3,2,1,0:T(8,128)S(1)} %get-tuple-element.55.refs_5_.refs_1_, ...), custom_call_target="tpu_custom_call" | custom-call | flops 13107200 | bytes 2400000 | tf_op jit(solution)/shard_map/sweep_14/pallas_call | solution.py:372
  118.4 5.3 %chain_12.1 = f32[3072,128]{1,0:T(8,128)S(1)} custom-call(s32[5]{0:T(128)S(1)} %pad_add_fusion.scalars, f32[2,3,2,2,8,8,128]{6,5,4,3,2,1,0:T(8,128)S(1)} %get-tuple-element.62.refs_4_.refs_0_, f32[2,3,2,2,8,8,128]{6,5,4,3,2,1,0:T(8,128)S(1)} %get-tuple-element.66.refs_1_, f32[4,1,6,8,128]{4,3,2,1,0:T(8,128)S(1)} %get-tuple-element.64.refs_4_.refs_0_.refs_2_, ...), custom_call_target="tpu_custom_call" | custom-call | flops 15728640 | bytes 2000000 | tf_op jit(solution)/shard_map/chain_12/pallas_call | solution.py:540
  123.7 31.6 %all_to_all.10 = f32[128,24,128]{2,1,0:T(8,128)S(1)} all-to-all(f32[128,24,128]{2,1,0:T(8,128)S(1)} %bitcast.11), channel_id=1, replica_groups=mesh['tm'=16,'space'=8] {'tm','space'}, dimensions={0} | all-to-all | bytes 3145728 | tf_op jit(solution)/shard_map/all_to_all | solution.py:589
  155.4 4.1 %collect.1 = (f32[2,2,128,256]{3,2,1,0:T(8,128)}, f32[2,2,2,128,256]{4,3,2,1,0:T(8,128)}) custom-call(f32[3072,128]{1,0:T(8,128)S(1)} %bitcast.12), custom_call_target="tpu_custom_call" | custom-call | tf_op jit(solution)/shard_map/collect/pallas_call | solution.py:178
  (44 shorter events, 16.0 us)
Async XLA Ops:
  0.6 1.2 copy-start
  1.9 1.0 copy-start.1
  7.5 12.3 %copy-start.2 = (s32[2]{0:T(128)S(1)}, s32[2]{0:T(128)}, u32[]{:S(2)}) copy-start(s32[2]{0:T(128)} %param.7) | copy-start | bytes 28
  7.5 36.4 %all-to-all-start = ((f32[128,24,128]{2,1,0:T(8,128)}), f32[128,24,128]{2,1,0:T(8,128)S(1)}, u32[]{:S(2)}, u32[]{:S(2)}) async-start(f32[128,24,128]{2,1,0:T(8,128)} %bitcast.4), calls=%async_computation | async-start | bytes 3145728 | tf_op jit(solution)/shard_map/all_to_all | solution.py:556
  44.9 7.4 %collective-permute-start = (f32[2,6,6,8,128]{4,3,2,1,0:T(8,128)S(1)}, f32[2,6,6,8,128]{4,3,2,1,0:T(8,128)S(1)}, u32[]{:S(2)}, u32[]{:S(2)}) collective-permute-start(f32[2,6,6,8,128]{4,3,2,1,0:T(8,128)S(1)} %get-tuple-element.37.refs_1_), channel_id=1, source_target_pairs={{4,0},{12,8},{44,40},{36,32},{68,64},{76,72},{108,104},{100,96},{1... | collective-permute-start | bytes 884744 | tf_op jit(solution)/shard_map/ppermute | solution.py:222
  45.4 7.2 %collective-permute-start.1 = (f32[2,6,6,8,128]{4,3,2,1,0:T(8,128)S(1)}, f32[2,6,6,8,128]{4,3,2,1,0:T(8,128)S(1)}, u32[]{:S(2)}, u32[]{:S(2)}) collective-permute-start(f32[2,6,6,8,128]{4,3,2,1,0:T(8,128)S(1)} %get-tuple-element.36.refs_0_), channel_id=1, source_target_pairs={{1,0},{9,8},{41,40},{33,32},{65,64},{73,72},{105,104},{97,96},{117... | collective-permute-start | bytes 884744 | tf_op jit(solution)/shard_map/ppermute | solution.py:222
  54.5 8.5 %collective-permute-start.4 = (f32[4,6,6,8,128]{4,3,2,1,0:T(8,128)S(1)}, f32[4,6,6,8,128]{4,3,2,1,0:T(8,128)S(1)}, u32[]{:S(2)}, u32[]{:S(2)}) collective-permute-start(f32[4,6,6,8,128]{4,3,2,1,0:T(8,128)S(1)} %get-tuple-element.42.refs_1_), channel_id=1, source_target_pairs={{20,0},{0,8},{8,40},{40,32},{32,64},{64,72},{72,104},{104,96},{96,... | collective-permute-start | bytes 1769480 | tf_op jit(solution)/shard_map/ppermute | solution.py:222
  54.9 9.8 %collective-permute-start.5 = (f32[4,6,6,8,128]{4,3,2,1,0:T(8,128)S(1)}, f32[4,6,6,8,128]{4,3,2,1,0:T(8,128)S(1)}, u32[]{:S(2)}, u32[]{:S(2)}) collective-permute-start(f32[4,6,6,8,128]{4,3,2,1,0:T(8,128)S(1)} %get-tuple-element.43.refs_0_), channel_id=1, source_target_pairs={{8,0},{40,8},{32,40},{64,32},{72,64},{104,72},{96,104},{116,96},{1... | collective-permute-start | bytes 1769480 | tf_op jit(solution)/shard_map/ppermute | solution.py:222
  56.9 5.9 %collective-permute-start.2 = (f32[2,6,6,8,128]{4,3,2,1,0:T(8,128)S(1)}, f32[2,6,6,8,128]{4,3,2,1,0:T(8,128)S(1)}, u32[]{:S(2)}, u32[]{:S(2)}) collective-permute-start(f32[2,6,6,8,128]{4,3,2,1,0:T(8,128)S(1)} %get-tuple-element.41.refs_1_), channel_id=1, source_target_pairs={{4,0},{12,8},{44,40},{36,32},{68,64},{76,72},{108,104},{100,96},{1... | collective-permute-start | bytes 884744 | tf_op jit(solution)/shard_map/ppermute | solution.py:222
  57.1 5.9 %collective-permute-start.3 = (f32[2,6,6,8,128]{4,3,2,1,0:T(8,128)S(1)}, f32[2,6,6,8,128]{4,3,2,1,0:T(8,128)S(1)}, u32[]{:S(2)}, u32[]{:S(2)}) collective-permute-start(f32[2,6,6,8,128]{4,3,2,1,0:T(8,128)S(1)} %get-tuple-element.40.refs_0_), channel_id=1, source_target_pairs={{1,0},{9,8},{41,40},{33,32},{65,64},{73,72},{105,104},{97,96},{117... | collective-permute-start | bytes 884744 | tf_op jit(solution)/shard_map/ppermute | solution.py:222
  66.7 20.7 %collective-permute-start.10 = (f32[4,6,6,8,128]{4,3,2,1,0:T(8,128)S(1)}, f32[4,6,6,8,128]{4,3,2,1,0:T(8,128)S(1)}, u32[]{:S(2)}, u32[]{:S(2)}) collective-permute-start(f32[4,6,6,8,128]{4,3,2,1,0:T(8,128)S(1)} %get-tuple-element.49.refs_5_.refs_1_), channel_id=1, source_target_pairs={{20,0},{0,8},{8,40},{40,32},{32,64},{64,72},{72,104},{104,96},{96,... | collective-permute-start | bytes 1769480 | tf_op jit(solution)/shard_map/ppermute | solution.py:222
  67.3 20.9 %collective-permute-start.11 = (f32[4,6,6,8,128]{4,3,2,1,0:T(8,128)S(1)}, f32[4,6,6,8,128]{4,3,2,1,0:T(8,128)S(1)}, u32[]{:S(2)}, u32[]{:S(2)}) collective-permute-start(f32[4,6,6,8,128]{4,3,2,1,0:T(8,128)S(1)} %get-tuple-element.48.refs_4_.refs_0_), channel_id=1, source_target_pairs={{8,0},{40,8},{32,40},{64,32},{72,64},{104,72},{96,104},{116,96},{1... | collective-permute-start | bytes 1769480 | tf_op jit(solution)/shard_map/ppermute | solution.py:222
  70.1 11.4 %collective-permute-start.6 = (f32[2,4,6,8,128]{4,3,2,1,0:T(8,128)S(1)}, f32[2,4,6,8,128]{4,3,2,1,0:T(8,128)S(1)}, u32[]{:S(2)}, u32[]{:S(2)}) collective-permute-start(f32[2,4,6,8,128]{4,3,2,1,0:T(8,128)S(1)} %get-tuple-element.47.refs_1_), channel_id=1, source_target_pairs={{4,0},{12,8},{44,40},{36,32},{68,64},{76,72},{108,104},{100,96},{1... | collective-permute-start | bytes 589832 | tf_op jit(solution)/shard_map/ppermute | solution.py:222
  70.9 10.6 %collective-permute-start.7 = (f32[2,4,6,8,128]{4,3,2,1,0:T(8,128)S(1)}, f32[2,4,6,8,128]{4,3,2,1,0:T(8,128)S(1)}, u32[]{:S(2)}, u32[]{:S(2)}) collective-permute-start(f32[2,4,6,8,128]{4,3,2,1,0:T(8,128)S(1)} %get-tuple-element.46.refs_0_), channel_id=1, source_target_pairs={{1,0},{9,8},{41,40},{33,32},{65,64},{73,72},{105,104},{97,96},{117... | collective-permute-start | bytes 589832 | tf_op jit(solution)/shard_map/ppermute | solution.py:222
  82.8 24.4 %collective-permute-start.8 = (f32[4,4,6,8,128]{4,3,2,1,0:T(8,128)S(1)}, f32[4,4,6,8,128]{4,3,2,1,0:T(8,128)S(1)}, u32[]{:S(2)}, u32[]{:S(2)}) collective-permute-start(f32[4,4,6,8,128]{4,3,2,1,0:T(8,128)S(1)} %get-tuple-element.55.refs_5_.refs_1_), channel_id=1, source_target_pairs={{20,0},{0,8},{8,40},{40,32},{32,64},{64,72},{72,104},{104,96},{96,... | collective-permute-start | bytes 1179656 | tf_op jit(solution)/shard_map/ppermute | solution.py:222
  82.8 24.4 %collective-permute-start.9 = (f32[4,4,6,8,128]{4,3,2,1,0:T(8,128)S(1)}, f32[4,4,6,8,128]{4,3,2,1,0:T(8,128)S(1)}, u32[]{:S(2)}, u32[]{:S(2)}) collective-permute-start(f32[4,4,6,8,128]{4,3,2,1,0:T(8,128)S(1)} %get-tuple-element.54.refs_4_.refs_0_), channel_id=1, source_target_pairs={{8,0},{40,8},{32,40},{64,32},{72,64},{104,72},{96,104},{116,96},{1... | collective-permute-start | bytes 1179656 | tf_op jit(solution)/shard_map/ppermute | solution.py:222
  86.7 5.3 %collective-permute-start.12 = (f32[2,1,6,8,128]{4,3,2,1,0:T(8,128)S(1)}, f32[2,1,6,8,128]{4,3,2,1,0:T(8,128)S(1)}, u32[]{:S(2)}, u32[]{:S(2)}) collective-permute-start(f32[2,1,6,8,128]{4,3,2,1,0:T(8,128)S(1)} %get-tuple-element.53.refs_5_.refs_1_), channel_id=1, source_target_pairs={{4,0},{12,8},{44,40},{36,32},{68,64},{76,72},{108,104},{100,96},{1... | collective-permute-start | bytes 147464 | tf_op jit(solution)/shard_map/ppermute | solution.py:222
  87.4 4.6 %collective-permute-start.13 = (f32[2,1,6,8,128]{4,3,2,1,0:T(8,128)S(1)}, f32[2,1,6,8,128]{4,3,2,1,0:T(8,128)S(1)}, u32[]{:S(2)}, u32[]{:S(2)}) collective-permute-start(f32[2,1,6,8,128]{4,3,2,1,0:T(8,128)S(1)} %get-tuple-element.52.refs_4_.refs_0_), channel_id=1, source_target_pairs={{1,0},{9,8},{41,40},{33,32},{65,64},{73,72},{105,104},{97,96},{117... | collective-permute-start | bytes 147464 | tf_op jit(solution)/shard_map/ppermute | solution.py:222
  92.2 7.9 %collective-permute-start.14 = (f32[4,1,6,8,128]{4,3,2,1,0:T(8,128)S(1)}, f32[4,1,6,8,128]{4,3,2,1,0:T(8,128)S(1)}, u32[]{:S(2)}, u32[]{:S(2)}) collective-permute-start(f32[4,1,6,8,128]{4,3,2,1,0:T(8,128)S(1)} %get-tuple-element.58.refs_5_.refs_3_), channel_id=1, source_target_pairs={{20,0},{0,8},{8,40},{40,32},{32,64},{64,72},{72,104},{104,96},{96,... | collective-permute-start | bytes 294920 | tf_op jit(solution)/shard_map/ppermute | solution.py:222
  92.3 7.8 %collective-permute-start.15 = (f32[4,1,6,8,128]{4,3,2,1,0:T(8,128)S(1)}, f32[4,1,6,8,128]{4,3,2,1,0:T(8,128)S(1)}, u32[]{:S(2)}, u32[]{:S(2)}) collective-permute-start(f32[4,1,6,8,128]{4,3,2,1,0:T(8,128)S(1)} %get-tuple-element.57.refs_4_.refs_2_), channel_id=1, source_target_pairs={{8,0},{40,8},{32,40},{64,32},{72,64},{104,72},{96,104},{116,96},{1... | collective-permute-start | bytes 294920 | tf_op jit(solution)/shard_map/ppermute | solution.py:222
  103.8 6.1 %collective-permute-start.16 = (f32[2,1,6,8,128]{4,3,2,1,0:T(8,128)S(1)}, f32[2,1,6,8,128]{4,3,2,1,0:T(8,128)S(1)}, u32[]{:S(2)}, u32[]{:S(2)}) collective-permute-start(f32[2,1,6,8,128]{4,3,2,1,0:T(8,128)S(1)} %get-tuple-element.61.refs_5_.refs_1_), channel_id=1, source_target_pairs={{4,0},{12,8},{44,40},{36,32},{68,64},{76,72},{108,104},{100,96},{1... | collective-permute-start | bytes 147464 | tf_op jit(solution)/shard_map/ppermute | solution.py:222
  104.6 5.3 %collective-permute-start.17 = (f32[2,1,6,8,128]{4,3,2,1,0:T(8,128)S(1)}, f32[2,1,6,8,128]{4,3,2,1,0:T(8,128)S(1)}, u32[]{:S(2)}, u32[]{:S(2)}) collective-permute-start(f32[2,1,6,8,128]{4,3,2,1,0:T(8,128)S(1)} %get-tuple-element.60.refs_4_.refs_0_), channel_id=1, source_target_pairs={{1,0},{9,8},{41,40},{33,32},{65,64},{73,72},{105,104},{97,96},{117... | collective-permute-start | bytes 147464 | tf_op jit(solution)/shard_map/ppermute | solution.py:222
  110.1 8.3 %collective-permute-start.18 = (f32[4,1,6,8,128]{4,3,2,1,0:T(8,128)S(1)}, f32[4,1,6,8,128]{4,3,2,1,0:T(8,128)S(1)}, u32[]{:S(2)}, u32[]{:S(2)}) collective-permute-start(f32[4,1,6,8,128]{4,3,2,1,0:T(8,128)S(1)} %get-tuple-element.65.refs_5_.refs_1_.refs_3_), channel_id=1, source_target_pairs={{20,0},{0,8},{8,40},{40,32},{32,64},{64,72},{72,104},{104,96},{96,... | collective-permute-start | bytes 294920 | tf_op jit(solution)/shard_map/ppermute | solution.py:222
  110.2 8.2 %collective-permute-start.19 = (f32[4,1,6,8,128]{4,3,2,1,0:T(8,128)S(1)}, f32[4,1,6,8,128]{4,3,2,1,0:T(8,128)S(1)}, u32[]{:S(2)}, u32[]{:S(2)}) collective-permute-start(f32[4,1,6,8,128]{4,3,2,1,0:T(8,128)S(1)} %get-tuple-element.64.refs_4_.refs_0_.refs_2_), channel_id=1, source_target_pairs={{8,0},{40,8},{32,40},{64,32},{72,64},{104,72},{96,104},{116,96},{1... | collective-permute-start | bytes 294920 | tf_op jit(solution)/shard_map/ppermute | solution.py:222

commit v5 on v4

--- a/solution.py
+++ b/solution.py
@@ -13,6 +13,7 @@
 EDGE = 16
 RIM = 8
 BLOCKS = ((0, 6), (6, 6), (12, 4))
+SETS = ((0, 6), (6, 10))
 H = 0.5
 AXES = ("tm", "space")
 F32 = jnp.float32
@@ -21,6 +22,7 @@
 VMEM = pl.BlockSpec(memory_space=pltpu.VMEM)
 SMEM = pl.BlockSpec(memory_space=pltpu.SMEM)
 ANY = pl.BlockSpec(memory_space=pl.ANY)
+HBM = pl.BlockSpec(memory_space=pltpu.HBM)
 SLAB_ROWS = 192
 
 
@@ -61,12 +63,15 @@
     arrays, lane = list(arrays), lanes()
     for index_bit, lane_bit in pairs:
         step, low = 1 << lane_bit, (lane >> lane_bit) % 2 == 0
+        across = lane ^ step
         for a in range(len(arrays)):
             b = a | (1 << index_bit)
             if a != b:
                 u, v = arrays[a], arrays[b]
-                arrays[a] = jnp.where(low, u, roll(v, step))
-                arrays[b] = jnp.where(low, roll(u, -step), v)
+                moved = jnp.where(low, v, u)
+                moved = roll(moved, 64) if step == 64 else jnp.take_along_axis(moved, across, axis=1)
+                arrays[a] = jnp.where(low, u, moved)
+                arrays[b] = jnp.where(low, moved, v)
     return arrays
 
 
@@ -122,7 +127,7 @@
 def spread(starts, nodes):
     return pl.pallas_call(
         spread_kernel,
-        in_specs=[ANY, ANY],
+        in_specs=[HBM, HBM],
         out_specs=VMEM,
         out_shape=jax.ShapeDtypeStruct((128 * 24, 128), F32),
         scratch_shapes=[pltpu.VMEM((6, 2, 2, 128, 128), F32), pltpu.SemaphoreType.DMA((24,))],
@@ -190,7 +195,7 @@
 
 
 def deal_kernel(scalars, in_ref, *out_refs):
-    for b, (first, count) in enumerate(BLOCKS):
+    for b, (first, count) in enumerate(SETS):
 
         def position(i, carry, b=b, first=first):
             base = lax.rem(scalars[0] + (first + i), SLABS) * SLAB_ROWS
@@ -208,13 +213,13 @@
     outs = pl.pallas_call(
         deal_kernel,
         in_specs=[SMEM, VMEM],
-        out_specs=(VMEM,) * (2 * len(BLOCKS)),
-        out_shape=tuple(jax.ShapeDtypeStruct((2, n, 6, 8, 128), F32) for _, n in BLOCKS for _ in range(2)),
+        out_specs=(VMEM,) * (2 * len(SETS)),
+        out_shape=tuple(jax.ShapeDtypeStruct((2, n, 6, 8, 128), F32) for _, n in SETS for _ in range(2)),
         compiler_params=pltpu.CompilerParams(vmem_limit_bytes=VMEM_LIMIT),
         cost_estimate=pl.CostEstimate(flops=0, bytes_accessed=3000000, transcendentals=0),
         name="deal",
     )(scalars, tiles)
-    return [outs[2 * b : 2 * b + 2] for b in range(len(BLOCKS))]
+    return [outs[2 * b : 2 * b + 2] for b in range(len(SETS))]
 
 
 def from_neighbour(payload, di, dj):
@@ -555,35 +560,30 @@
     chunks = spread(slab_starts[0], slab_nodes[0])
     tiles = lax.all_to_all(chunks.reshape(128, 24, 128), AXES, 0, 0, tiled=True).reshape(SLABS * SLAB_ROWS, 128)
 
-    half_a, half_b, half_c = deal(scalars, tiles)
+    half_a, half_b = deal(scalars, tiles)
 
     rows = rows_beside(*half_a)
     columns_a, half_b = columns(*half_a, *rows, held=half_b)
     beside = columns_beside(columns_a)
     rows = rows_beside(*half_b)
-    columns_b, half_c = columns(*half_b, *rows, after=beside, held=half_c)
-    beside_b = columns_beside(columns_b)
-    rows_c = rows_beside(*half_c)
+    columns_b, _ = columns(*half_b, *rows, after=beside)
+    halo = [*columns_b, *columns_beside(columns_b)]
     swept, start = sweep(scalars, [*columns_a, *beside], 0, 0, 6, after=columns_b)
     raw, *state = chain(scalars, *BLOCKS[0], [swept, start])
 
     rows = rows_beside(*state)
-    columns_c, _ = columns(*half_c, *rows_c, after=state)
-    beside_c = columns_beside(columns_c)
-    halo_b = [*columns_b, *beside_b]
-    swept, _ = sweep(scalars, halo_b, 6, 0, 3, after=columns_c)
+    swept, _ = sweep(scalars, halo, 6, 0, 3, after=state)
     inside, _ = columns(*state, *rows, after=[swept])
     beside = columns_beside(inside)
-    more, _ = sweep(scalars, halo_b, 6, 3, 3, after=inside)
+    more, _ = sweep(scalars, halo, 6, 3, 3, after=inside)
     raw_b, *state = chain(scalars, *BLOCKS[1], [swept, more, *inside, *beside])
 
     rows = rows_beside(*state)
-    halo_c = [*columns_c, *beside_c]
     packs_a = pack(raw, after=state)
-    swept, _ = sweep(scalars, halo_c, 12, 0, 2, after=state)
+    swept, _ = sweep(scalars, halo, 6, 6, 2, after=state)
     inside, _ = columns(*state, *rows, after=[swept, packs_a])
     beside = columns_beside(inside)
-    more, _ = sweep(scalars, halo_c, 12, 2, 2, after=inside)
+    more, _ = sweep(scalars, halo, 6, 8, 2, after=inside)
     packs_b = pack(raw_b, after=inside)
     out = chain(scalars, *BLOCKS[2], [swept, more, *inside, *beside, packs_a, packs_b])
     out = lax.all_to_all(out.reshape(128, 24, 128), AXES, 0, 0, tiled=True)

time: 160 us -> 156 us (0.975)
  starting transfers between devices: 36.4 us -> 30.6 us
  waiting for transfers between devices: 36.6 us -> 41.3 us
  Pallas kernels: 50.9 us -> 46.3 us
    ppermute x20 -> x16, starting transfers between devices: 24.9 us -> 19.1 us  [from_neighbour(): return lax.ppermute(payload, AXES, pairs)]
    ppermute x20 -> x16, waiting for transfers between devices: 12.5 us -> 17.2 us  [from_neighbour(): return lax.ppermute(payload, AXES, pairs)]
    pallas_call x5, Pallas kernels: 19.8 us -> 17 us  [sweep(): pl.pallas_call(functools.partial(sweep_kernel, first, begin, count), in_s...]
    pallas_call x5 -> x4, Pallas kernels: 5.6 us -> 5.36 us  [columns(): pl.pallas_call(lambda *refs: columns_kernel(*refs[:4], *refs[-2:]), in_sp...]
  transfers between devices with their start and end apart: 21 -> 17, of which waited for: 6 -> 6; matrix products, arithmetic and copies ran while one was open for 0% -> 0% of each run, Pallas kernels for 20% -> 15%
where the time goes in v5:
time: 156 us; the launch traced here: 155 us
  Pallas kernels  46.3 us (30%)
  waiting for transfers between devices  41.3 us (26%)
  blocking collectives  33 us (21%)
  starting transfers between devices  30.6 us (20%)
  local copies, waits for them, and re-layouts  2.27 us (1%)
  between operations  1.75 us (1%)
    all_to_all x1, blocking collectives, body(): out = lax.all_to_all(out.reshape(128, 24, 128), AXES, 0, 0, tiled=True)  33 us
    all_to_all x1, waiting for transfers between devices, body(): lax.all_to_all(chunks.reshape(128, 24, 128), AXES, 0, 0, tiled=True)  24.1 us
    ppermute x16, starting transfers between devices, from_neighbour(): return lax.ppermute(payload, AXES, pairs)  19.1 us
    ppermute x16, waiting for transfers between devices, from_neighbour(): return lax.ppermute(payload, AXES, pairs)  17.2 us
    pallas_call x5, Pallas kernels, sweep(): pl.pallas_call(functools.partial(sweep_kernel, first, begin, count), in_s...  17 us
    pallas_call x3, Pallas kernels, chain(): pl.pallas_call(functools.partial(chain_kernel, first, count), in_specs=[S...  11.8 us
    all_to_all x1, starting transfers between devices, body(): lax.all_to_all(chunks.reshape(128, 24, 128), AXES, 0, 0, tiled=True)  11.5 us
    pallas_call x4, Pallas kernels, columns(): pl.pallas_call(lambda *refs: columns_kernel(*refs[:4], *refs[-2:]), in_sp...  5.36 us
  transfers between devices with their start and end apart: 17, of which 6 were waited for; matrix products, arithmetic and copies ran while one was open for 0% of the time, Pallas kernels for 15%

profile of v5, /device:TPU:1, one launch (start us, length us, event | category | flops | bytes accessed | tf_op | source)
XLA Modules:
  0.0 155.3 jit_solution(18418609843423255622)
XLA Ops:
  2.9 3.6 %spread.1 = f32[3072,128]{1,0:T(8,128)} custom-call(f32[2,2,128,256]{3,2,1,0:T(8,128)S(1)} %bitcast.14, f32[2,2,2,128,256]{4,3,2,1,0:T(8,128)S(1)} %bitcast.13), custom_call_target="tpu_custom_call" | custom-call | tf_op jit(solution)/shard_map/spread/pallas_call | solution.py:128
  6.5 11.5 %all-to-all-start = ((f32[128,24,128]{2,1,0:T(8,128)}), f32[128,24,128]{2,1,0:T(8,128)S(1)}, u32[]{:S(2)}, u32[]{:S(2)}) async-start(f32[128,24,128]{2,1,0:T(8,128)} %bitcast.4), calls=%async_computation | async-start | bytes 3145728 | tf_op jit(solution)/shard_map/all_to_all | solution.py:561
  18.9 24.1 %all-to-all-done = f32[128,24,128]{2,1,0:T(8,128)S(1)} async-done(((f32[128,24,128]{2,1,0:T(8,128)}), f32[128,24,128]{2,1,0:T(8,128)S(1)}, u32[]{:S(2)}, u32[]{:S(2)}) %all-to-all-start) | async-done | bytes 1572896 | tf_op jit(solution)/shard_map/all_to_all | solution.py:561
  45.5 5.9 %collective-permute-done.1.refs_3_ = f32[2,6,6,8,128]{4,3,2,1,0:T(8,128)S(1)} collective-permute-done((f32[2,6,6,8,128]{4,3,2,1,0:T(8,128)S(1)}, f32[2,6,6,8,128]{4,3,2,1,0:T(8,128)S(1)}, u32[]{:S(2)}, u32[]{:S(2)}) %collective-permute-start.1) | collective-permute-done | bytes 294944 | tf_op jit(solution)/shard_map/ppermute | solution.py:227
  52.2 1.9 %columns.4 = (f32[2,10,6,8,128]{4,3,2,1,0:T(8,128)S(1)}, f32[2,10,6,8,128]{4,3,2,1,0:T(8,128)S(1)}, f32[4,6,6,8,128]{4,3,2,1,0:T(8,128)S(1)}, f32[4,6,6,8,128]{4,3,2,1,0:T(8,128)S(1)}) custom-call(f32[2,6,6,8,128]{4,3,2,1,0:T(8,128)S(1)} %get-tuple-element.30.refs_0_, ...), custom_call_target="tpu_custom_call", output_to_operand_aliasing={{0}: (4, {}), {1}: (5, {})} | custom-call | bytes 4800000 | tf_op jit(solution)/shard_map/columns/pallas_call | solution.py:253
  54.5 1.4 collective-permute-start.5
  57.4 8.1 %collective-permute-done.3.refs_3_ = f32[2,10,6,8,128]{4,3,2,1,0:T(8,128)S(1)} collective-permute-done((f32[2,10,6,8,128]{4,3,2,1,0:T(8,128)S(1)}, f32[2,10,6,8,128]{4,3,2,1,0:T(8,128)S(1)}, u32[]{:S(2)}, u32[]{:S(2)}) %collective-permute-start.3) | collective-permute-done | bytes 491552 | tf_op jit(solution)/shard_map/ppermute | solution.py:227
  66.5 3.1 %columns.5 = (f32[4,10,6,8,128]{4,3,2,1,0:T(8,128)S(1)}, f32[4,10,6,8,128]{4,3,2,1,0:T(8,128)S(1)}) custom-call(f32[2,10,6,8,128]{4,3,2,1,0:T(8,128)S(1)} %get-tuple-element.34.refs_0_, f32[2,10,6,8,128]{4,3,2,1,0:T(8,128)S(1)} %get-tuple-element.35.refs_1_, f32[2,10,6,8,128]{4,3,2,1,0:T(8,128)S(1)} %collective-permute-done.2.refs_2_, ...), custom_call_target="tpu_custom_call" | custom-call | bytes 8000000 | tf_op jit(solution)/shard_map/columns/pallas_call | solution.py:253
  69.6 3.7 %collective-permute-start.7 = (f32[4,10,6,8,128]{4,3,2,1,0:T(8,128)S(1)}, f32[4,10,6,8,128]{4,3,2,1,0:T(8,128)S(1)}, u32[]{:S(2)}, u32[]{:S(2)}) collective-permute-start(f32[4,10,6,8,128]{4,3,2,1,0:T(8,128)S(1)} %get-tuple-element.38.refs_4_.refs_0_), channel_id=1, source_target_pairs={{8,0},{40,8},{32,40},{64,32},{72,64},{104,72},{96,104},{116,96},{1... | collective-permute-start | bytes 2949128 | tf_op jit(solution)/shard_map/ppermute | solution.py:227
  73.4 5.7 %sweep_0.1 = (f32[6,3,2,2,8,8,128]{6,5,4,3,2,1,0:T(8,128)S(1)}, f32[2,2,8,8,128]{4,3,2,1,0:T(8,128)S(1)}) custom-call(s32[5]{0:T(128)S(1)} %pad_add_fusion.scalars, f32[4,6,6,8,128]{4,3,2,1,0:T(8,128)S(1)} %get-tuple-element.37.refs_0_, f32[4,6,6,8,128]{4,3,2,1,0:T(8,128)S(1)} %get-tuple-element.36.refs_1_, ...), custom_call_target="tpu_custom_call" | custom-call | flops 39321600 | bytes 7200000 | tf_op jit(solution)/shard_map/sweep_0/pallas_call | solution.py:377
  79.1 3.1 %chain_0.1 = (f32[6,3,2,2,8,8,128]{6,5,4,3,2,1,0:T(8,128)S(1)}, f32[2,1,6,8,128]{4,3,2,1,0:T(8,128)S(1)}, f32[2,1,6,8,128]{4,3,2,1,0:T(8,128)S(1)}) custom-call(s32[5]{0:T(128)S(1)} %pad_add_fusion.scalars, f32[6,3,2,2,8,8,128]{6,5,4,3,2,1,0:T(8,128)S(1)} %get-tuple-element.40.refs_0_, f32[2,2,8,8,128]{4,3,2,1,0:T(8,128)S(1)} %get-tuple-element.41.refs_1_), custom_call_target="tpu_custom_call" | custom-call | flops 23592960 | bytes 3000000 | tf_op jit(solution)/shard_map/chain_0/pallas_call | solution.py:545
  85.1 3.3 %sweep_6.1 = (f32[3,3,2,2,8,8,128]{6,5,4,3,2,1,0:T(8,128)S(1)}, f32[2,2,8,8,128]{4,3,2,1,0:T(8,128)}) custom-call(s32[5]{0:T(128)S(1)} %pad_add_fusion.scalars, f32[4,10,6,8,128]{4,3,2,1,0:T(8,128)S(1)} %get-tuple-element.38.refs_4_.refs_0_, f32[4,10,6,8,128]{4,3,2,1,0:T(8,128)S(1)} %get-tuple-element.39.refs_5_.refs_1_, ...), custom_call_target="tpu_custom_call" | custom-call | flops 19660800 | bytes 3600000 | tf_op jit(solution)/shard_map/sweep_6/pallas_call | solution.py:377
  88.6 4.2 %collective-permute-start.11 = (f32[4,1,6,8,128]{4,3,2,1,0:T(8,128)S(1)}, f32[4,1,6,8,128]{4,3,2,1,0:T(8,128)S(1)}, u32[]{:S(2)}, u32[]{:S(2)}) collective-permute-start(f32[4,1,6,8,128]{4,3,2,1,0:T(8,128)S(1)} %get-tuple-element.45.refs_4_.refs_2_), channel_id=1, source_target_pairs={{8,0},{40,8},{32,40},{64,32},{72,64},{104,72},{96,104},{116,96},{1... | collective-permute-start | bytes 294920 | tf_op jit(solution)/shard_map/ppermute | solution.py:227
  92.8 3.3 %sweep_9.1 = (f32[3,3,2,2,8,8,128]{6,5,4,3,2,1,0:T(8,128)S(1)}, f32[2,2,8,8,128]{4,3,2,1,0:T(8,128)}) custom-call(s32[5]{0:T(128)S(1)} %pad_add_fusion.scalars, f32[4,10,6,8,128]{4,3,2,1,0:T(8,128)S(1)} %get-tuple-element.38.refs_4_.refs_0_, f32[4,10,6,8,128]{4,3,2,1,0:T(8,128)S(1)} %get-tuple-element.39.refs_5_.refs_1_, ...), custom_call_target="tpu_custom_call" | custom-call | flops 19660800 | bytes 3600000 | tf_op jit(solution)/shard_map/sweep_9/pallas_call | solution.py:377
  96.1 3.5 %chain_6.1 = (f32[6,3,2,2,8,8,128]{6,5,4,3,2,1,0:T(8,128)S(1)}, f32[2,1,6,8,128]{4,3,2,1,0:T(8,128)S(1)}, f32[2,1,6,8,128]{4,3,2,1,0:T(8,128)S(1)}) custom-call(s32[5]{0:T(128)S(1)} %pad_add_fusion.scalars, f32[3,3,2,2,8,8,128]{6,5,4,3,2,1,0:T(8,128)S(1)} %get-tuple-element.44.refs_4_.refs_0_, f32[3,3,2,2,8,8,128]{6,5,4,3,2,1,0:T(8,128)S(1)} %get-tuple-element.47.refs_1_, ...), custom_call_target="tpu_custom_call" | custom-call | flops 23592960 | bytes 3000000 | tf_op jit(solution)/shard_map/chain_6/pallas_call | solution.py:545
  99.7 1.7 %collective-permute-start.12 = (f32[2,1,6,8,128]{4,3,2,1,0:T(8,128)S(1)}, f32[2,1,6,8,128]{4,3,2,1,0:T(8,128)S(1)}, u32[]{:S(2)}, u32[]{:S(2)}) collective-permute-start(f32[2,1,6,8,128]{4,3,2,1,0:T(8,128)S(1)} %get-tuple-element.49.refs_5_.refs_1_), channel_id=1, source_target_pairs={{4,0},{12,8},{44,40},{36,32},{68,64},{76,72},{108,104},{100,96},{1... | collective-permute-start | bytes 147464 | tf_op jit(solution)/shard_map/ppermute | solution.py:227
  101.4 1.8 %pack.2.refs_5_.refs_6_ = f32[6,24,8,128]{3,2,1,0:T(8,128)S(1)} custom-call(f32[6,3,2,2,8,8,128]{6,5,4,3,2,1,0:T(8,128)S(1)} %get-tuple-element.51.in_ref, f32[2,1,6,8,128]{4,3,2,1,0:T(8,128)S(1)} %get-tuple-element.48.refs_4_.refs_0_, f32[2,1,6,8,128]{4,3,2,1,0:T(8,128)S(1)} %get-tuple-element.49.refs_5_.refs_1_), custom_call_target="tpu_custom_call" | custom-call | flops 6000000 | bytes 3000000 | tf_op jit(solution)/shard_map/pack/pallas_call | solution.py:412
  103.3 2.4 %sweep_12.1 = (f32[2,3,2,2,8,8,128]{6,5,4,3,2,1,0:T(8,128)S(1)}, f32[2,2,8,8,128]{4,3,2,1,0:T(8,128)}) custom-call(s32[5]{0:T(128)S(1)} %pad_add_fusion.scalars, f32[4,10,6,8,128]{4,3,2,1,0:T(8,128)S(1)} %get-tuple-element.38.refs_4_.refs_0_, f32[4,10,6,8,128]{4,3,2,1,0:T(8,128)S(1)} %get-tuple-element.39.refs_5_.refs_1_, ...), custom_call_target="tpu_custom_call" | custom-call | flops 13107200 | bytes 2400000 | tf_op jit(solution)/shard_map/sweep_12/pallas_call | solution.py:377
  105.9 3.0 %collective-permute-start.15 = (f32[4,1,6,8,128]{4,3,2,1,0:T(8,128)S(1)}, f32[4,1,6,8,128]{4,3,2,1,0:T(8,128)S(1)}, u32[]{:S(2)}, u32[]{:S(2)}) collective-permute-start(f32[4,1,6,8,128]{4,3,2,1,0:T(8,128)S(1)} %get-tuple-element.52.refs_4_.refs_0_.refs_2_), channel_id=1, source_target_pairs={{8,0},{40,8},{32,40},{64,32},{72,64},{104,72},{96,104},{116,96},{1... | collective-permute-start | bytes 294920 | tf_op jit(solution)/shard_map/ppermute | solution.py:227
  108.8 1.8 %pack.3.refs_7_ = f32[6,24,8,128]{3,2,1,0:T(8,128)S(1)} custom-call(f32[6,3,2,2,8,8,128]{6,5,4,3,2,1,0:T(8,128)S(1)} %get-tuple-element.55.in_ref, f32[4,1,6,8,128]{4,3,2,1,0:T(8,128)S(1)} %get-tuple-element.52.refs_4_.refs_0_.refs_2_, f32[4,1,6,8,128]{4,3,2,1,0:T(8,128)S(1)} %get-tuple-element.53.refs_5_.refs_1_.refs_3_), custom_call_target="tpu_custom_call" | custom-call | flops 6000000 | bytes 3000000 | tf_op jit(solution)/shard_map/pack/pallas_call | solution.py:412
  110.7 2.4 %sweep_14.1 = (f32[2,3,2,2,8,8,128]{6,5,4,3,2,1,0:T(8,128)S(1)}, f32[2,2,8,8,128]{4,3,2,1,0:T(8,128)}) custom-call(s32[5]{0:T(128)S(1)} %pad_add_fusion.scalars, f32[4,10,6,8,128]{4,3,2,1,0:T(8,128)S(1)} %get-tuple-element.38.refs_4_.refs_0_, f32[4,10,6,8,128]{4,3,2,1,0:T(8,128)S(1)} %get-tuple-element.39.refs_5_.refs_1_, ...), custom_call_target="tpu_custom_call" | custom-call | flops 13107200 | bytes 2400000 | tf_op jit(solution)/shard_map/sweep_14/pallas_call | solution.py:377
  113.1 5.1 %chain_12.1 = f32[3072,128]{1,0:T(8,128)S(1)} custom-call(s32[5]{0:T(128)S(1)} %pad_add_fusion.scalars, f32[2,3,2,2,8,8,128]{6,5,4,3,2,1,0:T(8,128)S(1)} %get-tuple-element.50.refs_4_.refs_0_, f32[2,3,2,2,8,8,128]{6,5,4,3,2,1,0:T(8,128)S(1)} %get-tuple-element.54.refs_1_, f32[4,1,6,8,128]{4,3,2,1,0:T(8,128)S(1)} %get-tuple-element.52.refs_4_.refs_0_.refs_2_, ...), custom_call_target="tpu_custom_call" | custom-call | flops 15728640 | bytes 2000000 | tf_op jit(solution)/shard_map/chain_12/pallas_call | solution.py:545
  118.2 33.0 %all_to_all.10 = f32[128,24,128]{2,1,0:T(8,128)S(1)} all-to-all(f32[128,24,128]{2,1,0:T(8,128)S(1)} %bitcast.11), channel_id=1, replica_groups=mesh['tm'=16,'space'=8] {'tm','space'}, dimensions={0} | all-to-all | bytes 3145728 | tf_op jit(solution)/shard_map/all_to_all | solution.py:589
  151.2 3.9 %collect.1 = (f32[2,2,128,256]{3,2,1,0:T(8,128)}, f32[2,2,2,128,256]{4,3,2,1,0:T(8,128)}) custom-call(f32[3072,128]{1,0:T(8,128)S(1)} %bitcast.12), custom_call_target="tpu_custom_call" | custom-call | tf_op jit(solution)/shard_map/collect/pallas_call | solution.py:183
  (35 shorter events, 12.0 us)
Async XLA Ops:
  0.6 1.2 copy-start
  1.9 1.0 copy-start.1
  6.5 12.3 %copy-start.2 = (s32[2]{0:T(128)S(1)}, s32[2]{0:T(128)}, u32[]{:S(2)}) copy-start(s32[2]{0:T(128)} %param.7) | copy-start | bytes 28
  6.5 36.4 %all-to-all-start = ((f32[128,24,128]{2,1,0:T(8,128)}), f32[128,24,128]{2,1,0:T(8,128)S(1)}, u32[]{:S(2)}, u32[]{:S(2)}) async-start(f32[128,24,128]{2,1,0:T(8,128)} %bitcast.4), calls=%async_computation | async-start | bytes 3145728 | tf_op jit(solution)/shard_map/all_to_all | solution.py:561
  43.9 7.4 %collective-permute-start.1 = (f32[2,6,6,8,128]{4,3,2,1,0:T(8,128)S(1)}, f32[2,6,6,8,128]{4,3,2,1,0:T(8,128)S(1)}, u32[]{:S(2)}, u32[]{:S(2)}) collective-permute-start(f32[2,6,6,8,128]{4,3,2,1,0:T(8,128)S(1)} %get-tuple-element.30.refs_0_), channel_id=1, source_target_pairs={{1,0},{9,8},{41,40},{33,32},{65,64},{73,72},{105,104},{97,96},{117... | collective-permute-start | bytes 884744 | tf_op jit(solution)/shard_map/ppermute | solution.py:227
  44.5 7.8 %collective-permute-start = (f32[2,6,6,8,128]{4,3,2,1,0:T(8,128)S(1)}, f32[2,6,6,8,128]{4,3,2,1,0:T(8,128)S(1)}, u32[]{:S(2)}, u32[]{:S(2)}) collective-permute-start(f32[2,6,6,8,128]{4,3,2,1,0:T(8,128)S(1)} %get-tuple-element.31.refs_1_), channel_id=1, source_target_pairs={{4,0},{12,8},{44,40},{36,32},{68,64},{76,72},{108,104},{100,96},{1... | collective-permute-start | bytes 884744 | tf_op jit(solution)/shard_map/ppermute | solution.py:227
  54.1 12.4 %collective-permute-start.4 = (f32[4,6,6,8,128]{4,3,2,1,0:T(8,128)S(1)}, f32[4,6,6,8,128]{4,3,2,1,0:T(8,128)S(1)}, u32[]{:S(2)}, u32[]{:S(2)}) collective-permute-start(f32[4,6,6,8,128]{4,3,2,1,0:T(8,128)S(1)} %get-tuple-element.36.refs_1_), channel_id=1, source_target_pairs={{20,0},{0,8},{8,40},{40,32},{32,64},{64,72},{72,104},{104,96},{96,... | collective-permute-start | bytes 1769480 | tf_op jit(solution)/shard_map/ppermute | solution.py:227
  54.5 12.0 %collective-permute-start.5 = (f32[4,6,6,8,128]{4,3,2,1,0:T(8,128)S(1)}, f32[4,6,6,8,128]{4,3,2,1,0:T(8,128)S(1)}, u32[]{:S(2)}, u32[]{:S(2)}) collective-permute-start(f32[4,6,6,8,128]{4,3,2,1,0:T(8,128)S(1)} %get-tuple-element.37.refs_0_), channel_id=1, source_target_pairs={{8,0},{40,8},{32,40},{64,32},{72,64},{104,72},{96,104},{116,96},{1... | collective-permute-start | bytes 1769480 | tf_op jit(solution)/shard_map/ppermute | solution.py:227
  55.9 9.6 %collective-permute-start.3 = (f32[2,10,6,8,128]{4,3,2,1,0:T(8,128)S(1)}, f32[2,10,6,8,128]{4,3,2,1,0:T(8,128)S(1)}, u32[]{:S(2)}, u32[]{:S(2)}) collective-permute-start(f32[2,10,6,8,128]{4,3,2,1,0:T(8,128)S(1)} %get-tuple-element.34.refs_0_), channel_id=1, source_target_pairs={{1,0},{9,8},{41,40},{33,32},{65,64},{73,72},{105,104},{97,96},{117... | collective-permute-start | bytes 1474568 | tf_op jit(solution)/shard_map/ppermute | solution.py:227
  56.4 10.1 %collective-permute-start.2 = (f32[2,10,6,8,128]{4,3,2,1,0:T(8,128)S(1)}, f32[2,10,6,8,128]{4,3,2,1,0:T(8,128)S(1)}, u32[]{:S(2)}, u32[]{:S(2)}) collective-permute-start(f32[2,10,6,8,128]{4,3,2,1,0:T(8,128)S(1)} %get-tuple-element.35.refs_1_), channel_id=1, source_target_pairs={{4,0},{12,8},{44,40},{36,32},{68,64},{76,72},{108,104},{100,96},{1... | collective-permute-start | bytes 1474568 | tf_op jit(solution)/shard_map/ppermute | solution.py:227
  69.6 15.4 %collective-permute-start.7 = (f32[4,10,6,8,128]{4,3,2,1,0:T(8,128)S(1)}, f32[4,10,6,8,128]{4,3,2,1,0:T(8,128)S(1)}, u32[]{:S(2)}, u32[]{:S(2)}) collective-permute-start(f32[4,10,6,8,128]{4,3,2,1,0:T(8,128)S(1)} %get-tuple-element.38.refs_4_.refs_0_), channel_id=1, source_target_pairs={{8,0},{40,8},{32,40},{64,32},{72,64},{104,72},{96,104},{116,96},{1... | collective-permute-start | bytes 2949128 | tf_op jit(solution)/shard_map/ppermute | solution.py:227
  73.3 11.8 %collective-permute-start.6 = (f32[4,10,6,8,128]{4,3,2,1,0:T(8,128)S(1)}, f32[4,10,6,8,128]{4,3,2,1,0:T(8,128)S(1)}, u32[]{:S(2)}, u32[]{:S(2)}) collective-permute-start(f32[4,10,6,8,128]{4,3,2,1,0:T(8,128)S(1)} %get-tuple-element.39.refs_5_.refs_1_), channel_id=1, source_target_pairs={{20,0},{0,8},{8,40},{40,32},{32,64},{64,72},{72,104},{104,96},{96,... | collective-permute-start | bytes 2949128 | tf_op jit(solution)/shard_map/ppermute | solution.py:227
  82.2 6.2 %collective-permute-start.9 = (f32[2,1,6,8,128]{4,3,2,1,0:T(8,128)S(1)}, f32[2,1,6,8,128]{4,3,2,1,0:T(8,128)S(1)}, u32[]{:S(2)}, u32[]{:S(2)}) collective-permute-start(f32[2,1,6,8,128]{4,3,2,1,0:T(8,128)S(1)} %get-tuple-element.42.refs_4_.refs_0_), channel_id=1, source_target_pairs={{1,0},{9,8},{41,40},{33,32},{65,64},{73,72},{105,104},{97,96},{117... | collective-permute-start | bytes 147464 | tf_op jit(solution)/shard_map/ppermute | solution.py:227
  82.6 5.7 %collective-permute-start.8 = (f32[2,1,6,8,128]{4,3,2,1,0:T(8,128)S(1)}, f32[2,1,6,8,128]{4,3,2,1,0:T(8,128)S(1)}, u32[]{:S(2)}, u32[]{:S(2)}) collective-permute-start(f32[2,1,6,8,128]{4,3,2,1,0:T(8,128)S(1)} %get-tuple-element.43.refs_5_.refs_1_), channel_id=1, source_target_pairs={{4,0},{12,8},{44,40},{36,32},{68,64},{76,72},{108,104},{100,96},{1... | collective-permute-start | bytes 147464 | tf_op jit(solution)/shard_map/ppermute | solution.py:227
  88.6 7.5 %collective-permute-start.11 = (f32[4,1,6,8,128]{4,3,2,1,0:T(8,128)S(1)}, f32[4,1,6,8,128]{4,3,2,1,0:T(8,128)S(1)}, u32[]{:S(2)}, u32[]{:S(2)}) collective-permute-start(f32[4,1,6,8,128]{4,3,2,1,0:T(8,128)S(1)} %get-tuple-element.45.refs_4_.refs_2_), channel_id=1, source_target_pairs={{8,0},{40,8},{32,40},{64,32},{72,64},{104,72},{96,104},{116,96},{1... | collective-permute-start | bytes 294920 | tf_op jit(solution)/shard_map/ppermute | solution.py:227
  92.8 3.3 %collective-permute-start.10 = (f32[4,1,6,8,128]{4,3,2,1,0:T(8,128)S(1)}, f32[4,1,6,8,128]{4,3,2,1,0:T(8,128)S(1)}, u32[]{:S(2)}, u32[]{:S(2)}) collective-permute-start(f32[4,1,6,8,128]{4,3,2,1,0:T(8,128)S(1)} %get-tuple-element.46.refs_5_.refs_3_), channel_id=1, source_target_pairs={{20,0},{0,8},{8,40},{40,32},{32,64},{64,72},{72,104},{104,96},{96,... | collective-permute-start | bytes 294920 | tf_op jit(solution)/shard_map/ppermute | solution.py:227
  99.6 6.0 %collective-permute-start.13 = (f32[2,1,6,8,128]{4,3,2,1,0:T(8,128)S(1)}, f32[2,1,6,8,128]{4,3,2,1,0:T(8,128)S(1)}, u32[]{:S(2)}, u32[]{:S(2)}) collective-permute-start(f32[2,1,6,8,128]{4,3,2,1,0:T(8,128)S(1)} %get-tuple-element.48.refs_4_.refs_0_), channel_id=1, source_target_pairs={{1,0},{9,8},{41,40},{33,32},{65,64},{73,72},{105,104},{97,96},{117... | collective-permute-start | bytes 147464 | tf_op jit(solution)/shard_map/ppermute | solution.py:227
  99.7 6.0 %collective-permute-start.12 = (f32[2,1,6,8,128]{4,3,2,1,0:T(8,128)S(1)}, f32[2,1,6,8,128]{4,3,2,1,0:T(8,128)S(1)}, u32[]{:S(2)}, u32[]{:S(2)}) collective-permute-start(f32[2,1,6,8,128]{4,3,2,1,0:T(8,128)S(1)} %get-tuple-element.49.refs_5_.refs_1_), channel_id=1, source_target_pairs={{4,0},{12,8},{44,40},{36,32},{68,64},{76,72},{108,104},{100,96},{1... | collective-permute-start | bytes 147464 | tf_op jit(solution)/shard_map/ppermute | solution.py:227
  105.9 7.2 %collective-permute-start.15 = (f32[4,1,6,8,128]{4,3,2,1,0:T(8,128)S(1)}, f32[4,1,6,8,128]{4,3,2,1,0:T(8,128)S(1)}, u32[]{:S(2)}, u32[]{:S(2)}) collective-permute-start(f32[4,1,6,8,128]{4,3,2,1,0:T(8,128)S(1)} %get-tuple-element.52.refs_4_.refs_0_.refs_2_), channel_id=1, source_target_pairs={{8,0},{40,8},{32,40},{64,32},{72,64},{104,72},{96,104},{116,96},{1... | collective-permute-start | bytes 294920 | tf_op jit(solution)/shard_map/ppermute | solution.py:227
  108.8 4.2 %collective-permute-start.14 = (f32[4,1,6,8,128]{4,3,2,1,0:T(8,128)S(1)}, f32[4,1,6,8,128]{4,3,2,1,0:T(8,128)S(1)}, u32[]{:S(2)}, u32[]{:S(2)}) collective-permute-start(f32[4,1,6,8,128]{4,3,2,1,0:T(8,128)S(1)} %get-tuple-element.53.refs_5_.refs_1_.refs_3_), channel_id=1, source_target_pairs={{20,0},{0,8},{8,40},{40,32},{32,64},{64,72},{72,104},{104,96},{96,... | collective-permute-start | bytes 294920 | tf_op jit(solution)/shard_map/ppermute | solution.py:227

commit v6 on v5

--- a/solution.py
+++ b/solution.py
@@ -75,6 +75,17 @@
     return arrays
 
 
+def turn_blocks(arrays, width):
+    n, block = len(arrays), lanes() // width
+    arrays = [roll(arrays[-k % n], width * (-k % n)) for k in range(n)]
+    step = 1
+    while step < n:
+        here = block // step % 2 == 0
+        arrays = [jnp.where(here, arrays[k], arrays[(k - step) % n]) for k in range(n)]
+        step *= 2
+    return [roll(v, -width * k) for k, v in enumerate(arrays)]
+
+
 def turn_pairs(v):
     v = roll(v, 4, 0)
     return jnp.where(rows() // 2 % 2 == 0, roll(v, -2, 0), roll(v, 2, 0))
@@ -98,14 +109,17 @@
     def unit(u):
         row = u // 2 * 4 + u % 2 * 2
         for half in range(2):
+            found = []
             for upper in range(2):
                 loads = [
                     planes[u, xp, half, pl.ds(64 * upper + ys, 8, stride=8)] for ys in range(8) for xp in range(2)
                 ]
-                for k, v in enumerate(swap_bits(loads, [(3, 6), (2, 5), (1, 4), (0, 3)])):
+                for k, v in enumerate(turn_blocks(loads, 8)):
                     tj, rz = 8 * half + k // 2, k % 2
-                    device = device_of(7 if upper else 0, tj)
-                    out_ref[pl.ds(device * 24 + rz + row, 8, stride=12)] = turn_pairs(v) if upper else v
+                    at = device_of(7 if upper else 0, tj) * 24 + rz
+                    found.append((at, turn_pairs(v) if upper else v))
+            for at, v in found:
+                out_ref[pl.ds(at + row, 8, stride=12)] = v
 
     for copy in copies(0) + copies(1):
         copy.wait()
@@ -131,13 +145,14 @@
         out_specs=VMEM,
         out_shape=jax.ShapeDtypeStruct((128 * 24, 128), F32),
         scratch_shapes=[pltpu.VMEM((6, 2, 2, 128, 128), F32), pltpu.SemaphoreType.DMA((24,))],
-        compiler_params=pltpu.CompilerParams(vmem_limit_bytes=VMEM_LIMIT),
+        compiler_params=pltpu.CompilerParams(vmem_limit_bytes=62 * 1024 * 1024),
         name="spread",
     )(starts, nodes)
 
 
 def collect_kernel(in_ref, starts_ref, nodes_ref, planes, left):
     def unit(u, carry):
+        found = []
         for half in range(2):
             for upper in range(2):
                 loads = []
@@ -145,8 +160,10 @@
                     device = device_of(7 if upper else 0, 8 * half + t)
                     v = in_ref[pl.ds(device * 24 + u, 8, stride=12)]
                     loads.append(turn_pairs(v) if upper else v)
-                for ys, v in enumerate(swap_bits(loads, [(2, 6), (1, 5), (0, 4)])):
-                    planes[u, half, pl.ds(64 * upper + ys, 8, stride=8)] = v
+                for ys, v in enumerate(turn_blocks(loads, 16)):
+                    found.append((half, 64 * upper + ys, v))
+        for half, at, v in found:
+            planes[u, half, pl.ds(at, 8, stride=8)] = v
         return carry
 
     def copies(array):
@@ -199,11 +216,10 @@
 
         def position(i, carry, b=b, first=first):
             base = lax.rem(scalars[0] + (first + i), SLABS) * SLAB_ROWS
-            for u in range(6):
-                for ry in range(2):
-                    for rz in range(2):
-                        v = in_ref[pl.ds(base + ry * 12 + 2 * u + rz, 8, stride=24)]
-                        out_refs[2 * b + ry][rz, i, u] = v
+            parts = [(u, ry, rz) for u in range(6) for ry in range(2) for rz in range(2)]
+            values = [in_ref[pl.ds(base + ry * 12 + 2 * u + rz, 8, stride=24)] for u, ry, rz in parts]
+            for (u, ry, rz), v in zip(parts, values, strict=True):
+                out_refs[2 * b + ry][rz, i, u] = v
             return carry
 
         lax.fori_loop(0, count, position, 0)
@@ -236,16 +252,18 @@
 
 
 def columns_kernel(low, high, up, down, *refs):
-    for rz, ref in enumerate(refs[-2:]):
-
-        def position(i, carry, rz=rz, ref=ref):
-            for u in range(6):
-                arrays = [r[rz, i, u] for r in (up, low, high, down)]
-                for k, v in enumerate(swap_bits(arrays, [(1, 6), (0, 5)])):
-                    ref[k, i, u] = v
-            return carry
-
-        lax.fori_loop(0, ref.shape[1], position, 0)
+    def position(i, carry):
+        values = [
+            (ref, u, swap_bits([r[rz, i, u] for r in (up, low, high, down)], [(1, 6), (0, 5)]))
+            for rz, ref in enumerate(refs[-2:])
+            for u in range(6)
+        ]
+        for ref, u, arrays in values:
+            for k, v in enumerate(arrays):
+                ref[k, i, u] = v
+        return carry
+
+    lax.fori_loop(0, refs[-1].shape[1], position, 0)
 
 
 def columns(low, high, up, down, after=(), held=()):
@@ -386,45 +404,51 @@
     )(scalars, *halo, *after)
 
 
-def write_packs(ref, at, loads):
+def pack_values(loads):
     values = {}
     for array, load in enumerate(loads):
         for f in range(2):
             for xp in range(2):
                 for ry, v in enumerate(core_rows([load(f, xp, ys) for ys in range(8)])):
                     values[ry * 12 + array * 4 + f * 2 + xp] = v
+    return values
+
+
+def put(out_ref, scalars, p, values):
+    base = lax.rem(scalars[0] + p, SLABS) * SLAB_ROWS
     for r, v in values.items():
-        ref[at, r] = v
-
-
-def pack_kernel(in_ref, *refs):
+        out_ref[pl.ds(base + r, 8, stride=24)] = v
+
+
+def pack_kernel(first, scalars, raw, *refs):
     out_ref = refs[-1]
+    if first > 0:
+        out_ref[...] = refs[0][...]
 
     def position(i, carry):
-        write_packs(out_ref, i, [reader(in_ref, i, array) for array in range(3)])
+        put(out_ref, scalars, first + i, pack_values([reader(raw, i, array) for array in range(3)]))
         return carry
 
-    lax.fori_loop(0, out_ref.shape[0], position, 0)
-
-
-def pack(raw, after=()):
-    count = raw.shape[0]
+    lax.fori_loop(0, raw.shape[0], position, 0)
+
+
+def pack(scalars, first, raw, earlier=(), after=()):
     return pl.pallas_call(
-        pack_kernel,
-        in_specs=[VMEM] + [ANY] * len(after),
+        functools.partial(pack_kernel, first),
+        in_specs=[SMEM, VMEM] + [VMEM] * len(earlier) + [ANY] * len(after),
         out_specs=VMEM,
-        out_shape=jax.ShapeDtypeStruct((count, 24, 8, 128), F32),
+        out_shape=jax.ShapeDtypeStruct((SLABS * SLAB_ROWS, 128), F32),
         compiler_params=pltpu.CompilerParams(vmem_limit_bytes=VMEM_LIMIT),
-        cost_estimate=pl.CostEstimate(flops=count * 1000000, bytes_accessed=count * 500000, transcendentals=0),
-        name="pack",
-    )(raw, *after)
+        cost_estimate=pl.CostEstimate(flops=6000000, bytes_accessed=3000000, transcendentals=0),
+        name=f"pack_{first}",
+    )(scalars, raw, *earlier, *after)
 
 
 def chain_kernel(first, count, scalars, *refs):
     tile = Tile(scalars)
     last = first + count >= SLABS
     z, late, corr, one, two, ahead, next_z, next_late = refs[-8:]
-    parts = 1 if first == 0 else 2
+    parts = 2 if last else 1
     swept, refs = refs[:parts], refs[parts:-8]
     take_first = scalars[1] > 0
     if first == 0:
@@ -495,49 +519,33 @@
         fl, l = tile.tendency(reader(late), xp, ys)
         for f in range(2):
             raw[count + 1, 0, f, xp, ys] = l[f] + H * fl[f] + corr[f, xp, ys]
-    leader, conv_one, conv_two = scalars[0], scalars[1] > 0, scalars[2] > 0
-    *earlier, out_ref, packs, _ = refs
+    conv_one, conv_two = scalars[1] > 0, scalars[2] > 0
+    earlier, out_ref, _ = refs
+    out_ref[...] = earlier[...]
 
     def pack_at(i, carry):
-        write_packs(packs, i, [reader(raw, i, array) for array in range(3)])
+        put(out_ref, scalars, first + i, pack_values([reader(raw, i, array) for array in range(3)]))
         return carry
 
-    lax.fori_loop(0, count + 2, pack_at, 0)
-
-    def put(p, ref, i, newest=False):
-        base = lax.rem(leader + p, SLABS) * SLAB_ROWS
-        for ry in range(2):
-            for array in range(3):
-                for k in range(4):
-                    r = ry * 12 + array * 4 + k
-                    out_ref[pl.ds(base + r, 8, stride=24)] = ref[i, ry * 12 + k] if newest else ref[i, r]
-
-    for b, ref in enumerate((*earlier, packs)):
-
-        def move(i, carry, b=b, ref=ref):
-            put(BLOCKS[b][0] + i, ref, i)
-            return carry
-
-        lax.fori_loop(0, BLOCKS[b][1], move, 0)
+    lax.fori_loop(0, count, pack_at, 0)
 
     @pl.when(conv_one)
     def _():
-        put(0, packs, count)
-
-    @pl.when(conv_two & conv_one)
+        put(out_ref, scalars, 0, pack_values([reader(raw, count, array) for array in range(3)]))
+
+    @pl.when(conv_two)
     def _():
-        put(1, packs, count + 1, newest=True)
-
-    @pl.when(conv_two & jnp.logical_not(conv_one))
-    def _():
-        put(0, packs, count, newest=True)
+        at = jnp.where(conv_one, count + 1, count)
+        values = pack_values([reader(raw, at, 0)])
+        newest = {ry * 12 + array * 4 + k: values[ry * 12 + k] for ry in range(2) for array in range(3) for k in range(4)}
+        put(out_ref, scalars, jnp.where(conv_one, 1, 0), newest)
 
 
 def chain(scalars, first, count, inputs):
     last = first + count >= SLABS
     if last:
         out_shape = jax.ShapeDtypeStruct((SLABS * SLAB_ROWS, 128), F32)
-        scratch = [pltpu.VMEM((count + 2, 24, 8, 128), F32), pltpu.VMEM((count + 2, 3) + FIELD, F32)]
+        scratch = [pltpu.VMEM((count + 2, 3) + FIELD, F32)]
     else:
         out_shape = (jax.ShapeDtypeStruct((count, 3) + FIELD, F32),)
         out_shape += (jax.ShapeDtypeStruct((2, 1, 6, 8, 128), F32),) * 2
@@ -572,20 +580,19 @@
     raw, *state = chain(scalars, *BLOCKS[0], [swept, start])
 
     rows = rows_beside(*state)
-    swept, _ = sweep(scalars, halo, 6, 0, 3, after=state)
+    out = pack(scalars, 0, raw, after=state)
+    inside, _ = columns(*state, *rows, after=[out])
+    beside = columns_beside(inside)
+    swept, _ = sweep(scalars, halo, 6, 0, 6, after=inside)
+    raw, *state = chain(scalars, *BLOCKS[1], [swept, *inside, *beside])
+
+    rows = rows_beside(*state)
+    swept, _ = sweep(scalars, halo, 6, 6, 2, after=state)
     inside, _ = columns(*state, *rows, after=[swept])
     beside = columns_beside(inside)
-    more, _ = sweep(scalars, halo, 6, 3, 3, after=inside)
-    raw_b, *state = chain(scalars, *BLOCKS[1], [swept, more, *inside, *beside])
-
-    rows = rows_beside(*state)
-    packs_a = pack(raw, after=state)
-    swept, _ = sweep(scalars, halo, 6, 6, 2, after=state)
-    inside, _ = columns(*state, *rows, after=[swept, packs_a])
-    beside = columns_beside(inside)
     more, _ = sweep(scalars, halo, 6, 8, 2, after=inside)
-    packs_b = pack(raw_b, after=inside)
-    out = chain(scalars, *BLOCKS[2], [swept, more, *inside, *beside, packs_a, packs_b])
+    out = pack(scalars, 6, raw, [out], after=inside)
+    out = chain(scalars, *BLOCKS[2], [swept, more, *inside, *beside, out])
     out = lax.all_to_all(out.reshape(128, 24, 128), AXES, 0, 0, tiled=True)
     starts, nodes = collect(out.reshape(128 * 24, 128))
     return starts[None], nodes[None]

time: 156 us -> 150 us (0.962)
  blocking collectives: 33 us -> 36.3 us
  starting transfers between devices: 30.6 us -> 28.2 us
  Pallas kernels: 46.3 us -> 43.9 us
  local copies, waits for them, and re-layouts: 2.27 us -> 0.01 us
    all_to_all x1, blocking collectives: 33 us -> 36.3 us  [body(): out = lax.all_to_all(out.reshape(128, 24, 128), AXES, 0, 0, tiled=True)]
    ppermute x16, starting transfers between devices: 19.1 us -> 16.7 us  [from_neighbour(): return lax.ppermute(payload, AXES, pairs)]
    unnamed x6 -> x2, local copies, waits for them, and re-layouts: 2.27 us -> 0.01 us
    pallas_call x4, Pallas kernels: 5.36 us -> 3.15 us  [columns(): pl.pallas_call(lambda *refs: columns_kernel(*refs[:4], *refs[-2:]), in_sp...]
    pallas_call x5 -> x4, Pallas kernels: 17 us -> 16.5 us  [sweep(): pl.pallas_call(functools.partial(sweep_kernel, first, begin, count), in_s...]
  transfers between devices with their start and end apart: 17 -> 17, of which waited for: 6 -> 5; matrix products, arithmetic and copies ran while one was open for 0% -> 0% of each run, Pallas kernels for 15% -> 16%
where the time goes in v6:
time: 150 us
  Pallas kernels  43.9 us (29%)
  waiting for transfers between devices  39.9 us (27%)
  blocking collectives  36.3 us (24%)
  starting transfers between devices  28.2 us (19%)
  between operations  1.71 us (1%)
    all_to_all x1, blocking collectives, body(): out = lax.all_to_all(out.reshape(128, 24, 128), AXES, 0, 0, tiled=True)  36.3 us
    all_to_all x1, waiting for transfers between devices, body(): lax.all_to_all(chunks.reshape(128, 24, 128), AXES, 0, 0, tiled=True)  24.1 us
    ppermute x16, starting transfers between devices, from_neighbour(): return lax.ppermute(payload, AXES, pairs)  16.7 us
    pallas_call x4, Pallas kernels, sweep(): pl.pallas_call(functools.partial(sweep_kernel, first, begin, count), in_s...  16.5 us
    ppermute x16, waiting for transfers between devices, from_neighbour(): return lax.ppermute(payload, AXES, pairs)  15.9 us
    all_to_all x1, starting transfers between devices, body(): lax.all_to_all(chunks.reshape(128, 24, 128), AXES, 0, 0, tiled=True)  11.5 us
    pallas_call x3, Pallas kernels, chain(): pl.pallas_call(functools.partial(chain_kernel, first, count), in_specs=[S...  11 us
    pallas_call x2, Pallas kernels, pack(): pl.pallas_call(functools.partial(pack_kernel, first), in_specs=[SMEM, VME...  4.88 us
  transfers between devices with their start and end apart: 17, of which 5 were waited for; matrix products, arithmetic and copies ran while one was open for 0% of the time, Pallas kernels for 16%

profile of v6, /device:TPU:1, one launch (start us, length us, event | category | flops | bytes accessed | tf_op | source)
XLA Modules:
  0.0 150.1 jit_solution(14032760970212766715)
XLA Ops:
  0.6 4.1 %spread.1 = f32[3072,128]{1,0:T(8,128)} custom-call(f32[2,2,128,256]{3,2,1,0:T(8,128)} %bitcast.15, f32[2,2,2,128,256]{4,3,2,1,0:T(8,128)} %bitcast.14), custom_call_target="tpu_custom_call" | custom-call | tf_op jit(solution)/shard_map/spread/pallas_call | solution.py:142
  4.8 11.5 %all-to-all-start = ((f32[128,24,128]{2,1,0:T(8,128)}), f32[128,24,128]{2,1,0:T(8,128)S(1)}, u32[]{:S(2)}, u32[]{:S(2)}) async-start(f32[128,24,128]{2,1,0:T(8,128)} %bitcast.13), calls=%async_computation | async-start | bytes 3145728 | tf_op jit(solution)/shard_map/all_to_all | solution.py:569
  17.1 24.1 %all-to-all-done = f32[128,24,128]{2,1,0:T(8,128)S(1)} async-done(((f32[128,24,128]{2,1,0:T(8,128)}), f32[128,24,128]{2,1,0:T(8,128)S(1)}, u32[]{:S(2)}, u32[]{:S(2)}) %all-to-all-start) | async-done | bytes 1572896 | tf_op jit(solution)/shard_map/all_to_all | solution.py:569
  42.7 1.0 collective-permute-start
  43.7 5.9 %collective-permute-done.1.refs_3_ = f32[2,6,6,8,128]{4,3,2,1,0:T(8,128)S(1)} collective-permute-done((f32[2,6,6,8,128]{4,3,2,1,0:T(8,128)S(1)}, f32[2,6,6,8,128]{4,3,2,1,0:T(8,128)S(1)}, u32[]{:S(2)}, u32[]{:S(2)}) %collective-permute-start.1) | collective-permute-done | bytes 294944 | tf_op jit(solution)/shard_map/ppermute | solution.py:243
  50.5 1.0 columns.4
  52.0 1.4 collective-permute-start.5
  54.8 8.1 %collective-permute-done.3.refs_3_ = f32[2,10,6,8,128]{4,3,2,1,0:T(8,128)S(1)} collective-permute-done((f32[2,10,6,8,128]{4,3,2,1,0:T(8,128)S(1)}, f32[2,10,6,8,128]{4,3,2,1,0:T(8,128)S(1)}, u32[]{:S(2)}, u32[]{:S(2)}) %collective-permute-start.3) | collective-permute-done | bytes 491552 | tf_op jit(solution)/shard_map/ppermute | solution.py:243
  63.9 1.8 %columns.5 = (f32[4,10,6,8,128]{4,3,2,1,0:T(8,128)S(1)}, f32[4,10,6,8,128]{4,3,2,1,0:T(8,128)S(1)}) custom-call(f32[2,10,6,8,128]{4,3,2,1,0:T(8,128)S(1)} %get-tuple-element.33.refs_0_, f32[2,10,6,8,128]{4,3,2,1,0:T(8,128)S(1)} %get-tuple-element.34.refs_1_, f32[2,10,6,8,128]{4,3,2,1,0:T(8,128)S(1)} %collective-permute-done.2.refs_2_, ...), custom_call_target="tpu_custom_call" | custom-call | bytes 8000000 | tf_op jit(solution)/shard_map/columns/pallas_call | solution.py:271
  65.7 3.7 %collective-permute-start.7 = (f32[4,10,6,8,128]{4,3,2,1,0:T(8,128)S(1)}, f32[4,10,6,8,128]{4,3,2,1,0:T(8,128)S(1)}, u32[]{:S(2)}, u32[]{:S(2)}) collective-permute-start(f32[4,10,6,8,128]{4,3,2,1,0:T(8,128)S(1)} %get-tuple-element.37.refs_4_.refs_0_), channel_id=1, source_target_pairs={{8,0},{40,8},{32,40},{64,32},{72,64},{104,72},{96,104},{116,96},{1... | collective-permute-start | bytes 2949128 | tf_op jit(solution)/shard_map/ppermute | solution.py:243
  69.4 5.7 %sweep_0.1 = (f32[6,3,2,2,8,8,128]{6,5,4,3,2,1,0:T(8,128)S(1)}, f32[2,2,8,8,128]{4,3,2,1,0:T(8,128)S(1)}) custom-call(s32[5]{0:T(128)S(1)} %pad_add_fusion.scalars, f32[4,6,6,8,128]{4,3,2,1,0:T(8,128)S(1)} %get-tuple-element.36.refs_0_, f32[4,6,6,8,128]{4,3,2,1,0:T(8,128)S(1)} %get-tuple-element.35.refs_1_, ...), custom_call_target="tpu_custom_call" | custom-call | flops 39321600 | bytes 7200000 | tf_op jit(solution)/shard_map/sweep_0/pallas_call | solution.py:395
  75.1 3.1 %chain_0.1 = (f32[6,3,2,2,8,8,128]{6,5,4,3,2,1,0:T(8,128)S(1)}, f32[2,1,6,8,128]{4,3,2,1,0:T(8,128)S(1)}, f32[2,1,6,8,128]{4,3,2,1,0:T(8,128)S(1)}) custom-call(s32[5]{0:T(128)S(1)} %pad_add_fusion.scalars, f32[6,3,2,2,8,8,128]{6,5,4,3,2,1,0:T(8,128)S(1)} %get-tuple-element.39.refs_0_, f32[2,2,8,8,128]{4,3,2,1,0:T(8,128)S(1)} %get-tuple-element.40.refs_1_), custom_call_target="tpu_custom_call" | custom-call | flops 23592960 | bytes 3000000 | tf_op jit(solution)/shard_map/chain_0/pallas_call | solution.py:553
  78.7 1.1 collective-permute-start.8
  79.8 2.4 %pack_0.1.refs_4_.refs_0_ = f32[3072,128]{1,0:T(8,128)S(1)} custom-call(s32[5]{0:T(128)S(1)} %pad_add_fusion.scalars, f32[6,3,2,2,8,8,128]{6,5,4,3,2,1,0:T(8,128)S(1)} %get-tuple-element.43.raw, f32[2,1,6,8,128]{4,3,2,1,0:T(8,128)S(1)} %get-tuple-element.41.refs_0_, f32[2,1,6,8,128]{4,3,2,1,0:T(8,128)S(1)} %get-tuple-element.42.refs_1_), custom_call_target="tpu_custom_call" | custom-call | flops 6000000 | bytes 3000000 | tf_op jit(solution)/shard_map/pack_0/pallas_call | solution.py:436
  82.4 1.6 %collective-permute-start.11 = (f32[4,1,6,8,128]{4,3,2,1,0:T(8,128)S(1)}, f32[4,1,6,8,128]{4,3,2,1,0:T(8,128)S(1)}, u32[]{:S(2)}, u32[]{:S(2)}) collective-permute-start(f32[4,1,6,8,128]{4,3,2,1,0:T(8,128)S(1)} %get-tuple-element.44.refs_4_.refs_1_), channel_id=1, source_target_pairs={{8,0},{40,8},{32,40},{64,32},{72,64},{104,72},{96,104},{116,96},{1... | collective-permute-start | bytes 294920 | tf_op jit(solution)/shard_map/ppermute | solution.py:243
  84.0 6.0 %sweep_6.1 = (f32[6,3,2,2,8,8,128]{6,5,4,3,2,1,0:T(8,128)S(1)}, f32[2,2,8,8,128]{4,3,2,1,0:T(8,128)}) custom-call(s32[5]{0:T(128)S(1)} %pad_add_fusion.scalars, f32[4,10,6,8,128]{4,3,2,1,0:T(8,128)S(1)} %get-tuple-element.37.refs_4_.refs_0_, f32[4,10,6,8,128]{4,3,2,1,0:T(8,128)S(1)} %get-tuple-element.38.refs_5_.refs_1_, ...), custom_call_target="tpu_custom_call" | custom-call | flops 39321600 | bytes 7200000 | tf_op jit(solution)/shard_map/sweep_6/pallas_call | solution.py:395
  90.0 3.4 %chain_6.1 = (f32[6,3,2,2,8,8,128]{6,5,4,3,2,1,0:T(8,128)S(1)}, f32[2,1,6,8,128]{4,3,2,1,0:T(8,128)S(1)}, f32[2,1,6,8,128]{4,3,2,1,0:T(8,128)S(1)}) custom-call(s32[5]{0:T(128)S(1)} %pad_add_fusion.scalars, f32[6,3,2,2,8,8,128]{6,5,4,3,2,1,0:T(8,128)S(1)} %get-tuple-element.46.refs_0_, f32[4,1,6,8,128]{4,3,2,1,0:T(8,128)S(1)} %get-tuple-element.44.refs_4_.refs_1_, ...), custom_call_target="tpu_custom_call" | custom-call | flops 23592960 | bytes 3000000 | tf_op jit(solution)/shard_map/chain_6/pallas_call | solution.py:553
  94.9 2.4 %sweep_12.1 = (f32[2,3,2,2,8,8,128]{6,5,4,3,2,1,0:T(8,128)S(1)}, f32[2,2,8,8,128]{4,3,2,1,0:T(8,128)}) custom-call(s32[5]{0:T(128)S(1)} %pad_add_fusion.scalars, f32[4,10,6,8,128]{4,3,2,1,0:T(8,128)S(1)} %get-tuple-element.37.refs_4_.refs_0_, f32[4,10,6,8,128]{4,3,2,1,0:T(8,128)S(1)} %get-tuple-element.38.refs_5_.refs_1_, ...), custom_call_target="tpu_custom_call" | custom-call | flops 13107200 | bytes 2400000 | tf_op jit(solution)/shard_map/sweep_12/pallas_call | solution.py:395
  97.5 3.4 %collective-permute-start.15 = (f32[4,1,6,8,128]{4,3,2,1,0:T(8,128)S(1)}, f32[4,1,6,8,128]{4,3,2,1,0:T(8,128)S(1)}, u32[]{:S(2)}, u32[]{:S(2)}) collective-permute-start(f32[4,1,6,8,128]{4,3,2,1,0:T(8,128)S(1)} %get-tuple-element.50.refs_4_.refs_1_.refs_2_), channel_id=1, source_target_pairs={{8,0},{40,8},{32,40},{64,32},{72,64},{104,72},{96,104},{116,96},{1... | collective-permute-start | bytes 294920 | tf_op jit(solution)/shard_map/ppermute | solution.py:243
  100.9 2.5 %pack_6.1.refs_6_ = f32[3072,128]{1,0:T(8,128)S(1)} custom-call(s32[5]{0:T(128)S(1)} %pad_add_fusion.scalars, f32[6,3,2,2,8,8,128]{6,5,4,3,2,1,0:T(8,128)S(1)} %get-tuple-element.53.raw, f32[3072,128]{1,0:T(8,128)S(1)} %pack_0.1.refs_4_.refs_0_, f32[4,1,6,8,128]{4,3,2,1,0:T(8,128)S(1)} %get-tuple-element.50.refs_4_.refs_1_.refs_2_, ...), custom_call_target="tpu_custom_call" | custom-call | flops 6000000 | bytes 3000000 | tf_op jit(solution)/shard_map/pack_6/pallas_call | solution.py:436
  103.4 2.4 %sweep_14.1 = (f32[2,3,2,2,8,8,128]{6,5,4,3,2,1,0:T(8,128)S(1)}, f32[2,2,8,8,128]{4,3,2,1,0:T(8,128)}) custom-call(s32[5]{0:T(128)S(1)} %pad_add_fusion.scalars, f32[4,10,6,8,128]{4,3,2,1,0:T(8,128)S(1)} %get-tuple-element.37.refs_4_.refs_0_, f32[4,10,6,8,128]{4,3,2,1,0:T(8,128)S(1)} %get-tuple-element.38.refs_5_.refs_1_, ...), custom_call_target="tpu_custom_call" | custom-call | flops 13107200 | bytes 2400000 | tf_op jit(solution)/shard_map/sweep_14/pallas_call | solution.py:395
  105.8 4.5 %chain_12.1 = f32[3072,128]{1,0:T(8,128)S(1)} custom-call(s32[5]{0:T(128)S(1)} %pad_add_fusion.scalars, f32[2,3,2,2,8,8,128]{6,5,4,3,2,1,0:T(8,128)S(1)} %get-tuple-element.49.refs_4_.refs_0_, f32[2,3,2,2,8,8,128]{6,5,4,3,2,1,0:T(8,128)S(1)} %get-tuple-element.52.refs_1_, f32[4,1,6,8,128]{4,3,2,1,0:T(8,128)S(1)} %get-tuple-element.50.refs_4_.refs_1_.refs_2_, ...), custom_call_target="tpu_custom_call" | custom-call | flops 15728640 | bytes 2000000 | tf_op jit(solution)/shard_map/chain_12/pallas_call | solution.py:553
  110.4 36.3 %all_to_all.10 = f32[128,24,128]{2,1,0:T(8,128)S(1)} all-to-all(f32[128,24,128]{2,1,0:T(8,128)S(1)} %bitcast.12), channel_id=1, replica_groups=mesh['tm'=16,'space'=8] {'tm','space'}, dimensions={0} | all-to-all | bytes 3145728 | tf_op jit(solution)/shard_map/all_to_all | solution.py:596
  146.7 3.3 %collect.1 = (f32[2,2,128,256]{3,2,1,0:T(8,128)}, f32[2,2,2,128,256]{4,3,2,1,0:T(8,128)}) custom-call(f32[3072,128]{1,0:T(8,128)S(1)} %bitcast.11), custom_call_target="tpu_custom_call" | custom-call | tf_op jit(solution)/shard_map/collect/pallas_call | solution.py:200
  (30 shorter events, 7.8 us)
Async XLA Ops:
  4.8 12.3 %copy-start = (s32[2]{0:T(128)S(1)}, s32[2]{0:T(128)}, u32[]{:S(2)}) copy-start(s32[2]{0:T(128)} %param.7) | copy-start | bytes 28
  4.8 36.4 %all-to-all-start = ((f32[128,24,128]{2,1,0:T(8,128)}), f32[128,24,128]{2,1,0:T(8,128)S(1)}, u32[]{:S(2)}, u32[]{:S(2)}) async-start(f32[128,24,128]{2,1,0:T(8,128)} %bitcast.13), calls=%async_computation | async-start | bytes 3145728 | tf_op jit(solution)/shard_map/all_to_all | solution.py:569
  42.2 7.4 %collective-permute-start.1 = (f32[2,6,6,8,128]{4,3,2,1,0:T(8,128)S(1)}, f32[2,6,6,8,128]{4,3,2,1,0:T(8,128)S(1)}, u32[]{:S(2)}, u32[]{:S(2)}) collective-permute-start(f32[2,6,6,8,128]{4,3,2,1,0:T(8,128)S(1)} %get-tuple-element.29.refs_0_), channel_id=1, source_target_pairs={{1,0},{9,8},{41,40},{33,32},{65,64},{73,72},{105,104},{97,96},{117... | collective-permute-start | bytes 884744 | tf_op jit(solution)/shard_map/ppermute | solution.py:243
  42.7 7.8 %collective-permute-start = (f32[2,6,6,8,128]{4,3,2,1,0:T(8,128)S(1)}, f32[2,6,6,8,128]{4,3,2,1,0:T(8,128)S(1)}, u32[]{:S(2)}, u32[]{:S(2)}) collective-permute-start(f32[2,6,6,8,128]{4,3,2,1,0:T(8,128)S(1)} %get-tuple-element.30.refs_1_), channel_id=1, source_target_pairs={{4,0},{12,8},{44,40},{36,32},{68,64},{76,72},{108,104},{100,96},{1... | collective-permute-start | bytes 884744 | tf_op jit(solution)/shard_map/ppermute | solution.py:243
  51.5 12.4 %collective-permute-start.4 = (f32[4,6,6,8,128]{4,3,2,1,0:T(8,128)S(1)}, f32[4,6,6,8,128]{4,3,2,1,0:T(8,128)S(1)}, u32[]{:S(2)}, u32[]{:S(2)}) collective-permute-start(f32[4,6,6,8,128]{4,3,2,1,0:T(8,128)S(1)} %get-tuple-element.35.refs_1_), channel_id=1, source_target_pairs={{20,0},{0,8},{8,40},{40,32},{32,64},{64,72},{72,104},{104,96},{96,... | collective-permute-start | bytes 1769480 | tf_op jit(solution)/shard_map/ppermute | solution.py:243
  52.0 12.0 %collective-permute-start.5 = (f32[4,6,6,8,128]{4,3,2,1,0:T(8,128)S(1)}, f32[4,6,6,8,128]{4,3,2,1,0:T(8,128)S(1)}, u32[]{:S(2)}, u32[]{:S(2)}) collective-permute-start(f32[4,6,6,8,128]{4,3,2,1,0:T(8,128)S(1)} %get-tuple-element.36.refs_0_), channel_id=1, source_target_pairs={{8,0},{40,8},{32,40},{64,32},{72,64},{104,72},{96,104},{116,96},{1... | collective-permute-start | bytes 1769480 | tf_op jit(solution)/shard_map/ppermute | solution.py:243
  53.4 9.6 %collective-permute-start.3 = (f32[2,10,6,8,128]{4,3,2,1,0:T(8,128)S(1)}, f32[2,10,6,8,128]{4,3,2,1,0:T(8,128)S(1)}, u32[]{:S(2)}, u32[]{:S(2)}) collective-permute-start(f32[2,10,6,8,128]{4,3,2,1,0:T(8,128)S(1)} %get-tuple-element.33.refs_0_), channel_id=1, source_target_pairs={{1,0},{9,8},{41,40},{33,32},{65,64},{73,72},{105,104},{97,96},{117... | collective-permute-start | bytes 1474568 | tf_op jit(solution)/shard_map/ppermute | solution.py:243
  53.9 10.1 %collective-permute-start.2 = (f32[2,10,6,8,128]{4,3,2,1,0:T(8,128)S(1)}, f32[2,10,6,8,128]{4,3,2,1,0:T(8,128)S(1)}, u32[]{:S(2)}, u32[]{:S(2)}) collective-permute-start(f32[2,10,6,8,128]{4,3,2,1,0:T(8,128)S(1)} %get-tuple-element.34.refs_1_), channel_id=1, source_target_pairs={{4,0},{12,8},{44,40},{36,32},{68,64},{76,72},{108,104},{100,96},{1... | collective-permute-start | bytes 1474568 | tf_op jit(solution)/shard_map/ppermute | solution.py:243
  65.7 18.3 %collective-permute-start.7 = (f32[4,10,6,8,128]{4,3,2,1,0:T(8,128)S(1)}, f32[4,10,6,8,128]{4,3,2,1,0:T(8,128)S(1)}, u32[]{:S(2)}, u32[]{:S(2)}) collective-permute-start(f32[4,10,6,8,128]{4,3,2,1,0:T(8,128)S(1)} %get-tuple-element.37.refs_4_.refs_0_), channel_id=1, source_target_pairs={{8,0},{40,8},{32,40},{64,32},{72,64},{104,72},{96,104},{116,96},{1... | collective-permute-start | bytes 2949128 | tf_op jit(solution)/shard_map/ppermute | solution.py:243
  69.3 14.6 %collective-permute-start.6 = (f32[4,10,6,8,128]{4,3,2,1,0:T(8,128)S(1)}, f32[4,10,6,8,128]{4,3,2,1,0:T(8,128)S(1)}, u32[]{:S(2)}, u32[]{:S(2)}) collective-permute-start(f32[4,10,6,8,128]{4,3,2,1,0:T(8,128)S(1)} %get-tuple-element.38.refs_5_.refs_1_), channel_id=1, source_target_pairs={{20,0},{0,8},{8,40},{40,32},{32,64},{64,72},{72,104},{104,96},{96,... | collective-permute-start | bytes 2949128 | tf_op jit(solution)/shard_map/ppermute | solution.py:243
  78.2 3.9 %collective-permute-start.9 = (f32[2,1,6,8,128]{4,3,2,1,0:T(8,128)S(1)}, f32[2,1,6,8,128]{4,3,2,1,0:T(8,128)S(1)}, u32[]{:S(2)}, u32[]{:S(2)}) collective-permute-start(f32[2,1,6,8,128]{4,3,2,1,0:T(8,128)S(1)} %get-tuple-element.41.refs_0_), channel_id=1, source_target_pairs={{1,0},{9,8},{41,40},{33,32},{65,64},{73,72},{105,104},{97,96},{117... | collective-permute-start | bytes 147464 | tf_op jit(solution)/shard_map/ppermute | solution.py:243
  78.7 3.5 %collective-permute-start.8 = (f32[2,1,6,8,128]{4,3,2,1,0:T(8,128)S(1)}, f32[2,1,6,8,128]{4,3,2,1,0:T(8,128)S(1)}, u32[]{:S(2)}, u32[]{:S(2)}) collective-permute-start(f32[2,1,6,8,128]{4,3,2,1,0:T(8,128)S(1)} %get-tuple-element.42.refs_1_), channel_id=1, source_target_pairs={{4,0},{12,8},{44,40},{36,32},{68,64},{76,72},{108,104},{100,96},{1... | collective-permute-start | bytes 147464 | tf_op jit(solution)/shard_map/ppermute | solution.py:243
  82.4 7.6 %collective-permute-start.11 = (f32[4,1,6,8,128]{4,3,2,1,0:T(8,128)S(1)}, f32[4,1,6,8,128]{4,3,2,1,0:T(8,128)S(1)}, u32[]{:S(2)}, u32[]{:S(2)}) collective-permute-start(f32[4,1,6,8,128]{4,3,2,1,0:T(8,128)S(1)} %get-tuple-element.44.refs_4_.refs_1_), channel_id=1, source_target_pairs={{8,0},{40,8},{32,40},{64,32},{72,64},{104,72},{96,104},{116,96},{1... | collective-permute-start | bytes 294920 | tf_op jit(solution)/shard_map/ppermute | solution.py:243
  83.9 6.1 %collective-permute-start.10 = (f32[4,1,6,8,128]{4,3,2,1,0:T(8,128)S(1)}, f32[4,1,6,8,128]{4,3,2,1,0:T(8,128)S(1)}, u32[]{:S(2)}, u32[]{:S(2)}) collective-permute-start(f32[4,1,6,8,128]{4,3,2,1,0:T(8,128)S(1)} %get-tuple-element.45.refs_5_.refs_2_), channel_id=1, source_target_pairs={{20,0},{0,8},{8,40},{40,32},{32,64},{64,72},{72,104},{104,96},{96,... | collective-permute-start | bytes 294920 | tf_op jit(solution)/shard_map/ppermute | solution.py:243
  93.4 3.9 %collective-permute-start.13 = (f32[2,1,6,8,128]{4,3,2,1,0:T(8,128)S(1)}, f32[2,1,6,8,128]{4,3,2,1,0:T(8,128)S(1)}, u32[]{:S(2)}, u32[]{:S(2)}) collective-permute-start(f32[2,1,6,8,128]{4,3,2,1,0:T(8,128)S(1)} %get-tuple-element.47.refs_4_.refs_0_), channel_id=1, source_target_pairs={{1,0},{9,8},{41,40},{33,32},{65,64},{73,72},{105,104},{97,96},{117... | collective-permute-start | bytes 147464 | tf_op jit(solution)/shard_map/ppermute | solution.py:243
  94.0 3.3 %collective-permute-start.12 = (f32[2,1,6,8,128]{4,3,2,1,0:T(8,128)S(1)}, f32[2,1,6,8,128]{4,3,2,1,0:T(8,128)S(1)}, u32[]{:S(2)}, u32[]{:S(2)}) collective-permute-start(f32[2,1,6,8,128]{4,3,2,1,0:T(8,128)S(1)} %get-tuple-element.48.refs_5_.refs_1_), channel_id=1, source_target_pairs={{4,0},{12,8},{44,40},{36,32},{68,64},{76,72},{108,104},{100,96},{1... | collective-permute-start | bytes 147464 | tf_op jit(solution)/shard_map/ppermute | solution.py:243
  97.5 8.3 %collective-permute-start.15 = (f32[4,1,6,8,128]{4,3,2,1,0:T(8,128)S(1)}, f32[4,1,6,8,128]{4,3,2,1,0:T(8,128)S(1)}, u32[]{:S(2)}, u32[]{:S(2)}) collective-permute-start(f32[4,1,6,8,128]{4,3,2,1,0:T(8,128)S(1)} %get-tuple-element.50.refs_4_.refs_1_.refs_2_), channel_id=1, source_target_pairs={{8,0},{40,8},{32,40},{64,32},{72,64},{104,72},{96,104},{116,96},{1... | collective-permute-start | bytes 294920 | tf_op jit(solution)/shard_map/ppermute | solution.py:243
  100.9 4.9 %collective-permute-start.14 = (f32[4,1,6,8,128]{4,3,2,1,0:T(8,128)S(1)}, f32[4,1,6,8,128]{4,3,2,1,0:T(8,128)S(1)}, u32[]{:S(2)}, u32[]{:S(2)}) collective-permute-start(f32[4,1,6,8,128]{4,3,2,1,0:T(8,128)S(1)} %get-tuple-element.51.refs_5_.refs_2_.refs_3_), channel_id=1, source_target_pairs={{20,0},{0,8},{8,40},{40,32},{32,64},{64,72},{72,104},{104,96},{96,... | collective-permute-start | bytes 294920 | tf_op jit(solution)/shard_map/ppermute | solution.py:243

commit v7 on v6

--- a/solution.py
+++ b/solution.py
@@ -251,35 +251,37 @@
     return from_neighbour(columns[1], 0, -1), from_neighbour(columns[0], 0, 1)
 
 
-def columns_kernel(low, high, up, down, *refs):
-    def position(i, carry):
-        values = [
-            (ref, u, swap_bits([r[rz, i, u] for r in (up, low, high, down)], [(1, 6), (0, 5)]))
-            for rz, ref in enumerate(refs[-2:])
-            for u in range(6)
-        ]
-        for ref, u, arrays in values:
-            for k, v in enumerate(arrays):
-                ref[k, i, u] = v
-        return carry
-
-    lax.fori_loop(0, refs[-1].shape[1], position, 0)
-
-
-def columns(low, high, up, down, after=(), held=()):
-    n = low.shape[1]
+def columns_kernel(ranges, low, high, up, down, *refs):
+    for b, (first, count) in enumerate(ranges):
+
+        def position(i, carry, first=first, outs=refs[2 * b : 2 * b + 2]):
+            values = [
+                (ref, u, swap_bits([r[rz, first + i, u] for r in (up, low, high, down)], [(1, 6), (0, 5)]))
+                for rz, ref in enumerate(outs)
+                for u in range(6)
+            ]
+            for ref, u, arrays in values:
+                for k, v in enumerate(arrays):
+                    ref[k, i, u] = v
+            return carry
+
+        lax.fori_loop(0, count, position, 0)
+
+
+def columns(low, high, up, down, after=(), held=(), ranges=None):
+    ranges = ranges or [(0, low.shape[1])]
     outs = pl.pallas_call(
-        lambda *refs: columns_kernel(*refs[:4], *refs[-2:]),
+        lambda *refs: columns_kernel(ranges, *refs[:4], *refs[-2 * len(ranges) :]),
         in_specs=[VMEM] * 4 + [ANY] * (len(after) + len(held)),
-        out_specs=(ANY,) * len(held) + (VMEM,) * 2,
+        out_specs=(ANY,) * len(held) + (VMEM,) * (2 * len(ranges)),
         out_shape=tuple(jax.ShapeDtypeStruct(h.shape, F32) for h in held)
-        + (jax.ShapeDtypeStruct((4, n, 6, 8, 128), F32),) * 2,
+        + tuple(jax.ShapeDtypeStruct((4, n, 6, 8, 128), F32) for _, n in ranges for _ in range(2)),
         input_output_aliases={4 + len(after) + k: k for k in range(len(held))},
         compiler_params=pltpu.CompilerParams(vmem_limit_bytes=VMEM_LIMIT),
-        cost_estimate=pl.CostEstimate(flops=0, bytes_accessed=n * 800000, transcendentals=0),
+        cost_estimate=pl.CostEstimate(flops=0, bytes_accessed=low.shape[1] * 800000, transcendentals=0),
         name="columns",
     )(low, high, up, down, *after, *held)
-    return outs[-2:], outs[:-2]
+    return outs[len(held) :], outs[: len(held)]
 
 
 def assemble(tile, p, u, first_half, second_half, left, right):
@@ -344,8 +346,9 @@
     return lambda f, xp, ys: ref[at + (f, xp, ys)]
 
 
-def sweep_kernel(first, begin, count, scalars, *refs):
-    halo, (out_ref, start_ref, old, one, two, ahead, rate, base) = refs[:4], refs[-8:]
+def sweep_kernel(first, begin, count, skipped, scalars, *refs):
+    halo, (out_ref, *start_ref) = refs[:4], refs[4 + skipped : -6]
+    old, one, two, ahead, rate, base = refs[-6:]
     tile = Tile(scalars)
 
     def position(at, carry):
@@ -355,11 +358,11 @@
                 for (xp, ys), v in zip(CELLS, both[f], strict=True):
                     old[array, f, xp, ys] = v
 
-        if first == begin == 0:
+        for ref in start_ref:
 
             @pl.when(at == 0)
-            def _():
-                start_ref[...] = old[0]
+            def _(ref=ref):
+                ref[...] = old[0]
 
         for xp, ys in CELLS:
             f0, y0 = tile.tendency(reader(old, 0), xp, ys)
@@ -390,18 +393,23 @@
     lax.fori_loop(0, count, position, 0)
 
 
-def sweep(scalars, halo, first, begin, count, after=()):
+def sweep(scalars, halo, first, begin, count, after=(), held=()):
     field = pltpu.VMEM(FIELD, F32)
-    return pl.pallas_call(
-        functools.partial(sweep_kernel, first, begin, count),
-        in_specs=[SMEM] + [VMEM] * 4 + [ANY] * len(after),
-        out_specs=(VMEM,) * 2,
+    start = first == begin == 0
+    out = pl.pallas_call(
+        functools.partial(sweep_kernel, first, begin, count, len(after) + 2 * len(held)),
+        in_specs=[SMEM] + [VMEM] * 4 + [ANY] * (len(after) + len(held)),
+        out_specs=(ANY,) * len(held) + (VMEM,) * (1 + start),
         scratch_shapes=[pltpu.VMEM((3,) + FIELD, F32)] + [field] * 5,
-        out_shape=(jax.ShapeDtypeStruct((count, 3) + FIELD, F32), jax.ShapeDtypeStruct(FIELD, F32)),
+        out_shape=tuple(jax.ShapeDtypeStruct(h.shape, F32) for h in held)
+        + (jax.ShapeDtypeStruct((count, 3) + FIELD, F32),)
+        + (jax.ShapeDtypeStruct(FIELD, F32),) * start,
+        input_output_aliases={5 + len(after) + k: k for k in range(len(held))},
         compiler_params=pltpu.CompilerParams(vmem_limit_bytes=VMEM_LIMIT),
         cost_estimate=pl.CostEstimate(flops=count * 5 * 32 * 1024 * 40, bytes_accessed=count * 1200000, transcendentals=0),
         name=f"sweep_{first + begin}",
-    )(scalars, *halo, *after)
+    )(scalars, *halo, *after, *held)
+    return out[len(held) :], out[: len(held)]
 
 
 def pack_values(loads):
@@ -432,23 +440,25 @@
     lax.fori_loop(0, raw.shape[0], position, 0)
 
 
-def pack(scalars, first, raw, earlier=(), after=()):
-    return pl.pallas_call(
+def pack(scalars, first, raw, earlier=(), after=(), held=()):
+    out = pl.pallas_call(
         functools.partial(pack_kernel, first),
-        in_specs=[SMEM, VMEM] + [VMEM] * len(earlier) + [ANY] * len(after),
-        out_specs=VMEM,
-        out_shape=jax.ShapeDtypeStruct((SLABS * SLAB_ROWS, 128), F32),
+        in_specs=[SMEM, VMEM] + [VMEM] * len(earlier) + [ANY] * (len(after) + len(held)),
+        out_specs=(ANY,) * len(held) + (VMEM,),
+        out_shape=tuple(jax.ShapeDtypeStruct(h.shape, F32) for h in held)
+        + (jax.ShapeDtypeStruct((SLABS * SLAB_ROWS, 128), F32),),
+        input_output_aliases={2 + len(earlier) + len(after) + k: k for k in range(len(held))},
         compiler_params=pltpu.CompilerParams(vmem_limit_bytes=VMEM_LIMIT),
         cost_estimate=pl.CostEstimate(flops=6000000, bytes_accessed=3000000, transcendentals=0),
         name=f"pack_{first}",
-    )(scalars, raw, *earlier, *after)
-
-
-def chain_kernel(first, count, scalars, *refs):
+    )(scalars, raw, *earlier, *after, *held)
+    return out[-1], out[:-1]
+
+
+def chain_kernel(first, count, parts, scalars, *refs):
     tile = Tile(scalars)
     last = first + count >= SLABS
     z, late, corr, one, two, ahead, next_z, next_late = refs[-8:]
-    parts = 2 if last else 1
     swept, refs = refs[:parts], refs[parts:-8]
     take_first = scalars[1] > 0
     if first == 0:
@@ -541,7 +551,7 @@
         put(out_ref, scalars, jnp.where(conv_one, 1, 0), newest)
 
 
-def chain(scalars, first, count, inputs):
+def chain(scalars, first, count, swept, inputs):
     last = first + count >= SLABS
     if last:
         out_shape = jax.ShapeDtypeStruct((SLABS * SLAB_ROWS, 128), F32)
@@ -551,15 +561,15 @@
         out_shape += (jax.ShapeDtypeStruct((2, 1, 6, 8, 128), F32),) * 2
         scratch = []
     return pl.pallas_call(
-        functools.partial(chain_kernel, first, count),
-        in_specs=[SMEM] + [VMEM] * len(inputs),
+        functools.partial(chain_kernel, first, count, len(swept)),
+        in_specs=[SMEM] + [VMEM] * (len(swept) + len(inputs)),
         out_specs=VMEM if last else (VMEM,) * 3,
         scratch_shapes=scratch + [pltpu.VMEM(FIELD, F32)] * 8,
         out_shape=out_shape,
         compiler_params=pltpu.CompilerParams(vmem_limit_bytes=VMEM_LIMIT),
         cost_estimate=pl.CostEstimate(flops=count * 3 * 32 * 1024 * 40, bytes_accessed=count * 500000, transcendentals=0),
         name=f"chain_{first}",
-    )(scalars, *inputs)
+    )(scalars, *swept, *inputs)
 
 
 def body(slab_starts, slab_nodes, first_slab, converged):
@@ -574,25 +584,32 @@
     columns_a, half_b = columns(*half_a, *rows, held=half_b)
     beside = columns_beside(columns_a)
     rows = rows_beside(*half_b)
-    columns_b, _ = columns(*half_b, *rows, after=beside)
-    halo = [*columns_b, *columns_beside(columns_b)]
-    swept, start = sweep(scalars, [*columns_a, *beside], 0, 0, 6, after=columns_b)
-    raw, *state = chain(scalars, *BLOCKS[0], [swept, start])
-
-    rows = rows_beside(*state)
-    out = pack(scalars, 0, raw, after=state)
-    inside, _ = columns(*state, *rows, after=[out])
-    beside = columns_beside(inside)
-    swept, _ = sweep(scalars, halo, 6, 0, 6, after=inside)
-    raw, *state = chain(scalars, *BLOCKS[1], [swept, *inside, *beside])
-
-    rows = rows_beside(*state)
-    swept, _ = sweep(scalars, halo, 6, 6, 2, after=state)
-    inside, _ = columns(*state, *rows, after=[swept])
-    beside = columns_beside(inside)
-    more, _ = sweep(scalars, halo, 6, 8, 2, after=inside)
-    out = pack(scalars, 6, raw, [out], after=inside)
-    out = chain(scalars, *BLOCKS[2], [swept, more, *inside, *beside, out])
+    (low_b, high_b, *columns_c), _ = columns(*half_b, *rows, after=beside, ranges=[(0, 6), (6, 4)])
+    halo_b = [low_b, high_b, *columns_beside((low_b, high_b))]
+    (swept, start), columns_c = sweep(scalars, [*columns_a, *beside], 0, 0, 6, after=[low_b], held=columns_c)
+    halo_c = [*columns_c, *columns_beside(columns_c)]
+    raw, low, high = chain(scalars, *BLOCKS[0], [swept], [start])
+
+    up = from_neighbour(high, -1, 0)
+    out, (low,) = pack(scalars, 0, raw, after=[high], held=[low])
+    down = from_neighbour(low, 1, 0)
+    (first,), _ = sweep(scalars, halo_b, 6, 0, 2, after=[low])
+    inside, _ = columns(low, high, up, down, after=[first])
+    left = from_neighbour(inside[1], 0, -1)
+    (second,), (low_half,) = sweep(scalars, halo_b, 6, 2, 3, after=[inside[1]], held=[inside[0]])
+    right = from_neighbour(low_half, 0, 1)
+    (third,), _ = sweep(scalars, halo_b, 6, 5, 1, after=[low_half])
+    raw, low, high = chain(scalars, *BLOCKS[1], [first, second, third], [low_half, inside[1], left, right])
+
+    up = from_neighbour(high, -1, 0)
+    (first,), (low,) = sweep(scalars, halo_c, 12, 0, 2, after=[high], held=[low])
+    down = from_neighbour(low, 1, 0)
+    out, _ = pack(scalars, 6, raw, [out], after=[low])
+    inside, _ = columns(low, high, up, down, after=[out])
+    left = from_neighbour(inside[1], 0, -1)
+    (second,), (low_half,) = sweep(scalars, halo_c, 12, 2, 2, after=[inside[1]], held=[inside[0]])
+    right = from_neighbour(low_half, 0, 1)
+    out = chain(scalars, *BLOCKS[2], [first, second], [low_half, inside[1], left, right, out])
     out = lax.all_to_all(out.reshape(128, 24, 128), AXES, 0, 0, tiled=True)
     starts, nodes = collect(out.reshape(128 * 24, 128))
     return starts[None], nodes[None]

time: 150 us -> 158 us (1.053)
  starting transfers between devices: 28.2 us -> 36.6 us
  blocking collectives: 36.3 us -> 33.8 us
    ppermute x16 -> x18, starting transfers between devices: 16.7 us -> 25.1 us  [from_neighbour(): return lax.ppermute(payload, AXES, pairs)]
    all_to_all x1, blocking collectives: 36.3 us -> 33.8 us  [body(): out = lax.all_to_all(out.reshape(128, 24, 128), AXES, 0, 0, tiled=True)]
    pallas_call x11 -> x13, Pallas kernels: 30.6 us -> 32.1 us  [the longest x6 17.5 us: sweep(): pl.pallas_call(functools.partial(sweep_kernel, first, begin, count, len(a...]
    ppermute x16 -> x18, waiting for transfers between devices: 15.9 us -> 16.1 us  [from_neighbour(): return lax.ppermute(payload, AXES, pairs)]
  transfers between devices with their start and end apart: 17 -> 19, of which waited for: 5 -> 7; matrix products, arithmetic and copies ran while one was open for 0% -> 0% of each run, Pallas kernels for 16% -> 16%
where the time goes in v7:
time: 158 us
  Pallas kernels  45.3 us (29%)
  waiting for transfers between devices  40.1 us (25%)
  starting transfers between devices  36.6 us (23%)
  blocking collectives  33.8 us (21%)
  between operations  1.72 us (1%)
    all_to_all x1, blocking collectives, body(): out = lax.all_to_all(out.reshape(128, 24, 128), AXES, 0, 0, tiled=True)  33.8 us
    ppermute x18, starting transfers between devices, from_neighbour(): return lax.ppermute(payload, AXES, pairs)  25.1 us
    all_to_all x1, waiting for transfers between devices, body(): lax.all_to_all(chunks.reshape(128, 24, 128), AXES, 0, 0, tiled=True)  24.1 us
    pallas_call x6, Pallas kernels, sweep(): pl.pallas_call(functools.partial(sweep_kernel, first, begin, count, len(a...  17.5 us
    ppermute x18, waiting for transfers between devices, from_neighbour(): return lax.ppermute(payload, AXES, pairs)  16.1 us
    all_to_all x1, starting transfers between devices, body(): lax.all_to_all(chunks.reshape(128, 24, 128), AXES, 0, 0, tiled=True)  11.5 us
    pallas_call x3, Pallas kernels, chain(): pl.pallas_call(functools.partial(chain_kernel, first, count, len(swept)),...  11.4 us
    pallas_call x2, Pallas kernels, pack(): pl.pallas_call(functools.partial(pack_kernel, first), in_specs=[SMEM, VME...  4.88 us
  transfers between devices with their start and end apart: 19, of which 7 were waited for; matrix products, arithmetic and copies ran while one was open for 0% of the time, Pallas kernels for 16%

profile of v7, /device:TPU:1, one launch (start us, length us, event | category | flops | bytes accessed | tf_op | source)
XLA Modules:
  0.0 157.7 jit_solution(15944164285193636072)
XLA Ops:
  0.6 4.1 %spread.1 = f32[3072,128]{1,0:T(8,128)} custom-call(f32[2,2,128,256]{3,2,1,0:T(8,128)} %bitcast.15, f32[2,2,2,128,256]{4,3,2,1,0:T(8,128)} %bitcast.14), custom_call_target="tpu_custom_call" | custom-call | tf_op jit(solution)/shard_map/spread/pallas_call | solution.py:142
  4.8 11.5 %all-to-all-start = ((f32[128,24,128]{2,1,0:T(8,128)}), f32[128,24,128]{2,1,0:T(8,128)S(1)}, u32[]{:S(2)}, u32[]{:S(2)}) async-start(f32[128,24,128]{2,1,0:T(8,128)} %bitcast.13), calls=%async_computation | async-start | bytes 3145728 | tf_op jit(solution)/shard_map/all_to_all | solution.py:579
  17.1 24.1 %all-to-all-done = f32[128,24,128]{2,1,0:T(8,128)S(1)} async-done(((f32[128,24,128]{2,1,0:T(8,128)}), f32[128,24,128]{2,1,0:T(8,128)S(1)}, u32[]{:S(2)}, u32[]{:S(2)}) %all-to-all-start) | async-done | bytes 1572896 | tf_op jit(solution)/shard_map/all_to_all | solution.py:579
  43.7 5.9 %collective-permute-done.refs_2_ = f32[2,6,6,8,128]{4,3,2,1,0:T(8,128)S(1)} collective-permute-done((f32[2,6,6,8,128]{4,3,2,1,0:T(8,128)S(1)}, f32[2,6,6,8,128]{4,3,2,1,0:T(8,128)S(1)}, u32[]{:S(2)}, u32[]{:S(2)}) %collective-permute-start) | collective-permute-done | bytes 294944 | tf_op jit(solution)/shard_map/ppermute | solution.py:243
  51.3 2.0 %collective-permute-start.3 = (f32[4,6,6,8,128]{4,3,2,1,0:T(8,128)S(1)}, f32[4,6,6,8,128]{4,3,2,1,0:T(8,128)S(1)}, u32[]{:S(2)}, u32[]{:S(2)}) collective-permute-start(f32[4,6,6,8,128]{4,3,2,1,0:T(8,128)S(1)} %get-tuple-element.42.refs_0_), channel_id=1, source_target_pairs={{8,0},{40,8},{32,40},{64,32},{72,64},{104,72},{96,104},{116,96},{1... | collective-permute-start | bytes 1769480 | tf_op jit(solution)/shard_map/ppermute | solution.py:243
  54.8 8.1 %collective-permute-done.4.refs_2_ = f32[2,10,6,8,128]{4,3,2,1,0:T(8,128)S(1)} collective-permute-done((f32[2,10,6,8,128]{4,3,2,1,0:T(8,128)S(1)}, f32[2,10,6,8,128]{4,3,2,1,0:T(8,128)S(1)}, u32[]{:S(2)}, u32[]{:S(2)}) %collective-permute-start.4) | collective-permute-done | bytes 491552 | tf_op jit(solution)/shard_map/ppermute | solution.py:243
  62.9 1.7 %columns.5 = (f32[4,6,6,8,128]{4,3,2,1,0:T(8,128)S(1)}, f32[4,6,6,8,128]{4,3,2,1,0:T(8,128)S(1)}, f32[4,4,6,8,128]{4,3,2,1,0:T(8,128)S(1)}, f32[4,4,6,8,128]{4,3,2,1,0:T(8,128)S(1)}) custom-call(f32[2,10,6,8,128]{4,3,2,1,0:T(8,128)S(1)} %get-tuple-element.44.refs_0_, f32[2,10,6,8,128]{4,3,2,1,0:T(8,128)S(1)} %get-tuple-element.45.refs_1_, ...), custom_call_target="tpu_custom_call" | custom-call | bytes 8000000 | tf_op jit(solution)/shard_map/columns/pallas_call | solution.py:273
  64.6 3.0 %collective-permute-start.8 = (f32[4,6,6,8,128]{4,3,2,1,0:T(8,128)S(1)}, f32[4,6,6,8,128]{4,3,2,1,0:T(8,128)S(1)}, u32[]{:S(2)}, u32[]{:S(2)}) collective-permute-start(f32[4,6,6,8,128]{4,3,2,1,0:T(8,128)S(1)} %get-tuple-element.51.refs_1_), channel_id=1, source_target_pairs={{20,0},{0,8},{8,40},{40,32},{32,64},{64,72},{72,104},{104,96},{96,... | collective-permute-start | bytes 1769480 | tf_op jit(solution)/shard_map/ppermute | solution.py:243
  69.0 5.7 %sweep_0.1 = (f32[4,4,6,8,128]{4,3,2,1,0:T(8,128)S(1)}, f32[4,4,6,8,128]{4,3,2,1,0:T(8,128)S(1)}, f32[6,3,2,2,8,8,128]{6,5,4,3,2,1,0:T(8,128)S(1)}, f32[2,2,8,8,128]{4,3,2,1,0:T(8,128)S(1)}) custom-call(s32[5]{0:T(128)S(1)} %pad_add_fusion.scalars, f32[4,6,6,8,128]{4,3,2,1,0:T(8,128)S(1)} %get-tuple-element.42.refs_0_, ...), custom_call_target="tpu_custom_call", output_to_operand_aliasing={{0}: (6, {}), {1}: (7, {})} | custom-call | flops 39321600 | bytes 7200000 | tf_op jit(solution)/shard_map/sweep_0/pallas_call | solution.py:399
  75.0 3.1 %collective-permute-start.7 = (f32[4,4,6,8,128]{4,3,2,1,0:T(8,128)S(1)}, f32[4,4,6,8,128]{4,3,2,1,0:T(8,128)S(1)}, u32[]{:S(2)}, u32[]{:S(2)}) collective-permute-start(f32[4,4,6,8,128]{4,3,2,1,0:T(8,128)S(1)} %get-tuple-element.49.refs_0_), channel_id=1, source_target_pairs={{8,0},{40,8},{32,40},{64,32},{72,64},{104,72},{96,104},{116,96},{1... | collective-permute-start | bytes 1179656 | tf_op jit(solution)/shard_map/ppermute | solution.py:243
  78.0 3.1 %chain_0.1 = (f32[6,3,2,2,8,8,128]{6,5,4,3,2,1,0:T(8,128)S(1)}, f32[2,1,6,8,128]{4,3,2,1,0:T(8,128)S(1)}, f32[2,1,6,8,128]{4,3,2,1,0:T(8,128)S(1)}) custom-call(s32[5]{0:T(128)S(1)} %pad_add_fusion.scalars, f32[6,3,2,2,8,8,128]{6,5,4,3,2,1,0:T(8,128)S(1)} %get-tuple-element.52.refs_0_, f32[2,2,8,8,128]{4,3,2,1,0:T(8,128)S(1)} %get-tuple-element.53.refs_1_), custom_call_target="tpu_custom_call" | custom-call | flops 23592960 | bytes 3000000 | tf_op jit(solution)/shard_map/chain_0/pallas_call | solution.py:563
  81.2 2.4 %pack_0.1 = (f32[2,1,6,8,128]{4,3,2,1,0:T(8,128)S(1)}, f32[3072,128]{1,0:T(8,128)S(1)}) custom-call(s32[5]{0:T(128)S(1)} %pad_add_fusion.scalars, f32[6,3,2,2,8,8,128]{6,5,4,3,2,1,0:T(8,128)S(1)} %get-tuple-element.54.raw, f32[2,1,6,8,128]{4,3,2,1,0:T(8,128)S(1)} %get-tuple-element.55.refs_0_.refs_1_, ...), custom_call_target="tpu_custom_call", output_to_operand_aliasing={{0}: (3, {})} | custom-call | flops 6000000 | bytes 3000000 | tf_op jit(solution)/shard_map/pack_0/pallas_call | solution.py:444
  85.2 2.4 %sweep_6.1.refs_4_.refs_0_ = f32[2,3,2,2,8,8,128]{6,5,4,3,2,1,0:T(8,128)S(1)} custom-call(s32[5]{0:T(128)S(1)} %pad_add_fusion.scalars, f32[4,6,6,8,128]{4,3,2,1,0:T(8,128)S(1)} %get-tuple-element.46.refs_4_.refs_0_, f32[4,6,6,8,128]{4,3,2,1,0:T(8,128)S(1)} %get-tuple-element.51.refs_1_, f32[4,6,6,8,128]{4,3,2,1,0:T(8,128)S(1)} %collective-permute-done.8.refs_2_, ...), custom_call_target="tpu_custom_call" | custom-call | flops 13107200 | bytes 2400000 | tf_op jit(solution)/shard_map/sweep_6/pallas_call | solution.py:399
  87.7 3.3 %sweep_8.1 = (f32[4,1,6,8,128]{4,3,2,1,0:T(8,128)S(1)}, f32[3,3,2,2,8,8,128]{6,5,4,3,2,1,0:T(8,128)S(1)}) custom-call(s32[5]{0:T(128)S(1)} %pad_add_fusion.scalars, f32[4,6,6,8,128]{4,3,2,1,0:T(8,128)S(1)} %get-tuple-element.46.refs_4_.refs_0_, f32[4,6,6,8,128]{4,3,2,1,0:T(8,128)S(1)} %get-tuple-element.51.refs_1_, ...), custom_call_target="tpu_custom_call", output_to_operand_aliasing={{0}: (6, {})} | custom-call | flops 19660800 | bytes 3600000 | tf_op jit(solution)/shard_map/sweep_8/pallas_call | solution.py:399
  91.0 3.7 %collective-permute-start.13 = (f32[4,1,6,8,128]{4,3,2,1,0:T(8,128)S(1)}, f32[4,1,6,8,128]{4,3,2,1,0:T(8,128)S(1)}, u32[]{:S(2)}, u32[]{:S(2)}) collective-permute-start(f32[4,1,6,8,128]{4,3,2,1,0:T(8,128)S(1)} %get-tuple-element.61.refs_4_.refs_3_), channel_id=1, source_target_pairs={{8,0},{40,8},{32,40},{64,32},{72,64},{104,72},{96,104},{116,96},{1... | collective-permute-start | bytes 294920 | tf_op jit(solution)/shard_map/ppermute | solution.py:243
  96.4 3.8 %chain_6.1 = (f32[6,3,2,2,8,8,128]{6,5,4,3,2,1,0:T(8,128)S(1)}, f32[2,1,6,8,128]{4,3,2,1,0:T(8,128)S(1)}, f32[2,1,6,8,128]{4,3,2,1,0:T(8,128)S(1)}) custom-call(s32[5]{0:T(128)S(1)} %pad_add_fusion.scalars, f32[2,3,2,2,8,8,128]{6,5,4,3,2,1,0:T(8,128)S(1)} %sweep_6.1.refs_4_.refs_0_, f32[3,3,2,2,8,8,128]{6,5,4,3,2,1,0:T(8,128)S(1)} %get-tuple-element.60.refs_1_, ...), custom_call_target="tpu_custom_call" | custom-call | flops 23592960 | bytes 3000000 | tf_op jit(solution)/shard_map/chain_6/pallas_call | solution.py:563
  100.2 2.4 %sweep_12.1 = (f32[2,1,6,8,128]{4,3,2,1,0:T(8,128)S(1)}, f32[2,3,2,2,8,8,128]{6,5,4,3,2,1,0:T(8,128)S(1)}) custom-call(s32[5]{0:T(128)S(1)} %pad_add_fusion.scalars, f32[4,4,6,8,128]{4,3,2,1,0:T(8,128)S(1)} %get-tuple-element.49.refs_0_, f32[4,4,6,8,128]{4,3,2,1,0:T(8,128)S(1)} %get-tuple-element.50.refs_1_, ...), custom_call_target="tpu_custom_call", output_to_operand_aliasing={{0}: (6, {})} | custom-call | flops 13107200 | bytes 2400000 | tf_op jit(solution)/shard_map/sweep_12/pallas_call | solution.py:399
  102.6 1.5 collective-permute-start.14
  104.2 2.5 %pack_6.1.refs_4_.refs_6_ = f32[3072,128]{1,0:T(8,128)S(1)} custom-call(s32[5]{0:T(128)S(1)} %pad_add_fusion.scalars, f32[6,3,2,2,8,8,128]{6,5,4,3,2,1,0:T(8,128)S(1)} %get-tuple-element.66.raw, f32[3072,128]{1,0:T(8,128)S(1)} %get-tuple-element.67.refs_0_, f32[2,1,6,8,128]{4,3,2,1,0:T(8,128)S(1)} %get-tuple-element.65.refs_1_.refs_0_), custom_call_target="tpu_custom_call" | custom-call | flops 6000000 | bytes 3000000 | tf_op jit(solution)/shard_map/pack_6/pallas_call | solution.py:444
  106.8 2.4 %sweep_14.1 = (f32[4,1,6,8,128]{4,3,2,1,0:T(8,128)S(1)}, f32[2,3,2,2,8,8,128]{6,5,4,3,2,1,0:T(8,128)S(1)}) custom-call(s32[5]{0:T(128)S(1)} %pad_add_fusion.scalars, f32[4,4,6,8,128]{4,3,2,1,0:T(8,128)S(1)} %get-tuple-element.49.refs_0_, f32[4,4,6,8,128]{4,3,2,1,0:T(8,128)S(1)} %get-tuple-element.50.refs_1_, ...), custom_call_target="tpu_custom_call", output_to_operand_aliasing={{0}: (6, {})} | custom-call | flops 13107200 | bytes 2400000 | tf_op jit(solution)/shard_map/sweep_14/pallas_call | solution.py:399
  109.2 5.0 %collective-permute-start.17 = (f32[4,1,6,8,128]{4,3,2,1,0:T(8,128)S(1)}, f32[4,1,6,8,128]{4,3,2,1,0:T(8,128)S(1)}, u32[]{:S(2)}, u32[]{:S(2)}) collective-permute-start(f32[4,1,6,8,128]{4,3,2,1,0:T(8,128)S(1)} %get-tuple-element.71.refs_2_), channel_id=1, source_target_pairs={{8,0},{40,8},{32,40},{64,32},{72,64},{104,72},{96,104},{116,96},{1... | collective-permute-start | bytes 294920 | tf_op jit(solution)/shard_map/ppermute | solution.py:243
  115.9 4.5 %chain_12.1 = f32[3072,128]{1,0:T(8,128)S(1)} custom-call(s32[5]{0:T(128)S(1)} %pad_add_fusion.scalars, f32[2,3,2,2,8,8,128]{6,5,4,3,2,1,0:T(8,128)S(1)} %get-tuple-element.64.refs_0_, f32[2,3,2,2,8,8,128]{6,5,4,3,2,1,0:T(8,128)S(1)} %get-tuple-element.70.refs_1_, f32[4,1,6,8,128]{4,3,2,1,0:T(8,128)S(1)} %get-tuple-element.71.refs_2_, ...), custom_call_target="tpu_custom_call" | custom-call | flops 15728640 | bytes 2000000 | tf_op jit(solution)/shard_map/chain_12/pallas_call | solution.py:563
  120.4 33.8 %all_to_all.10 = f32[128,24,128]{2,1,0:T(8,128)S(1)} all-to-all(f32[128,24,128]{2,1,0:T(8,128)S(1)} %bitcast.12), channel_id=1, replica_groups=mesh['tm'=16,'space'=8] {'tm','space'}, dimensions={0} | all-to-all | bytes 3145728 | tf_op jit(solution)/shard_map/all_to_all | solution.py:613
  154.3 3.3 %collect.1 = (f32[2,2,128,256]{3,2,1,0:T(8,128)}, f32[2,2,2,128,256]{4,3,2,1,0:T(8,128)}) custom-call(f32[3072,128]{1,0:T(8,128)S(1)} %bitcast.11), custom_call_target="tpu_custom_call" | custom-call | tf_op jit(solution)/shard_map/collect/pallas_call | solution.py:200
  (36 shorter events, 12.7 us)
Async XLA Ops:
  4.8 12.3 %copy-start = (s32[2]{0:T(128)S(1)}, s32[2]{0:T(128)}, u32[]{:S(2)}) copy-start(s32[2]{0:T(128)} %param.7) | copy-start | bytes 28
  4.8 36.4 %all-to-all-start = ((f32[128,24,128]{2,1,0:T(8,128)}), f32[128,24,128]{2,1,0:T(8,128)S(1)}, u32[]{:S(2)}, u32[]{:S(2)}) async-start(f32[128,24,128]{2,1,0:T(8,128)} %bitcast.13), calls=%async_computation | async-start | bytes 3145728 | tf_op jit(solution)/shard_map/all_to_all | solution.py:579
  42.2 7.4 %collective-permute-start = (f32[2,6,6,8,128]{4,3,2,1,0:T(8,128)S(1)}, f32[2,6,6,8,128]{4,3,2,1,0:T(8,128)S(1)}, u32[]{:S(2)}, u32[]{:S(2)}) collective-permute-start(f32[2,6,6,8,128]{4,3,2,1,0:T(8,128)S(1)} %get-tuple-element.39.refs_1_), channel_id=1, source_target_pairs={{4,0},{12,8},{44,40},{36,32},{68,64},{76,72},{108,104},{100,96},{1... | collective-permute-start | bytes 884744 | tf_op jit(solution)/shard_map/ppermute | solution.py:243
  42.6 7.2 %collective-permute-start.1 = (f32[2,6,6,8,128]{4,3,2,1,0:T(8,128)S(1)}, f32[2,6,6,8,128]{4,3,2,1,0:T(8,128)S(1)}, u32[]{:S(2)}, u32[]{:S(2)}) collective-permute-start(f32[2,6,6,8,128]{4,3,2,1,0:T(8,128)S(1)} %get-tuple-element.38.refs_0_), channel_id=1, source_target_pairs={{1,0},{9,8},{41,40},{33,32},{65,64},{73,72},{105,104},{97,96},{117... | collective-permute-start | bytes 884744 | tf_op jit(solution)/shard_map/ppermute | solution.py:243
  50.9 12.0 %collective-permute-start.2 = (f32[4,6,6,8,128]{4,3,2,1,0:T(8,128)S(1)}, f32[4,6,6,8,128]{4,3,2,1,0:T(8,128)S(1)}, u32[]{:S(2)}, u32[]{:S(2)}) collective-permute-start(f32[4,6,6,8,128]{4,3,2,1,0:T(8,128)S(1)} %get-tuple-element.43.refs_1_), channel_id=1, source_target_pairs={{20,0},{0,8},{8,40},{40,32},{32,64},{64,72},{72,104},{104,96},{96,... | collective-permute-start | bytes 1769480 | tf_op jit(solution)/shard_map/ppermute | solution.py:243
  51.3 11.6 %collective-permute-start.3 = (f32[4,6,6,8,128]{4,3,2,1,0:T(8,128)S(1)}, f32[4,6,6,8,128]{4,3,2,1,0:T(8,128)S(1)}, u32[]{:S(2)}, u32[]{:S(2)}) collective-permute-start(f32[4,6,6,8,128]{4,3,2,1,0:T(8,128)S(1)} %get-tuple-element.42.refs_0_), channel_id=1, source_target_pairs={{8,0},{40,8},{32,40},{64,32},{72,64},{104,72},{96,104},{116,96},{1... | collective-permute-start | bytes 1769480 | tf_op jit(solution)/shard_map/ppermute | solution.py:243
  53.3 9.6 %collective-permute-start.4 = (f32[2,10,6,8,128]{4,3,2,1,0:T(8,128)S(1)}, f32[2,10,6,8,128]{4,3,2,1,0:T(8,128)S(1)}, u32[]{:S(2)}, u32[]{:S(2)}) collective-permute-start(f32[2,10,6,8,128]{4,3,2,1,0:T(8,128)S(1)} %get-tuple-element.45.refs_1_), channel_id=1, source_target_pairs={{4,0},{12,8},{44,40},{36,32},{68,64},{76,72},{108,104},{100,96},{1... | collective-permute-start | bytes 1474568 | tf_op jit(solution)/shard_map/ppermute | solution.py:243
  53.5 9.4 %collective-permute-start.5 = (f32[2,10,6,8,128]{4,3,2,1,0:T(8,128)S(1)}, f32[2,10,6,8,128]{4,3,2,1,0:T(8,128)S(1)}, u32[]{:S(2)}, u32[]{:S(2)}) collective-permute-start(f32[2,10,6,8,128]{4,3,2,1,0:T(8,128)S(1)} %get-tuple-element.44.refs_0_), channel_id=1, source_target_pairs={{1,0},{9,8},{41,40},{33,32},{65,64},{73,72},{105,104},{97,96},{117... | collective-permute-start | bytes 1474568 | tf_op jit(solution)/shard_map/ppermute | solution.py:243
  64.6 19.1 %collective-permute-start.8 = (f32[4,6,6,8,128]{4,3,2,1,0:T(8,128)S(1)}, f32[4,6,6,8,128]{4,3,2,1,0:T(8,128)S(1)}, u32[]{:S(2)}, u32[]{:S(2)}) collective-permute-start(f32[4,6,6,8,128]{4,3,2,1,0:T(8,128)S(1)} %get-tuple-element.51.refs_1_), channel_id=1, source_target_pairs={{20,0},{0,8},{8,40},{40,32},{32,64},{64,72},{72,104},{104,96},{96,... | collective-permute-start | bytes 1769480 | tf_op jit(solution)/shard_map/ppermute | solution.py:243
  67.6 17.5 %collective-permute-start.9 = (f32[4,6,6,8,128]{4,3,2,1,0:T(8,128)S(1)}, f32[4,6,6,8,128]{4,3,2,1,0:T(8,128)S(1)}, u32[]{:S(2)}, u32[]{:S(2)}) collective-permute-start(f32[4,6,6,8,128]{4,3,2,1,0:T(8,128)S(1)} %get-tuple-element.46.refs_4_.refs_0_), channel_id=1, source_target_pairs={{8,0},{40,8},{32,40},{64,32},{72,64},{104,72},{96,104},{116,96},{1... | collective-permute-start | bytes 1769480 | tf_op jit(solution)/shard_map/ppermute | solution.py:243
  74.7 25.4 %collective-permute-start.6 = (f32[4,4,6,8,128]{4,3,2,1,0:T(8,128)S(1)}, f32[4,4,6,8,128]{4,3,2,1,0:T(8,128)S(1)}, u32[]{:S(2)}, u32[]{:S(2)}) collective-permute-start(f32[4,4,6,8,128]{4,3,2,1,0:T(8,128)S(1)} %get-tuple-element.50.refs_1_), channel_id=1, source_target_pairs={{20,0},{0,8},{8,40},{40,32},{32,64},{64,72},{72,104},{104,96},{96,... | collective-permute-start | bytes 1179656 | tf_op jit(solution)/shard_map/ppermute | solution.py:243
  75.0 25.2 %collective-permute-start.7 = (f32[4,4,6,8,128]{4,3,2,1,0:T(8,128)S(1)}, f32[4,4,6,8,128]{4,3,2,1,0:T(8,128)S(1)}, u32[]{:S(2)}, u32[]{:S(2)}) collective-permute-start(f32[4,4,6,8,128]{4,3,2,1,0:T(8,128)S(1)} %get-tuple-element.49.refs_0_), channel_id=1, source_target_pairs={{8,0},{40,8},{32,40},{64,32},{72,64},{104,72},{96,104},{116,96},{1... | collective-permute-start | bytes 1179656 | tf_op jit(solution)/shard_map/ppermute | solution.py:243
  83.5 4.0 %collective-permute-start.11 = (f32[2,1,6,8,128]{4,3,2,1,0:T(8,128)S(1)}, f32[2,1,6,8,128]{4,3,2,1,0:T(8,128)S(1)}, u32[]{:S(2)}, u32[]{:S(2)}) collective-permute-start(f32[2,1,6,8,128]{4,3,2,1,0:T(8,128)S(1)} %get-tuple-element.57.refs_4_.refs_0_), channel_id=1, source_target_pairs={{1,0},{9,8},{41,40},{33,32},{65,64},{73,72},{105,104},{97,96},{117... | collective-permute-start | bytes 147464 | tf_op jit(solution)/shard_map/ppermute | solution.py:243
  83.7 3.9 %collective-permute-start.10 = (f32[2,1,6,8,128]{4,3,2,1,0:T(8,128)S(1)}, f32[2,1,6,8,128]{4,3,2,1,0:T(8,128)S(1)}, u32[]{:S(2)}, u32[]{:S(2)}) collective-permute-start(f32[2,1,6,8,128]{4,3,2,1,0:T(8,128)S(1)} %get-tuple-element.55.refs_0_.refs_1_), channel_id=1, source_target_pairs={{4,0},{12,8},{44,40},{36,32},{68,64},{76,72},{108,104},{100,96},{1... | collective-permute-start | bytes 147464 | tf_op jit(solution)/shard_map/ppermute | solution.py:243
  91.0 5.2 %collective-permute-start.13 = (f32[4,1,6,8,128]{4,3,2,1,0:T(8,128)S(1)}, f32[4,1,6,8,128]{4,3,2,1,0:T(8,128)S(1)}, u32[]{:S(2)}, u32[]{:S(2)}) collective-permute-start(f32[4,1,6,8,128]{4,3,2,1,0:T(8,128)S(1)} %get-tuple-element.61.refs_4_.refs_3_), channel_id=1, source_target_pairs={{8,0},{40,8},{32,40},{64,32},{72,64},{104,72},{96,104},{116,96},{1... | collective-permute-start | bytes 294920 | tf_op jit(solution)/shard_map/ppermute | solution.py:243
  94.7 1.6 %collective-permute-start.12 = (f32[4,1,6,8,128]{4,3,2,1,0:T(8,128)S(1)}, f32[4,1,6,8,128]{4,3,2,1,0:T(8,128)S(1)}, u32[]{:S(2)}, u32[]{:S(2)}) collective-permute-start(f32[4,1,6,8,128]{4,3,2,1,0:T(8,128)S(1)} %get-tuple-element.58.refs_4_), channel_id=1, source_target_pairs={{20,0},{0,8},{8,40},{40,32},{32,64},{64,72},{72,104},{104,96},{96,... | collective-permute-start | bytes 294920 | tf_op jit(solution)/shard_map/ppermute | solution.py:243
  102.5 4.1 %collective-permute-start.15 = (f32[2,1,6,8,128]{4,3,2,1,0:T(8,128)S(1)}, f32[2,1,6,8,128]{4,3,2,1,0:T(8,128)S(1)}, u32[]{:S(2)}, u32[]{:S(2)}) collective-permute-start(f32[2,1,6,8,128]{4,3,2,1,0:T(8,128)S(1)} %get-tuple-element.65.refs_1_.refs_0_), channel_id=1, source_target_pairs={{1,0},{9,8},{41,40},{33,32},{65,64},{73,72},{105,104},{97,96},{117... | collective-permute-start | bytes 147464 | tf_op jit(solution)/shard_map/ppermute | solution.py:243
  102.6 4.0 %collective-permute-start.14 = (f32[2,1,6,8,128]{4,3,2,1,0:T(8,128)S(1)}, f32[2,1,6,8,128]{4,3,2,1,0:T(8,128)S(1)}, u32[]{:S(2)}, u32[]{:S(2)}) collective-permute-start(f32[2,1,6,8,128]{4,3,2,1,0:T(8,128)S(1)} %get-tuple-element.62.refs_4_.refs_1_), channel_id=1, source_target_pairs={{4,0},{12,8},{44,40},{36,32},{68,64},{76,72},{108,104},{100,96},{1... | collective-permute-start | bytes 147464 | tf_op jit(solution)/shard_map/ppermute | solution.py:243
  109.2 6.0 %collective-permute-start.17 = (f32[4,1,6,8,128]{4,3,2,1,0:T(8,128)S(1)}, f32[4,1,6,8,128]{4,3,2,1,0:T(8,128)S(1)}, u32[]{:S(2)}, u32[]{:S(2)}) collective-permute-start(f32[4,1,6,8,128]{4,3,2,1,0:T(8,128)S(1)} %get-tuple-element.71.refs_2_), channel_id=1, source_target_pairs={{8,0},{40,8},{32,40},{64,32},{72,64},{104,72},{96,104},{116,96},{1... | collective-permute-start | bytes 294920 | tf_op jit(solution)/shard_map/ppermute | solution.py:243
  114.2 1.6 %collective-permute-start.16 = (f32[4,1,6,8,128]{4,3,2,1,0:T(8,128)S(1)}, f32[4,1,6,8,128]{4,3,2,1,0:T(8,128)S(1)}, u32[]{:S(2)}, u32[]{:S(2)}) collective-permute-start(f32[4,1,6,8,128]{4,3,2,1,0:T(8,128)S(1)} %get-tuple-element.68.refs_4_.refs_3_), channel_id=1, source_target_pairs={{20,0},{0,8},{8,40},{40,32},{32,64},{64,72},{72,104},{104,96},{96,... | collective-permute-start | bytes 294920 | tf_op jit(solution)/shard_map/ppermute | solution.py:243

commit v8 on v6

--- a/solution.py
+++ b/solution.py
@@ -102,6 +102,12 @@
             for half in range(2)
         ]
 
+    def arrival(u):
+        for xp in range(2):
+            for half in range(2):
+                here = planes.at[u, xp, half]
+                pltpu.make_async_copy(here, here, arrived.at[4 * u + 2 * xp + half]).wait()
+
     for u in range(6):
         for copy in copies(u):
             copy.start()
@@ -121,21 +127,12 @@
             for at, v in found:
                 out_ref[pl.ds(at + row, 8, stride=12)] = v
 
-    for copy in copies(0) + copies(1):
-        copy.wait()
-
-    def pair(k, carry):
-        for n in (1, 2):
-
-            @pl.when(k == n)
-            def _(n=n):
-                for copy in copies(2 * n) + copies(2 * n + 1):
-                    copy.wait()
-
-        lax.fori_loop(2 * k, 2 * k + 2, lambda u, c: (unit(u), c)[1], 0)
+    def units(u, carry):
+        arrival(u)
+        unit(u)
         return carry
 
-    lax.fori_loop(0, 3, pair, 0)
+    lax.fori_loop(0, 6, units, 0)
 
 
 def spread(starts, nodes):
@@ -448,7 +445,7 @@
     tile = Tile(scalars)
     last = first + count >= SLABS
     z, late, corr, one, two, ahead, next_z, next_late = refs[-8:]
-    parts = 2 if last else 1
+    parts = 1 if first == BLOCKS[1][0] else 2
     swept, refs = refs[:parts], refs[parts:-8]
     take_first = scalars[1] > 0
     if first == 0:
@@ -574,10 +571,11 @@
     columns_a, half_b = columns(*half_a, *rows, held=half_b)
     beside = columns_beside(columns_a)
     rows = rows_beside(*half_b)
-    columns_b, _ = columns(*half_b, *rows, after=beside)
+    swept, start = sweep(scalars, [*columns_a, *beside], 0, 0, 3)
+    columns_b, _ = columns(*half_b, *rows, after=[swept])
     halo = [*columns_b, *columns_beside(columns_b)]
-    swept, start = sweep(scalars, [*columns_a, *beside], 0, 0, 6, after=columns_b)
-    raw, *state = chain(scalars, *BLOCKS[0], [swept, start])
+    more, _ = sweep(scalars, [*columns_a, *beside], 0, 3, 3, after=columns_b)
+    raw, *state = chain(scalars, *BLOCKS[0], [swept, more, start])
 
     rows = rows_beside(*state)
     out = pack(scalars, 0, raw, after=state)

time: 150 us -> 148 us (0.987)
  starting transfers between devices: 28.2 us -> 25.7 us
    ppermute x16, starting transfers between devices: 16.7 us -> 14.2 us  [from_neighbour(): return lax.ppermute(payload, AXES, pairs)]
    pallas_call x4 -> x5, Pallas kernels: 16.5 us -> 17.2 us  [sweep(): pl.pallas_call(functools.partial(sweep_kernel, first, begin, count), in_s...]
  transfers between devices with their start and end apart: 17 -> 17, of which waited for: 5 -> 6; matrix products, arithmetic and copies ran while one was open for 0% -> 0% of each run, Pallas kernels for 16% -> 17%
where the time goes in v8:
time: 148 us
  Pallas kernels  44.7 us (30%)
  waiting for transfers between devices  40.1 us (27%)
  blocking collectives  35.2 us (24%)
  starting transfers between devices  25.7 us (17%)
  between operations  1.72 us (1%)
    all_to_all x1, blocking collectives, body(): out = lax.all_to_all(out.reshape(128, 24, 128), AXES, 0, 0, tiled=True)  35.2 us
    all_to_all x1, waiting for transfers between devices, body(): lax.all_to_all(chunks.reshape(128, 24, 128), AXES, 0, 0, tiled=True)  24.1 us
    pallas_call x5, Pallas kernels, sweep(): pl.pallas_call(functools.partial(sweep_kernel, first, begin, count), in_s...  17.2 us
    ppermute x16, waiting for transfers between devices, from_neighbour(): return lax.ppermute(payload, AXES, pairs)  16 us
    ppermute x16, starting transfers between devices, from_neighbour(): return lax.ppermute(payload, AXES, pairs)  14.2 us
    all_to_all x1, starting transfers between devices, body(): lax.all_to_all(chunks.reshape(128, 24, 128), AXES, 0, 0, tiled=True)  11.5 us
    pallas_call x3, Pallas kernels, chain(): pl.pallas_call(functools.partial(chain_kernel, first, count), in_specs=[S...  11.3 us
    pallas_call x2, Pallas kernels, pack(): pl.pallas_call(functools.partial(pack_kernel, first), in_specs=[SMEM, VME...  4.88 us
  transfers between devices with their start and end apart: 17, of which 6 were waited for; matrix products, arithmetic and copies ran while one was open for 0% of the time, Pallas kernels for 17%

profile of v8, /device:TPU:1, one launch (start us, length us, event | category | flops | bytes accessed | tf_op | source)
XLA Modules:
  0.0 147.6 jit_solution(10615005654145387943)
XLA Ops:
  0.6 4.0 %spread.1 = f32[3072,128]{1,0:T(8,128)} custom-call(f32[2,2,128,256]{3,2,1,0:T(8,128)} %bitcast.15, f32[2,2,2,128,256]{4,3,2,1,0:T(8,128)} %bitcast.14), custom_call_target="tpu_custom_call" | custom-call | tf_op jit(solution)/shard_map/spread/pallas_call | solution.py:139
  4.6 11.5 %all-to-all-start = ((f32[128,24,128]{2,1,0:T(8,128)}), f32[128,24,128]{2,1,0:T(8,128)S(1)}, u32[]{:S(2)}, u32[]{:S(2)}) async-start(f32[128,24,128]{2,1,0:T(8,128)} %bitcast.13), calls=%async_computation | async-start | bytes 3145728 | tf_op jit(solution)/shard_map/all_to_all | solution.py:566
  17.0 24.1 %all-to-all-done = f32[128,24,128]{2,1,0:T(8,128)S(1)} async-done(((f32[128,24,128]{2,1,0:T(8,128)}), f32[128,24,128]{2,1,0:T(8,128)S(1)}, u32[]{:S(2)}, u32[]{:S(2)}) %all-to-all-start) | async-done | bytes 1572896 | tf_op jit(solution)/shard_map/all_to_all | solution.py:566
  43.6 5.9 %collective-permute-done.1.refs_3_ = f32[2,6,6,8,128]{4,3,2,1,0:T(8,128)S(1)} collective-permute-done((f32[2,6,6,8,128]{4,3,2,1,0:T(8,128)S(1)}, f32[2,6,6,8,128]{4,3,2,1,0:T(8,128)S(1)}, u32[]{:S(2)}, u32[]{:S(2)}) %collective-permute-start.1) | collective-permute-done | bytes 294944 | tf_op jit(solution)/shard_map/ppermute | solution.py:240
  51.4 1.7 %collective-permute-start.5 = (f32[4,6,6,8,128]{4,3,2,1,0:T(8,128)S(1)}, f32[4,6,6,8,128]{4,3,2,1,0:T(8,128)S(1)}, u32[]{:S(2)}, u32[]{:S(2)}) collective-permute-start(f32[4,6,6,8,128]{4,3,2,1,0:T(8,128)S(1)} %get-tuple-element.36.refs_0_), channel_id=1, source_target_pairs={{8,0},{40,8},{32,40},{64,32},{72,64},{104,72},{96,104},{116,96},{1... | collective-permute-start | bytes 1769480 | tf_op jit(solution)/shard_map/ppermute | solution.py:240
  54.6 5.9 %collective-permute-done.5.refs_3_ = f32[4,6,6,8,128]{4,3,2,1,0:T(8,128)S(1)} collective-permute-done((f32[4,6,6,8,128]{4,3,2,1,0:T(8,128)S(1)}, f32[4,6,6,8,128]{4,3,2,1,0:T(8,128)S(1)}, u32[]{:S(2)}, u32[]{:S(2)}) %collective-permute-start.5) | collective-permute-done | bytes 589856 | tf_op jit(solution)/shard_map/ppermute | solution.py:240
  60.5 3.1 %sweep_0.1 = (f32[3,3,2,2,8,8,128]{6,5,4,3,2,1,0:T(8,128)S(1)}, f32[2,2,8,8,128]{4,3,2,1,0:T(8,128)S(1)}) custom-call(s32[5]{0:T(128)S(1)} %pad_add_fusion.scalars, f32[4,6,6,8,128]{4,3,2,1,0:T(8,128)S(1)} %get-tuple-element.36.refs_0_, f32[4,6,6,8,128]{4,3,2,1,0:T(8,128)S(1)} %get-tuple-element.37.refs_1_, ...), custom_call_target="tpu_custom_call" | custom-call | flops 19660800 | bytes 3600000 | tf_op jit(solution)/shard_map/sweep_0/pallas_call | solution.py:392
  63.6 1.8 %collective-permute-done.3.refs_3_ = f32[2,10,6,8,128]{4,3,2,1,0:T(8,128)S(1)} collective-permute-done((f32[2,10,6,8,128]{4,3,2,1,0:T(8,128)S(1)}, f32[2,10,6,8,128]{4,3,2,1,0:T(8,128)S(1)}, u32[]{:S(2)}, u32[]{:S(2)}) %collective-permute-start.3) | collective-permute-done | bytes 491552 | tf_op jit(solution)/shard_map/ppermute | solution.py:240
  65.4 1.6 %collective-permute-done.2.refs_2_ = f32[2,10,6,8,128]{4,3,2,1,0:T(8,128)S(1)} collective-permute-done((f32[2,10,6,8,128]{4,3,2,1,0:T(8,128)S(1)}, f32[2,10,6,8,128]{4,3,2,1,0:T(8,128)S(1)}, u32[]{:S(2)}, u32[]{:S(2)}) %collective-permute-start.2) | collective-permute-done | bytes 491552 | tf_op jit(solution)/shard_map/ppermute | solution.py:240
  67.0 1.7 %columns.5 = (f32[4,10,6,8,128]{4,3,2,1,0:T(8,128)S(1)}, f32[4,10,6,8,128]{4,3,2,1,0:T(8,128)S(1)}) custom-call(f32[2,10,6,8,128]{4,3,2,1,0:T(8,128)S(1)} %get-tuple-element.34.refs_0_, f32[2,10,6,8,128]{4,3,2,1,0:T(8,128)S(1)} %get-tuple-element.35.refs_1_, f32[2,10,6,8,128]{4,3,2,1,0:T(8,128)S(1)} %collective-permute-done.2.refs_2_, ...), custom_call_target="tpu_custom_call" | custom-call | bytes 8000000 | tf_op jit(solution)/shard_map/columns/pallas_call | solution.py:268
  70.3 3.3 %sweep_3.1 = (f32[3,3,2,2,8,8,128]{6,5,4,3,2,1,0:T(8,128)S(1)}, f32[2,2,8,8,128]{4,3,2,1,0:T(8,128)}) custom-call(s32[5]{0:T(128)S(1)} %pad_add_fusion.scalars, f32[4,6,6,8,128]{4,3,2,1,0:T(8,128)S(1)} %get-tuple-element.36.refs_0_, f32[4,6,6,8,128]{4,3,2,1,0:T(8,128)S(1)} %get-tuple-element.37.refs_1_, ...), custom_call_target="tpu_custom_call" | custom-call | flops 19660800 | bytes 3600000 | tf_op jit(solution)/shard_map/sweep_3/pallas_call | solution.py:392
  73.6 3.4 %chain_0.1 = (f32[6,3,2,2,8,8,128]{6,5,4,3,2,1,0:T(8,128)S(1)}, f32[2,1,6,8,128]{4,3,2,1,0:T(8,128)S(1)}, f32[2,1,6,8,128]{4,3,2,1,0:T(8,128)S(1)}) custom-call(s32[5]{0:T(128)S(1)} %pad_add_fusion.scalars, f32[3,3,2,2,8,8,128]{6,5,4,3,2,1,0:T(8,128)S(1)} %get-tuple-element.38.refs_4_.refs_0_, f32[3,3,2,2,8,8,128]{6,5,4,3,2,1,0:T(8,128)S(1)} %get-tuple-element.41.refs_1_, ...), custom_call_target="tpu_custom_call" | custom-call | flops 23592960 | bytes 3000000 | tf_op jit(solution)/shard_map/chain_0/pallas_call | solution.py:550
  77.4 1.2 collective-permute-start.8
  78.6 2.4 %pack_0.1.refs_4_.refs_0_ = f32[3072,128]{1,0:T(8,128)S(1)} custom-call(s32[5]{0:T(128)S(1)} %pad_add_fusion.scalars, f32[6,3,2,2,8,8,128]{6,5,4,3,2,1,0:T(8,128)S(1)} %get-tuple-element.45.raw, f32[2,1,6,8,128]{4,3,2,1,0:T(8,128)S(1)} %get-tuple-element.43.refs_0_, f32[2,1,6,8,128]{4,3,2,1,0:T(8,128)S(1)} %get-tuple-element.44.refs_1_), custom_call_target="tpu_custom_call" | custom-call | flops 6000000 | bytes 3000000 | tf_op jit(solution)/shard_map/pack_0/pallas_call | solution.py:433
  82.7 6.0 %sweep_6.1 = (f32[6,3,2,2,8,8,128]{6,5,4,3,2,1,0:T(8,128)S(1)}, f32[2,2,8,8,128]{4,3,2,1,0:T(8,128)}) custom-call(s32[5]{0:T(128)S(1)} %pad_add_fusion.scalars, f32[4,10,6,8,128]{4,3,2,1,0:T(8,128)S(1)} %get-tuple-element.39.refs_4_.refs_0_, f32[4,10,6,8,128]{4,3,2,1,0:T(8,128)S(1)} %get-tuple-element.40.refs_5_.refs_1_, ...), custom_call_target="tpu_custom_call" | custom-call | flops 39321600 | bytes 7200000 | tf_op jit(solution)/shard_map/sweep_6/pallas_call | solution.py:392
  88.7 3.4 %chain_6.1 = (f32[6,3,2,2,8,8,128]{6,5,4,3,2,1,0:T(8,128)S(1)}, f32[2,1,6,8,128]{4,3,2,1,0:T(8,128)S(1)}, f32[2,1,6,8,128]{4,3,2,1,0:T(8,128)S(1)}) custom-call(s32[5]{0:T(128)S(1)} %pad_add_fusion.scalars, f32[6,3,2,2,8,8,128]{6,5,4,3,2,1,0:T(8,128)S(1)} %get-tuple-element.48.refs_0_, f32[4,1,6,8,128]{4,3,2,1,0:T(8,128)S(1)} %get-tuple-element.46.refs_4_.refs_1_, ...), custom_call_target="tpu_custom_call" | custom-call | flops 23592960 | bytes 3000000 | tf_op jit(solution)/shard_map/chain_6/pallas_call | solution.py:550
  92.4 1.2 collective-permute-start.12
  93.6 2.4 %sweep_12.1 = (f32[2,3,2,2,8,8,128]{6,5,4,3,2,1,0:T(8,128)S(1)}, f32[2,2,8,8,128]{4,3,2,1,0:T(8,128)}) custom-call(s32[5]{0:T(128)S(1)} %pad_add_fusion.scalars, f32[4,10,6,8,128]{4,3,2,1,0:T(8,128)S(1)} %get-tuple-element.39.refs_4_.refs_0_, f32[4,10,6,8,128]{4,3,2,1,0:T(8,128)S(1)} %get-tuple-element.40.refs_5_.refs_1_, ...), custom_call_target="tpu_custom_call" | custom-call | flops 13107200 | bytes 2400000 | tf_op jit(solution)/shard_map/sweep_12/pallas_call | solution.py:392
  96.2 3.3 %collective-permute-start.15 = (f32[4,1,6,8,128]{4,3,2,1,0:T(8,128)S(1)}, f32[4,1,6,8,128]{4,3,2,1,0:T(8,128)S(1)}, u32[]{:S(2)}, u32[]{:S(2)}) collective-permute-start(f32[4,1,6,8,128]{4,3,2,1,0:T(8,128)S(1)} %get-tuple-element.52.refs_4_.refs_1_.refs_2_), channel_id=1, source_target_pairs={{8,0},{40,8},{32,40},{64,32},{72,64},{104,72},{96,104},{116,96},{1... | collective-permute-start | bytes 294920 | tf_op jit(solution)/shard_map/ppermute | solution.py:240
  99.5 2.5 %pack_6.1.refs_6_ = f32[3072,128]{1,0:T(8,128)S(1)} custom-call(s32[5]{0:T(128)S(1)} %pad_add_fusion.scalars, f32[6,3,2,2,8,8,128]{6,5,4,3,2,1,0:T(8,128)S(1)} %get-tuple-element.55.raw, f32[3072,128]{1,0:T(8,128)S(1)} %pack_0.1.refs_4_.refs_0_, f32[4,1,6,8,128]{4,3,2,1,0:T(8,128)S(1)} %get-tuple-element.52.refs_4_.refs_1_.refs_2_, ...), custom_call_target="tpu_custom_call" | custom-call | flops 6000000 | bytes 3000000 | tf_op jit(solution)/shard_map/pack_6/pallas_call | solution.py:433
  102.0 2.4 %sweep_14.1 = (f32[2,3,2,2,8,8,128]{6,5,4,3,2,1,0:T(8,128)S(1)}, f32[2,2,8,8,128]{4,3,2,1,0:T(8,128)}) custom-call(s32[5]{0:T(128)S(1)} %pad_add_fusion.scalars, f32[4,10,6,8,128]{4,3,2,1,0:T(8,128)S(1)} %get-tuple-element.39.refs_4_.refs_0_, f32[4,10,6,8,128]{4,3,2,1,0:T(8,128)S(1)} %get-tuple-element.40.refs_5_.refs_1_, ...), custom_call_target="tpu_custom_call" | custom-call | flops 13107200 | bytes 2400000 | tf_op jit(solution)/shard_map/sweep_14/pallas_call | solution.py:392
  104.4 4.5 %chain_12.1 = f32[3072,128]{1,0:T(8,128)S(1)} custom-call(s32[5]{0:T(128)S(1)} %pad_add_fusion.scalars, f32[2,3,2,2,8,8,128]{6,5,4,3,2,1,0:T(8,128)S(1)} %get-tuple-element.51.refs_4_.refs_0_, f32[2,3,2,2,8,8,128]{6,5,4,3,2,1,0:T(8,128)S(1)} %get-tuple-element.54.refs_1_, f32[4,1,6,8,128]{4,3,2,1,0:T(8,128)S(1)} %get-tuple-element.52.refs_4_.refs_1_.refs_2_, ...), custom_call_target="tpu_custom_call" | custom-call | flops 15728640 | bytes 2000000 | tf_op jit(solution)/shard_map/chain_12/pallas_call | solution.py:550
  108.9 35.2 %all_to_all.10 = f32[128,24,128]{2,1,0:T(8,128)S(1)} all-to-all(f32[128,24,128]{2,1,0:T(8,128)S(1)} %bitcast.12), channel_id=1, replica_groups=mesh['tm'=16,'space'=8] {'tm','space'}, dimensions={0} | all-to-all | bytes 3145728 | tf_op jit(solution)/shard_map/all_to_all | solution.py:594
  144.1 3.3 %collect.1 = (f32[2,2,128,256]{3,2,1,0:T(8,128)}, f32[2,2,2,128,256]{4,3,2,1,0:T(8,128)}) custom-call(f32[3072,128]{1,0:T(8,128)S(1)} %bitcast.11), custom_call_target="tpu_custom_call" | custom-call | tf_op jit(solution)/shard_map/collect/pallas_call | solution.py:197
  (31 shorter events, 10.1 us)
Async XLA Ops:
  4.6 12.3 %copy-start = (s32[2]{0:T(128)S(1)}, s32[2]{0:T(128)}, u32[]{:S(2)}) copy-start(s32[2]{0:T(128)} %param.7) | copy-start | bytes 28
  4.6 36.4 %all-to-all-start = ((f32[128,24,128]{2,1,0:T(8,128)}), f32[128,24,128]{2,1,0:T(8,128)S(1)}, u32[]{:S(2)}, u32[]{:S(2)}) async-start(f32[128,24,128]{2,1,0:T(8,128)} %bitcast.13), calls=%async_computation | async-start | bytes 3145728 | tf_op jit(solution)/shard_map/all_to_all | solution.py:566
  42.0 7.4 %collective-permute-start.1 = (f32[2,6,6,8,128]{4,3,2,1,0:T(8,128)S(1)}, f32[2,6,6,8,128]{4,3,2,1,0:T(8,128)S(1)}, u32[]{:S(2)}, u32[]{:S(2)}) collective-permute-start(f32[2,6,6,8,128]{4,3,2,1,0:T(8,128)S(1)} %get-tuple-element.30.refs_0_), channel_id=1, source_target_pairs={{1,0},{9,8},{41,40},{33,32},{65,64},{73,72},{105,104},{97,96},{117... | collective-permute-start | bytes 884744 | tf_op jit(solution)/shard_map/ppermute | solution.py:240
  42.6 7.8 %collective-permute-start = (f32[2,6,6,8,128]{4,3,2,1,0:T(8,128)S(1)}, f32[2,6,6,8,128]{4,3,2,1,0:T(8,128)S(1)}, u32[]{:S(2)}, u32[]{:S(2)}) collective-permute-start(f32[2,6,6,8,128]{4,3,2,1,0:T(8,128)S(1)} %get-tuple-element.31.refs_1_), channel_id=1, source_target_pairs={{4,0},{12,8},{44,40},{36,32},{68,64},{76,72},{108,104},{100,96},{1... | collective-permute-start | bytes 884744 | tf_op jit(solution)/shard_map/ppermute | solution.py:240
  51.4 9.1 %collective-permute-start.5 = (f32[4,6,6,8,128]{4,3,2,1,0:T(8,128)S(1)}, f32[4,6,6,8,128]{4,3,2,1,0:T(8,128)S(1)}, u32[]{:S(2)}, u32[]{:S(2)}) collective-permute-start(f32[4,6,6,8,128]{4,3,2,1,0:T(8,128)S(1)} %get-tuple-element.36.refs_0_), channel_id=1, source_target_pairs={{8,0},{40,8},{32,40},{64,32},{72,64},{104,72},{96,104},{116,96},{1... | collective-permute-start | bytes 1769480 | tf_op jit(solution)/shard_map/ppermute | solution.py:240
  53.1 7.4 %collective-permute-start.4 = (f32[4,6,6,8,128]{4,3,2,1,0:T(8,128)S(1)}, f32[4,6,6,8,128]{4,3,2,1,0:T(8,128)S(1)}, u32[]{:S(2)}, u32[]{:S(2)}) collective-permute-start(f32[4,6,6,8,128]{4,3,2,1,0:T(8,128)S(1)} %get-tuple-element.37.refs_1_), channel_id=1, source_target_pairs={{20,0},{0,8},{8,40},{40,32},{32,64},{64,72},{72,104},{104,96},{96,... | collective-permute-start | bytes 1769480 | tf_op jit(solution)/shard_map/ppermute | solution.py:240
  53.1 12.3 %collective-permute-start.3 = (f32[2,10,6,8,128]{4,3,2,1,0:T(8,128)S(1)}, f32[2,10,6,8,128]{4,3,2,1,0:T(8,128)S(1)}, u32[]{:S(2)}, u32[]{:S(2)}) collective-permute-start(f32[2,10,6,8,128]{4,3,2,1,0:T(8,128)S(1)} %get-tuple-element.34.refs_0_), channel_id=1, source_target_pairs={{1,0},{9,8},{41,40},{33,32},{65,64},{73,72},{105,104},{97,96},{117... | collective-permute-start | bytes 1474568 | tf_op jit(solution)/shard_map/ppermute | solution.py:240
  54.3 12.7 %collective-permute-start.2 = (f32[2,10,6,8,128]{4,3,2,1,0:T(8,128)S(1)}, f32[2,10,6,8,128]{4,3,2,1,0:T(8,128)S(1)}, u32[]{:S(2)}, u32[]{:S(2)}) collective-permute-start(f32[2,10,6,8,128]{4,3,2,1,0:T(8,128)S(1)} %get-tuple-element.35.refs_1_), channel_id=1, source_target_pairs={{4,0},{12,8},{44,40},{36,32},{68,64},{76,72},{108,104},{100,96},{1... | collective-permute-start | bytes 1474568 | tf_op jit(solution)/shard_map/ppermute | solution.py:240
  68.7 14.0 %collective-permute-start.7 = (f32[4,10,6,8,128]{4,3,2,1,0:T(8,128)S(1)}, f32[4,10,6,8,128]{4,3,2,1,0:T(8,128)S(1)}, u32[]{:S(2)}, u32[]{:S(2)}) collective-permute-start(f32[4,10,6,8,128]{4,3,2,1,0:T(8,128)S(1)} %get-tuple-element.39.refs_4_.refs_0_), channel_id=1, source_target_pairs={{8,0},{40,8},{32,40},{64,32},{72,64},{104,72},{96,104},{116,96},{1... | collective-permute-start | bytes 2949128 | tf_op jit(solution)/shard_map/ppermute | solution.py:240
  69.8 12.9 %collective-permute-start.6 = (f32[4,10,6,8,128]{4,3,2,1,0:T(8,128)S(1)}, f32[4,10,6,8,128]{4,3,2,1,0:T(8,128)S(1)}, u32[]{:S(2)}, u32[]{:S(2)}) collective-permute-start(f32[4,10,6,8,128]{4,3,2,1,0:T(8,128)S(1)} %get-tuple-element.40.refs_5_.refs_1_), channel_id=1, source_target_pairs={{20,0},{0,8},{8,40},{40,32},{32,64},{64,72},{72,104},{104,96},{96,... | collective-permute-start | bytes 2949128 | tf_op jit(solution)/shard_map/ppermute | solution.py:240
  77.0 3.9 %collective-permute-start.9 = (f32[2,1,6,8,128]{4,3,2,1,0:T(8,128)S(1)}, f32[2,1,6,8,128]{4,3,2,1,0:T(8,128)S(1)}, u32[]{:S(2)}, u32[]{:S(2)}) collective-permute-start(f32[2,1,6,8,128]{4,3,2,1,0:T(8,128)S(1)} %get-tuple-element.43.refs_0_), channel_id=1, source_target_pairs={{1,0},{9,8},{41,40},{33,32},{65,64},{73,72},{105,104},{97,96},{117... | collective-permute-start | bytes 147464 | tf_op jit(solution)/shard_map/ppermute | solution.py:240
  77.4 3.6 %collective-permute-start.8 = (f32[2,1,6,8,128]{4,3,2,1,0:T(8,128)S(1)}, f32[2,1,6,8,128]{4,3,2,1,0:T(8,128)S(1)}, u32[]{:S(2)}, u32[]{:S(2)}) collective-permute-start(f32[2,1,6,8,128]{4,3,2,1,0:T(8,128)S(1)} %get-tuple-element.44.refs_1_), channel_id=1, source_target_pairs={{4,0},{12,8},{44,40},{36,32},{68,64},{76,72},{108,104},{100,96},{1... | collective-permute-start | bytes 147464 | tf_op jit(solution)/shard_map/ppermute | solution.py:240
  81.1 7.6 %collective-permute-start.11 = (f32[4,1,6,8,128]{4,3,2,1,0:T(8,128)S(1)}, f32[4,1,6,8,128]{4,3,2,1,0:T(8,128)S(1)}, u32[]{:S(2)}, u32[]{:S(2)}) collective-permute-start(f32[4,1,6,8,128]{4,3,2,1,0:T(8,128)S(1)} %get-tuple-element.46.refs_4_.refs_1_), channel_id=1, source_target_pairs={{8,0},{40,8},{32,40},{64,32},{72,64},{104,72},{96,104},{116,96},{1... | collective-permute-start | bytes 294920 | tf_op jit(solution)/shard_map/ppermute | solution.py:240
  82.0 6.8 %collective-permute-start.10 = (f32[4,1,6,8,128]{4,3,2,1,0:T(8,128)S(1)}, f32[4,1,6,8,128]{4,3,2,1,0:T(8,128)S(1)}, u32[]{:S(2)}, u32[]{:S(2)}) collective-permute-start(f32[4,1,6,8,128]{4,3,2,1,0:T(8,128)S(1)} %get-tuple-element.47.refs_5_.refs_2_), channel_id=1, source_target_pairs={{20,0},{0,8},{8,40},{40,32},{32,64},{64,72},{72,104},{104,96},{96,... | collective-permute-start | bytes 294920 | tf_op jit(solution)/shard_map/ppermute | solution.py:240
  92.1 3.9 %collective-permute-start.13 = (f32[2,1,6,8,128]{4,3,2,1,0:T(8,128)S(1)}, f32[2,1,6,8,128]{4,3,2,1,0:T(8,128)S(1)}, u32[]{:S(2)}, u32[]{:S(2)}) collective-permute-start(f32[2,1,6,8,128]{4,3,2,1,0:T(8,128)S(1)} %get-tuple-element.49.refs_4_.refs_0_), channel_id=1, source_target_pairs={{1,0},{9,8},{41,40},{33,32},{65,64},{73,72},{105,104},{97,96},{117... | collective-permute-start | bytes 147464 | tf_op jit(solution)/shard_map/ppermute | solution.py:240
  92.4 3.6 %collective-permute-start.12 = (f32[2,1,6,8,128]{4,3,2,1,0:T(8,128)S(1)}, f32[2,1,6,8,128]{4,3,2,1,0:T(8,128)S(1)}, u32[]{:S(2)}, u32[]{:S(2)}) collective-permute-start(f32[2,1,6,8,128]{4,3,2,1,0:T(8,128)S(1)} %get-tuple-element.50.refs_5_.refs_1_), channel_id=1, source_target_pairs={{4,0},{12,8},{44,40},{36,32},{68,64},{76,72},{108,104},{100,96},{1... | collective-permute-start | bytes 147464 | tf_op jit(solution)/shard_map/ppermute | solution.py:240
  96.2 8.2 %collective-permute-start.15 = (f32[4,1,6,8,128]{4,3,2,1,0:T(8,128)S(1)}, f32[4,1,6,8,128]{4,3,2,1,0:T(8,128)S(1)}, u32[]{:S(2)}, u32[]{:S(2)}) collective-permute-start(f32[4,1,6,8,128]{4,3,2,1,0:T(8,128)S(1)} %get-tuple-element.52.refs_4_.refs_1_.refs_2_), channel_id=1, source_target_pairs={{8,0},{40,8},{32,40},{64,32},{72,64},{104,72},{96,104},{116,96},{1... | collective-permute-start | bytes 294920 | tf_op jit(solution)/shard_map/ppermute | solution.py:240
  99.5 4.9 %collective-permute-start.14 = (f32[4,1,6,8,128]{4,3,2,1,0:T(8,128)S(1)}, f32[4,1,6,8,128]{4,3,2,1,0:T(8,128)S(1)}, u32[]{:S(2)}, u32[]{:S(2)}) collective-permute-start(f32[4,1,6,8,128]{4,3,2,1,0:T(8,128)S(1)} %get-tuple-element.53.refs_5_.refs_2_.refs_3_), channel_id=1, source_target_pairs={{20,0},{0,8},{8,40},{40,32},{32,64},{64,72},{72,104},{104,96},{96,... | collective-permute-start | bytes 294920 | tf_op jit(solution)/shard_map/ppermute | solution.py:240

commit v9 on v8

--- a/solution.py
+++ b/solution.py
@@ -330,7 +330,10 @@
         reaction = (1.0 - p) * (v * v)
         rate_p = 0.2 * around_p + (reaction - 1.24 * p)
         rate_v = 0.1 * around_v + (reaction - 0.7 * v)
-        return (jnp.where(self.inside, rate_p, 0.0), jnp.where(self.inside, rate_v, 0.0)), (p, v)
+        return (rate_p, rate_v), (p, v)
+
+    def within(self, v):
+        return jnp.where(self.inside, v, 0.0)
 
 
 CELLS = [(xp, ys) for ys in range(8) for xp in range(2)]
@@ -363,7 +366,7 @@
             f1, _ = tile.tendency(reader(old, 1), xp, ys)
             f2, _ = tile.tendency(reader(old, 2), xp, ys)
             for f in range(2):
-                one[f, xp, ys] = y0[f] + (5 * H / 24) * f0[f] + ((H / 3) * f1[f] - (H / 24) * f2[f])
+                one[f, xp, ys] = tile.within(y0[f] + (5 * H / 24) * f0[f] + ((H / 3) * f1[f] - (H / 24) * f2[f]))
                 base[f, xp, ys] = (H / 6) * (f1[f] + f2[f]) - (5 * H / 6) * f0[f]
                 ahead[f, xp, ys] = y0[f] + H * f0[f]
         for xp, ys in CELLS:
@@ -371,7 +374,7 @@
             for f in range(2):
                 correction = base[f, xp, ys] + (H / 2) * r1[f]
                 base[f, xp, ys] = correction
-                two[f, xp, ys] = ahead[f, xp, ys] + correction
+                two[f, xp, ys] = tile.within(ahead[f, xp, ys] + correction)
                 rate[f, xp, ys] = r1[f]
         for xp, ys in CELLS:
             r2, _ = tile.tendency(reader(two), xp, ys)
@@ -468,15 +471,15 @@
             fl, l = tile.tendency(reader(late), xp, ys)
             f0, y0 = tile.tendency(reader(z), xp, ys)
             for f in range(2):
-                next_late[f, xp, ys] = jnp.where(reset, y0[f], l[f] + H * fl[f] + corr[f, xp, ys])
+                next_late[f, xp, ys] = jnp.where(reset, y0[f], tile.within(l[f] + H * fl[f] + corr[f, xp, ys]))
                 g = y0[f] + H * f0[f]
                 ahead[f, xp, ys] = g
                 if final:
-                    one[f, xp, ys] = y0[f] + (H / 2) * f0[f]
+                    one[f, xp, ys] = tile.within(y0[f] + (H / 2) * f0[f])
                     two[f, xp, ys] = (-H / 2) * f0[f]
                 else:
-                    next_z[f, xp, ys] = g + sweeps[j, 0, f, xp, ys]
-                    one[f, xp, ys] = y0[f] + (5 * H / 24) * f0[f] + sweeps[j, 1, f, xp, ys]
+                    next_z[f, xp, ys] = tile.within(g + sweeps[j, 0, f, xp, ys])
+                    one[f, xp, ys] = tile.within(y0[f] + (5 * H / 24) * f0[f] + sweeps[j, 1, f, xp, ys])
                     two[f, xp, ys] = sweeps[j, 2, f, xp, ys] - (5 * H / 6) * f0[f]
         for xp, ys in CELLS:
             f1, _ = tile.tendency(reader(one), xp, ys)

time: 148 us -> 148 us (level)
  no operation moved by 1% of the time
where the time goes in v9:
time: 148 us
  Pallas kernels  44.9 us (30%)
  waiting for transfers between devices  40.1 us (27%)
  blocking collectives  35.3 us (24%)
  starting transfers between devices  25.7 us (17%)
  between operations  1.71 us (1%)
    all_to_all x1, blocking collectives, body(): out = lax.all_to_all(out.reshape(128, 24, 128), AXES, 0, 0, tiled=True)  35.3 us
    all_to_all x1, waiting for transfers between devices, body(): lax.all_to_all(chunks.reshape(128, 24, 128), AXES, 0, 0, tiled=True)  24.1 us
    pallas_call x5, Pallas kernels, sweep(): pl.pallas_call(functools.partial(sweep_kernel, first, begin, count), in_s...  17.2 us
    ppermute x16, waiting for transfers between devices, from_neighbour(): return lax.ppermute(payload, AXES, pairs)  16 us
    ppermute x16, starting transfers between devices, from_neighbour(): return lax.ppermute(payload, AXES, pairs)  14.2 us
    all_to_all x1, starting transfers between devices, body(): lax.all_to_all(chunks.reshape(128, 24, 128), AXES, 0, 0, tiled=True)  11.5 us
    pallas_call x3, Pallas kernels, chain(): pl.pallas_call(functools.partial(chain_kernel, first, count), in_specs=[S...  11.5 us
    pallas_call x2, Pallas kernels, pack(): pl.pallas_call(functools.partial(pack_kernel, first), in_specs=[SMEM, VME...  4.88 us
  transfers between devices with their start and end apart: 17, of which 6 were waited for; matrix products, arithmetic and copies ran while one was open for 0% of the time, Pallas kernels for 17%

profile of v9, /device:TPU:1, one launch (start us, length us, event | category | flops | bytes accessed | tf_op | source)
XLA Modules:
  0.0 147.8 jit_solution(8951642379700117859)
XLA Ops:
  0.6 4.0 %spread.1 = f32[3072,128]{1,0:T(8,128)} custom-call(f32[2,2,128,256]{3,2,1,0:T(8,128)} %bitcast.15, f32[2,2,2,128,256]{4,3,2,1,0:T(8,128)} %bitcast.14), custom_call_target="tpu_custom_call" | custom-call | tf_op jit(solution)/shard_map/spread/pallas_call | solution.py:139
  4.6 11.5 %all-to-all-start = ((f32[128,24,128]{2,1,0:T(8,128)}), f32[128,24,128]{2,1,0:T(8,128)S(1)}, u32[]{:S(2)}, u32[]{:S(2)}) async-start(f32[128,24,128]{2,1,0:T(8,128)} %bitcast.13), calls=%async_computation | async-start | bytes 3145728 | tf_op jit(solution)/shard_map/all_to_all | solution.py:569
  17.0 24.1 %all-to-all-done = f32[128,24,128]{2,1,0:T(8,128)S(1)} async-done(((f32[128,24,128]{2,1,0:T(8,128)}), f32[128,24,128]{2,1,0:T(8,128)S(1)}, u32[]{:S(2)}, u32[]{:S(2)}) %all-to-all-start) | async-done | bytes 1572896 | tf_op jit(solution)/shard_map/all_to_all | solution.py:569
  43.6 5.9 %collective-permute-done.1.refs_3_ = f32[2,6,6,8,128]{4,3,2,1,0:T(8,128)S(1)} collective-permute-done((f32[2,6,6,8,128]{4,3,2,1,0:T(8,128)S(1)}, f32[2,6,6,8,128]{4,3,2,1,0:T(8,128)S(1)}, u32[]{:S(2)}, u32[]{:S(2)}) %collective-permute-start.1) | collective-permute-done | bytes 294944 | tf_op jit(solution)/shard_map/ppermute | solution.py:240
  51.4 1.7 %collective-permute-start.5 = (f32[4,6,6,8,128]{4,3,2,1,0:T(8,128)S(1)}, f32[4,6,6,8,128]{4,3,2,1,0:T(8,128)S(1)}, u32[]{:S(2)}, u32[]{:S(2)}) collective-permute-start(f32[4,6,6,8,128]{4,3,2,1,0:T(8,128)S(1)} %get-tuple-element.36.refs_0_), channel_id=1, source_target_pairs={{8,0},{40,8},{32,40},{64,32},{72,64},{104,72},{96,104},{116,96},{1... | collective-permute-start | bytes 1769480 | tf_op jit(solution)/shard_map/ppermute | solution.py:240
  54.6 5.9 %collective-permute-done.5.refs_3_ = f32[4,6,6,8,128]{4,3,2,1,0:T(8,128)S(1)} collective-permute-done((f32[4,6,6,8,128]{4,3,2,1,0:T(8,128)S(1)}, f32[4,6,6,8,128]{4,3,2,1,0:T(8,128)S(1)}, u32[]{:S(2)}, u32[]{:S(2)}) %collective-permute-start.5) | collective-permute-done | bytes 589856 | tf_op jit(solution)/shard_map/ppermute | solution.py:240
  60.5 3.1 %sweep_0.1 = (f32[3,3,2,2,8,8,128]{6,5,4,3,2,1,0:T(8,128)S(1)}, f32[2,2,8,8,128]{4,3,2,1,0:T(8,128)S(1)}) custom-call(s32[5]{0:T(128)S(1)} %pad_add_fusion.scalars, f32[4,6,6,8,128]{4,3,2,1,0:T(8,128)S(1)} %get-tuple-element.36.refs_0_, f32[4,6,6,8,128]{4,3,2,1,0:T(8,128)S(1)} %get-tuple-element.37.refs_1_, ...), custom_call_target="tpu_custom_call" | custom-call | flops 19660800 | bytes 3600000 | tf_op jit(solution)/shard_map/sweep_0/pallas_call | solution.py:395
  63.6 1.8 %collective-permute-done.3.refs_3_ = f32[2,10,6,8,128]{4,3,2,1,0:T(8,128)S(1)} collective-permute-done((f32[2,10,6,8,128]{4,3,2,1,0:T(8,128)S(1)}, f32[2,10,6,8,128]{4,3,2,1,0:T(8,128)S(1)}, u32[]{:S(2)}, u32[]{:S(2)}) %collective-permute-start.3) | collective-permute-done | bytes 491552 | tf_op jit(solution)/shard_map/ppermute | solution.py:240
  65.4 1.6 %collective-permute-done.2.refs_2_ = f32[2,10,6,8,128]{4,3,2,1,0:T(8,128)S(1)} collective-permute-done((f32[2,10,6,8,128]{4,3,2,1,0:T(8,128)S(1)}, f32[2,10,6,8,128]{4,3,2,1,0:T(8,128)S(1)}, u32[]{:S(2)}, u32[]{:S(2)}) %collective-permute-start.2) | collective-permute-done | bytes 491552 | tf_op jit(solution)/shard_map/ppermute | solution.py:240
  67.0 1.7 %columns.5 = (f32[4,10,6,8,128]{4,3,2,1,0:T(8,128)S(1)}, f32[4,10,6,8,128]{4,3,2,1,0:T(8,128)S(1)}) custom-call(f32[2,10,6,8,128]{4,3,2,1,0:T(8,128)S(1)} %get-tuple-element.34.refs_0_, f32[2,10,6,8,128]{4,3,2,1,0:T(8,128)S(1)} %get-tuple-element.35.refs_1_, f32[2,10,6,8,128]{4,3,2,1,0:T(8,128)S(1)} %collective-permute-done.2.refs_2_, ...), custom_call_target="tpu_custom_call" | custom-call | bytes 8000000 | tf_op jit(solution)/shard_map/columns/pallas_call | solution.py:268
  70.3 3.3 %sweep_3.1 = (f32[3,3,2,2,8,8,128]{6,5,4,3,2,1,0:T(8,128)S(1)}, f32[2,2,8,8,128]{4,3,2,1,0:T(8,128)}) custom-call(s32[5]{0:T(128)S(1)} %pad_add_fusion.scalars, f32[4,6,6,8,128]{4,3,2,1,0:T(8,128)S(1)} %get-tuple-element.36.refs_0_, f32[4,6,6,8,128]{4,3,2,1,0:T(8,128)S(1)} %get-tuple-element.37.refs_1_, ...), custom_call_target="tpu_custom_call" | custom-call | flops 19660800 | bytes 3600000 | tf_op jit(solution)/shard_map/sweep_3/pallas_call | solution.py:395
  73.6 3.5 %chain_0.1 = (f32[6,3,2,2,8,8,128]{6,5,4,3,2,1,0:T(8,128)S(1)}, f32[2,1,6,8,128]{4,3,2,1,0:T(8,128)S(1)}, f32[2,1,6,8,128]{4,3,2,1,0:T(8,128)S(1)}) custom-call(s32[5]{0:T(128)S(1)} %pad_add_fusion.scalars, f32[3,3,2,2,8,8,128]{6,5,4,3,2,1,0:T(8,128)S(1)} %get-tuple-element.38.refs_4_.refs_0_, f32[3,3,2,2,8,8,128]{6,5,4,3,2,1,0:T(8,128)S(1)} %get-tuple-element.41.refs_1_, ...), custom_call_target="tpu_custom_call" | custom-call | flops 23592960 | bytes 3000000 | tf_op jit(solution)/shard_map/chain_0/pallas_call | solution.py:553
  77.4 1.2 collective-permute-start.8
  78.6 2.4 %pack_0.1.refs_4_.refs_0_ = f32[3072,128]{1,0:T(8,128)S(1)} custom-call(s32[5]{0:T(128)S(1)} %pad_add_fusion.scalars, f32[6,3,2,2,8,8,128]{6,5,4,3,2,1,0:T(8,128)S(1)} %get-tuple-element.45.raw, f32[2,1,6,8,128]{4,3,2,1,0:T(8,128)S(1)} %get-tuple-element.43.refs_0_, f32[2,1,6,8,128]{4,3,2,1,0:T(8,128)S(1)} %get-tuple-element.44.refs_1_), custom_call_target="tpu_custom_call" | custom-call | flops 6000000 | bytes 3000000 | tf_op jit(solution)/shard_map/pack_0/pallas_call | solution.py:436
  82.7 6.0 %sweep_6.1 = (f32[6,3,2,2,8,8,128]{6,5,4,3,2,1,0:T(8,128)S(1)}, f32[2,2,8,8,128]{4,3,2,1,0:T(8,128)}) custom-call(s32[5]{0:T(128)S(1)} %pad_add_fusion.scalars, f32[4,10,6,8,128]{4,3,2,1,0:T(8,128)S(1)} %get-tuple-element.39.refs_4_.refs_0_, f32[4,10,6,8,128]{4,3,2,1,0:T(8,128)S(1)} %get-tuple-element.40.refs_5_.refs_1_, ...), custom_call_target="tpu_custom_call" | custom-call | flops 39321600 | bytes 7200000 | tf_op jit(solution)/shard_map/sweep_6/pallas_call | solution.py:395
  88.8 3.4 %chain_6.1 = (f32[6,3,2,2,8,8,128]{6,5,4,3,2,1,0:T(8,128)S(1)}, f32[2,1,6,8,128]{4,3,2,1,0:T(8,128)S(1)}, f32[2,1,6,8,128]{4,3,2,1,0:T(8,128)S(1)}) custom-call(s32[5]{0:T(128)S(1)} %pad_add_fusion.scalars, f32[6,3,2,2,8,8,128]{6,5,4,3,2,1,0:T(8,128)S(1)} %get-tuple-element.48.refs_0_, f32[4,1,6,8,128]{4,3,2,1,0:T(8,128)S(1)} %get-tuple-element.46.refs_4_.refs_1_, ...), custom_call_target="tpu_custom_call" | custom-call | flops 23592960 | bytes 3000000 | tf_op jit(solution)/shard_map/chain_6/pallas_call | solution.py:553
  92.5 1.2 collective-permute-start.12
  93.7 2.4 %sweep_12.1 = (f32[2,3,2,2,8,8,128]{6,5,4,3,2,1,0:T(8,128)S(1)}, f32[2,2,8,8,128]{4,3,2,1,0:T(8,128)}) custom-call(s32[5]{0:T(128)S(1)} %pad_add_fusion.scalars, f32[4,10,6,8,128]{4,3,2,1,0:T(8,128)S(1)} %get-tuple-element.39.refs_4_.refs_0_, f32[4,10,6,8,128]{4,3,2,1,0:T(8,128)S(1)} %get-tuple-element.40.refs_5_.refs_1_, ...), custom_call_target="tpu_custom_call" | custom-call | flops 13107200 | bytes 2400000 | tf_op jit(solution)/shard_map/sweep_12/pallas_call | solution.py:395
  96.3 3.2 %collective-permute-start.15 = (f32[4,1,6,8,128]{4,3,2,1,0:T(8,128)S(1)}, f32[4,1,6,8,128]{4,3,2,1,0:T(8,128)S(1)}, u32[]{:S(2)}, u32[]{:S(2)}) collective-permute-start(f32[4,1,6,8,128]{4,3,2,1,0:T(8,128)S(1)} %get-tuple-element.52.refs_4_.refs_1_.refs_2_), channel_id=1, source_target_pairs={{8,0},{40,8},{32,40},{64,32},{72,64},{104,72},{96,104},{116,96},{1... | collective-permute-start | bytes 294920 | tf_op jit(solution)/shard_map/ppermute | solution.py:240
  99.6 2.5 %pack_6.1.refs_6_ = f32[3072,128]{1,0:T(8,128)S(1)} custom-call(s32[5]{0:T(128)S(1)} %pad_add_fusion.scalars, f32[6,3,2,2,8,8,128]{6,5,4,3,2,1,0:T(8,128)S(1)} %get-tuple-element.55.raw, f32[3072,128]{1,0:T(8,128)S(1)} %pack_0.1.refs_4_.refs_0_, f32[4,1,6,8,128]{4,3,2,1,0:T(8,128)S(1)} %get-tuple-element.52.refs_4_.refs_1_.refs_2_, ...), custom_call_target="tpu_custom_call" | custom-call | flops 6000000 | bytes 3000000 | tf_op jit(solution)/shard_map/pack_6/pallas_call | solution.py:436
  102.0 2.4 %sweep_14.1 = (f32[2,3,2,2,8,8,128]{6,5,4,3,2,1,0:T(8,128)S(1)}, f32[2,2,8,8,128]{4,3,2,1,0:T(8,128)}) custom-call(s32[5]{0:T(128)S(1)} %pad_add_fusion.scalars, f32[4,10,6,8,128]{4,3,2,1,0:T(8,128)S(1)} %get-tuple-element.39.refs_4_.refs_0_, f32[4,10,6,8,128]{4,3,2,1,0:T(8,128)S(1)} %get-tuple-element.40.refs_5_.refs_1_, ...), custom_call_target="tpu_custom_call" | custom-call | flops 13107200 | bytes 2400000 | tf_op jit(solution)/shard_map/sweep_14/pallas_call | solution.py:395
  104.4 4.6 %chain_12.1 = f32[3072,128]{1,0:T(8,128)S(1)} custom-call(s32[5]{0:T(128)S(1)} %pad_add_fusion.scalars, f32[2,3,2,2,8,8,128]{6,5,4,3,2,1,0:T(8,128)S(1)} %get-tuple-element.51.refs_4_.refs_0_, f32[2,3,2,2,8,8,128]{6,5,4,3,2,1,0:T(8,128)S(1)} %get-tuple-element.54.refs_1_, f32[4,1,6,8,128]{4,3,2,1,0:T(8,128)S(1)} %get-tuple-element.52.refs_4_.refs_1_.refs_2_, ...), custom_call_target="tpu_custom_call" | custom-call | flops 15728640 | bytes 2000000 | tf_op jit(solution)/shard_map/chain_12/pallas_call | solution.py:553
  109.0 35.3 %all_to_all.10 = f32[128,24,128]{2,1,0:T(8,128)S(1)} all-to-all(f32[128,24,128]{2,1,0:T(8,128)S(1)} %bitcast.12), channel_id=1, replica_groups=mesh['tm'=16,'space'=8] {'tm','space'}, dimensions={0} | all-to-all | bytes 3145728 | tf_op jit(solution)/shard_map/all_to_all | solution.py:597
  144.3 3.3 %collect.1 = (f32[2,2,128,256]{3,2,1,0:T(8,128)}, f32[2,2,2,128,256]{4,3,2,1,0:T(8,128)}) custom-call(f32[3072,128]{1,0:T(8,128)S(1)} %bitcast.11), custom_call_target="tpu_custom_call" | custom-call | tf_op jit(solution)/shard_map/collect/pallas_call | solution.py:197
  (31 shorter events, 10.1 us)
Async XLA Ops:
  4.6 12.3 %copy-start = (s32[2]{0:T(128)S(1)}, s32[2]{0:T(128)}, u32[]{:S(2)}) copy-start(s32[2]{0:T(128)} %param.7) | copy-start | bytes 28
  4.6 36.4 %all-to-all-start = ((f32[128,24,128]{2,1,0:T(8,128)}), f32[128,24,128]{2,1,0:T(8,128)S(1)}, u32[]{:S(2)}, u32[]{:S(2)}) async-start(f32[128,24,128]{2,1,0:T(8,128)} %bitcast.13), calls=%async_computation | async-start | bytes 3145728 | tf_op jit(solution)/shard_map/all_to_all | solution.py:569
  42.0 7.4 %collective-permute-start.1 = (f32[2,6,6,8,128]{4,3,2,1,0:T(8,128)S(1)}, f32[2,6,6,8,128]{4,3,2,1,0:T(8,128)S(1)}, u32[]{:S(2)}, u32[]{:S(2)}) collective-permute-start(f32[2,6,6,8,128]{4,3,2,1,0:T(8,128)S(1)} %get-tuple-element.30.refs_0_), channel_id=1, source_target_pairs={{1,0},{9,8},{41,40},{33,32},{65,64},{73,72},{105,104},{97,96},{117... | collective-permute-start | bytes 884744 | tf_op jit(solution)/shard_map/ppermute | solution.py:240
  42.6 7.8 %collective-permute-start = (f32[2,6,6,8,128]{4,3,2,1,0:T(8,128)S(1)}, f32[2,6,6,8,128]{4,3,2,1,0:T(8,128)S(1)}, u32[]{:S(2)}, u32[]{:S(2)}) collective-permute-start(f32[2,6,6,8,128]{4,3,2,1,0:T(8,128)S(1)} %get-tuple-element.31.refs_1_), channel_id=1, source_target_pairs={{4,0},{12,8},{44,40},{36,32},{68,64},{76,72},{108,104},{100,96},{1... | collective-permute-start | bytes 884744 | tf_op jit(solution)/shard_map/ppermute | solution.py:240
  51.4 9.1 %collective-permute-start.5 = (f32[4,6,6,8,128]{4,3,2,1,0:T(8,128)S(1)}, f32[4,6,6,8,128]{4,3,2,1,0:T(8,128)S(1)}, u32[]{:S(2)}, u32[]{:S(2)}) collective-permute-start(f32[4,6,6,8,128]{4,3,2,1,0:T(8,128)S(1)} %get-tuple-element.36.refs_0_), channel_id=1, source_target_pairs={{8,0},{40,8},{32,40},{64,32},{72,64},{104,72},{96,104},{116,96},{1... | collective-permute-start | bytes 1769480 | tf_op jit(solution)/shard_map/ppermute | solution.py:240
  53.1 7.4 %collective-permute-start.4 = (f32[4,6,6,8,128]{4,3,2,1,0:T(8,128)S(1)}, f32[4,6,6,8,128]{4,3,2,1,0:T(8,128)S(1)}, u32[]{:S(2)}, u32[]{:S(2)}) collective-permute-start(f32[4,6,6,8,128]{4,3,2,1,0:T(8,128)S(1)} %get-tuple-element.37.refs_1_), channel_id=1, source_target_pairs={{20,0},{0,8},{8,40},{40,32},{32,64},{64,72},{72,104},{104,96},{96,... | collective-permute-start | bytes 1769480 | tf_op jit(solution)/shard_map/ppermute | solution.py:240
  53.1 12.3 %collective-permute-start.3 = (f32[2,10,6,8,128]{4,3,2,1,0:T(8,128)S(1)}, f32[2,10,6,8,128]{4,3,2,1,0:T(8,128)S(1)}, u32[]{:S(2)}, u32[]{:S(2)}) collective-permute-start(f32[2,10,6,8,128]{4,3,2,1,0:T(8,128)S(1)} %get-tuple-element.34.refs_0_), channel_id=1, source_target_pairs={{1,0},{9,8},{41,40},{33,32},{65,64},{73,72},{105,104},{97,96},{117... | collective-permute-start | bytes 1474568 | tf_op jit(solution)/shard_map/ppermute | solution.py:240
  54.3 12.7 %collective-permute-start.2 = (f32[2,10,6,8,128]{4,3,2,1,0:T(8,128)S(1)}, f32[2,10,6,8,128]{4,3,2,1,0:T(8,128)S(1)}, u32[]{:S(2)}, u32[]{:S(2)}) collective-permute-start(f32[2,10,6,8,128]{4,3,2,1,0:T(8,128)S(1)} %get-tuple-element.35.refs_1_), channel_id=1, source_target_pairs={{4,0},{12,8},{44,40},{36,32},{68,64},{76,72},{108,104},{100,96},{1... | collective-permute-start | bytes 1474568 | tf_op jit(solution)/shard_map/ppermute | solution.py:240
  68.7 14.0 %collective-permute-start.7 = (f32[4,10,6,8,128]{4,3,2,1,0:T(8,128)S(1)}, f32[4,10,6,8,128]{4,3,2,1,0:T(8,128)S(1)}, u32[]{:S(2)}, u32[]{:S(2)}) collective-permute-start(f32[4,10,6,8,128]{4,3,2,1,0:T(8,128)S(1)} %get-tuple-element.39.refs_4_.refs_0_), channel_id=1, source_target_pairs={{8,0},{40,8},{32,40},{64,32},{72,64},{104,72},{96,104},{116,96},{1... | collective-permute-start | bytes 2949128 | tf_op jit(solution)/shard_map/ppermute | solution.py:240
  69.8 13.0 %collective-permute-start.6 = (f32[4,10,6,8,128]{4,3,2,1,0:T(8,128)S(1)}, f32[4,10,6,8,128]{4,3,2,1,0:T(8,128)S(1)}, u32[]{:S(2)}, u32[]{:S(2)}) collective-permute-start(f32[4,10,6,8,128]{4,3,2,1,0:T(8,128)S(1)} %get-tuple-element.40.refs_5_.refs_1_), channel_id=1, source_target_pairs={{20,0},{0,8},{8,40},{40,32},{32,64},{64,72},{72,104},{104,96},{96,... | collective-permute-start | bytes 2949128 | tf_op jit(solution)/shard_map/ppermute | solution.py:240
  77.1 3.9 %collective-permute-start.9 = (f32[2,1,6,8,128]{4,3,2,1,0:T(8,128)S(1)}, f32[2,1,6,8,128]{4,3,2,1,0:T(8,128)S(1)}, u32[]{:S(2)}, u32[]{:S(2)}) collective-permute-start(f32[2,1,6,8,128]{4,3,2,1,0:T(8,128)S(1)} %get-tuple-element.43.refs_0_), channel_id=1, source_target_pairs={{1,0},{9,8},{41,40},{33,32},{65,64},{73,72},{105,104},{97,96},{117... | collective-permute-start | bytes 147464 | tf_op jit(solution)/shard_map/ppermute | solution.py:240
  77.4 3.6 %collective-permute-start.8 = (f32[2,1,6,8,128]{4,3,2,1,0:T(8,128)S(1)}, f32[2,1,6,8,128]{4,3,2,1,0:T(8,128)S(1)}, u32[]{:S(2)}, u32[]{:S(2)}) collective-permute-start(f32[2,1,6,8,128]{4,3,2,1,0:T(8,128)S(1)} %get-tuple-element.44.refs_1_), channel_id=1, source_target_pairs={{4,0},{12,8},{44,40},{36,32},{68,64},{76,72},{108,104},{100,96},{1... | collective-permute-start | bytes 147464 | tf_op jit(solution)/shard_map/ppermute | solution.py:240
  81.2 7.6 %collective-permute-start.11 = (f32[4,1,6,8,128]{4,3,2,1,0:T(8,128)S(1)}, f32[4,1,6,8,128]{4,3,2,1,0:T(8,128)S(1)}, u32[]{:S(2)}, u32[]{:S(2)}) collective-permute-start(f32[4,1,6,8,128]{4,3,2,1,0:T(8,128)S(1)} %get-tuple-element.46.refs_4_.refs_1_), channel_id=1, source_target_pairs={{8,0},{40,8},{32,40},{64,32},{72,64},{104,72},{96,104},{116,96},{1... | collective-permute-start | bytes 294920 | tf_op jit(solution)/shard_map/ppermute | solution.py:240
  82.0 6.8 %collective-permute-start.10 = (f32[4,1,6,8,128]{4,3,2,1,0:T(8,128)S(1)}, f32[4,1,6,8,128]{4,3,2,1,0:T(8,128)S(1)}, u32[]{:S(2)}, u32[]{:S(2)}) collective-permute-start(f32[4,1,6,8,128]{4,3,2,1,0:T(8,128)S(1)} %get-tuple-element.47.refs_5_.refs_2_), channel_id=1, source_target_pairs={{20,0},{0,8},{8,40},{40,32},{32,64},{64,72},{72,104},{104,96},{96,... | collective-permute-start | bytes 294920 | tf_op jit(solution)/shard_map/ppermute | solution.py:240
  92.2 3.9 %collective-permute-start.13 = (f32[2,1,6,8,128]{4,3,2,1,0:T(8,128)S(1)}, f32[2,1,6,8,128]{4,3,2,1,0:T(8,128)S(1)}, u32[]{:S(2)}, u32[]{:S(2)}) collective-permute-start(f32[2,1,6,8,128]{4,3,2,1,0:T(8,128)S(1)} %get-tuple-element.49.refs_4_.refs_0_), channel_id=1, source_target_pairs={{1,0},{9,8},{41,40},{33,32},{65,64},{73,72},{105,104},{97,96},{117... | collective-permute-start | bytes 147464 | tf_op jit(solution)/shard_map/ppermute | solution.py:240
  92.5 3.6 %collective-permute-start.12 = (f32[2,1,6,8,128]{4,3,2,1,0:T(8,128)S(1)}, f32[2,1,6,8,128]{4,3,2,1,0:T(8,128)S(1)}, u32[]{:S(2)}, u32[]{:S(2)}) collective-permute-start(f32[2,1,6,8,128]{4,3,2,1,0:T(8,128)S(1)} %get-tuple-element.50.refs_5_.refs_1_), channel_id=1, source_target_pairs={{4,0},{12,8},{44,40},{36,32},{68,64},{76,72},{108,104},{100,96},{1... | collective-permute-start | bytes 147464 | tf_op jit(solution)/shard_map/ppermute | solution.py:240
  96.3 8.1 %collective-permute-start.15 = (f32[4,1,6,8,128]{4,3,2,1,0:T(8,128)S(1)}, f32[4,1,6,8,128]{4,3,2,1,0:T(8,128)S(1)}, u32[]{:S(2)}, u32[]{:S(2)}) collective-permute-start(f32[4,1,6,8,128]{4,3,2,1,0:T(8,128)S(1)} %get-tuple-element.52.refs_4_.refs_1_.refs_2_), channel_id=1, source_target_pairs={{8,0},{40,8},{32,40},{64,32},{72,64},{104,72},{96,104},{116,96},{1... | collective-permute-start | bytes 294920 | tf_op jit(solution)/shard_map/ppermute | solution.py:240
  99.6 4.9 %collective-permute-start.14 = (f32[4,1,6,8,128]{4,3,2,1,0:T(8,128)S(1)}, f32[4,1,6,8,128]{4,3,2,1,0:T(8,128)S(1)}, u32[]{:S(2)}, u32[]{:S(2)}) collective-permute-start(f32[4,1,6,8,128]{4,3,2,1,0:T(8,128)S(1)} %get-tuple-element.53.refs_5_.refs_2_.refs_3_), channel_id=1, source_target_pairs={{20,0},{0,8},{8,40},{40,32},{32,64},{64,72},{72,104},{104,96},{96,... | collective-permute-start | bytes 294920 | tf_op jit(solution)/shard_map/ppermute | solution.py:240
